TPU v7x, 32 devices: a whole 2x2x4 slice. The times are simulated.
32 devices in a mesh: px: 4 (over z), py: 4 (over y, core), ch: 2 (over x).
Axes of the slice: x: 2, y: 2, z: 4, core: 2. Of those that a mesh axis runs over, the one named last changes fastest.
Arguments:
- features: bfloat16 [128, 12, 4, 4, 1024], P('ch', None, 'py', 'px'), may hold values from -6 to 6
- cotangent: bfloat16 [128, 12, 4, 4, 1024], P('ch', None, 'py', 'px'), may hold values from -6 to 6
- weight: bfloat16 [3, 3, 128, 128], replicated, may hold values from -0.1875 to 0.1875
- edge_table: int32 [12, 4, 3], replicated, may hold values from 0 to 11, as said below
- corner_table: int32 [12, 4, 2], replicated, may hold values from 0 to 11, as said below
Outputs:
- activation: bfloat16 [128, 12, 4, 4, 1024], P('ch', None, 'py', 'px')
- input_grad: bfloat16 [128, 12, 4, 4, 1024], P('ch', None, 'py', 'px')
Inputs may be any that keep to these rules, and one draw needn't show every extreme that they name: edge_table[f, e] = (g, s, r): beyond edge e of face f lie the pixels of side s of face g, in reverse order if r = 1; every side of every face is named exactly once, and if (f, e) names (g, s) then (g, s) names (f, e) with the same r. corner_table[f, c] = (h, q): corner c of face f takes corner pixel q of face h; in each corner column every face appears once, and each q appears 12 times.
All inputs are finite; a program needn't handle non-finite values.
Results may differ from a plain program's by a relative error of at most 0.0049.
Values may be sent and summed in bfloat16 or wider, within the bound.
No kernel may reach another device: no remote copies, remote signals or barrier semaphores. Data moves between devices by JAX's collectives and lax.ppermute only.
A program may use at most 192 MiB of HBM per device.

v0:
```python
import jax
import jax.numpy as jnp
from jax import lax
from jax.sharding import PartitionSpec as P

RB = 32


def with_halo(array, sides, width):
    for axis, dim in sides:
        size, length = (lax.axis_size(axis), array.shape[dim])
        up = [(i, (i + 1) % size) for i in range(size - 1)]
        down = [(j, i) for i, j in up]
        last = lax.slice_in_dim(array, length - width, length, axis=dim)
        leading = lax.slice_in_dim(array, 0, width, axis=dim)
        before = lax.ppermute(last, axis, up)
        after = lax.ppermute(leading, axis, down)
        array = jnp.concatenate([before, array, after], axis=dim)
    return array


def edge_strips(lines, edge_table, corner_table):
    chan_count = lines.shape[0]
    face_count = lines.shape[1]
    side_len = lines.shape[3]
    flat_lines = lines.reshape(chan_count, face_count * 4, side_len)
    pixels = jnp.stack(
        [lines[:, :, 0, 0], lines[:, :, 0, -1], lines[:, :, 1, 0], lines[:, :, 1, -1]], axis=2
    ).reshape(chan_count, face_count * 4)
    corner_index = corner_table[:, :, 0] * 4 + corner_table[:, :, 1]
    corner_vals = jnp.take(pixels, corner_index, axis=1)
    strips = []
    for edge_num, start_corner, end_corner in ((0, 0, 1), (1, 2, 3), (2, 0, 2), (3, 1, 3)):
        source_row = edge_table[:, edge_num, 0] * 4 + edge_table[:, edge_num, 1]
        strip_line = jnp.take(flat_lines, source_row, axis=1)
        flipped = (edge_table[:, edge_num, 2] == 1)[None, :, None]
        strip_line = jnp.where(flipped, strip_line[:, :, ::-1], strip_line)
        strips.append(
            jnp.concatenate(
                [
                    corner_vals[:, :, start_corner : start_corner + 1],
                    strip_line,
                    corner_vals[:, :, end_corner : end_corner + 1],
                ],
                axis=2,
            )
        )
    return strips


def face_lines_of(field, row_pos, col_pos, px_count, py_count):
    chan_block = field.shape[0]
    face_count = field.shape[1]
    col_len = field.shape[2]
    row_len = field.shape[3]
    side_len = row_len * px_count
    blank = jnp.zeros((chan_block, face_count, side_len), jnp.float32)

    def placed(values, offset, active):
        return jnp.where(
            active,
            lax.dynamic_update_slice_in_dim(blank, values.astype(jnp.float32), offset, 2),
            0.0,
        )

    contrib = jnp.stack(
        [
            placed(field[:, :, 0, :], row_pos * row_len, col_pos == 0),
            placed(field[:, :, -1, :], row_pos * row_len, col_pos == py_count - 1),
            placed(field[:, :, :, 0], col_pos * col_len, row_pos == 0),
            placed(field[:, :, :, -1], col_pos * col_len, row_pos == px_count - 1),
        ],
        axis=2,
    )
    return lax.psum(contrib.astype(jnp.bfloat16), ("px", "py"))


def pad_field(field, edge_table, corner_table):
    col_len = field.shape[2]
    row_len = field.shape[3]
    row_pos = lax.axis_index("px")
    col_pos = lax.axis_index("py")
    px_count = lax.axis_size("px")
    py_count = lax.axis_size("py")
    padded = with_halo(field, (("px", 3), ("py", 2)), 1)
    lines = face_lines_of(field, row_pos, col_pos, px_count, py_count)
    strips = edge_strips(lines, edge_table, corner_table)
    top_row = lax.dynamic_slice_in_dim(strips[0], row_pos * row_len, row_len + 2, 2)
    bottom_row = lax.dynamic_slice_in_dim(strips[1], row_pos * row_len, row_len + 2, 2)
    left_col = lax.dynamic_slice_in_dim(strips[2], col_pos * col_len, col_len + 2, 2)
    right_col = lax.dynamic_slice_in_dim(strips[3], col_pos * col_len, col_len + 2, 2)
    padded = padded.at[:, :, 0, :].set(jnp.where(col_pos == 0, top_row, padded[:, :, 0, :]))
    padded = padded.at[:, :, -1, :].set(
        jnp.where(col_pos == py_count - 1, bottom_row, padded[:, :, -1, :])
    )
    padded = padded.at[:, :, :, 0].set(jnp.where(row_pos == 0, left_col, padded[:, :, :, 0]))
    padded = padded.at[:, :, :, -1].set(
        jnp.where(row_pos == px_count - 1, right_col, padded[:, :, :, -1])
    )
    return padded


def forward_taps(padded, taps, out_cols, out_rows):
    summed = None
    for tap_row in range(3):
        for tap_col in range(3):
            window = padded[:, :, tap_row : tap_row + out_cols, tap_col : tap_col + out_rows]
            term_val = jnp.einsum(
                "oc,cfab->ofab", taps[tap_row, tap_col], window, preferred_element_type=jnp.float32
            )
            summed = term_val if summed is None else summed + term_val
    return summed


def backward_taps(padded, taps, out_cols, out_rows):
    summed = None
    for tap_row in range(3):
        for tap_col in range(3):
            window = padded[
                :, :, 2 - tap_row : 2 - tap_row + out_cols, 2 - tap_col : 2 - tap_col + out_rows
            ]
            term_val = jnp.einsum(
                "oc,ofab->cfab", taps[tap_row, tap_col], window, preferred_element_type=jnp.float32
            )
            summed = term_val if summed is None else summed + term_val
    return summed


def gate_outputs(preact, cotangent):
    sigmoid_val = jax.nn.sigmoid(preact)
    activation = (preact * sigmoid_val).astype(jnp.bfloat16)
    gated = (
        cotangent.astype(jnp.float32) * sigmoid_val * (1.0 + preact * (1.0 - sigmoid_val))
    ).astype(jnp.bfloat16)
    return (activation, gated)


def local(features, cotangent, weight, edge_table, corner_table):
    chan_block = features.shape[0]
    face_count = features.shape[1]
    tile_len = features.shape[4]
    row_len = RB
    col_len = tile_len // row_len
    features = features.reshape(chan_block, face_count, col_len, row_len)
    cotangent = cotangent.reshape(chan_block, face_count, col_len, row_len)
    ch_pos = lax.axis_index("ch")
    feat_pad = pad_field(features, edge_table, corner_table)
    own_taps = lax.dynamic_slice_in_dim(weight, ch_pos * chan_block, chan_block, 2)
    piece_taps = own_taps
    preact = forward_taps(
        lax.all_gather(feat_pad, "ch", axis=0, tiled=True), piece_taps, col_len, row_len
    )
    activation, gated = gate_outputs(preact, cotangent)
    grad_pad = pad_field(gated, edge_table, corner_table)
    input_taps = lax.dynamic_slice_in_dim(weight, ch_pos * chan_block, chan_block, 3)
    piece_taps = input_taps
    input_grad = backward_taps(
        lax.all_gather(grad_pad, "ch", axis=0, tiled=True), piece_taps, col_len, row_len
    ).astype(jnp.bfloat16)
    out_shape = (chan_block, face_count, 1, 1, tile_len)
    return (activation.reshape(out_shape), input_grad.reshape(out_shape))


def solution(mesh):
    return jax.shard_map(
        local,
        mesh=mesh,
        in_specs=(P("ch", None, "py", "px", None), P("ch", None, "py", "px", None), P(), P(), P()),
        out_specs=(P("ch", None, "py", "px", None), P("ch", None, "py", "px", None)),
        check_vma=False,
    )
```

profile of v0, /device:TPU:0, one launch (start us, length us, event | category | flops | bytes accessed | tf_op | source)
XLA Modules:
  0.0 1334.5 jit_solution(6370745873503948025)
XLA Ops:
  60.5 90.2 %all-reduce.3.cloned.1.call-done = bf16[64,12,4,128]{0,1,3,2:T(8,128)(2,1)} async-done(((bf16[64,12,4,128]{0,1,3,2:T(8,128)(2,1)}), bf16[64,12,4,128]{0,1,3,2:T(8,128)(2,1)}) %all-reduce.3.cloned.1.call-update) | async-done | bytes 786448 | tf_op jit(solution)/shard_map/psum | solution.py:75
  195.8 182.3 %all-gather.3.cloned.1.call-done = bf16[128,12,34,34]{3,2,1,0:T(8,128)(2,1)} async-done(((bf16[64,12,34,34]{3,2,1,0:T(8,128)(2,1)}), bf16[128,12,34,34]{3,2,1,0:T(8,128)(2,1)}) %all-gather.3.cloned.1.call-update) | async-done | bytes 3551248 | tf_op jit(solution)/shard_map/all_gather | solution.py:151
  378.1 96.4 %fusion.72 = (bf16[128,12,32,32]{3,2,1,0:T(8,128)(2,1)}, bf16[128,12,32,32]{3,2,1,0:T(8,128)(2,1)}, bf16[128,12,32,32]{3,2,1,0:T(8,128)(2,1)}, bf16[128,12,32,32...) fusion(bf16[128,12,34,34]{3,2,1,0:T(8,128)(2,1)} %all-gather.3., ...), kind=kLoop, calls=%fused_computation.203 | loop fusion | bytes 56623104 | tf_op jit(solution)/shard_map/slice | solution.py:107
  474.5 15.8 %copy.554 = bf16[128,12,32,32]{0,3,2,1:T(8,128)(2,1)} copy(bf16[128,12,32,32]{3,2,1,0:T(8,128)(2,1)} %get-tuple-element.143) | data formatting | bytes 6291456
  490.4 14.6 %copy.553 = bf16[128,12,32,32]{0,3,2,1:T(8,128)(2,1)S(1)} copy(bf16[128,12,32,32]{3,2,1,0:T(8,128)(2,1)} %get-tuple-element.136) | data formatting | bytes 6291456
  505.0 15.8 %copy.552 = bf16[128,12,32,32]{0,3,2,1:T(8,128)(2,1)} copy(bf16[128,12,32,32]{3,2,1,0:T(8,128)(2,1)} %get-tuple-element.137) | data formatting | bytes 6291456
  530.1 16.0 %copy.551 = bf16[128,12,32,32]{0,3,2,1:T(8,128)(2,1)} copy(bf16[128,12,32,32]{3,2,1,0:T(8,128)(2,1)} %get-tuple-element.138) | data formatting | bytes 6291456
  553.4 14.6 %copy.550 = bf16[128,12,32,32]{0,3,2,1:T(8,128)(2,1)S(1)} copy(bf16[128,12,32,32]{3,2,1,0:T(8,128)(2,1)} %get-tuple-element.139) | data formatting | bytes 6291456
  571.6 14.6 %copy.549 = bf16[128,12,32,32]{0,3,2,1:T(8,128)(2,1)S(1)} copy(bf16[128,12,32,32]{3,2,1,0:T(8,128)(2,1)} %get-tuple-element.140) | data formatting | bytes 6291456
  589.8 14.6 %copy.548 = bf16[128,12,32,32]{0,3,2,1:T(8,128)(2,1)S(1)} copy(bf16[128,12,32,32]{3,2,1,0:T(8,128)(2,1)} %get-tuple-element.141) | data formatting | bytes 6291456
  608.1 14.6 %copy.546 = bf16[128,12,32,32]{0,3,2,1:T(8,128)(2,1)S(1)} copy(bf16[128,12,32,32]{3,2,1,0:T(8,128)(2,1)} %get-tuple-element.142) | data formatting | bytes 6291456
  626.4 14.6 %copy.547 = bf16[128,12,32,32]{0,3,2,1:T(8,128)(2,1)S(1)} copy(bf16[128,12,32,32]{3,2,1,0:T(8,128)(2,1)} %get-tuple-element.135) | data formatting | bytes 6291456
  645.8 22.0 %fusion.1 = (bf16[64,12,32,32]{0,3,2,1:T(8,128)(2,1)S(1)}, f32[64,12,32,32]{0,3,2,1:T(8,128)}) fusion(bf16[64,12,32,32]{0,3,2,1:T(8,128)(2,1)} %bitcast.291, f32[64,12,32,32]{0,3,2,1:T(8,128)S(1)} %bitcast.251, f32[64,12,32,32]{0,3,2,1:T(8,128)} %bitcast.253, f32[64,12,32,32]{0,3,2,1:T(8,128)} %bitcast.252, f32[64,12,32,32]{0,3,2,1:T(8,128)} %bitcast.254, ...), kind=kLoop, calls=%fused_computation.12 | loop fusion | flops 14155776 | bytes 34603008 | tf_op jit(solution)/shard_map/convert_element_type | solution.py:134
  717.7 97.3 %all-reduce.5.cloned.1.call-done = bf16[64,12,4,128]{0,1,3,2:T(8,128)(2,1)} async-done(((bf16[64,12,4,128]{0,1,3,2:T(8,128)(2,1)}), bf16[64,12,4,128]{0,1,3,2:T(8,128)(2,1)}) %all-reduce.5.cloned.1.call-update) | async-done | bytes 786448 | tf_op jit(solution)/shard_map/psum | solution.py:75
  862.9 179.7 %all-gather.5.cloned.1.call-done = bf16[128,12,34,34]{3,2,1,0:T(8,128)(2,1)} async-done(((bf16[64,12,34,34]{3,2,1,0:T(8,128)(2,1)}), bf16[128,12,34,34]{3,2,1,0:T(8,128)(2,1)}) %all-gather.5.cloned.1.call-update) | async-done | bytes 3551248 | tf_op jit(solution)/shard_map/all_gather | solution.py:158
  1042.6 96.5 %fusion.71 = (bf16[128,12,32,32]{3,2,1,0:T(8,128)(2,1)}, bf16[128,12,32,32]{3,2,1,0:T(8,128)(2,1)}, bf16[128,12,32,32]{3,2,1,0:T(8,128)(2,1)}, bf16[128,12,32,32...) fusion(bf16[128,12,34,34]{3,2,1,0:T(8,128)(2,1)} %all-gather.5., ...), kind=kLoop, calls=%fused_computation.202 | loop fusion | bytes 56623104 | tf_op jit(solution)/shard_map/slice | solution.py:119
  1139.0 14.6 %copy.575 = bf16[128,12,32,32]{0,3,2,1:T(8,128)(2,1)S(1)} copy(bf16[128,12,32,32]{3,2,1,0:T(8,128)(2,1)} %get-tuple-element.134) | data formatting | bytes 6291456
  1157.4 14.6 %copy.573 = bf16[128,12,32,32]{0,3,2,1:T(8,128)(2,1)S(1)} copy(bf16[128,12,32,32]{3,2,1,0:T(8,128)(2,1)} %get-tuple-element.127) | data formatting | bytes 6291456
  1175.7 14.6 %copy.571 = bf16[128,12,32,32]{0,3,2,1:T(8,128)(2,1)S(1)} copy(bf16[128,12,32,32]{3,2,1,0:T(8,128)(2,1)} %get-tuple-element.128) | data formatting | bytes 6291456
  1194.2 14.8 %copy.569 = bf16[128,12,32,32]{0,3,2,1:T(8,128)(2,1)S(1)} copy(bf16[128,12,32,32]{3,2,1,0:T(8,128)(2,1)} %get-tuple-element.129) | data formatting | bytes 6291456
  1212.7 14.6 %copy.567 = bf16[128,12,32,32]{0,3,2,1:T(8,128)(2,1)S(1)} copy(bf16[128,12,32,32]{3,2,1,0:T(8,128)(2,1)} %get-tuple-element.130) | data formatting | bytes 6291456
  1231.0 14.6 %copy.565 = bf16[128,12,32,32]{0,3,2,1:T(8,128)(2,1)S(1)} copy(bf16[128,12,32,32]{3,2,1,0:T(8,128)(2,1)} %get-tuple-element.131) | data formatting | bytes 6291456
  1249.3 14.6 %copy.563 = bf16[128,12,32,32]{0,3,2,1:T(8,128)(2,1)S(1)} copy(bf16[128,12,32,32]{3,2,1,0:T(8,128)(2,1)} %get-tuple-element.132) | data formatting | bytes 6291456
  1304.2 21.0 %add_convert_fusion = bf16[64,12,32,32]{0,3,2,1:T(8,128)(2,1)S(1)} fusion(f32[64,12,32,32]{0,3,2,1:T(8,128)} %bitcast.261, f32[64,12,32,32]{0,3,2,1:T(8,128)} %bitcast.262, f32[64,12,32,32]{0,3,2,1:T(8,128)} %bitcast.263, f32[64,12,32,32]{0,3,2,1:T(8,128)} %bitcast.264, f32[64,12,32,32]{0,3,2,1:T(8,128)} %bitcast.265, f32[64,12,32,32]{0,3,2,1:T(8,128)} %bitcast.266, ...), kind=kLoop, calls=%fused_computation.13 | loop fusion | flops 7077888 | bytes 29884416 | tf_op jit(solution)/shard_map/convert_element_type | solution.py:159
  (253 shorter events, 296.0 us)
Async XLA Ops:
  7.2 513.7 %copy-start = (bf16[3,3,128,128]{3,2,1,0:T(8,128)(2,1)S(1)}, bf16[3,3,128,128]{3,2,1,0:T(8,128)(2,1)}, u32[]{:S(2)}) copy-start(bf16[3,3,128,128]{3,2,1,0:T(8,128)(2,1)} %param.27) | copy-start | bytes 884740
  7.2 143.5 %all-reduce.3.cloned.1.call-start = ((), (), s32[]{:S(2)}) async-start(), calls=%async_computation | async-start | bytes 4194304 | tf_op jit(solution)/shard_map/psum | solution.py:75
  11.7 35.5 %collective-permute-start.1 = (bf16[64,12,32,1]{0,3,1,2:T(2,128)(2,1)}, bf16[64,12,32,1]{0,3,1,2:T(2,128)(2,1)}, u32[]{:S(2)}, u32[]{:S(2)}) collective-permute-start(bf16[64,12,32,1]{0,3,1,2:T(2,128)(2,1)} %get-tuple-element.156), channel_id=1, source_target_pairs={{8,0},{16,8},{24,16},{9,1},{17,9},{25,17},{10,2},{18,10},{26,18},{... | collective-permute-start | bytes 147464 | tf_op jit(solution)/shard_map/ppermute | solution.py:17
  13.0 34.2 %collective-permute-start = (bf16[64,12,32,1]{0,3,1,2:T(2,128)(2,1)}, bf16[64,12,32,1]{0,3,1,2:T(2,128)(2,1)}, u32[]{:S(2)}, u32[]{:S(2)}) collective-permute-start(bf16[64,12,32,1]{0,3,1,2:T(2,128)(2,1)} %get-tuple-element.157), channel_id=1, source_target_pairs={{0,8},{8,16},{16,24},{1,9},{9,17},{17,25},{2,10},{10,18},{18,26},{... | collective-permute-start | bytes 147464 | tf_op jit(solution)/shard_map/ppermute | solution.py:16
  46.8 331.3 %all-gather.3.cloned.1.call-start = ((), (), s32[]{:S(2)}) async-start(), calls=%async_computation.1 | async-start | bytes 23592960 | tf_op jit(solution)/shard_map/all_gather | solution.py:151
  46.9 109.6 %copy-start.15 = (pred[12]{0:T(512)(128)(4,1)}, pred[12]{0:T(512)(128)(4,1)S(1)}, u32[]{:S(2)}) copy-start(pred[12]{0:T(512)(128)(4,1)S(1)} %get-tuple-element.186) | copy-start | bytes 40
  46.9 113.7 %copy-start.13 = (pred[12]{0:T(512)(128)(4,1)}, pred[12]{0:T(512)(128)(4,1)S(1)}, u32[]{:S(2)}) copy-start(pred[12]{0:T(512)(128)(4,1)S(1)} %get-tuple-element.182) | copy-start | bytes 40
  46.9 117.3 %copy-start.11 = (pred[12]{0:T(512)(128)(4,1)}, pred[12]{0:T(512)(128)(4,1)S(1)}, u32[]{:S(2)}) copy-start(pred[12]{0:T(512)(128)(4,1)S(1)} %get-tuple-element.184) | copy-start | bytes 40
  46.9 126.8 %copy-start.9 = (pred[12]{0:T(512)(128)(4,1)}, pred[12]{0:T(512)(128)(4,1)S(1)}, u32[]{:S(2)}) copy-start(pred[12]{0:T(512)(128)(4,1)S(1)} %get-tuple-element.118) | copy-start | bytes 40
  47.0 113.7 %copy-start.26 = (pred[12]{0:T(512)(128)(4,1)}, pred[12]{0:T(512)(128)(4,1)S(1)}, u32[]{:S(2)}) copy-start(pred[12]{0:T(512)(128)(4,1)S(1)} %get-tuple-element.179) | copy-start | bytes 40
  47.0 117.3 %copy-start.24 = (pred[12]{0:T(512)(128)(4,1)}, pred[12]{0:T(512)(128)(4,1)S(1)}, u32[]{:S(2)}) copy-start(pred[12]{0:T(512)(128)(4,1)S(1)} %get-tuple-element.180) | copy-start | bytes 40
  47.0 126.7 %copy-start.22 = (pred[12]{0:T(512)(128)(4,1)}, pred[12]{0:T(512)(128)(4,1)S(1)}, u32[]{:S(2)}) copy-start(pred[12]{0:T(512)(128)(4,1)S(1)} %get-tuple-element.178) | copy-start | bytes 40
  47.0 112.6 %copy-start.17 = (s32[1024]{0:T(1024)}, s32[1024]{0:T(1024)S(1)}, u32[]{:S(2)}) copy-start(s32[1024]{0:T(1024)S(1)} %get-tuple-element.192) | copy-start | bytes 12292
  47.1 114.9 %copy-start.20 = (s32[1024]{0:T(1024)}, s32[1024]{0:T(1024)S(1)}, u32[]{:S(2)}) copy-start(s32[1024]{0:T(1024)S(1)} %get-tuple-element.191) | copy-start | bytes 12292
  47.1 124.2 %copy-start.19 = (s32[1024]{0:T(1024)}, s32[1024]{0:T(1024)S(1)}, u32[]{:S(2)}) copy-start(s32[1024]{0:T(1024)S(1)} %get-tuple-element.190) | copy-start | bytes 12292
  48.8 6.8 collective-permute-start.3
  50.1 5.8 collective-permute-start.2
  191.6 623.3 %all-reduce.5.cloned.1.call-start = ((), (), s32[]{:S(2)}) async-start(), calls=%async_computation.2 | async-start | bytes 4194304 | tf_op jit(solution)/shard_map/psum | solution.py:75
  669.2 29.6 %collective-permute-start.4 = (bf16[64,12,32,1]{0,3,1,2:T(2,128)(2,1)}, bf16[64,12,32,1]{0,3,1,2:T(2,128)(2,1)}, u32[]{:S(2)}, u32[]{:S(2)}) collective-permute-start(bf16[64,12,32,1]{0,3,1,2:T(2,128)(2,1)} %get-tuple-element.169), channel_id=1, source_target_pairs={{0,8},{8,16},{16,24},{1,9},{9,17},{17,25},{2,10},{10,18},{18,26},{... | collective-permute-start | bytes 147464 | tf_op jit(solution)/shard_map/ppermute | solution.py:16
  674.4 24.5 %collective-permute-start.5 = (bf16[64,12,32,1]{0,3,1,2:T(2,128)(2,1)}, bf16[64,12,32,1]{0,3,1,2:T(2,128)(2,1)}, u32[]{:S(2)}, u32[]{:S(2)}) collective-permute-start(bf16[64,12,32,1]{0,3,1,2:T(2,128)(2,1)} %get-tuple-element.167), channel_id=1, source_target_pairs={{8,0},{16,8},{24,16},{9,1},{17,9},{25,17},{10,2},{18,10},{26,18},{... | collective-permute-start | bytes 147464 | tf_op jit(solution)/shard_map/ppermute | solution.py:17
  700.4 12.2 collective-permute-start.7
  701.7 10.9 collective-permute-start.6
  712.6 109.5 %copy-start.16 = (pred[12]{0:T(512)(128)(4,1)S(1)}, pred[12]{0:T(512)(128)(4,1)}, u32[]{:S(2)}) copy-start(pred[12]{0:T(512)(128)(4,1)} %copy-done.15) | copy-start | bytes 40
  712.6 330.0 %all-gather.5.cloned.1.call-start = ((), (), s32[]{:S(2)}) async-start(), calls=%async_computation.3 | async-start | bytes 23592960 | tf_op jit(solution)/shard_map/all_gather | solution.py:158
  (19 other events, 1092.4 us)
Sparse Core Ops, SparseCore 0:
  46.9 103.7 all-reduce.2
  191.8 186.2 all-gather.2
  712.7 102.2 all-reduce.4
  856.2 186.2 all-gather.4
where the time goes:
time: 1350 us; the launch traced here: 1330 us
  local copies, waits for them, and re-layouts  598 us (44%)
  waiting for transfers between devices  550 us (41%)
  other arithmetic  76.7 us (6%)
  matrix products  68.4 us (5%)
  starting transfers between devices  26.6 us (2%)
  between operations  15.1 us (1%)
    unnamed x84, local copies, waits for them, and re-layouts  279 us
    psum x2, waiting for transfers between devices, face_lines_of(): return lax.psum(contrib.astype(jnp.bfloat16), ('px', 'py'))  187 us
    all_gather x1, waiting for transfers between devices, local(): lax.all_gather(feat_pad, 'ch', axis=0, tiled=True)  182 us
    all_gather x1, waiting for transfers between devices, local(): lax.all_gather(grad_pad, 'ch', axis=0, tiled=True)  180 us
    slice x1, local copies, waits for them, and re-layouts, backward_taps(): padded[:, :, 2 - tap_row:2 - tap_row + out_cols, 2 - tap_col:2 - tap_col...  96.5 us
    slice x1, local copies, waits for them, and re-layouts, forward_taps(): padded[:, :, tap_row:tap_row + out_cols, tap_col:tap_col + out_rows]  96.4 us
    unnamed x18, matrix products  68.4 us
    select_n x19, local copies, waits for them, and re-layouts, placed(): jnp.where(active, lax.dynamic_update_slice_in_dim(blank, values.astype(jn...  37.9 us
  transfers between devices with their start and end apart: 12, of which 5 were waited for; matrix products, arithmetic and copies ran while one was open for 6% of the time, Pallas kernels for 0%

commit v1 on v0

v1 whole, which is shorter than its diff:
```python
import jax
import jax.numpy as jnp
import numpy as np
from jax import lax
from jax.experimental import pallas as pl
from jax.experimental.pallas import tpu as pltpu
from jax.sharding import PartitionSpec as P

RB = 32
GROUP = 4
LANES = 128
VMEM_LIMIT = 48 * 1024 * 1024
STRIP_LANE = (96, 0, 32, 64)


def ring_matrix(col_len):
    mat = np.zeros((col_len * RB, LANES), np.float32)
    for b in range(RB):
        mat[b, b] = 1
        mat[(col_len - 1) * RB + b, 32 + b] = 1
    for a in range(col_len):
        mat[a * RB, 64 + a] = 1
        mat[a * RB + RB - 1, 96 + a] = 1
    return mat


def corner_matrix():
    mat = np.zeros((LANES, LANES), np.float32)
    for q, lane in enumerate((0, RB - 1, 32, 32 + RB - 1)):
        mat[lane, q] = 1
    return mat


def reverse_matrix(unit):
    mat = np.zeros((LANES, LANES), np.float32)
    for lane in range(LANES):
        mat[lane, (lane // unit) * unit + unit - 1 - lane % unit] = 1
    return mat


def spread_matrix(col_len):
    width = col_len * RB + LANES
    mat = np.zeros((LANES, width), np.float32)
    top, bottom = (col_len + 3) * RB, col_len * RB
    mat[0, top] = 1
    mat[1, top + RB - 1] = 1
    mat[2, bottom] = 1
    mat[3, bottom + RB - 1] = 1
    for a in range(col_len):
        mat[STRIP_LANE[2] + a, a * RB] = 1
        mat[STRIP_LANE[3] + a, a * RB + RB - 1] = 1
    return mat


def lane_iota(shape):
    return lax.broadcasted_iota(jnp.int32, shape, len(shape) - 1)


def emit_rings(step, steps, fields, pos_ref, ring_ref, cornsel_ref, packs_ref, shard_ref, corner_acc):
    chan = fields[0].shape[0]
    lane = lane_iota((chan, LANES))
    rings = [
        jnp.dot(field, ring_ref[...], preferred_element_type=jnp.float32) for field in fields
    ]
    for side in range(4):
        tile = jnp.zeros((chan, LANES), jnp.float32)
        for g, ring in enumerate(rings):
            moved = pltpu.roll(ring, ((g - side) * 32) % LANES, 1) if g != side else ring
            tile = jnp.where(lane // 32 == g, moved, tile)
        packs_ref[side * steps + step] = tile.astype(jnp.bfloat16)

    @pl.when(step == 0)
    def _():
        corner_acc[...] = jnp.zeros_like(corner_acc)

    for g, ring in enumerate(rings):
        picked = jnp.dot(
            ring.astype(jnp.bfloat16), cornsel_ref[...], preferred_element_type=jnp.float32
        )
        corner_acc[...] += pltpu.roll(picked, (step * GROUP + g) * 4, 1)

    @pl.when(step == steps - 1)
    def _():
        row_first = pos_ref[0] == 1
        col_first = pos_ref[1] == 1
        for q in range(steps):
            shard_ref[q] = jnp.where(row_first, packs_ref[q], packs_ref[steps + q])
            shard_ref[steps + q] = jnp.where(
                col_first, packs_ref[2 * steps + q], packs_ref[3 * steps + q]
            )
        shard_ref[2 * steps] = corner_acc[...].astype(jnp.bfloat16)


def rings_kernel(steps, pos_ref, field_ref, ring_ref, cornsel_ref, packs_ref, shard_ref, corner_acc):
    step = pl.program_id(0)
    fields = [field_ref[g] for g in range(GROUP)]
    emit_rings(step, steps, fields, pos_ref, ring_ref, cornsel_ref, packs_ref, shard_ref, corner_acc)


def whole_spec(array):
    zeros = (0,) * array.ndim
    return pl.BlockSpec(array.shape, lambda *_: zeros)


def rings_of(field, pos, ring, cornsel):
    faces, chan, tile = field.shape
    steps = faces // GROUP
    packs = jax.ShapeDtypeStruct((4 * steps, chan, LANES), jnp.bfloat16)
    shard = jax.ShapeDtypeStruct((2 * steps + 1, chan, LANES), jnp.bfloat16)
    return pl.pallas_call(
        lambda *refs: rings_kernel(steps, *refs),
        grid=(steps,),
        in_specs=[
            pl.BlockSpec(memory_space=pltpu.SMEM),
            pl.BlockSpec((GROUP, chan, tile), lambda i: (i, 0, 0)),
            whole_spec(ring),
            whole_spec(cornsel),
        ],
        out_specs=[whole_spec(packs), whole_spec(shard)],
        out_shape=[packs, shard],
        scratch_shapes=[pltpu.VMEM((chan, LANES), jnp.float32)],
        compiler_params=pltpu.CompilerParams(vmem_limit_bytes=VMEM_LIMIT),
        name="rings",
    )(pos, field, ring, cornsel)


def halo_kernel(faces, units, unit, meta_ref, lines_ref, n0, n1, n2, n3, rev_ref, halo_ref, rev_acc):
    steps = faces // GROUP
    near = (n0, n1, n2, n3)
    chan = halo_ref.shape[1]
    lane = lane_iota((chan, LANES))
    per_face = sum(units) * 3 + 8
    corner_tile = jnp.zeros((chan, LANES), jnp.float32)
    plain = []
    for f in range(faces):
        tile = jnp.zeros((chan, LANES), jnp.float32)
        flipped = jnp.zeros((chan, LANES), jnp.float32)
        at = f * per_face
        for e in range(4):
            for un in range(units[e]):
                index, shift, mode = (meta_ref[at], meta_ref[at + 1], meta_ref[at + 2])
                at += 3
                base = STRIP_LANE[e] + un * unit
                span = (lane >= base) & (lane < base + unit)
                source = jnp.where(mode == 0, near[e][f // GROUP], lines_ref[index])
                moved = pltpu.roll(source.astype(jnp.float32), shift, 1)
                tile = jnp.where(span & (mode != 2), moved, tile)
                flipped = jnp.where(span & (mode == 2), moved, flipped)
        rev_acc[f] = flipped.astype(jnp.bfloat16)
        plain.append(tile)
        for c in range(4):
            index, shift = (meta_ref[at], meta_ref[at + 1])
            at += 2
            moved = pltpu.roll(lines_ref[index].astype(jnp.float32), shift, 1)
            corner_tile = jnp.where(lane == f * 4 + c, moved, corner_tile)
    turned = jnp.dot(
        rev_acc[...].reshape(faces * chan, LANES), rev_ref[...], preferred_element_type=jnp.float32
    ).reshape(faces, chan, LANES)
    for f in range(faces):
        halo_ref[f] = (plain[f] + turned[f]).astype(jnp.bfloat16)
    halo_ref[faces] = corner_tile.astype(jnp.bfloat16)


def assemble_halo(meta, lines, near, rev, units, unit):
    chan = lines.shape[1]
    faces = near[0].shape[0] * GROUP
    halo = jax.ShapeDtypeStruct((faces + 1, chan, LANES), jnp.bfloat16)
    vmem = pl.BlockSpec(memory_space=pltpu.VMEM)
    return pl.pallas_call(
        lambda *refs: halo_kernel(faces, units, unit, *refs),
        in_specs=[pl.BlockSpec(memory_space=pltpu.SMEM)] + [vmem] * 6,
        out_specs=vmem,
        out_shape=halo,
        scratch_shapes=[pltpu.VMEM((faces, chan, LANES), jnp.bfloat16)],
        compiler_params=pltpu.CompilerParams(vmem_limit_bytes=VMEM_LIMIT),
        name="halo",
    )(meta, lines, *near, rev)


def conv_face(g, step, field_refs, halo_refs, corner_refs, taps_ref, spread_ref, stack_ref):
    chan, tile = field_refs[0].shape[1:]
    pieces = len(field_refs)
    total = chan * pieces
    width = tile + LANES
    for k in range(pieces):
        stack_ref[total + k * chan : total + (k + 1) * chan, :tile] = field_refs[k][g]
        stack_ref[total + k * chan : total + (k + 1) * chan, tile:] = halo_refs[k][g]
    halo = stack_ref[total : 2 * total, tile:].astype(jnp.float32)
    corners = jnp.concatenate([ref[0].astype(jnp.float32) for ref in corner_refs], axis=0)
    corners = pltpu.roll(corners, (LANES - (step * GROUP + g) * 4) % LANES, 1)
    lane = lane_iota((total, LANES))
    sides = jnp.where(lane < 4, corners, halo).astype(jnp.bfloat16)
    beside = jnp.dot(sides, spread_ref[...], preferred_element_type=jnp.float32)
    middle = stack_ref[total : 2 * total].astype(jnp.float32)
    col = lane_iota((total, width)) % RB
    stack_ref[:total] = jnp.where(col == 0, beside, pltpu.roll(middle, 1, 1)).astype(jnp.bfloat16)
    stack_ref[2 * total :] = jnp.where(
        col == RB - 1, beside, pltpu.roll(middle, width - 1, 1)
    ).astype(jnp.bfloat16)
    sums = jnp.dot(taps_ref[...], stack_ref[...], preferred_element_type=jnp.float32)
    above = pltpu.roll(sums[:chan], RB, 1)
    below = pltpu.roll(sums[2 * chan :], width - RB, 1)
    return (above + sums[chan : 2 * chan] + below)[:, :tile]


def forward_kernel(steps, pieces, pos_ref, *refs):
    field_refs, refs = (refs[:pieces], refs[pieces:])
    halo_refs, refs = (refs[:pieces], refs[pieces:])
    corner_refs, refs = (refs[:pieces], refs[pieces:])
    (cot_ref, taps_ref, spread_ref, ring_ref, cornsel_ref) = refs[:5]
    (act_ref, gated_ref, packs_ref, shard_ref, stack_ref, corner_acc) = refs[5:]
    step = pl.program_id(0)
    fields = []
    for g in range(GROUP):
        pre = conv_face(g, step, field_refs, halo_refs, corner_refs, taps_ref, spread_ref, stack_ref)
        sig = 1.0 / (1.0 + jnp.exp(-pre))
        act_ref[g] = (pre * sig).astype(jnp.bfloat16)
        gated = cot_ref[g].astype(jnp.float32) * sig * (1.0 + pre * (1.0 - sig))
        gated_ref[g] = gated.astype(jnp.bfloat16)
        fields.append(gated.astype(jnp.bfloat16))
    emit_rings(step, steps, fields, pos_ref, ring_ref, cornsel_ref, packs_ref, shard_ref, corner_acc)


def backward_kernel(steps, pieces, *refs):
    field_refs, refs = (refs[:pieces], refs[pieces:])
    halo_refs, refs = (refs[:pieces], refs[pieces:])
    corner_refs, refs = (refs[:pieces], refs[pieces:])
    (taps_ref, spread_ref, grad_ref, stack_ref) = refs
    step = pl.program_id(0)
    for g in range(GROUP):
        total = conv_face(
            g, step, field_refs, halo_refs, corner_refs, taps_ref, spread_ref, stack_ref
        )
        grad_ref[g] = total.astype(jnp.bfloat16)


def conv_specs(fields, halos):
    faces, chan, tile = fields[0].shape
    group = lambda i: (i, 0, 0)
    return (
        [pl.BlockSpec((GROUP, chan, tile), group) for _ in fields]
        + [pl.BlockSpec((GROUP, chan, LANES), group) for _ in halos]
        + [pl.BlockSpec((1, chan, LANES), lambda i: (faces, 0, 0)) for _ in halos]
    )


def forward(pos, fields, halos, cot, taps, spread, ring, cornsel):
    faces, chan, tile = fields[0].shape
    steps = faces // GROUP
    pieces = len(fields)
    packs = jax.ShapeDtypeStruct((4 * steps, chan, LANES), jnp.bfloat16)
    shard = jax.ShapeDtypeStruct((2 * steps + 1, chan, LANES), jnp.bfloat16)
    out = jax.ShapeDtypeStruct((faces, chan, tile), jnp.bfloat16)
    block = pl.BlockSpec((GROUP, chan, tile), lambda i: (i, 0, 0))
    return pl.pallas_call(
        lambda *refs: forward_kernel(steps, pieces, *refs),
        grid=(steps,),
        in_specs=[pl.BlockSpec(memory_space=pltpu.SMEM)]
        + conv_specs(fields, halos)
        + [block, whole_spec(taps), whole_spec(spread), whole_spec(ring), whole_spec(cornsel)],
        out_specs=[block, block, whole_spec(packs), whole_spec(shard)],
        out_shape=[out, out, packs, shard],
        scratch_shapes=[
            pltpu.VMEM((3 * chan * pieces, tile + LANES), jnp.bfloat16),
            pltpu.VMEM((chan, LANES), jnp.float32),
        ],
        compiler_params=pltpu.CompilerParams(vmem_limit_bytes=VMEM_LIMIT),
        name="forward",
    )(pos, *fields, *halos, *halos, cot, taps, spread, ring, cornsel)


def backward(fields, halos, taps, spread):
    faces, chan, tile = fields[0].shape
    steps = faces // GROUP
    pieces = len(fields)
    return pl.pallas_call(
        lambda *refs: backward_kernel(steps, pieces, *refs),
        grid=(steps,),
        in_specs=conv_specs(fields, halos) + [whole_spec(taps), whole_spec(spread)],
        out_specs=pl.BlockSpec((GROUP, chan, tile), lambda i: (i, 0, 0)),
        out_shape=jax.ShapeDtypeStruct((faces, chan, tile), jnp.bfloat16),
        scratch_shapes=[pltpu.VMEM((3 * chan * pieces, tile + LANES), jnp.bfloat16)],
        compiler_params=pltpu.CompilerParams(vmem_limit_bytes=VMEM_LIMIT),
        name="backward",
    )(*fields, *halos, *halos, taps, spread)


def halo_meta(edge_table, corner_table, row_pos, col_pos, px_count, py_count, col_len, unit):
    faces = edge_table.shape[0]
    steps = faces // GROUP
    tiles = 2 * steps + 1
    side_len = px_count * RB
    face = jnp.arange(faces)
    on_border = (col_pos == 0, col_pos == py_count - 1, row_pos == 0, row_pos == px_count - 1)

    def line_cell(g, s, at):
        along_px = s < 2
        length = jnp.where(along_px, RB, col_len)
        seg = at // length
        px_of = jnp.where(along_px, seg, jnp.where(s == 2, 0, px_count - 1))
        py_of = jnp.where(along_px, jnp.where(s == 0, 0, py_count - 1), seg)
        tile = (px_of * py_count + py_of) * tiles + jnp.where(along_px, 0, steps) + g // GROUP
        return (tile, (g % GROUP) * 32 + at % length)

    def linked(e, at):
        g, s, r = (edge_table[:, e, 0], edge_table[:, e, 1], edge_table[:, e, 2])
        return (g, s, r, jnp.where(r == 1, side_len - 1 - at, at))

    columns = []
    for e in range(4):
        start = row_pos * RB if e < 2 else col_pos * col_len
        for un in range((RB if e < 2 else col_len) // unit):
            g, s, r, at = linked(e, start + un * unit)
            tile, lane = line_cell(g, s, at - jnp.where(r == 1, unit - 1, 0))
            near_lane = (face % GROUP) * 32 + un * unit
            lane = jnp.where(on_border[e], lane, near_lane)
            tile = jnp.where(on_border[e], tile, 0)
            mode = jnp.where(on_border[e], 1 + r, 0)
            columns += [tile, (STRIP_LANE[e] + un * unit - lane) % LANES, mode]
    for c in range(4):
        down, right = (c // 2, c % 2)
        row_edge, col_edge = (down, 2 + right)
        along_row = row_pos * RB + (RB if right else -1)
        along_col = col_pos * col_len + (col_len if down else -1)
        g, s, _, at = linked(row_edge, jnp.clip(along_row, 0, side_len - 1))
        row_tile, row_lane = line_cell(g, s, at)
        g, s, _, at = linked(col_edge, jnp.clip(along_col, 0, side_len - 1))
        col_tile, col_lane = line_cell(g, s, at)
        h, q = (corner_table[:, c, 0], corner_table[:, c, 1])
        face_tile, face_lane = line_cell(h, q // 2, (q % 2) * (side_len - 1))
        diag_px = jnp.clip(row_pos + (1 if right else -1), 0, px_count - 1)
        diag_py = jnp.clip(col_pos + (1 if down else -1), 0, py_count - 1)
        diag_tile = (diag_px * py_count + diag_py) * tiles + 2 * steps
        diag_lane = face * 4 + 3 - c
        row_on, col_on = (on_border[row_edge], on_border[col_edge])
        pick = lambda both, row, col, diag: jnp.where(
            row_on & col_on, both, jnp.where(row_on, row, jnp.where(col_on, col, diag))
        )
        tile = pick(face_tile, row_tile, col_tile, diag_tile)
        lane = pick(face_lane, row_lane, col_lane, diag_lane)
        columns += [tile, (face * 4 + c - lane) % LANES]
    return jnp.stack([jnp.broadcast_to(col, (faces,)) for col in columns], axis=1).reshape(-1)


def from_others(array, ch_count):
    return [array] + [
        lax.ppermute(array, "ch", [(i, (i + k) % ch_count) for i in range(ch_count)])
        for k in range(1, ch_count)
    ]


def exchange_halo(packs, shard, meta, rev, units, unit, px_count, py_count):
    steps = packs.shape[0] // 4
    top, bottom, left, right = [packs[s * steps : (s + 1) * steps] for s in range(4)]
    up = lambda n: [(i, i + 1) for i in range(n - 1)]
    down = lambda n: [(i + 1, i) for i in range(n - 1)]
    near = (
        lax.ppermute(bottom, "py", up(py_count)),
        lax.ppermute(top, "py", down(py_count)),
        lax.ppermute(right, "px", up(px_count)),
        lax.ppermute(left, "px", down(px_count)),
    )
    lines = lax.all_gather(shard, ("px", "py"), axis=0, tiled=True)
    return assemble_halo(meta, lines, near, rev, units, unit)


def local(features, cotangent, weight, edge_table, corner_table):
    chan, faces = features.shape[:2]
    tile = features.shape[4]
    col_len = tile // RB
    unit = min(RB, col_len)
    units = (RB // unit, RB // unit, col_len // unit, col_len // unit)
    px_count, py_count, ch_count = [lax.axis_size(name) for name in ("px", "py", "ch")]
    row_pos, col_pos, ch_pos = [lax.axis_index(name) for name in ("px", "py", "ch")]
    ring = jnp.asarray(ring_matrix(col_len), jnp.bfloat16)
    cornsel = jnp.asarray(corner_matrix(), jnp.bfloat16)
    spread = jnp.asarray(spread_matrix(col_len), jnp.bfloat16)
    rev = jnp.asarray(reverse_matrix(unit), jnp.bfloat16)
    pos = jnp.stack([col_pos == 0, row_pos == 0]).astype(jnp.int32)
    meta = halo_meta(
        edge_table, corner_table, row_pos, col_pos, px_count, py_count, col_len, unit
    )

    feats = jnp.transpose(features.reshape(chan, faces, tile), (1, 0, 2))
    cot = jnp.transpose(cotangent.reshape(chan, faces, tile), (1, 0, 2))

    def blocks(array, axis):
        order = [(ch_pos - k) % ch_count for k in range(ch_count)]
        return jnp.concatenate(
            [lax.dynamic_slice_in_dim(array, at * chan, chan, axis) for at in order], axis
        )

    own_out = lax.dynamic_slice_in_dim(weight, ch_pos * chan, chan, 2)
    taps = blocks(own_out, 3).transpose(0, 2, 1, 3).reshape(3 * chan, -1)
    own_in = lax.dynamic_slice_in_dim(weight, ch_pos * chan, chan, 3)
    back_taps = blocks(own_in, 2)[::-1, ::-1].transpose(0, 3, 1, 2).reshape(3 * chan, -1)

    packs, shard = rings_of(feats, pos, ring, cornsel)
    fields = from_others(feats, ch_count)
    halo = exchange_halo(packs, shard, meta, rev, units, unit, px_count, py_count)
    halos = from_others(halo, ch_count)
    act, gated, packs, shard = forward(pos, fields, halos, cot, taps, spread, ring, cornsel)

    fields = from_others(gated, ch_count)
    halo = exchange_halo(packs, shard, meta, rev, units, unit, px_count, py_count)
    halos = from_others(halo, ch_count)
    grad = backward(fields, halos, back_taps, spread)

    shape = (chan, faces, 1, 1, tile)
    return (
        jnp.transpose(act, (1, 0, 2)).reshape(shape),
        jnp.transpose(grad, (1, 0, 2)).reshape(shape),
    )


def solution(mesh):
    spec = P("ch", None, "py", "px", None)
    return jax.shard_map(
        local,
        mesh=mesh,
        in_specs=(spec, spec, P(), P(), P()),
        out_specs=(spec, spec),
        check_vma=False,
    )
```

time: 1350 us -> 149 us (0.11); the launches traced: 1330 us -> 148 us
  local copies, waits for them, and re-layouts: 598 us -> 17.3 us
  waiting for transfers between devices: 550 us -> 55.5 us
  other arithmetic: 76.7 us -> 7 us
  matrix products: 68.4 us -> 0 us
  Pallas kernels: 0 us -> 25.7 us
    all_gather x2, waiting for transfers between devices: 362 us -> 48.4 us  [exchange_halo(): lines = lax.all_gather(shard, ('px', 'py'), axis=0, tiled=True)]
    unnamed x84 -> x44, local copies, waits for them, and re-layouts: 279 us -> 10.7 us
    slice x17 -> x2, local copies, waits for them, and re-layouts: 200 us -> 0.65 us  [exchange_halo(): packs[s * steps:(s + 1) * steps]]
    psum x2 -> x0, waiting for transfers between devices: 187 us -> none  [face_lines_of(): return lax.psum(contrib.astype(jnp.bfloat16), ('px', 'py'))]
    unnamed x18 -> x0, matrix products: 68.4 us -> none
    scatter x8 -> x0, local copies, waits for them, and re-layouts: 48.1 us -> none  [the longest x4 34.2 us: pad_field(): padded.at[:, :, :, -1]]
    convert_element_type x3 -> x1, other arithmetic: 47.5 us -> 0.08 us  [local(): pos = jnp.stack([col_pos == 0, row_pos == 0]).astype(jnp.int32)]
    select_n x21 -> x0, local copies, waits for them, and re-layouts: 38.1 us -> none  [the longest x19 37.9 us: placed(): jnp.where(active, lax.dynamic_update_slice_in_dim(blank, values.astype(jn...]
  transfers between devices with their start and end apart: 12 -> 14, of which waited for: 5 -> 5; matrix products, arithmetic and copies ran while one was open for 6% -> 10% of each run, Pallas kernels for 0% -> 2%
where the time goes in v1:
time: 149 us; the launch traced here: 148 us
  waiting for transfers between devices  55.5 us (37%)
  starting transfers between devices  28 us (19%)
  Pallas kernels  25.7 us (17%)
  local copies, waits for them, and re-layouts  17.3 us (12%)
  between operations  14.4 us (10%)
  other arithmetic  7 us (5%)
    all_gather x2, waiting for transfers between devices, exchange_halo(): lines = lax.all_gather(shard, ('px', 'py'), axis=0, tiled=True)  48.4 us
    pallas_call x1, Pallas kernels, forward(): pl.pallas_call(lambda *refs: forward_kernel(steps, pieces, *refs), grid=(...  11.2 us
    unnamed x44, local copies, waits for them, and re-layouts  10.7 us
    ppermute x2, starting transfers between devices, exchange_halo(): lax.ppermute(right, 'px', up(px_count))  9.1 us
    pallas_call x1, Pallas kernels, backward(): pl.pallas_call(lambda *refs: backward_kernel(steps, pieces, *refs), grid=...  8.91 us
    ppermute x4, starting transfers between devices, from_others(): lax.ppermute(array, 'ch', [(i, (i + k) % ch_count) for i in range(ch_coun...  7.61 us
    ppermute x4, waiting for transfers between devices, from_others(): lax.ppermute(array, 'ch', [(i, (i + k) % ch_count) for i in range(ch_coun...  6.21 us
    ppermute x2, starting transfers between devices, exchange_halo(): lax.ppermute(bottom, 'py', up(py_count))  6.07 us
  transfers between devices with their start and end apart: 14, of which 5 were waited for; matrix products, arithmetic and copies ran while one was open for 10% of the time, Pallas kernels for 2%

profile of v1, /device:TPU:0, one launch (start us, length us, event | category | flops | bytes accessed | tf_op | source)
XLA Modules:
  0.0 147.9 jit_solution(11573100286841760442)
XLA Ops:
  7.3 1.4 copy-done
  10.4 3.1 %rings.1 = (bf16[12,64,128]{2,1,0:T(8,128)(2,1)S(1)}, bf16[7,64,128]{2,1,0:T(8,128)(2,1)}) custom-call(s32[2]{0:T(128)S(1)} %add_convert_fusion.refs_0_, bf16[12,64,1024]{2,1,0:T(8,128)(2,1)S(1)} %bitcast.712, bf16[1024,128]{1,0:T(8,128)(2,1)S(1)} %copy-done.8, bf16[128,128]{1,0:T(8,128)(2,1)S(1)} %copy-done.12), custom_call_target="tpu_custom_call" | custom-call | tf_op jit(solution)/shard_map/rings/pallas_call | solution.py:110
  13.6 3.0 %collective-permute-start = (bf16[12,64,1024]{2,1,0:T(8,128)(2,1)S(1)}, bf16[12,64,1024]{2,1,0:T(8,128)(2,1)S(1)}, u32[]{:S(2)}, u32[]{:S(2)}) collective-permute-start(bf16[12,64,1024]{2,1,0:T(8,128)(2,1)S(1)} %bitcast.713), channel_id=1, source_target_pairs={{0,1},{1,0},{2,3},{3,2},{4,5},{5,4},{6,7},{7,6},{8,9},{9,8},{10,11... | collective-permute-start | bytes 4718600 | tf_op jit(solution)/shard_map/ppermute | solution.py:347
  17.3 1.3 collective-permute-start.4
  18.6 4.5 %collective-permute-start.3 = (bf16[3,64,128]{2,1,0:T(8,128)(2,1)S(1)}, bf16[3,64,128]{2,1,0:T(8,128)(2,1)S(1)}, u32[]{:S(2)}, u32[]{:S(2)}) collective-permute-start(bf16[3,64,128]{2,1,0:T(8,128)(2,1)S(1)} %get-tuple-element.29), channel_id=1, source_target_pairs={{0,8},{8,16},{16,24},{1,9},{9,17},{17,25},{2,10},{10,18},{18,26},{... | collective-permute-start | bytes 147464 | tf_op jit(solution)/shard_map/ppermute | solution.py:360
  23.1 1.3 collective-permute-start.2
  24.4 3.0 %collective-permute-start.1 = (bf16[3,64,128]{2,1,0:T(8,128)(2,1)S(1)}, bf16[3,64,128]{2,1,0:T(8,128)(2,1)S(1)}, u32[]{:S(2)}, u32[]{:S(2)}) collective-permute-start(bf16[3,64,128]{2,1,0:T(8,128)(2,1)S(1)} %get-tuple-element.31), channel_id=1, source_target_pairs={{0,2},{2,4},{4,6},{1,3},{3,5},{5,7},{8,10},{10,12},{12,14},{9,11},... | collective-permute-start | bytes 147464 | tf_op jit(solution)/shard_map/ppermute | solution.py:358
  33.4 2.1 %stack.11 = s32[12,20]{0,1:T(8,128)S(1)} concatenate(s32[12,1]{0,1:T(1,128)} %broadcast_select_fusion.35, s32[12,1]{0,1:T(1,128)} %get-tuple-element.35, s32[12,1]{0,1:T(1,128)} %get-tuple-element.41, s32[12,1]{0,1:T(1,128)S(1)} %get-tuple-element.46, s32[12,1]{0,1:T(1,128)} %get-tuple-element.37, s32[12,1]{0,1:T(1,128)} %get-tuple-element.42, s32[12,1]{0,1:T(1,128)S(1)} %get-tuple-element.45, ...), dimensions={1} | concatenate | bytes 1920 | tf_op jit(solution)/shard_map/stack | solution.py:342
  35.8 21.3 %all-gather.3.cloned.1.call-done.refs_1_ = bf16[112,64,128]{2,1,0:T(8,128)(2,1)} async-done(((bf16[7,64,128]{2,1,0:T(8,128)(2,1)}), bf16[112,64,128]{2,1,0:T(8,128)(2,1)}) %all-gather.3.cloned.1.call-update) | async-done | bytes 1835024 | tf_op jit(solution)/shard_map/all_gather | solution.py:363
  57.1 1.5 %copy-done.2 = bf16[112,64,128]{2,1,0:T(8,128)(2,1)S(1)} copy-done((bf16[112,64,128]{2,1,0:T(8,128)(2,1)S(1)}, bf16[112,64,128]{2,1,0:T(8,128)(2,1)}, u32[]{:S(2)}) %copy-start.2) | copy-done | bytes 1835032
  59.9 1.5 %collective-permute-start.5 = (bf16[13,64,128]{2,1,0:T(8,128)(2,1)S(1)}, bf16[13,64,128]{2,1,0:T(8,128)(2,1)S(1)}, u32[]{:S(2)}, u32[]{:S(2)}) collective-permute-start(bf16[13,64,128]{2,1,0:T(8,128)(2,1)S(1)} %halo.2.refs_3_.refs_5_), channel_id=1, source_target_pairs={{0,1},{1,0},{2,3},{3,2},{4,5},{5,4},{6,7},{7,6},{8,9},{9,8},{10,11... | collective-permute-start | bytes 638984 | tf_op jit(solution)/shard_map/ppermute | solution.py:347
  62.7 4.7 %collective-permute-done.5.refs_4_.refs_6_ = bf16[13,64,128]{2,1,0:T(8,128)(2,1)S(1)} collective-permute-done((bf16[13,64,128]{2,1,0:T(8,128)(2,1)S(1)}, bf16[13,64,128]{2,1,0:T(8,128)(2,1)S(1)}, u32[]{:S(2)}, u32[]{:S(2)}) %collective-permute-start.5) | collective-permute-done | bytes 213024 | tf_op jit(solution)/shard_map/ppermute | solution.py:347
  67.4 11.2 %forward.1 = (bf16[12,64,1024]{2,1,0:T(8,128)(2,1)}, bf16[12,64,1024]{2,1,0:T(8,128)(2,1)S(1)}, bf16[12,64,128]{2,1,0:T(8,128)(2,1)S(1)}, bf16[7,64,128]{2,1,0:T(8,128)(2,1)}) custom-call(s32[2]{0:T(128)S(1)} %copy-done.17, bf16[12,64,1024]{2,1,0:T(8,128)(2,1)S(1)} %bitcast.714, bf16[12,64,1024]{2,1,0:T(8,128)(2,1)S(1)} %collective-permute-done.refs_2_, ...), custom_call_target="tpu_custom_call" | custom-call | tf_op jit(solution)/shard_map/forward/pallas_call | solution.py:255
  79.7 1.5 %collective-permute-start.6 = (bf16[12,64,1024]{2,1,0:T(8,128)(2,1)}, bf16[12,64,1024]{2,1,0:T(8,128)(2,1)S(1)}, u32[]{:S(2)}, u32[]{:S(2)}) collective-permute-start(bf16[12,64,1024]{2,1,0:T(8,128)(2,1)} %copy-done.4), channel_id=1, source_target_pairs={{0,1},{1,0},{2,3},{3,2},{4,5},{5,4},{6,7},{7,6},{8,9},{9,8},{10,11... | collective-permute-start | bytes 4718600 | tf_op jit(solution)/shard_map/ppermute | solution.py:347
  81.3 1.3 collective-permute-start.10
  82.6 4.5 %collective-permute-start.9 = (bf16[3,64,128]{2,1,0:T(8,128)(2,1)S(1)}, bf16[3,64,128]{2,1,0:T(8,128)(2,1)S(1)}, u32[]{:S(2)}, u32[]{:S(2)}) collective-permute-start(bf16[3,64,128]{2,1,0:T(8,128)(2,1)S(1)} %get-tuple-element.25), channel_id=1, source_target_pairs={{0,8},{8,16},{16,24},{1,9},{9,17},{17,25},{2,10},{10,18},{18,26},{... | collective-permute-start | bytes 147464 | tf_op jit(solution)/shard_map/ppermute | solution.py:360
  87.1 1.3 collective-permute-start.8
  88.4 3.0 %collective-permute-start.7 = (bf16[3,64,128]{2,1,0:T(8,128)(2,1)S(1)}, bf16[3,64,128]{2,1,0:T(8,128)(2,1)S(1)}, u32[]{:S(2)}, u32[]{:S(2)}) collective-permute-start(bf16[3,64,128]{2,1,0:T(8,128)(2,1)S(1)} %get-tuple-element.27), channel_id=1, source_target_pairs={{0,2},{2,4},{4,6},{1,3},{3,5},{5,7},{8,10},{10,12},{12,14},{9,11},... | collective-permute-start | bytes 147464 | tf_op jit(solution)/shard_map/ppermute | solution.py:358
  92.3 27.1 %all-gather.5.cloned.1.call-done.refs_1_ = bf16[112,64,128]{2,1,0:T(8,128)(2,1)} async-done(((bf16[7,64,128]{2,1,0:T(8,128)(2,1)}), bf16[112,64,128]{2,1,0:T(8,128)(2,1)}) %all-gather.5.cloned.1.call-update) | async-done | bytes 1835024 | tf_op jit(solution)/shard_map/all_gather | solution.py:363
  119.4 1.5 %copy-done.3 = bf16[112,64,128]{2,1,0:T(8,128)(2,1)S(1)} copy-done((bf16[112,64,128]{2,1,0:T(8,128)(2,1)S(1)}, bf16[112,64,128]{2,1,0:T(8,128)(2,1)}, u32[]{:S(2)}) %copy-start.3) | copy-done | bytes 1835032
  123.6 1.5 %collective-permute-start.11 = (bf16[13,64,128]{2,1,0:T(8,128)(2,1)S(1)}, bf16[13,64,128]{2,1,0:T(8,128)(2,1)}, u32[]{:S(2)}, u32[]{:S(2)}) collective-permute-start(bf16[13,64,128]{2,1,0:T(8,128)(2,1)S(1)} %halo.3.refs_2_.refs_4_), channel_id=1, source_target_pairs={{0,1},{1,0},{2,3},{3,2},{4,5},{5,4},{6,7},{7,6},{8,9},{9,8},{10,11... | collective-permute-start | bytes 638984 | tf_op jit(solution)/shard_map/ppermute | solution.py:347
  126.8 1.8 %copy.22 = bf16[3,64,3,128]{3,2,1,0:T(4,128)(2,1)} copy(bf16[3,64,3,128]{1,3,2,0:T(8,128)(2,1)} %reverse_bitcast_fusion) | data formatting | bytes 294912 | tf_op jit(solution)/shard_map/transpose | solution.py:396
  129.6 1.6 %collective-permute-done.11.refs_3_.refs_5_ = bf16[13,64,128]{2,1,0:T(8,128)(2,1)} collective-permute-done((bf16[13,64,128]{2,1,0:T(8,128)(2,1)S(1)}, bf16[13,64,128]{2,1,0:T(8,128)(2,1)}, u32[]{:S(2)}, u32[]{:S(2)}) %collective-permute-start.11) | collective-permute-done | bytes 213024 | tf_op jit(solution)/shard_map/ppermute | solution.py:347
  132.1 8.9 %backward.1 = bf16[12,64,1024]{2,1,0:T(8,128)(2,1)} custom-call(bf16[12,64,1024]{2,1,0:T(8,128)(2,1)S(1)} %copy-done.5, bf16[12,64,1024]{2,1,0:T(8,128)(2,1)S(1)} %collective-permute-done.6.refs_1_, bf16[13,64,128]{2,1,0:T(8,128)(2,1)S(1)} %halo.3.refs_2_.refs_4_, bf16[13,64,128]{2,1,0:T(8,128)(2,1)} %collective-permute-done.11.refs_3_.refs_5_, ...), custom_call_target="tpu_custom_call" | custom-call | tf_op jit(solution)/shard_map/backward/pallas_call | solution.py:276
  (78 shorter events, 19.4 us)
Async XLA Ops:
  7.2 20.4 %copy-start.19 = (s32[12,4,3]{0,1,2:T(4,128)S(1)}, s32[12,4,3]{0,1,2:T(4,128)}, u32[]{:S(2)}) copy-start(s32[12,4,3]{0,1,2:T(4,128)} %param.12) | copy-start | bytes 1732
  7.2 20.4 %copy-start.20 = (s32[12,4,2]{0,2,1:T(2,128)S(1)}, s32[12,4,2]{0,2,1:T(2,128)}, u32[]{:S(2)}) copy-start(s32[12,4,2]{0,2,1:T(2,128)} %param.13) | copy-start | bytes 1156
  7.2 49.9 %all-gather.3.cloned.1.call-start = ((), (), s32[]{:S(2)}) async-start(), calls=%async_computation | async-start | bytes 1949696 | tf_op jit(solution)/shard_map/all_gather | solution.py:363
  7.3 6.2 %copy-start.16 = (s32[2]{0:T(128)}, s32[2]{0:T(128)S(1)}, u32[]{:S(2)}) copy-start(s32[2]{0:T(128)S(1)} %add_convert_fusion.refs_0_) | copy-start | bytes 28
  10.4 46.6 %copy-start.10 = (bf16[128,128]{1,0:T(8,128)(2,1)S(1)}, bf16[128,128]{1,0:T(8,128)(2,1)}, u32[]{:S(2)}) copy-start(bf16[128,128]{1,0:T(8,128)(2,1)} %constant.648.clone.refs_6_) | copy-start | bytes 98308
  13.6 105.8 %all-gather.5.cloned.1.call-start = ((), (), s32[]{:S(2)}) async-start(), calls=%async_computation.1 | async-start | bytes 1949696 | tf_op jit(solution)/shard_map/all_gather | solution.py:363
  13.6 49.1 %collective-permute-start = (bf16[12,64,1024]{2,1,0:T(8,128)(2,1)S(1)}, bf16[12,64,1024]{2,1,0:T(8,128)(2,1)S(1)}, u32[]{:S(2)}, u32[]{:S(2)}) collective-permute-start(bf16[12,64,1024]{2,1,0:T(8,128)(2,1)S(1)} %bitcast.713), channel_id=1, source_target_pairs={{0,1},{1,0},{2,3},{3,2},{4,5},{5,4},{6,7},{7,6},{8,9},{9,8},{10,11... | collective-permute-start | bytes 4718600 | tf_op jit(solution)/shard_map/ppermute | solution.py:347
  17.3 18.4 %collective-permute-start.4 = (bf16[3,64,128]{2,1,0:T(8,128)(2,1)}, bf16[3,64,128]{2,1,0:T(8,128)(2,1)S(1)}, u32[]{:S(2)}, u32[]{:S(2)}) collective-permute-start(bf16[3,64,128]{2,1,0:T(8,128)(2,1)} %get-tuple-element.28), channel_id=1, source_target_pairs={{8,0},{16,8},{24,16},{9,1},{17,9},{25,17},{10,2},{18,10},{26,18},{... | collective-permute-start | bytes 147464 | tf_op jit(solution)/shard_map/ppermute | solution.py:361
  18.6 17.2 %collective-permute-start.3 = (bf16[3,64,128]{2,1,0:T(8,128)(2,1)S(1)}, bf16[3,64,128]{2,1,0:T(8,128)(2,1)S(1)}, u32[]{:S(2)}, u32[]{:S(2)}) collective-permute-start(bf16[3,64,128]{2,1,0:T(8,128)(2,1)S(1)} %get-tuple-element.29), channel_id=1, source_target_pairs={{0,8},{8,16},{16,24},{1,9},{9,17},{17,25},{2,10},{10,18},{18,26},{... | collective-permute-start | bytes 147464 | tf_op jit(solution)/shard_map/ppermute | solution.py:360
  23.1 12.6 %collective-permute-start.2 = (bf16[3,64,128]{2,1,0:T(8,128)(2,1)S(1)}, bf16[3,64,128]{2,1,0:T(8,128)(2,1)S(1)}, u32[]{:S(2)}, u32[]{:S(2)}) collective-permute-start(bf16[3,64,128]{2,1,0:T(8,128)(2,1)S(1)} %get-tuple-element.30), channel_id=1, source_target_pairs={{2,0},{4,2},{6,4},{3,1},{5,3},{7,5},{10,8},{12,10},{14,12},{11,9},... | collective-permute-start | bytes 147464 | tf_op jit(solution)/shard_map/ppermute | solution.py:359
  24.4 11.3 %collective-permute-start.1 = (bf16[3,64,128]{2,1,0:T(8,128)(2,1)S(1)}, bf16[3,64,128]{2,1,0:T(8,128)(2,1)S(1)}, u32[]{:S(2)}, u32[]{:S(2)}) collective-permute-start(bf16[3,64,128]{2,1,0:T(8,128)(2,1)S(1)} %get-tuple-element.31), channel_id=1, source_target_pairs={{0,2},{2,4},{4,6},{1,3},{3,5},{5,7},{8,10},{10,12},{12,14},{9,11},... | collective-permute-start | bytes 147464 | tf_op jit(solution)/shard_map/ppermute | solution.py:358
  35.7 26.7 %copy-start.14 = (s32[240]{0:T(256)}, s32[240]{0:T(256)S(1)}, u32[]{:S(2)}) copy-start(s32[240]{0:T(256)S(1)} %reshape.3984.refs_0_) | copy-start | bytes 2884
  59.8 7.5 %copy-start.6 = (bf16[128,1152]{1,0:T(8,128)(2,1)S(1)}, bf16[128,1152]{1,0:T(8,128)(2,1)}, u32[]{:S(2)}) copy-start(bf16[128,1152]{1,0:T(8,128)(2,1)} %constant.647.clone.refs_9_.refs_7_) | copy-start | bytes 884740
  59.8 7.5 %copy-start.9 = (bf16[1024,128]{1,0:T(8,128)(2,1)S(1)}, bf16[1024,128]{1,0:T(8,128)(2,1)}, u32[]{:S(2)}) copy-start(bf16[1024,128]{1,0:T(8,128)(2,1)} %constant.645.clone.refs_2_.refs_10_) | copy-start | bytes 786436
  59.9 7.5 %copy-start.13 = (bf16[128,128]{1,0:T(8,128)(2,1)S(1)}, bf16[128,128]{1,0:T(8,128)(2,1)}, u32[]{:S(2)}) copy-start(bf16[128,128]{1,0:T(8,128)(2,1)} %constant.646.clone.refs_3_.refs_11_) | copy-start | bytes 98308
  59.9 7.5 %copy-start.17 = (s32[2]{0:T(128)S(1)}, s32[2]{0:T(128)}, u32[]{:S(2)}) copy-start(s32[2]{0:T(128)} %copy-done.16) | copy-start | bytes 28
  59.9 7.5 %collective-permute-start.5 = (bf16[13,64,128]{2,1,0:T(8,128)(2,1)S(1)}, bf16[13,64,128]{2,1,0:T(8,128)(2,1)S(1)}, u32[]{:S(2)}, u32[]{:S(2)}) collective-permute-start(bf16[13,64,128]{2,1,0:T(8,128)(2,1)S(1)} %halo.2.refs_3_.refs_5_), channel_id=1, source_target_pairs={{0,1},{1,0},{2,3},{3,2},{4,5},{5,4},{6,7},{7,6},{8,9},{9,8},{10,11... | collective-permute-start | bytes 638984 | tf_op jit(solution)/shard_map/ppermute | solution.py:347
  79.7 49.9 %collective-permute-start.6 = (bf16[12,64,1024]{2,1,0:T(8,128)(2,1)}, bf16[12,64,1024]{2,1,0:T(8,128)(2,1)S(1)}, u32[]{:S(2)}, u32[]{:S(2)}) collective-permute-start(bf16[12,64,1024]{2,1,0:T(8,128)(2,1)} %copy-done.4), channel_id=1, source_target_pairs={{0,1},{1,0},{2,3},{3,2},{4,5},{5,4},{6,7},{7,6},{8,9},{9,8},{10,11... | collective-permute-start | bytes 4718600 | tf_op jit(solution)/shard_map/ppermute | solution.py:347
  81.3 10.2 %collective-permute-start.10 = (bf16[3,64,128]{2,1,0:T(8,128)(2,1)S(1)}, bf16[3,64,128]{2,1,0:T(8,128)(2,1)S(1)}, u32[]{:S(2)}, u32[]{:S(2)}) collective-permute-start(bf16[3,64,128]{2,1,0:T(8,128)(2,1)S(1)} %get-tuple-element.24), channel_id=1, source_target_pairs={{8,0},{16,8},{24,16},{9,1},{17,9},{25,17},{10,2},{18,10},{26,18},{... | collective-permute-start | bytes 147464 | tf_op jit(solution)/shard_map/ppermute | solution.py:361
  82.6 8.9 %collective-permute-start.9 = (bf16[3,64,128]{2,1,0:T(8,128)(2,1)S(1)}, bf16[3,64,128]{2,1,0:T(8,128)(2,1)S(1)}, u32[]{:S(2)}, u32[]{:S(2)}) collective-permute-start(bf16[3,64,128]{2,1,0:T(8,128)(2,1)S(1)} %get-tuple-element.25), channel_id=1, source_target_pairs={{0,8},{8,16},{16,24},{1,9},{9,17},{17,25},{2,10},{10,18},{18,26},{... | collective-permute-start | bytes 147464 | tf_op jit(solution)/shard_map/ppermute | solution.py:360
  87.1 4.4 %collective-permute-start.8 = (bf16[3,64,128]{2,1,0:T(8,128)(2,1)S(1)}, bf16[3,64,128]{2,1,0:T(8,128)(2,1)S(1)}, u32[]{:S(2)}, u32[]{:S(2)}) collective-permute-start(bf16[3,64,128]{2,1,0:T(8,128)(2,1)S(1)} %get-tuple-element.26), channel_id=1, source_target_pairs={{2,0},{4,2},{6,4},{3,1},{5,3},{7,5},{10,8},{12,10},{14,12},{11,9},... | collective-permute-start | bytes 147464 | tf_op jit(solution)/shard_map/ppermute | solution.py:359
  88.4 3.9 %collective-permute-start.7 = (bf16[3,64,128]{2,1,0:T(8,128)(2,1)S(1)}, bf16[3,64,128]{2,1,0:T(8,128)(2,1)S(1)}, u32[]{:S(2)}, u32[]{:S(2)}) collective-permute-start(bf16[3,64,128]{2,1,0:T(8,128)(2,1)S(1)} %get-tuple-element.27), channel_id=1, source_target_pairs={{0,2},{2,4},{4,6},{1,3},{3,5},{5,7},{8,10},{10,12},{12,14},{9,11},... | collective-permute-start | bytes 147464 | tf_op jit(solution)/shard_map/ppermute | solution.py:358
  123.6 7.6 %copy-start.5 = (bf16[12,64,1024]{2,1,0:T(8,128)(2,1)S(1)}, bf16[12,64,1024]{2,1,0:T(8,128)(2,1)}, u32[]{:S(2)}) copy-start(bf16[12,64,1024]{2,1,0:T(8,128)(2,1)} %copy-done.4) | copy-start | bytes 4718596
  123.6 7.6 %collective-permute-start.11 = (bf16[13,64,128]{2,1,0:T(8,128)(2,1)S(1)}, bf16[13,64,128]{2,1,0:T(8,128)(2,1)}, u32[]{:S(2)}, u32[]{:S(2)}) collective-permute-start(bf16[13,64,128]{2,1,0:T(8,128)(2,1)S(1)} %halo.3.refs_2_.refs_4_), channel_id=1, source_target_pairs={{0,1},{1,0},{2,3},{3,2},{4,5},{5,4},{6,7},{7,6},{8,9},{9,8},{10,11... | collective-permute-start | bytes 638984 | tf_op jit(solution)/shard_map/ppermute | solution.py:347
  (11 other events, 15.7 us)
Sparse Core Ops, SparseCore 0:
  13.7 43.3 all-gather.2
  79.9 39.5 all-gather.4

commit v2 on v1

v2 whole, which is shorter than its diff:
```python
import jax
import jax.numpy as jnp
import numpy as np
from jax import lax
from jax.experimental import pallas as pl
from jax.experimental.pallas import tpu as pltpu
from jax.sharding import PartitionSpec as P

RB = 32
GROUP = 4
LANES = 128
VMEM_LIMIT = 48 * 1024 * 1024
STRIP_LANE = (96, 0, 32, 64)


def ring_matrix(col_len):
    mat = np.zeros((col_len * RB, LANES), np.float32)
    for b in range(RB):
        mat[b, b] = 1
        mat[(col_len - 1) * RB + b, 32 + b] = 1
    for a in range(col_len):
        mat[a * RB, 64 + a] = 1
        mat[a * RB + RB - 1, 96 + a] = 1
    return mat


def corner_matrix():
    mat = np.zeros((LANES, LANES), np.float32)
    for q, lane in enumerate((0, RB - 1, 32, 32 + RB - 1)):
        mat[lane, q] = 1
    return mat


def reverse_matrix(unit):
    mat = np.zeros((LANES, LANES), np.float32)
    for lane in range(LANES):
        mat[lane, (lane // unit) * unit + unit - 1 - lane % unit] = 1
    return mat


def spread_matrix(col_len):
    width = col_len * RB + LANES
    mat = np.zeros((LANES, width), np.float32)
    top, bottom = (col_len + 3) * RB, col_len * RB
    mat[0, top] = 1
    mat[1, top + RB - 1] = 1
    mat[2, bottom] = 1
    mat[3, bottom + RB - 1] = 1
    for a in range(col_len):
        mat[STRIP_LANE[2] + a, a * RB] = 1
        mat[STRIP_LANE[3] + a, a * RB + RB - 1] = 1
    return mat


def lane_iota(shape):
    return lax.broadcasted_iota(jnp.int32, shape, len(shape) - 1)


def emit_rings(step, steps, fields, sel_ref, ring_ref, cornsel_ref, outs, packs_acc, corner_acc):
    chan = fields[0].shape[0]
    lane = lane_iota((chan, LANES))
    rings = [
        jnp.dot(field, ring_ref[...], preferred_element_type=jnp.float32) for field in fields
    ]
    for side in range(4):
        tile = jnp.zeros((chan, LANES), jnp.float32)
        for g, ring in enumerate(rings):
            moved = pltpu.roll(ring, ((g - side) * 32) % LANES, 1) if g != side else ring
            tile = jnp.where(lane // 32 == g, moved, tile)
        packs_acc[side * steps + step] = tile.astype(jnp.bfloat16)

    @pl.when(step == 0)
    def _():
        corner_acc[...] = jnp.zeros_like(corner_acc)

    for g, ring in enumerate(rings):
        picked = jnp.dot(
            ring.astype(jnp.bfloat16), cornsel_ref[...], preferred_element_type=jnp.float32
        )
        corner_acc[...] += pltpu.roll(picked, (step * GROUP + g) * 4, 1)

    @pl.when(step == steps - 1)
    def _():
        pack = 0
        for out in outs[:-1]:
            for at in range(0, out.shape[0], steps):
                base = sel_ref[pack] * steps
                for q in range(steps):
                    out[at + q] = packs_acc[base + q]
                pack += 1
        outs[-1][0] = corner_acc[...].astype(jnp.bfloat16)


def ring_outs(faces, chan, counts):
    steps = faces // GROUP
    tiles = [count * steps for count in counts] + [1]
    return [jax.ShapeDtypeStruct((n, chan, LANES), jnp.bfloat16) for n in tiles]


def ring_scratch(faces, chan):
    steps = faces // GROUP
    return [
        pltpu.VMEM((4 * steps, chan, LANES), jnp.bfloat16),
        pltpu.VMEM((chan, LANES), jnp.float32),
    ]


def rings_kernel(steps, sel_ref, field_ref, ring_ref, cornsel_ref, *refs):
    fields = [field_ref[g] for g in range(GROUP)]
    emit_rings(
        pl.program_id(0), steps, fields, sel_ref, ring_ref, cornsel_ref, refs[:-2], *refs[-2:]
    )


def whole_spec(array):
    zeros = (0,) * array.ndim
    return pl.BlockSpec(array.shape, lambda *_: zeros)


def rings_of(field, sel, ring, cornsel, counts):
    faces, chan, tile = field.shape
    steps = faces // GROUP
    outs = ring_outs(faces, chan, counts)
    return pl.pallas_call(
        lambda *refs: rings_kernel(steps, *refs),
        grid=(steps,),
        in_specs=[
            pl.BlockSpec(memory_space=pltpu.SMEM),
            pl.BlockSpec((GROUP, chan, tile), lambda i: (i, 0, 0)),
            whole_spec(ring),
            whole_spec(cornsel),
        ],
        out_specs=[whole_spec(out) for out in outs],
        out_shape=outs,
        scratch_shapes=ring_scratch(faces, chan),
        name="rings",
    )(sel, field, ring, cornsel)


def halo_kernel(faces, units, unit, *refs):
    (strip_tile, strip_shift, strip_rev, corner_at, corner_shift), refs = (refs[:5], refs[5:])
    tile_refs, (rev_ref, halo_ref, pool, turn_acc) = (refs[:-4], refs[-4:])
    chan = halo_ref.shape[1]
    lane = lane_iota((chan, LANES))
    at = 0
    for ref in tile_refs:
        pool[at : at + ref.shape[0]] = ref[...]
        at += ref.shape[0]
    corner_tile = jnp.zeros((chan, LANES), jnp.float32)
    most = max(units)
    for f in range(faces):
        tile = jnp.zeros((chan, LANES), jnp.float32)
        turned = jnp.zeros((chan, LANES), jnp.float32)
        for e in range(4):
            for un in range(units[e]):
                base = STRIP_LANE[e] + un * unit
                span = (lane >= base) & (lane < base + unit)
                entry = e * most + un
                moved = pltpu.roll(
                    pool[strip_tile[f, entry]].astype(jnp.float32), strip_shift[f, entry], 1
                )
                flip = strip_rev[f, entry] == 1
                tile = jnp.where(span & jnp.logical_not(flip), moved, tile)
                turned = jnp.where(span & flip, moved, turned)
        halo_ref[f] = tile.astype(jnp.bfloat16)
        turn_acc[f] = turned.astype(jnp.bfloat16)
        for c in range(4):
            moved = pltpu.roll(pool[corner_at[f, c]].astype(jnp.float32), corner_shift[f, c], 1)
            corner_tile = jnp.where(lane == f * 4 + c, moved, corner_tile)
    turned = jnp.dot(
        turn_acc[...].reshape(faces * chan, LANES), rev_ref[...], preferred_element_type=jnp.float32
    ).reshape(faces, chan, LANES)
    for f in range(faces):
        halo_ref[f] += turned[f].astype(jnp.bfloat16)
    halo_ref[faces] = corner_tile.astype(jnp.bfloat16)


def assemble_halo(tables, tiles, rev, faces, units, unit):
    chan = tiles[0].shape[1]
    halo = jax.ShapeDtypeStruct((faces + 1, chan, LANES), jnp.bfloat16)
    vmem = pl.BlockSpec(memory_space=pltpu.VMEM)
    smem = pl.BlockSpec(memory_space=pltpu.SMEM)
    return pl.pallas_call(
        lambda *refs: halo_kernel(faces, units, unit, *refs),
        in_specs=[smem] * len(tables) + [vmem] * (len(tiles) + 1),
        out_specs=vmem,
        out_shape=halo,
        scratch_shapes=[
            pltpu.VMEM((sum(t.shape[0] for t in tiles), chan, LANES), jnp.bfloat16),
            pltpu.VMEM((faces, chan, LANES), jnp.bfloat16),
        ],
        name="halo",
    )(*tables, *tiles, rev)


def conv_face(g, step, field_refs, halo_refs, corner_refs, taps_ref, spread_ref, stack_ref):
    chan, tile = field_refs[0].shape[1:]
    pieces = len(field_refs)
    total = chan * pieces
    width = tile + LANES
    for k in range(pieces):
        stack_ref[total + k * chan : total + (k + 1) * chan, :tile] = field_refs[k][g]
        stack_ref[total + k * chan : total + (k + 1) * chan, tile:] = halo_refs[k][g]
    halo = stack_ref[total : 2 * total, tile:].astype(jnp.float32)
    corners = jnp.concatenate([ref[0].astype(jnp.float32) for ref in corner_refs], axis=0)
    corners = pltpu.roll(corners, (LANES - (step * GROUP + g) * 4) % LANES, 1)
    lane = lane_iota((total, LANES))
    sides = jnp.where(lane < 4, corners, halo).astype(jnp.bfloat16)
    beside = jnp.dot(sides, spread_ref[...], preferred_element_type=jnp.float32)
    middle = stack_ref[total : 2 * total].astype(jnp.float32)
    col = lane_iota((total, width)) % RB
    stack_ref[:total] = jnp.where(col == 0, beside, pltpu.roll(middle, 1, 1)).astype(jnp.bfloat16)
    stack_ref[2 * total :] = jnp.where(
        col == RB - 1, beside, pltpu.roll(middle, width - 1, 1)
    ).astype(jnp.bfloat16)
    sums = jnp.dot(taps_ref[...], stack_ref[...], preferred_element_type=jnp.float32)
    above = pltpu.roll(sums[:chan], RB, 1)
    below = pltpu.roll(sums[2 * chan :], width - RB, 1)
    return (above + sums[chan : 2 * chan] + below)[:, :tile]


def forward_kernel(steps, pieces, sel_ref, *refs):
    field_refs, refs = (refs[:pieces], refs[pieces:])
    halo_refs, refs = (refs[:pieces], refs[pieces:])
    corner_refs, refs = (refs[:pieces], refs[pieces:])
    (cot_ref, taps_ref, spread_ref, ring_ref, cornsel_ref, act_ref, gated_ref) = refs[:7]
    outs, (stack_ref, packs_acc, corner_acc) = (refs[7:-3], refs[-3:])
    step = pl.program_id(0)
    fields = []
    for g in range(GROUP):
        pre = conv_face(g, step, field_refs, halo_refs, corner_refs, taps_ref, spread_ref, stack_ref)
        sig = 1.0 / (1.0 + jnp.exp(-pre))
        act_ref[g] = (pre * sig).astype(jnp.bfloat16)
        gated = cot_ref[g].astype(jnp.float32) * sig * (1.0 + pre * (1.0 - sig))
        gated_ref[g] = gated.astype(jnp.bfloat16)
        fields.append(gated.astype(jnp.bfloat16))
    emit_rings(step, steps, fields, sel_ref, ring_ref, cornsel_ref, outs, packs_acc, corner_acc)


def backward_kernel(steps, pieces, *refs):
    field_refs, refs = (refs[:pieces], refs[pieces:])
    halo_refs, refs = (refs[:pieces], refs[pieces:])
    corner_refs, refs = (refs[:pieces], refs[pieces:])
    (taps_ref, spread_ref, grad_ref, stack_ref) = refs
    step = pl.program_id(0)
    for g in range(GROUP):
        total = conv_face(
            g, step, field_refs, halo_refs, corner_refs, taps_ref, spread_ref, stack_ref
        )
        grad_ref[g] = total.astype(jnp.bfloat16)


def conv_specs(fields, halos):
    faces, chan, tile = fields[0].shape
    group = lambda i: (i, 0, 0)
    return (
        [pl.BlockSpec((GROUP, chan, tile), group) for _ in fields]
        + [pl.BlockSpec((GROUP, chan, LANES), group) for _ in halos]
        + [pl.BlockSpec((1, chan, LANES), lambda i: (faces, 0, 0)) for _ in halos]
    )


def forward(sel, fields, halos, cot, taps, spread, ring, cornsel, counts):
    faces, chan, tile = fields[0].shape
    steps = faces // GROUP
    pieces = len(fields)
    outs = ring_outs(faces, chan, counts)
    out = jax.ShapeDtypeStruct((faces, chan, tile), jnp.bfloat16)
    block = pl.BlockSpec((GROUP, chan, tile), lambda i: (i, 0, 0))
    return pl.pallas_call(
        lambda *refs: forward_kernel(steps, pieces, *refs),
        grid=(steps,),
        in_specs=[pl.BlockSpec(memory_space=pltpu.SMEM)]
        + conv_specs(fields, halos)
        + [block, whole_spec(taps), whole_spec(spread), whole_spec(ring), whole_spec(cornsel)],
        out_specs=[block, block] + [whole_spec(o) for o in outs],
        out_shape=[out, out] + outs,
        scratch_shapes=[pltpu.VMEM((3 * chan * pieces, tile + LANES), jnp.bfloat16)]
        + ring_scratch(faces, chan),
        compiler_params=pltpu.CompilerParams(vmem_limit_bytes=VMEM_LIMIT),
        name="forward",
    )(sel, *fields, *halos, *halos, cot, taps, spread, ring, cornsel)


def backward(fields, halos, taps, spread):
    faces, chan, tile = fields[0].shape
    steps = faces // GROUP
    pieces = len(fields)
    return pl.pallas_call(
        lambda *refs: backward_kernel(steps, pieces, *refs),
        grid=(steps,),
        in_specs=conv_specs(fields, halos) + [whole_spec(taps), whole_spec(spread)],
        out_specs=pl.BlockSpec((GROUP, chan, tile), lambda i: (i, 0, 0)),
        out_shape=jax.ShapeDtypeStruct((faces, chan, tile), jnp.bfloat16),
        scratch_shapes=[pltpu.VMEM((3 * chan * pieces, tile + LANES), jnp.bfloat16)],
        compiler_params=pltpu.CompilerParams(vmem_limit_bytes=VMEM_LIMIT),
        name="backward",
    )(*fields, *halos, *halos, taps, spread)


def halo_tables(edge_table, corner_table, place, counts, col_len, unit, strip_cell, near_cell, corner_cell):
    row_pos, col_pos = place
    px_count, py_count = counts
    faces = edge_table.shape[0]
    side_len = px_count * RB
    most = RB // unit
    shape = (faces, 4, most)
    face = lax.broadcasted_iota(jnp.int32, shape, 0)
    edge = lax.broadcasted_iota(jnp.int32, shape, 1)
    un = lax.broadcasted_iota(jnp.int32, shape, 2)
    g, s, r = [edge_table[:, :, i, None] for i in range(3)]
    along_row = edge < 2
    border = ((edge == 0) & (col_pos == 0)) | ((edge == 1) & (col_pos == py_count - 1))
    border |= ((edge == 2) & (row_pos == 0)) | ((edge == 3) & (row_pos == px_count - 1))
    at = jnp.where(along_row, row_pos * RB, col_pos * col_len) + un * unit
    at = jnp.clip(at, 0, side_len - unit)
    at = jnp.where(r == 1, side_len - unit - at, at)
    line_tile, line_lane = strip_cell(g, s, at)
    tile = jnp.where(border, line_tile, near_cell(edge, face))
    lane = jnp.where(border, line_lane, (face % GROUP) * 32 + un * unit)
    first = jnp.where(edge == 0, STRIP_LANE[0], jnp.where(edge == 1, STRIP_LANE[1], edge * 32 - 32))
    shift = (first + un * unit - lane + LANES) % LANES
    flip = jnp.where(border & (r == 1), 1, 0)
    strips = [jnp.broadcast_to(v, shape).reshape(faces, 4 * most) for v in (tile, shift, flip)]

    shape = (faces, 2, 2)
    face = lax.broadcasted_iota(jnp.int32, shape, 0)
    down = lax.broadcasted_iota(jnp.int32, shape, 1)
    right = lax.broadcasted_iota(jnp.int32, shape, 2)
    row_on = ((down == 0) & (col_pos == 0)) | ((down == 1) & (col_pos == py_count - 1))
    col_on = ((right == 0) & (row_pos == 0)) | ((right == 1) & (row_pos == px_count - 1))
    row_at = row_pos * RB + jnp.where(right == 1, RB, -1)
    col_at = col_pos * col_len + jnp.where(down == 1, col_len, -1)
    row_edge = [edge_table[:, :2, None, i] for i in range(3)]
    col_edge = [edge_table[:, None, 2:, i] for i in range(3)]
    g, s, r = [jnp.where(row_on, row, col) for row, col in zip(row_edge, col_edge)]
    at = jnp.clip(jnp.where(row_on, row_at, col_at), 0, side_len - 1)
    at = jnp.where(r == 1, side_len - 1 - at, at)
    h, q = [corner_table[:, :, i].reshape(shape) for i in range(2)]
    both = row_on & col_on
    g, s, at = (
        jnp.where(both, h, g),
        jnp.where(both, q // 2, s),
        jnp.where(both, (q % 2) * (side_len - 1), at),
    )
    line_tile, line_lane = corner_cell(g, s, at, None, None)
    diag_px = jnp.clip(row_pos + 2 * right - 1, 0, px_count - 1)
    diag_py = jnp.clip(col_pos + 2 * down - 1, 0, py_count - 1)
    diag_tile, diag_lane = corner_cell(face, None, 3 - 2 * down - right, diag_px, diag_py)
    on = row_on | col_on
    corner_at = jnp.where(on, line_tile, diag_tile)
    corner_lane = jnp.where(on, line_lane, diag_lane)
    corner_shift = (face * 4 + 2 * down + right - corner_lane + LANES) % LANES
    return (
        *strips,
        corner_at.reshape(faces, 4),
        corner_shift.reshape(faces, 4),
    )


def from_others(array, ch_count):
    return [array] + [
        lax.ppermute(array, "ch", [(i, (i + k) % ch_count) for i in range(ch_count)])
        for k in range(1, ch_count)
    ]


class SquareHalo:
    counts = (1, 1, 2, 2)

    def __init__(self, row_pos, col_pos):
        self.place = (row_pos, col_pos)
        self.row_edge = (row_pos == 0) | (row_pos == 3)
        self.col_edge = (col_pos == 0) | (col_pos == 3)
        self.corner = self.row_edge & self.col_edge
        self.middle = self.row_edge != self.col_edge
        self.side = jnp.where(
            self.col_edge, jnp.where(col_pos == 0, 0, 1), jnp.where(row_pos == 0, 2, 3)
        )
        self.seg = jnp.where(self.col_edge, row_pos, col_pos)
        row_line = jnp.where(col_pos == 0, 0, 1)
        col_line = jnp.where(row_pos == 0, 2, 3)
        to_px, to_py = (jnp.where(row_pos == 1, 3, 2), jnp.where(col_pos == 1, 1, 0))
        self.sel = jnp.stack(
            [
                jnp.where(row_pos % 2 == 0, 3, 2),
                jnp.where(col_pos % 2 == 0, 1, 0),
                self.side,
                jnp.where(self.row_edge, to_py, to_px),
                jnp.where(self.corner, row_line, jnp.where(self.middle, self.side, to_py)),
                jnp.where(self.corner, col_line, self.side),
            ]
        ).astype(jnp.int32)

    def exchange(self, col_side, row_side, pair, lines, corner):
        every = [(x, y) for x in range(4) for y in range(4)]
        number = lambda x, y: x * 4 + y
        axes = ("px", "py")
        swap = lambda array, pairs: lax.ppermute(
            array, axes, [(number(*a), number(*b)) for a, b in pairs]
        )
        ends = (0, 3)
        corners = [(x, y) for x in ends for y in ends]
        spot = lambda side, seg: ((seg, 0), (seg, 3), (0, seg), (3, seg))[side]
        near_col = swap(col_side, [((x, y), (x ^ 1, y)) for x, y in every])
        near_row = swap(row_side, [((x, y), (x, y ^ 1)) for x, y in every])
        beside = [(spot(side, k), spot(side, 3 - k)) for side in range(4) for k in (1, 2)]
        beside += [((x, y), (3 - x, y)) for x in (1, 2) for y in (1, 2)]
        paired = swap(pair, beside)
        slot = lax.broadcasted_iota(jnp.int32, lines.shape, 0) // (lines.shape[0] // 2)
        theirs = self.middle & (slot != self.seg - 1)
        half = paired[: lines.shape[0] // 2]
        lines = jnp.where(theirs, jnp.concatenate([half, half], axis=0), lines)
        across = []
        for j in (1, 2, 3):
            pairs = [(spot(side, k), spot(side ^ j, k)) for side in range(4) for k in (1, 2)]
            pairs += [(corners[c], corners[c ^ j]) for c in range(4)]
            if j == 1:
                pairs += [((x, y), (x, 3 - y)) for x in (1, 2) for y in (1, 2)]
            across.append(swap(lines, pairs))
        ends_of = jnp.broadcast_to(corner, (16,) + corner.shape[1:])
        ends_of = lax.all_to_all(ends_of, axes, 0, 0, tiled=True)
        return [lines, *across, paired, near_col, near_row, ends_of]

    def tables(self, edge_table, corner_table, col_len, unit):
        row_pos, col_pos = self.place
        quads = edge_table.shape[0] // GROUP
        slot = 2 * quads

        def strip_cell(g, s, at):
            k = at // RB
            lane = (g % GROUP) * 32
            me = jnp.where(row_pos > 0, 2, 0) + jnp.where(col_pos > 0, 1, 0)
            far = jnp.where(k > 0, 1, 0)
            owner = jnp.where(s < 2, 2 * far + s, 2 * (s - 2) + far)
            corner = (me ^ owner) * slot + (s // 2) * quads
            middle = (self.side ^ s) * slot + (k - 1) * quads
            return (jnp.where(self.corner, corner, middle) + g // GROUP, lane)

        def near_cell(edge, face):
            paired, near_col, near_row = (4 * slot + quads, 5 * slot, 5 * slot + quads)
            by_col = jnp.where(row_pos % 2 == 3 - edge, near_col, paired)
            rest = jnp.where(self.row_edge, paired, slot)
            by_row = jnp.where(col_pos % 2 == 1 - edge, near_row, rest)
            return jnp.where(edge < 2, by_row, by_col) + face // GROUP

        def corner_cell(g, s, at, px, py):
            base = 5 * slot + 2 * quads
            if s is None:
                return (base + px * 4 + py, g * 4 + at)
            seg, hi = (at // RB, jnp.where(at % RB == 0, 0, 1))
            owner = jnp.where(s < 2, seg * 4 + 3 * s, 12 * (s - 2) + seg)
            q = jnp.where(s < 2, 2 * s + hi, s - 2 + 2 * hi)
            return (base + owner, g * 4 + q)

        return halo_tables(
            edge_table, corner_table, self.place, (4, 4), col_len, unit,
            strip_cell, near_cell, corner_cell,
        )


class GatheredHalo:
    counts = (1, 1, 1, 1, 2)

    def __init__(self, row_pos, col_pos, px_count, py_count):
        self.place = (row_pos, col_pos)
        self.size = (px_count, py_count)
        lines = [jnp.where(col_pos == 0, 0, 1), jnp.where(row_pos == 0, 2, 3)]
        self.sel = jnp.stack([jnp.int32(side) for side in range(4)] + lines).astype(jnp.int32)

    def exchange(self, top, bottom, left, right, lines, corner):
        px_count, py_count = self.size
        up = lambda n: [(i, i + 1) for i in range(n - 1)]
        down = lambda n: [(i + 1, i) for i in range(n - 1)]
        return [
            lax.ppermute(bottom, "py", up(py_count)),
            lax.ppermute(top, "py", down(py_count)),
            lax.ppermute(right, "px", up(px_count)),
            lax.ppermute(left, "px", down(px_count)),
            lax.all_gather(lines, ("px", "py"), axis=0, tiled=True),
            lax.all_gather(corner, ("px", "py"), axis=0, tiled=True),
        ]

    def tables(self, edge_table, corner_table, col_len, unit):
        px_count, py_count = self.size
        quads = edge_table.shape[0] // GROUP
        line_base = 4 * quads
        corner_base = line_base + px_count * py_count * 2 * quads

        def strip_cell(g, s, at):
            length = jnp.where(s < 2, RB, col_len)
            seg = at // length
            px = jnp.where(s < 2, seg, (s - 2) * (px_count - 1))
            py = jnp.where(s < 2, s * (py_count - 1), seg)
            tile = line_base + ((px * py_count + py) * 2 + s // 2) * quads + g // GROUP
            return (tile, (g % GROUP) * 32 + at % length)

        def near_cell(edge, face):
            return edge * quads + face // GROUP

        def corner_cell(g, s, at, px, py):
            if s is None:
                return (corner_base + px * py_count + py, g * 4 + at)
            return strip_cell(g, s, at)

        return halo_tables(
            edge_table, corner_table, self.place, self.size, col_len, unit,
            strip_cell, near_cell, corner_cell,
        )


def local(features, cotangent, weight, edge_table, corner_table):
    chan, faces = features.shape[:2]
    tile = features.shape[4]
    col_len = tile // RB
    unit = min(RB, col_len)
    units = (RB // unit, RB // unit, col_len // unit, col_len // unit)
    px_count, py_count, ch_count = [lax.axis_size(name) for name in ("px", "py", "ch")]
    row_pos, col_pos, ch_pos = [lax.axis_index(name) for name in ("px", "py", "ch")]
    ring = jnp.asarray(ring_matrix(col_len), jnp.bfloat16)
    cornsel = jnp.asarray(corner_matrix(), jnp.bfloat16)
    spread = jnp.asarray(spread_matrix(col_len), jnp.bfloat16)
    rev = jnp.asarray(reverse_matrix(unit), jnp.bfloat16)
    if px_count == py_count == 4 and col_len == RB:
        halo_plan = SquareHalo(row_pos, col_pos)
    else:
        halo_plan = GatheredHalo(row_pos, col_pos, px_count, py_count)
    counts, sel = (halo_plan.counts, halo_plan.sel)

    feats = jnp.transpose(features.reshape(chan, faces, tile), (1, 0, 2))
    cot = jnp.transpose(cotangent.reshape(chan, faces, tile), (1, 0, 2))
    fields = from_others(feats, ch_count)

    def blocks(array, axis):
        order = [(ch_pos - k) % ch_count for k in range(ch_count)]
        return jnp.concatenate(
            [lax.dynamic_slice_in_dim(array, at * chan, chan, axis) for at in order], axis
        )

    own_out = lax.dynamic_slice_in_dim(weight, ch_pos * chan, chan, 2)
    taps = blocks(own_out, 3).transpose(0, 2, 1, 3).reshape(3 * chan, -1)
    own_in = lax.dynamic_slice_in_dim(weight, ch_pos * chan, chan, 3)
    back_taps = blocks(own_in, 2)[::-1, ::-1].transpose(0, 3, 1, 2).reshape(3 * chan, -1)
    tables = halo_plan.tables(edge_table, corner_table, col_len, unit)

    parts = rings_of(feats, sel, ring, cornsel, counts)
    tiles = halo_plan.exchange(*parts)
    halo = assemble_halo(tables, tiles, rev, faces, units, unit)
    halo, taps, back_taps = lax.optimization_barrier((halo, taps, back_taps))
    halos = from_others(halo, ch_count)
    act, gated, *parts = forward(sel, fields, halos, cot, taps, spread, ring, cornsel, counts)

    fields = from_others(gated, ch_count)
    tiles = halo_plan.exchange(*parts)
    halo = assemble_halo(tables, tiles, rev, faces, units, unit)
    halos = from_others(halo, ch_count)
    grad = backward(fields, halos, back_taps, spread)

    shape = (chan, faces, 1, 1, tile)
    return (
        jnp.transpose(act, (1, 0, 2)).reshape(shape),
        jnp.transpose(grad, (1, 0, 2)).reshape(shape),
    )


def solution(mesh):
    spec = P("ch", None, "py", "px", None)
    return jax.shard_map(
        local,
        mesh=mesh,
        in_specs=(spec, spec, P(), P(), P()),
        out_specs=(spec, spec),
        check_vma=False,
    )
```

time: 149 us -> 136 us (0.913)
  waiting for transfers between devices: 55.5 us -> 14.6 us
  starting transfers between devices: 28 us -> 46.8 us
  between operations: 14.4 us -> 1.02 us
  other arithmetic: 7 us -> 15.9 us
  local copies, waits for them, and re-layouts: 17.3 us -> 25.5 us
  Pallas kernels: 25.7 us -> 30 us
    all_gather x2 -> x0, waiting for transfers between devices: 48.4 us -> none  [exchange_halo(): lines = lax.all_gather(shard, ('px', 'py'), axis=0, tiled=True)]
    all_to_all x0 -> x2, starting transfers between devices: none -> 11.1 us  [exchange(): ends_of = lax.all_to_all(ends_of, axes, 0, 0, tiled=True)]
    ppermute x8 -> x12, starting transfers between devices: 20.3 us -> 30.2 us  [exchange(): lax.ppermute(array, axes, [(number(*a), number(*b)) for a, b in pairs])]
    broadcast_in_dim x0 -> x15, local copies, waits for them, and re-layouts: none -> 5.17 us  [the longest x13 2.95 us: halo_tables(): jnp.where(row_on, row, col)]
    ppermute x4, waiting for transfers between devices: 6.21 us -> 11.1 us  [from_others(): lax.ppermute(array, 'ch', [(i, (i + k) % ch_count) for i in range(ch_coun...]
    reshape x1 -> x4, local copies, waits for them, and re-layouts: 0.08 us -> 4.39 us  [the longest x3 2.7 us: halo_tables(): jnp.broadcast_to(v, shape).reshape(faces, 4 * most)]
    unnamed x44 -> x56, local copies, waits for them, and re-layouts: 10.7 us -> 7.04 us
    iota x0 -> x12, local copies, waits for them, and re-layouts: none -> 3.27 us  [the longest x7 2.1 us: halo_tables(): down = lax.broadcasted_iota(jnp.int32, shape, 1)]
  transfers between devices with their start and end apart: 14 -> 18, of which waited for: 5 -> 4; matrix products, arithmetic and copies ran while one was open for 10% -> 26% of each run, Pallas kernels for 2% -> 7%
where the time goes in v2:
time: 136 us; the launch traced here: 134 us
  starting transfers between devices  46.8 us (34%)
  Pallas kernels  30 us (22%)
  local copies, waits for them, and re-layouts  25.5 us (19%)
  other arithmetic  15.9 us (12%)
  waiting for transfers between devices  14.6 us (11%)
    ppermute x12, starting transfers between devices, exchange(): lax.ppermute(array, axes, [(number(*a), number(*b)) for a, b in pairs])  30.2 us
    ppermute x4, waiting for transfers between devices, from_others(): lax.ppermute(array, 'ch', [(i, (i + k) % ch_count) for i in range(ch_coun...  11.1 us
    pallas_call x1, Pallas kernels, forward(): pl.pallas_call(lambda *refs: forward_kernel(steps, pieces, *refs), grid=(...  11.1 us
    all_to_all x2, starting transfers between devices, exchange(): ends_of = lax.all_to_all(ends_of, axes, 0, 0, tiled=True)  11.1 us
    pallas_call x1, Pallas kernels, backward(): pl.pallas_call(lambda *refs: backward_kernel(steps, pieces, *refs), grid=...  9.07 us
    unnamed x56, local copies, waits for them, and re-layouts  7.04 us
    pallas_call x2, Pallas kernels, assemble_halo(): pl.pallas_call(lambda *refs: halo_kernel(faces, units, unit, *refs), in_s...  5.71 us
    ppermute x4, starting transfers between devices, from_others(): lax.ppermute(array, 'ch', [(i, (i + k) % ch_count) for i in range(ch_coun...  5.57 us
  transfers between devices with their start and end apart: 18, of which 4 were waited for; matrix products, arithmetic and copies ran while one was open for 26% of the time, Pallas kernels for 7%

profile of v2, /device:TPU:0, one launch (start us, length us, event | category | flops | bytes accessed | tf_op | source)
XLA Modules:
  0.0 133.7 jit_solution(8721599342016561426)
XLA Ops:
  0.7 3.0 %collective-permute-start = (bf16[12,64,1024]{2,1,0:T(8,128)(2,1)}, bf16[12,64,1024]{2,1,0:T(8,128)(2,1)S(1)}, u32[]{:S(2)}, u32[]{:S(2)}) collective-permute-start(bf16[12,64,1024]{2,1,0:T(8,128)(2,1)} %bitcast.62), channel_id=1, source_target_pairs={{0,1},{1,0},{2,3},{3,2},{4,5},{5,4},{6,7},{7,6},{8,9},{9,8},{10,11... | collective-permute-start | bytes 4718600 | tf_op jit(solution)/shard_map/ppermute | solution.py:363
  4.3 4.2 %rings.1 = (bf16[3,64,128]{2,1,0:T(8,128)(2,1)}, bf16[3,64,128]{2,1,0:T(8,128)(2,1)}, bf16[6,64,128]{2,1,0:T(8,128)(2,1)}, bf16[6,64,128]{2,1,0:T(8,128)(2,1)}, bf16[1,64,128]{2,1,0:T(8,128)(2,1)}) custom-call(s32[6]{0:T(128)} %stack.27.refs_0_, bf16[12,64,1024]{2,1,0:T(8,128)(2,1)} %bitcast.63, bf16[1024,128]{1,0:T(8,128)(2,1)} %constant.292.clone.refs_2_.refs_10_, ...), custom_call_target="tpu_custom_call" | custom-call | tf_op jit(solution)/shard_map/rings/pallas_call | solution.py:124
  8.4 1.6 %collective-permute-start.5 = (bf16[3,64,128]{2,1,0:T(8,128)(2,1)}, bf16[3,64,128]{2,1,0:T(8,128)(2,1)S(1)}, u32[]{:S(2)}, u32[]{:S(2)}) collective-permute-start(bf16[3,64,128]{2,1,0:T(8,128)(2,1)} %get-tuple-element.19), channel_id=1, source_target_pairs={{0,8},{2,10},{4,12},{6,14},{8,0},{10,2},{12,4},{14,6},{16,24},{18,... | collective-permute-start | bytes 147464 | tf_op jit(solution)/shard_map/ppermute | solution.py:399
  11.3 1.5 %broadcast_in_dim.144 = bf16[16,64,128]{2,1,0:T(8,128)(2,1)} broadcast(bf16[64,128]{1,0:T(8,128)(2,1)} %bitcast.70), dimensions={1,2} | broadcast | bytes 278528 | tf_op jit(solution)/shard_map/broadcast_in_dim | solution.py:421
  12.8 6.2 %all-to-all-start = ((bf16[16,64,128]{2,1,0:T(8,128)(2,1)}), bf16[16,64,128]{2,1,0:T(8,128)(2,1)}, u32[]{:S(2)}, u32[]{:S(2)}) async-start(bf16[16,64,128]{2,1,0:T(8,128)(2,1)} %broadcast_in_dim.144), calls=%async_computation | async-start | bytes 524288 | tf_op jit(solution)/shard_map/all_to_all | solution.py:422
  37.8 1.4 %select_bitcast_fusion = (s32[12,4]{0,1:T(4,128)}, pred[12,4,1]{0,1,2:T(4,128)(4,1)}, s32[12,4]{0,1:T(4,128)S(1)}, pred[12,4,1]{0,1,2:T(4,128)(4,1)}) fusion(pred[4]{0:T(512)(128)(4,1)} %or_or_fusion, s32[12,4,3]{0,1,2:T(4,128)} %param.12, s32[12]{0:T(128)} %get-tuple-element.66, s32[12]{0:T(128)} %get-tuple-element.67, pred[12]{0:T(512)(128)(4,1)} %get-tuple-element.62, ...), kind=kLoop, calls=%fused_computation.84 | loop fusion | flops 1584 | bytes 1000 | tf_op jit(solution)/shard_map/reshape | solution.py:324
  39.2 1.5 %add_select_fusion = (s32[12,4]{1,0:T(8,128)}, s32[12,4]{1,0:T(8,128)S(1)}) fusion(s32[12,4]{1,0:T(8,128)} %copy.42, s32[12,4]{1,0:T(8,128)} %copy.40, s32[12,4]{1,0:T(8,128)} %copy.41, s32[4]{0:T(128)S(1)} %sub.126, s32[4]{0:T(128)} %iota.201, s32[4]{0:T(128)} %iota.198, s32[12]{0:T(128)S(1)} %iota_multiply_fusion, pred[4]{0:T(512)(128)(4,1)} %copy-done.23, ...), kind=kLoop, calls=%fused_computation.9 | loop fusion | flops 3360 | bytes 2060 | tf_op jit(solution)/shard_map/jit(remainder)/select_n | solution.py:353
  41.9 1.7 %copy_bitcast_fusion = (bf16[192,384]{1,0:T(8,128)(2,1)}, bf16[192,384]{1,0:T(8,128)(2,1)}) fusion(bf16[24,8,3,128]{3,2,1,0:T(4,128)(2,1)} %bitcast.68, bf16[24,8,3,128]{3,2,1,0:T(4,128)(2,1)S(1)} %bitcast.69), kind=kLoop, calls=%fused_computation.6 | loop fusion | bytes 589824 | tf_op jit(solution)/shard_map/reshape | solution.py:543
  44.4 1.6 %fusion.2.refs_5_ = bf16[6,64,128]{2,1,0:T(8,128)(2,1)} fusion(bf16[6,64,128]{2,1,0:T(8,128)(2,1)} %get-tuple-element.18, bf16[3,64,128]{2,1,0:T(8,128)(2,1)S(1)} %slice.52, s32[]{:T(128)S(6)} %sub.129, s32[6]{0:T(128)} %get-tuple-element.73, s32[6]{0:T(128)} %get-tuple-element.74, pred[6]{0:T(512)(128)(4,1)} %compare_and_fusion, pred[]{:T(512)S(6)} %ne.170), kind=kLoop, calls=%fused_computation.5 | loop fusion | flops 393216 | bytes 245819 | tf_op jit(solution)/shard_map/jit(_where)/select_n | solution.py:413
  46.0 6.2 %collective-permute-start.4 = (bf16[6,64,128]{2,1,0:T(8,128)(2,1)}, bf16[6,64,128]{2,1,0:T(8,128)(2,1)}, u32[]{:S(2)}, u32[]{:S(2)}) collective-permute-start(bf16[6,64,128]{2,1,0:T(8,128)(2,1)} %fusion.2.refs_5_), channel_id=1, source_target_pairs={{8,26},{16,28},{14,2},{22,4},{2,14},{4,22},{26,8},{28,16},{0,30},{... | collective-permute-start | bytes 294920 | tf_op jit(solution)/shard_map/ppermute | solution.py:399
  52.2 2.5 %collective-permute-start.3 = (bf16[6,64,128]{2,1,0:T(8,128)(2,1)}, bf16[6,64,128]{2,1,0:T(8,128)(2,1)}, u32[]{:S(2)}, u32[]{:S(2)}) collective-permute-start(bf16[6,64,128]{2,1,0:T(8,128)(2,1)} %fusion.2.refs_5_), channel_id=1, source_target_pairs={{8,2},{16,4},{14,26},{22,28},{2,8},{4,16},{26,14},{28,22},{0,24},{... | collective-permute-start | bytes 294920 | tf_op jit(solution)/shard_map/ppermute | solution.py:399
  58.3 2.6 %collective-permute-done.3.refs_7_ = bf16[6,64,128]{2,1,0:T(8,128)(2,1)} collective-permute-done((bf16[6,64,128]{2,1,0:T(8,128)(2,1)}, bf16[6,64,128]{2,1,0:T(8,128)(2,1)}, u32[]{:S(2)}, u32[]{:S(2)}) %collective-permute-start.3) | collective-permute-done | bytes 98336 | tf_op jit(solution)/shard_map/ppermute | solution.py:399
  60.9 2.9 %halo.2.refs_3_.refs_5_ = bf16[13,64,128]{2,1,0:T(8,128)(2,1)} custom-call(s32[12,4]{1,0:T(8,128)} %copy.43.refs_0_, s32[12,4]{1,0:T(8,128)} %copy.44.refs_1_, s32[12,4]{1,0:T(8,128)} %copy.45.refs_2_, s32[12,4]{1,0:T(8,128)} %add_select_fusion.5.refs_3_, s32[12,4]{1,0:T(8,128)} %get-tuple-element.36.refs_4_, bf16[6,64,128]{2,1,0:T(8,128)(2,1)} %fusion.2.refs_5_, ...), custom_call_target="tpu_custom_call" | custom-call | tf_op jit(solution)/shard_map/halo/pallas_call | solution.py:183
  64.3 5.6 %collective-permute-done.7.refs_4_.refs_6_ = bf16[13,64,128]{2,1,0:T(8,128)(2,1)S(1)} collective-permute-done((bf16[13,64,128]{2,1,0:T(8,128)(2,1)}, bf16[13,64,128]{2,1,0:T(8,128)(2,1)S(1)}, u32[]{:S(2)}, u32[]{:S(2)}) %collective-permute-start.7) | collective-permute-done | bytes 213024 | tf_op jit(solution)/shard_map/ppermute | solution.py:363
  72.7 11.1 %forward.1 = (bf16[12,64,1024]{2,1,0:T(8,128)(2,1)}, bf16[12,64,1024]{2,1,0:T(8,128)(2,1)}, bf16[3,64,128]{2,1,0:T(8,128)(2,1)S(1)}, bf16[3,64,128]{2,1,0:T(8,12...) custom-call(s32[6]{0:T(128)S(1)} %copy-done.9, ...), custom_call_target="tpu_custom_call" | custom-call | tf_op jit(solution)/shard_map/forward/pallas_call | solution.py:270
  87.0 4.9 %all-to-all-start.1 = ((bf16[16,64,128]{2,1,0:T(8,128)(2,1)}), bf16[16,64,128]{2,1,0:T(8,128)(2,1)S(1)}, u32[]{:S(2)}, u32[]{:S(2)}) async-start(bf16[16,64,128]{2,1,0:T(8,128)(2,1)} %broadcast_in_dim.146), calls=%async_computation.1 | async-start | bytes 524288 | tf_op jit(solution)/shard_map/all_to_all | solution.py:422
  92.6 4.7 %collective-permute-start.13 = (bf16[3,64,128]{2,1,0:T(8,128)(2,1)}, bf16[3,64,128]{2,1,0:T(8,128)(2,1)S(1)}, u32[]{:S(2)}, u32[]{:S(2)}) collective-permute-start(bf16[3,64,128]{2,1,0:T(8,128)(2,1)} %copy-done.11), channel_id=1, source_target_pairs={{0,8},{2,10},{4,12},{6,14},{8,0},{10,2},{12,4},{14,6},{16,24},{18,... | collective-permute-start | bytes 147464 | tf_op jit(solution)/shard_map/ppermute | solution.py:399
  98.3 3.5 %collective-permute-start.12 = (bf16[6,64,128]{2,1,0:T(8,128)(2,1)S(1)}, bf16[6,64,128]{2,1,0:T(8,128)(2,1)S(1)}, u32[]{:S(2)}, u32[]{:S(2)}) collective-permute-start(bf16[6,64,128]{2,1,0:T(8,128)(2,1)S(1)} %fusion.1.refs_5_), channel_id=1, source_target_pairs={{8,26},{16,28},{14,2},{22,4},{2,14},{4,22},{26,8},{28,16},{0,30},{... | collective-permute-start | bytes 294920 | tf_op jit(solution)/shard_map/ppermute | solution.py:399
  101.8 4.3 %collective-permute-start.11 = (bf16[6,64,128]{2,1,0:T(8,128)(2,1)S(1)}, bf16[6,64,128]{2,1,0:T(8,128)(2,1)S(1)}, u32[]{:S(2)}, u32[]{:S(2)}) collective-permute-start(bf16[6,64,128]{2,1,0:T(8,128)(2,1)S(1)} %fusion.1.refs_5_), channel_id=1, source_target_pairs={{8,2},{16,4},{14,26},{22,28},{2,8},{4,16},{26,14},{28,22},{0,24},{... | collective-permute-start | bytes 294920 | tf_op jit(solution)/shard_map/ppermute | solution.py:399
  106.9 4.6 %collective-permute-start.14 = (bf16[3,64,128]{2,1,0:T(8,128)(2,1)S(1)}, bf16[3,64,128]{2,1,0:T(8,128)(2,1)S(1)}, u32[]{:S(2)}, u32[]{:S(2)}) collective-permute-start(bf16[3,64,128]{2,1,0:T(8,128)(2,1)S(1)} %get-tuple-element.29), channel_id=1, source_target_pairs={{0,2},{2,0},{4,6},{6,4},{8,10},{10,8},{12,14},{14,12},{16,18},{18,... | collective-permute-start | bytes 147464 | tf_op jit(solution)/shard_map/ppermute | solution.py:399
  113.9 2.8 %halo.3.refs_2_.refs_4_ = bf16[13,64,128]{2,1,0:T(8,128)(2,1)} custom-call(s32[12,4]{1,0:T(8,128)} %copy.43.refs_0_, s32[12,4]{1,0:T(8,128)} %copy.44.refs_1_, s32[12,4]{1,0:T(8,128)} %copy.45.refs_2_, s32[12,4]{1,0:T(8,128)} %add_select_fusion.5.refs_3_, s32[12,4]{1,0:T(8,128)} %get-tuple-element.36.refs_4_, bf16[6,64,128]{2,1,0:T(8,128)(2,1)} %copy-done.14, ...), custom_call_target="tpu_custom_call" | custom-call | tf_op jit(solution)/shard_map/halo/pallas_call | solution.py:183
  116.7 1.5 %collective-permute-start.15 = (bf16[13,64,128]{2,1,0:T(8,128)(2,1)}, bf16[13,64,128]{2,1,0:T(8,128)(2,1)S(1)}, u32[]{:S(2)}, u32[]{:S(2)}) collective-permute-start(bf16[13,64,128]{2,1,0:T(8,128)(2,1)} %halo.3.refs_2_.refs_4_), channel_id=1, source_target_pairs={{0,1},{1,0},{2,3},{3,2},{4,5},{5,4},{6,7},{7,6},{8,9},{9,8},{10,11... | collective-permute-start | bytes 638984 | tf_op jit(solution)/shard_map/ppermute | solution.py:363
  118.2 5.5 %collective-permute-done.15.refs_3_.refs_5_ = bf16[13,64,128]{2,1,0:T(8,128)(2,1)S(1)} collective-permute-done((bf16[13,64,128]{2,1,0:T(8,128)(2,1)}, bf16[13,64,128]{2,1,0:T(8,128)(2,1)S(1)}, u32[]{:S(2)}, u32[]{:S(2)}) %collective-permute-start.15) | collective-permute-done | bytes 213024 | tf_op jit(solution)/shard_map/ppermute | solution.py:363
  124.6 9.1 %backward.1 = bf16[12,64,1024]{2,1,0:T(8,128)(2,1)} custom-call(bf16[12,64,1024]{2,1,0:T(8,128)(2,1)} %get-tuple-element.25.refs_0_, bf16[12,64,1024]{2,1,0:T(8,128)(2,1)S(1)} %collective-permute-done.8.refs_1_, bf16[13,64,128]{2,1,0:T(8,128)(2,1)S(1)} %copy-done.2, bf16[13,64,128]{2,1,0:T(8,128)(2,1)S(1)} %collective-permute-done.15.refs_3_.refs_5_, ...), custom_call_target="tpu_custom_call" | custom-call | tf_op jit(solution)/shard_map/backward/pallas_call | solution.py:289
  (146 shorter events, 38.6 us)
Async XLA Ops:
  0.7 32.4 %copy-start.12 = (bf16[3,3,128,128]{3,2,1,0:T(8,128)(2,1)S(1)}, bf16[3,3,128,128]{3,2,1,0:T(8,128)(2,1)}, u32[]{:S(2)}) copy-start(bf16[3,3,128,128]{3,2,1,0:T(8,128)(2,1)} %param.11) | copy-start | bytes 884740
  0.7 69.2 %collective-permute-start = (bf16[12,64,1024]{2,1,0:T(8,128)(2,1)}, bf16[12,64,1024]{2,1,0:T(8,128)(2,1)S(1)}, u32[]{:S(2)}, u32[]{:S(2)}) collective-permute-start(bf16[12,64,1024]{2,1,0:T(8,128)(2,1)} %bitcast.62), channel_id=1, source_target_pairs={{0,1},{1,0},{2,3},{3,2},{4,5},{5,4},{6,7},{7,6},{8,9},{9,8},{10,11... | collective-permute-start | bytes 4718600 | tf_op jit(solution)/shard_map/ppermute | solution.py:363
  8.4 46.3 %collective-permute-start.5 = (bf16[3,64,128]{2,1,0:T(8,128)(2,1)}, bf16[3,64,128]{2,1,0:T(8,128)(2,1)S(1)}, u32[]{:S(2)}, u32[]{:S(2)}) collective-permute-start(bf16[3,64,128]{2,1,0:T(8,128)(2,1)} %get-tuple-element.19), channel_id=1, source_target_pairs={{0,8},{2,10},{4,12},{6,14},{8,0},{10,2},{12,4},{14,6},{16,24},{18,... | collective-permute-start | bytes 147464 | tf_op jit(solution)/shard_map/ppermute | solution.py:399
  10.1 48.3 %collective-permute-start.6 = (bf16[3,64,128]{2,1,0:T(8,128)(2,1)}, bf16[3,64,128]{2,1,0:T(8,128)(2,1)}, u32[]{:S(2)}, u32[]{:S(2)}) collective-permute-start(bf16[3,64,128]{2,1,0:T(8,128)(2,1)} %get-tuple-element.20), channel_id=1, source_target_pairs={{0,2},{2,0},{4,6},{6,4},{8,10},{10,8},{12,14},{14,12},{16,18},{18,... | collective-permute-start | bytes 147464 | tf_op jit(solution)/shard_map/ppermute | solution.py:399
  10.1 33.5 %collective-permute-start.1 = (bf16[6,64,128]{2,1,0:T(8,128)(2,1)}, bf16[6,64,128]{2,1,0:T(8,128)(2,1)}, u32[]{:S(2)}, u32[]{:S(2)}) collective-permute-start(bf16[6,64,128]{2,1,0:T(8,128)(2,1)} %get-tuple-element.17), channel_id=1, source_target_pairs={{8,16},{16,8},{14,22},{22,14},{2,4},{4,2},{26,28},{28,26},{10,18},... | collective-permute-start | bytes 294920 | tf_op jit(solution)/shard_map/ppermute | solution.py:399
  12.8 48.1 %all-to-all-start = ((bf16[16,64,128]{2,1,0:T(8,128)(2,1)}), bf16[16,64,128]{2,1,0:T(8,128)(2,1)}, u32[]{:S(2)}, u32[]{:S(2)}) async-start(bf16[16,64,128]{2,1,0:T(8,128)(2,1)} %broadcast_in_dim.144), calls=%async_computation | async-start | bytes 524288 | tf_op jit(solution)/shard_map/all_to_all | solution.py:422
  35.1 34.8 %copy-start = (bf16[64,12,1,1,1024]{4,0,3,2,1:T(8,128)(2,1)S(1)}, bf16[64,12,1,1,1024]{4,0,3,2,1:T(8,128)(2,1)}, u32[]{:S(2)}) copy-start(bf16[64,12,1,1,1024]{4,0,3,2,1:T(8,128)(2,1)} %param.9) | copy-start | bytes 4718596
  35.1 34.8 %copy-start.3 = (bf16[128,1152]{1,0:T(8,128)(2,1)S(1)}, bf16[128,1152]{1,0:T(8,128)(2,1)}, u32[]{:S(2)}) copy-start(bf16[128,1152]{1,0:T(8,128)(2,1)} %constant.294.clone.refs_9_.refs_7_) | copy-start | bytes 884740
  35.1 34.8 %copy-start.7 = (bf16[128,128]{1,0:T(8,128)(2,1)S(1)}, bf16[128,128]{1,0:T(8,128)(2,1)}, u32[]{:S(2)}) copy-start(bf16[128,128]{1,0:T(8,128)(2,1)} %constant.293.clone.refs_3_.refs_11_) | copy-start | bytes 98308
  35.1 34.8 %copy-start.9 = (s32[6]{0:T(128)S(1)}, s32[6]{0:T(128)}, u32[]{:S(2)}) copy-start(s32[6]{0:T(128)} %stack.27.refs_0_) | copy-start | bytes 76
  46.0 12.3 %collective-permute-start.4 = (bf16[6,64,128]{2,1,0:T(8,128)(2,1)}, bf16[6,64,128]{2,1,0:T(8,128)(2,1)}, u32[]{:S(2)}, u32[]{:S(2)}) collective-permute-start(bf16[6,64,128]{2,1,0:T(8,128)(2,1)} %fusion.2.refs_5_), channel_id=1, source_target_pairs={{8,26},{16,28},{14,2},{22,4},{2,14},{4,22},{26,8},{28,16},{0,30},{... | collective-permute-start | bytes 294920 | tf_op jit(solution)/shard_map/ppermute | solution.py:399
  52.2 8.7 %collective-permute-start.3 = (bf16[6,64,128]{2,1,0:T(8,128)(2,1)}, bf16[6,64,128]{2,1,0:T(8,128)(2,1)}, u32[]{:S(2)}, u32[]{:S(2)}) collective-permute-start(bf16[6,64,128]{2,1,0:T(8,128)(2,1)} %fusion.2.refs_5_), channel_id=1, source_target_pairs={{8,2},{16,4},{14,26},{22,28},{2,8},{4,16},{26,14},{28,22},{0,24},{... | collective-permute-start | bytes 294920 | tf_op jit(solution)/shard_map/ppermute | solution.py:399
  54.7 6.2 %collective-permute-start.2 = (bf16[6,64,128]{2,1,0:T(8,128)(2,1)}, bf16[6,64,128]{2,1,0:T(8,128)(2,1)}, u32[]{:S(2)}, u32[]{:S(2)}) collective-permute-start(bf16[6,64,128]{2,1,0:T(8,128)(2,1)} %fusion.2.refs_5_), channel_id=1, source_target_pairs={{8,14},{16,22},{14,8},{22,16},{2,26},{4,28},{26,2},{28,4},{0,6},{6... | collective-permute-start | bytes 294920 | tf_op jit(solution)/shard_map/ppermute | solution.py:399
  63.8 6.1 %collective-permute-start.7 = (bf16[13,64,128]{2,1,0:T(8,128)(2,1)}, bf16[13,64,128]{2,1,0:T(8,128)(2,1)S(1)}, u32[]{:S(2)}, u32[]{:S(2)}) collective-permute-start(bf16[13,64,128]{2,1,0:T(8,128)(2,1)} %halo.2.refs_3_.refs_5_), channel_id=1, source_target_pairs={{0,1},{1,0},{2,3},{3,2},{4,5},{5,4},{6,7},{7,6},{8,9},{9,8},{10,11... | collective-permute-start | bytes 638984 | tf_op jit(solution)/shard_map/ppermute | solution.py:363
  85.7 38.0 %copy-start.5 = (bf16[192,384]{1,0:T(8,128)(2,1)S(1)}, bf16[192,384]{1,0:T(8,128)(2,1)}, u32[]{:S(2)}) copy-start(bf16[192,384]{1,0:T(8,128)(2,1)} %get-tuple-element.31.refs_6_) | copy-start | bytes 442372
  85.7 38.0 %collective-permute-start.8 = (bf16[12,64,1024]{2,1,0:T(8,128)(2,1)}, bf16[12,64,1024]{2,1,0:T(8,128)(2,1)S(1)}, u32[]{:S(2)}, u32[]{:S(2)}) collective-permute-start(bf16[12,64,1024]{2,1,0:T(8,128)(2,1)} %get-tuple-element.25.refs_0_), channel_id=1, source_target_pairs={{0,1},{1,0},{2,3},{3,2},{4,5},{5,4},{6,7},{7,6},{8,9},{9,8},{10,11... | collective-permute-start | bytes 4718600 | tf_op jit(solution)/shard_map/ppermute | solution.py:363
  87.0 25.5 %all-to-all-start.1 = ((bf16[16,64,128]{2,1,0:T(8,128)(2,1)}), bf16[16,64,128]{2,1,0:T(8,128)(2,1)S(1)}, u32[]{:S(2)}, u32[]{:S(2)}) async-start(bf16[16,64,128]{2,1,0:T(8,128)(2,1)} %broadcast_in_dim.146), calls=%async_computation.1 | async-start | bytes 524288 | tf_op jit(solution)/shard_map/all_to_all | solution.py:422
  91.9 5.4 %collective-permute-start.9 = (bf16[6,64,128]{2,1,0:T(8,128)(2,1)}, bf16[6,64,128]{2,1,0:T(8,128)(2,1)S(1)}, u32[]{:S(2)}, u32[]{:S(2)}) collective-permute-start(bf16[6,64,128]{2,1,0:T(8,128)(2,1)} %copy-done.10), channel_id=1, source_target_pairs={{8,16},{16,8},{14,22},{22,14},{2,4},{4,2},{26,28},{28,26},{10,18},... | collective-permute-start | bytes 294920 | tf_op jit(solution)/shard_map/ppermute | solution.py:399
  92.6 14.4 %collective-permute-start.13 = (bf16[3,64,128]{2,1,0:T(8,128)(2,1)}, bf16[3,64,128]{2,1,0:T(8,128)(2,1)S(1)}, u32[]{:S(2)}, u32[]{:S(2)}) collective-permute-start(bf16[3,64,128]{2,1,0:T(8,128)(2,1)} %copy-done.11), channel_id=1, source_target_pairs={{0,8},{2,10},{4,12},{6,14},{8,0},{10,2},{12,4},{14,6},{16,24},{18,... | collective-permute-start | bytes 147464 | tf_op jit(solution)/shard_map/ppermute | solution.py:399
  98.3 14.1 %collective-permute-start.12 = (bf16[6,64,128]{2,1,0:T(8,128)(2,1)S(1)}, bf16[6,64,128]{2,1,0:T(8,128)(2,1)S(1)}, u32[]{:S(2)}, u32[]{:S(2)}) collective-permute-start(bf16[6,64,128]{2,1,0:T(8,128)(2,1)S(1)} %fusion.1.refs_5_), channel_id=1, source_target_pairs={{8,26},{16,28},{14,2},{22,4},{2,14},{4,22},{26,8},{28,16},{0,30},{... | collective-permute-start | bytes 294920 | tf_op jit(solution)/shard_map/ppermute | solution.py:399
  101.8 10.6 %collective-permute-start.11 = (bf16[6,64,128]{2,1,0:T(8,128)(2,1)S(1)}, bf16[6,64,128]{2,1,0:T(8,128)(2,1)S(1)}, u32[]{:S(2)}, u32[]{:S(2)}) collective-permute-start(bf16[6,64,128]{2,1,0:T(8,128)(2,1)S(1)} %fusion.1.refs_5_), channel_id=1, source_target_pairs={{8,2},{16,4},{14,26},{22,28},{2,8},{4,16},{26,14},{28,22},{0,24},{... | collective-permute-start | bytes 294920 | tf_op jit(solution)/shard_map/ppermute | solution.py:399
  106.1 6.4 %collective-permute-start.10 = (bf16[6,64,128]{2,1,0:T(8,128)(2,1)S(1)}, bf16[6,64,128]{2,1,0:T(8,128)(2,1)S(1)}, u32[]{:S(2)}, u32[]{:S(2)}) collective-permute-start(bf16[6,64,128]{2,1,0:T(8,128)(2,1)S(1)} %fusion.1.refs_5_), channel_id=1, source_target_pairs={{8,14},{16,22},{14,8},{22,16},{2,26},{4,28},{26,2},{28,4},{0,6},{6... | collective-permute-start | bytes 294920 | tf_op jit(solution)/shard_map/ppermute | solution.py:399
  106.9 5.5 %collective-permute-start.14 = (bf16[3,64,128]{2,1,0:T(8,128)(2,1)S(1)}, bf16[3,64,128]{2,1,0:T(8,128)(2,1)S(1)}, u32[]{:S(2)}, u32[]{:S(2)}) collective-permute-start(bf16[3,64,128]{2,1,0:T(8,128)(2,1)S(1)} %get-tuple-element.29), channel_id=1, source_target_pairs={{0,2},{2,0},{4,6},{6,4},{8,10},{10,8},{12,14},{14,12},{16,18},{18,... | collective-permute-start | bytes 147464 | tf_op jit(solution)/shard_map/ppermute | solution.py:399
  116.7 7.0 %collective-permute-start.15 = (bf16[13,64,128]{2,1,0:T(8,128)(2,1)}, bf16[13,64,128]{2,1,0:T(8,128)(2,1)S(1)}, u32[]{:S(2)}, u32[]{:S(2)}) collective-permute-start(bf16[13,64,128]{2,1,0:T(8,128)(2,1)} %halo.3.refs_2_.refs_4_), channel_id=1, source_target_pairs={{0,1},{1,0},{2,3},{3,2},{4,5},{5,4},{6,7},{7,6},{8,9},{9,8},{10,11... | collective-permute-start | bytes 638984 | tf_op jit(solution)/shard_map/ppermute | solution.py:363
  (22 other events, 192.9 us)

commit v3 on v2

v3 whole, which is shorter than its diff:
```python
import jax
import jax.numpy as jnp
import numpy as np
from jax import lax
from jax.experimental import pallas as pl
from jax.experimental.pallas import tpu as pltpu
from jax.sharding import PartitionSpec as P

RB = 32
GROUP = 4
LANES = 128
VMEM_LIMIT = 24 * 1024 * 1024
STRIP_LANE = (96, 0, 32, 64)


def ring_matrix(col_len):
    mat = np.zeros((col_len * RB, LANES), np.float32)
    for b in range(RB):
        mat[b, b] = 1
        mat[(col_len - 1) * RB + b, 32 + b] = 1
    for a in range(col_len):
        mat[a * RB, 64 + a] = 1
        mat[a * RB + RB - 1, 96 + a] = 1
    return mat


def corner_matrix():
    mat = np.zeros((LANES, LANES), np.float32)
    for q, lane in enumerate((0, RB - 1, 32, 32 + RB - 1)):
        mat[lane, q] = 1
    return mat


def reverse_matrix(unit):
    mat = np.zeros((LANES, LANES), np.float32)
    for lane in range(LANES):
        mat[lane, (lane // unit) * unit + unit - 1 - lane % unit] = 1
    return mat


def spread_matrix(col_len):
    width = col_len * RB + LANES
    mat = np.zeros((LANES, width), np.float32)
    top, bottom = (col_len + 3) * RB, col_len * RB
    mat[0, top] = 1
    mat[1, top + RB - 1] = 1
    mat[2, bottom] = 1
    mat[3, bottom + RB - 1] = 1
    for a in range(col_len):
        mat[STRIP_LANE[2] + a, a * RB] = 1
        mat[STRIP_LANE[3] + a, a * RB + RB - 1] = 1
    return mat


def lane_iota(shape):
    return lax.broadcasted_iota(jnp.int32, shape, len(shape) - 1)


def emit_rings(step, steps, fields, plan, ring_ref, cornsel_ref, outs, packs_acc, corner_acc):
    chan = fields[0].shape[0]
    lane = lane_iota((chan, LANES))
    rings = [
        jnp.dot(field, ring_ref[...], preferred_element_type=jnp.float32) for field in fields
    ]
    for side in range(4):
        tile = jnp.zeros((chan, LANES), jnp.float32)
        for g, ring in enumerate(rings):
            moved = pltpu.roll(ring, ((g - side) * 32) % LANES, 1) if g != side else ring
            tile = jnp.where(lane // 32 == g, moved, tile)
        packs_acc[side * steps + step] = tile.astype(jnp.bfloat16)

    @pl.when(step == 0)
    def _():
        corner_acc[...] = jnp.zeros_like(corner_acc)

    for g, ring in enumerate(rings):
        picked = jnp.dot(
            ring.astype(jnp.bfloat16), cornsel_ref[...], preferred_element_type=jnp.float32
        )
        corner_acc[...] += pltpu.roll(picked, (step * GROUP + g) * 4, 1)

    @pl.when(step == steps - 1)
    def _():
        chosen = iter(plan.chosen_sides())
        for out in outs[:-1]:
            for at in range(0, out.shape[0], steps):
                base = next(chosen) * steps
                for q in range(steps):
                    out[at + q] = packs_acc[base + q]
        outs[-1][0] = corner_acc[...].astype(jnp.bfloat16)


def ring_outs(faces, chan, counts):
    steps = faces // GROUP
    tiles = [count * steps for count in counts] + [1]
    return [jax.ShapeDtypeStruct((n, chan, LANES), jnp.bfloat16) for n in tiles]


def ring_scratch(faces, chan):
    steps = faces // GROUP
    return [
        pltpu.VMEM((4 * steps, chan, LANES), jnp.bfloat16),
        pltpu.VMEM((chan, LANES), jnp.float32),
    ]


def rings_kernel(steps, plan, field_ref, ring_ref, cornsel_ref, *refs):
    fields = [field_ref[g] for g in range(GROUP)]
    emit_rings(pl.program_id(0), steps, fields, plan, ring_ref, cornsel_ref, refs[:-2], *refs[-2:])


def whole_spec(array):
    zeros = (0,) * array.ndim
    return pl.BlockSpec(array.shape, lambda *_: zeros)


def rings_of(field, plan, ring, cornsel):
    faces, chan, tile = field.shape
    steps = faces // GROUP
    outs = ring_outs(faces, chan, plan.counts)
    return pl.pallas_call(
        lambda *refs: rings_kernel(steps, plan, *refs),
        grid=(steps,),
        in_specs=[
            pl.BlockSpec((GROUP, chan, tile), lambda i: (i, 0, 0)),
            whole_spec(ring),
            whole_spec(cornsel),
        ],
        out_specs=[whole_spec(out) for out in outs],
        out_shape=outs,
        scratch_shapes=ring_scratch(faces, chan),
        compiler_params=pltpu.CompilerParams(vmem_limit_bytes=VMEM_LIMIT),
        name="rings",
    )(field, ring, cornsel)


def halo_kernel(faces, units, unit, *refs):
    table, tile_refs, (rev_ref, halo_ref, pool, turn_acc) = (refs[0], refs[1:-4], refs[-4:])
    chan = halo_ref.shape[1]
    lane = lane_iota((chan, LANES))
    at = 0
    for ref in tile_refs:
        pool[at : at + ref.shape[0]] = ref[...]
        at += ref.shape[0]
    corner_tile = jnp.zeros((chan, LANES), jnp.float32)
    most = max(units)
    rows = 4 * most
    for f in range(faces):
        tile = jnp.zeros((chan, LANES), jnp.float32)
        turned = jnp.zeros((chan, LANES), jnp.float32)
        for e in range(4):
            for un in range(units[e]):
                base = STRIP_LANE[e] + un * unit
                span = (lane >= base) & (lane < base + unit)
                entry = e * most + un
                source = pool[table[entry, f]].astype(jnp.float32)
                moved = pltpu.roll(source, table[rows + entry, f], 1)
                flip = table[2 * rows + entry, f] == 1
                tile = jnp.where(span & jnp.logical_not(flip), moved, tile)
                turned = jnp.where(span & flip, moved, turned)
        halo_ref[f] = tile.astype(jnp.bfloat16)
        turn_acc[f] = turned.astype(jnp.bfloat16)
        for c in range(4):
            source = pool[table[3 * rows + c, f]].astype(jnp.float32)
            moved = pltpu.roll(source, table[3 * rows + 4 + c, f], 1)
            corner_tile = jnp.where(lane == f * 4 + c, moved, corner_tile)
    turned = jnp.dot(
        turn_acc[...].reshape(faces * chan, LANES), rev_ref[...], preferred_element_type=jnp.float32
    ).reshape(faces, chan, LANES)
    for f in range(faces):
        halo_ref[f] += turned[f].astype(jnp.bfloat16)
    halo_ref[faces] = corner_tile.astype(jnp.bfloat16)


def assemble_halo(table, tiles, rev, faces, units, unit):
    chan = tiles[0].shape[1]
    halo = jax.ShapeDtypeStruct((faces + 1, chan, LANES), jnp.bfloat16)
    vmem = pl.BlockSpec(memory_space=pltpu.VMEM)
    smem = pl.BlockSpec(memory_space=pltpu.SMEM)
    return pl.pallas_call(
        lambda *refs: halo_kernel(faces, units, unit, *refs),
        in_specs=[smem] + [vmem] * (len(tiles) + 1),
        out_specs=vmem,
        out_shape=halo,
        scratch_shapes=[
            pltpu.VMEM((sum(t.shape[0] for t in tiles), chan, LANES), jnp.bfloat16),
            pltpu.VMEM((faces, chan, LANES), jnp.bfloat16),
        ],
        compiler_params=pltpu.CompilerParams(vmem_limit_bytes=VMEM_LIMIT),
        name="halo",
    )(table, *tiles, rev)


def conv_face(g, step, field_refs, halo_refs, corner_refs, taps_ref, spread_ref, stack_ref):
    chan, tile = field_refs[0].shape[1:]
    pieces = len(field_refs)
    total = chan * pieces
    width = tile + LANES
    for k in range(pieces):
        stack_ref[total + k * chan : total + (k + 1) * chan, :tile] = field_refs[k][g]
        stack_ref[total + k * chan : total + (k + 1) * chan, tile:] = halo_refs[k][g]
    halo = stack_ref[total : 2 * total, tile:].astype(jnp.float32)
    corners = jnp.concatenate([ref[0].astype(jnp.float32) for ref in corner_refs], axis=0)
    corners = pltpu.roll(corners, (LANES - (step * GROUP + g) * 4) % LANES, 1)
    lane = lane_iota((total, LANES))
    sides = jnp.where(lane < 4, corners, halo).astype(jnp.bfloat16)
    beside = jnp.dot(sides, spread_ref[...], preferred_element_type=jnp.float32)
    middle = stack_ref[total : 2 * total].astype(jnp.float32)
    col = lane_iota((total, width)) % RB
    stack_ref[:total] = jnp.where(col == 0, beside, pltpu.roll(middle, 1, 1)).astype(jnp.bfloat16)
    stack_ref[2 * total :] = jnp.where(
        col == RB - 1, beside, pltpu.roll(middle, width - 1, 1)
    ).astype(jnp.bfloat16)
    sums = jnp.dot(taps_ref[...], stack_ref[...], preferred_element_type=jnp.float32)
    above = pltpu.roll(sums[:chan], RB, 1)
    below = pltpu.roll(sums[2 * chan :], width - RB, 1)
    return (above + sums[chan : 2 * chan] + below)[:, :tile]


def forward_kernel(steps, pieces, plan, *refs):
    field_refs, refs = (refs[:pieces], refs[pieces:])
    halo_refs, refs = (refs[:pieces], refs[pieces:])
    corner_refs, refs = (refs[:pieces], refs[pieces:])
    (cot_ref, taps_ref, spread_ref, ring_ref, cornsel_ref, act_ref, gated_ref) = refs[:7]
    outs, (stack_ref, packs_acc, corner_acc) = (refs[7:-3], refs[-3:])
    step = pl.program_id(0)
    fields = []
    for g in range(GROUP):
        pre = conv_face(g, step, field_refs, halo_refs, corner_refs, taps_ref, spread_ref, stack_ref)
        sig = 1.0 / (1.0 + jnp.exp(-pre))
        act_ref[g] = (pre * sig).astype(jnp.bfloat16)
        gated = cot_ref[g].astype(jnp.float32) * sig * (1.0 + pre * (1.0 - sig))
        gated_ref[g] = gated.astype(jnp.bfloat16)
        fields.append(gated.astype(jnp.bfloat16))
    emit_rings(step, steps, fields, plan, ring_ref, cornsel_ref, outs, packs_acc, corner_acc)


def backward_kernel(steps, pieces, *refs):
    field_refs, refs = (refs[:pieces], refs[pieces:])
    halo_refs, refs = (refs[:pieces], refs[pieces:])
    corner_refs, refs = (refs[:pieces], refs[pieces:])
    (taps_ref, spread_ref, grad_ref, stack_ref) = refs
    step = pl.program_id(0)
    for g in range(GROUP):
        total = conv_face(
            g, step, field_refs, halo_refs, corner_refs, taps_ref, spread_ref, stack_ref
        )
        grad_ref[g] = total.astype(jnp.bfloat16)


def conv_specs(fields, halos):
    faces, chan, tile = fields[0].shape
    group = lambda i: (i, 0, 0)
    return (
        [pl.BlockSpec((GROUP, chan, tile), group) for _ in fields]
        + [pl.BlockSpec((GROUP, chan, LANES), group) for _ in halos]
        + [pl.BlockSpec((1, chan, LANES), lambda i: (faces, 0, 0)) for _ in halos]
    )


def forward(plan, fields, halos, cot, taps, spread, ring, cornsel):
    faces, chan, tile = fields[0].shape
    steps = faces // GROUP
    pieces = len(fields)
    outs = ring_outs(faces, chan, plan.counts)
    out = jax.ShapeDtypeStruct((faces, chan, tile), jnp.bfloat16)
    block = pl.BlockSpec((GROUP, chan, tile), lambda i: (i, 0, 0))
    return pl.pallas_call(
        lambda *refs: forward_kernel(steps, pieces, plan, *refs),
        grid=(steps,),
        in_specs=conv_specs(fields, halos)
        + [block, whole_spec(taps), whole_spec(spread), whole_spec(ring), whole_spec(cornsel)],
        out_specs=[block, block] + [whole_spec(o) for o in outs],
        out_shape=[out, out] + outs,
        scratch_shapes=[pltpu.VMEM((3 * chan * pieces, tile + LANES), jnp.bfloat16)]
        + ring_scratch(faces, chan),
        compiler_params=pltpu.CompilerParams(vmem_limit_bytes=VMEM_LIMIT),
        name="forward",
    )(*fields, *halos, *halos, cot, taps, spread, ring, cornsel)


def backward(fields, halos, taps, spread):
    faces, chan, tile = fields[0].shape
    steps = faces // GROUP
    pieces = len(fields)
    return pl.pallas_call(
        lambda *refs: backward_kernel(steps, pieces, *refs),
        grid=(steps,),
        in_specs=conv_specs(fields, halos) + [whole_spec(taps), whole_spec(spread)],
        out_specs=pl.BlockSpec((GROUP, chan, tile), lambda i: (i, 0, 0)),
        out_shape=jax.ShapeDtypeStruct((faces, chan, tile), jnp.bfloat16),
        scratch_shapes=[pltpu.VMEM((3 * chan * pieces, tile + LANES), jnp.bfloat16)],
        compiler_params=pltpu.CompilerParams(vmem_limit_bytes=VMEM_LIMIT),
        name="backward",
    )(*fields, *halos, *halos, taps, spread)


def rows_of(*parts):
    return jnp.concatenate(parts, axis=0)


def halo_table(plan, edge_ref, corner_ref, px_count, py_count, col_len, unit):
    row_pos, col_pos = plan.place()
    faces = edge_ref.shape[2]
    side_len = px_count * RB
    most = RB // unit
    shape = (4 * most, faces)
    face = lane_iota(shape)
    row = lax.broadcasted_iota(jnp.int32, shape, 0)
    edge, un = (row // most, row % most)
    g, s, r = [
        rows_of(*[edge_ref[i, e : e + 1] for e in range(4) for _ in range(most)]) for i in range(3)
    ]
    border = ((edge == 0) & (col_pos == 0)) | ((edge == 1) & (col_pos == py_count - 1))
    border |= ((edge == 2) & (row_pos == 0)) | ((edge == 3) & (row_pos == px_count - 1))
    at = jnp.where(edge < 2, row_pos * RB, col_pos * col_len) + un * unit
    at = jnp.clip(at, 0, side_len - unit)
    at = jnp.where(r == 1, side_len - unit - at, at)
    line_tile, line_lane = plan.strip_cell(g, s, at)
    tile = jnp.where(border, line_tile, plan.near_cell(edge, face))
    lane = jnp.where(border, line_lane, (face % GROUP) * 32 + un * unit)
    first = jnp.where(edge == 0, STRIP_LANE[0], jnp.where(edge == 1, STRIP_LANE[1], edge * 32 - 32))
    shift = (first + un * unit - lane + LANES) % LANES
    flip = jnp.where(border & (r == 1), 1, 0)

    shape = (4, faces)
    face = lane_iota(shape)
    c = lax.broadcasted_iota(jnp.int32, shape, 0)
    down, right = (c // 2, c % 2)
    row_on = ((down == 0) & (col_pos == 0)) | ((down == 1) & (col_pos == py_count - 1))
    col_on = ((right == 0) & (row_pos == 0)) | ((right == 1) & (row_pos == px_count - 1))
    row_at = row_pos * RB + jnp.where(right == 1, RB, -1)
    col_at = col_pos * col_len + jnp.where(down == 1, col_len, -1)
    edge_of = lambda i, edges: rows_of(*[edge_ref[i, e : e + 1] for e in edges])
    g, s, r = [
        jnp.where(row_on, edge_of(i, (0, 0, 1, 1)), edge_of(i, (2, 3, 2, 3))) for i in range(3)
    ]
    at = jnp.clip(jnp.where(row_on, row_at, col_at), 0, side_len - 1)
    at = jnp.where(r == 1, side_len - 1 - at, at)
    h, q = [rows_of(*[corner_ref[k, i : i + 1] for k in range(4)]) for i in range(2)]
    both = row_on & col_on
    g = jnp.where(both, h, g)
    s = jnp.where(both, q // 2, s)
    at = jnp.where(both, (q % 2) * (side_len - 1), at)
    line_tile, line_lane = plan.corner_cell(g, s, at)
    diag_px = jnp.clip(row_pos + 2 * right - 1, 0, px_count - 1)
    diag_py = jnp.clip(col_pos + 2 * down - 1, 0, py_count - 1)
    diag_tile, diag_lane = plan.diagonal_cell(face, 3 - c, diag_px, diag_py)
    on = row_on | col_on
    corner_at = jnp.where(on, line_tile, diag_tile)
    corner_lane = jnp.where(on, line_lane, diag_lane)
    corner_shift = (face * 4 + c - corner_lane + LANES) % LANES
    return rows_of(tile, shift, flip, corner_at, corner_shift)


def setup_kernel(plan, chan, shape, edge_ref, corner_ref, weight_ref, table_ref, taps_ref, back_ref, turn):
    table_ref[...] = halo_table(plan, edge_ref, corner_ref, *shape)
    total = weight_ref.shape[2]
    own = lax.axis_index("ch") * chan
    shift = (total - own) % total
    for i in range(3):
        for j in range(3):
            turn[...] = weight_ref[i, j].astype(jnp.float32)
            rows = pltpu.roll(turn[pl.ds(pl.multiple_of(own, chan), chan)], shift, 1)
            cols = slice(j * total, (j + 1) * total)
            taps_ref[i * chan : (i + 1) * chan, cols] = rows.astype(jnp.bfloat16)
            turn[...] = turn[...].T
            rows = pltpu.roll(turn[pl.ds(pl.multiple_of(own, chan), chan)], shift, 1)
            cols = slice((2 - j) * total, (3 - j) * total)
            back_ref[(2 - i) * chan : (3 - i) * chan, cols] = rows.astype(jnp.bfloat16)


def setup(plan, edge_table, corner_table, weight, chan, counts, col_len, unit):
    edges = jnp.transpose(edge_table, (2, 1, 0))
    corners = jnp.transpose(corner_table, (1, 2, 0))
    total = weight.shape[2]
    vmem = pl.BlockSpec(memory_space=pltpu.VMEM)
    taps = jax.ShapeDtypeStruct((3 * chan, 3 * total), jnp.bfloat16)
    table = jax.ShapeDtypeStruct((12 * (RB // unit) + 8, edges.shape[2]), jnp.int32)
    return pl.pallas_call(
        lambda *refs: setup_kernel(plan, chan, (*counts, col_len, unit), *refs),
        in_specs=[vmem] * 3,
        out_specs=[vmem] * 3,
        out_shape=[table, taps, taps],
        scratch_shapes=[pltpu.VMEM((total, total), jnp.float32)],
        compiler_params=pltpu.CompilerParams(vmem_limit_bytes=VMEM_LIMIT),
        name="setup",
    )(edges, corners, weight)


def from_others(array, ch_count):
    return [array] + [
        lax.ppermute(array, "ch", [((i + k) % ch_count, i) for i in range(ch_count)])
        for k in range(1, ch_count)
    ]


class Place:
    @staticmethod
    def place():
        return (lax.axis_index("px"), lax.axis_index("py"))


class SquareHalo(Place):
    counts = (2, 1, 1, 2)

    def __init__(self, quads):
        self.quads = quads

    def roles(self):
        row_pos, col_pos = self.place()
        px_end = (row_pos == 0) | (row_pos == 3)
        py_end = (col_pos == 0) | (col_pos == 3)
        side = jnp.where(
            py_end, jnp.where(col_pos == 0, 0, 1), jnp.where(row_pos == 0, 2, 3)
        )
        corner = px_end & py_end
        middle = (px_end | py_end) & jnp.logical_not(corner)
        return (px_end, corner, middle, side, jnp.where(px_end, col_pos, row_pos))

    def chosen_sides(self):
        row_pos, col_pos = self.place()
        px_end, corner, middle, side, seg = self.roles()
        row_line = jnp.where(col_pos == 0, 0, 1)
        col_line = jnp.where(row_pos == 0, 2, 3)
        to_px, to_py = (jnp.where(row_pos == 1, 3, 2), jnp.where(col_pos == 1, 1, 0))
        facing = jnp.where(px_end, to_py, to_px)
        return [
            jnp.where(seg == 1, side, facing),
            jnp.where(seg == 1, facing, side),
            jnp.where(row_pos % 2 == 0, 3, 2),
            jnp.where(col_pos % 2 == 0, 1, 0),
            jnp.where(corner, row_line, jnp.where(middle, side, to_py)),
            jnp.where(corner, col_line, side),
        ]

    def exchange(self, pair, col_side, row_side, lines, corner):
        every = [(x, y) for x in range(4) for y in range(4)]
        axes = ("px", "py")
        swap = lambda array, pairs: lax.ppermute(
            array, axes, [(a[0] * 4 + a[1], b[0] * 4 + b[1]) for a, b in pairs]
        )
        ends = (0, 3)
        corners = [(x, y) for x in ends for y in ends]
        spot = lambda side, seg: ((seg, 0), (seg, 3), (0, seg), (3, seg))[side]
        beside = [(spot(side, k), spot(side, 3 - k)) for side in range(4) for k in (1, 2)]
        beside += [((x, y), (3 - x, y)) for x in (1, 2) for y in (1, 2)]
        paired = swap(pair, beside)
        near_col = swap(col_side, [((x, y), (x ^ 1, y)) for x, y in every])
        near_row = swap(row_side, [((x, y), (x, y ^ 1)) for x, y in every])
        _, _, middle, _, seg = self.roles()
        slot = lax.broadcasted_iota(jnp.int32, (2 * self.quads, 1, 1), 0) // self.quads
        lines = jnp.where(middle & (slot != seg - 1), paired, lines)
        across = []
        for j in (1, 2, 3):
            pairs = [(spot(side, k), spot(side ^ j, k)) for side in range(4) for k in (1, 2)]
            pairs += [(corners[c], corners[c ^ j]) for c in range(4)]
            if j == 1:
                pairs += [((x, y), (x, 3 - y)) for x in (1, 2) for y in (1, 2)]
            across.append(swap(lines, pairs))
        corner, lines = lax.optimization_barrier((corner, lines))
        ends_of = jnp.broadcast_to(corner, (16,) + corner.shape[1:])
        ends_of = lax.all_to_all(ends_of, axes, 0, 0, tiled=True)
        return [lines, *across, paired, near_col, near_row, ends_of]

    def strip_cell(self, g, s, at):
        row_pos, col_pos = self.place()
        _, corner, _, side, _ = self.roles()
        slot = 2 * self.quads
        k = at // RB
        me = jnp.where(row_pos > 0, 2, 0) + jnp.where(col_pos > 0, 1, 0)
        far = jnp.where(k > 0, 1, 0)
        owner = jnp.where(s < 2, 2 * far + s, 2 * (s - 2) + far)
        at_corner = (me ^ owner) * slot + (s // 2) * self.quads
        at_middle = (side ^ s) * slot + (k - 1) * self.quads
        return (jnp.where(corner, at_corner, at_middle) + g // GROUP, (g % GROUP) * 32)

    def near_cell(self, edge, face):
        row_pos, col_pos = self.place()
        px_end, _, _, _, seg = self.roles()
        slot = 2 * self.quads
        paired = 4 * slot + (seg - 1) * self.quads
        near_col, near_row = (5 * slot, 5 * slot + self.quads)
        by_col = jnp.where(row_pos % 2 == 3 - edge, near_col, paired)
        by_row = jnp.where(col_pos % 2 == 1 - edge, near_row, jnp.where(px_end, paired, slot))
        return jnp.where(edge < 2, by_row, by_col) + face // GROUP

    def corner_cell(self, g, s, at):
        seg, hi = (at // RB, jnp.where(at % RB == 0, 0, 1))
        owner = jnp.where(s < 2, seg * 4 + 3 * s, 12 * (s - 2) + seg)
        q = jnp.where(s < 2, 2 * s + hi, s - 2 + 2 * hi)
        return (12 * self.quads + owner, g * 4 + q)

    def diagonal_cell(self, face, q, px, py):
        return (12 * self.quads + px * 4 + py, face * 4 + q)


class GatheredHalo(Place):
    counts = (1, 1, 1, 1, 2)

    def __init__(self, quads, px_count, py_count, col_len):
        self.quads = quads
        self.size = (px_count, py_count)
        self.col_len = col_len

    def chosen_sides(self):
        row_pos, col_pos = self.place()
        return [0, 1, 2, 3, jnp.where(col_pos == 0, 0, 1), jnp.where(row_pos == 0, 2, 3)]

    def exchange(self, top, bottom, left, right, lines, corner):
        px_count, py_count = self.size
        up = lambda n: [(i, i + 1) for i in range(n - 1)]
        down = lambda n: [(i + 1, i) for i in range(n - 1)]
        return [
            lax.ppermute(bottom, "py", up(py_count)),
            lax.ppermute(top, "py", down(py_count)),
            lax.ppermute(right, "px", up(px_count)),
            lax.ppermute(left, "px", down(px_count)),
            lax.all_gather(lines, ("px", "py"), axis=0, tiled=True),
            lax.all_gather(corner, ("px", "py"), axis=0, tiled=True),
        ]

    def strip_cell(self, g, s, at):
        px_count, py_count = self.size
        length = jnp.where(s < 2, RB, self.col_len)
        seg = at // length
        px = jnp.where(s < 2, seg, (s - 2) * (px_count - 1))
        py = jnp.where(s < 2, s * (py_count - 1), seg)
        tile = (4 + (px * py_count + py) * 2 + s // 2) * self.quads + g // GROUP
        return (tile, (g % GROUP) * 32 + at % length)

    def near_cell(self, edge, face):
        return edge * self.quads + face // GROUP

    def corner_cell(self, g, s, at):
        return self.strip_cell(g, s, at)

    def diagonal_cell(self, face, q, px, py):
        px_count, py_count = self.size
        base = (4 + 2 * px_count * py_count) * self.quads
        return (base + px * py_count + py, face * 4 + q)


def local(features, cotangent, weight, edge_table, corner_table):
    chan, faces = features.shape[:2]
    tile = features.shape[4]
    col_len = tile // RB
    unit = min(RB, col_len)
    units = (RB // unit, RB // unit, col_len // unit, col_len // unit)
    px_count, py_count, ch_count = [lax.axis_size(name) for name in ("px", "py", "ch")]
    ring = jnp.asarray(ring_matrix(col_len), jnp.bfloat16)
    cornsel = jnp.asarray(corner_matrix(), jnp.bfloat16)
    spread = jnp.asarray(spread_matrix(col_len), jnp.bfloat16)
    rev = jnp.asarray(reverse_matrix(unit), jnp.bfloat16)
    if px_count == py_count == 4 and col_len == RB:
        plan = SquareHalo(faces // GROUP)
    else:
        plan = GatheredHalo(faces // GROUP, px_count, py_count, col_len)

    feats = jnp.transpose(features.reshape(chan, faces, tile), (1, 0, 2))
    cot = jnp.transpose(cotangent.reshape(chan, faces, tile), (1, 0, 2))
    fields = from_others(feats, ch_count)
    parts = rings_of(feats, plan, ring, cornsel)
    table, taps, back_taps = setup(
        plan, edge_table, corner_table, weight, chan, (px_count, py_count), col_len, unit
    )
    tiles = plan.exchange(*parts)
    halo = assemble_halo(table, tiles, rev, faces, units, unit)
    halos = from_others(halo, ch_count)
    act, gated, *parts = forward(plan, fields, halos, cot, taps, spread, ring, cornsel)

    fields = from_others(gated, ch_count)
    tiles = plan.exchange(*parts)
    halo = assemble_halo(table, tiles, rev, faces, units, unit)
    halos = from_others(halo, ch_count)
    grad = backward(fields, halos, back_taps, spread)

    shape = (chan, faces, 1, 1, tile)
    return (
        jnp.transpose(act, (1, 0, 2)).reshape(shape),
        jnp.transpose(grad, (1, 0, 2)).reshape(shape),
    )


def solution(mesh):
    spec = P("ch", None, "py", "px", None)
    return jax.shard_map(
        local,
        mesh=mesh,
        in_specs=(spec, spec, P(), P(), P()),
        out_specs=(spec, spec),
        check_vma=False,
    )
```

time: 136 us -> 124 us (0.912)
  other arithmetic: 15.9 us -> 1.71 us
  waiting for transfers between devices: 14.6 us -> 21.8 us
  Pallas kernels: 30 us -> 26.4 us
  local copies, waits for them, and re-layouts: 25.5 us -> 22.4 us
  starting transfers between devices: 46.8 us -> 49.6 us
    unnamed x56 -> x70, local copies, waits for them, and re-layouts: 7.04 us -> 20.9 us
    all_to_all x2, starting transfers between devices: 11.1 us -> 21.4 us  [exchange(): ends_of = lax.all_to_all(ends_of, axes, 0, 0, tiled=True)]
    ppermute x16, starting transfers between devices: 35.8 us -> 28.3 us  [the longest x12 22.5 us: exchange(): lax.ppermute(array, axes, [(a[0] * 4 + a[1], b[0] * 4 + b[1]) for a, b in...]
    ppermute x16, waiting for transfers between devices: 14.6 us -> 21.8 us  [the longest x4 16.8 us: from_others(): lax.ppermute(array, 'ch', [((i + k) % ch_count, i) for i in range(ch_coun...]
    reshape x4 -> x0, local copies, waits for them, and re-layouts: 4.39 us -> none  [the longest x3 2.7 us: halo_tables(): jnp.broadcast_to(v, shape).reshape(faces, 4 * most)]
    select_n x5 -> x2, other arithmetic: 5.91 us -> 1.69 us  [exchange(): lines = jnp.where(middle & (slot != seg - 1), paired, lines)]
    iota x12 -> x0, local copies, waits for them, and re-layouts: 3.27 us -> none  [the longest x7 2.1 us: halo_tables(): down = lax.broadcasted_iota(jnp.int32, shape, 1)]
    broadcast_in_dim x13 -> x0, local copies, waits for them, and re-layouts: 2.95 us -> none  [halo_tables(): jnp.where(row_on, row, col)]
  transfers between devices with their start and end apart: 18 -> 18, of which waited for: 4 -> 5; matrix products, arithmetic and copies ran while one was open for 26% -> 3% of each run, Pallas kernels for 7% -> 5%
where the time goes in v3:
time: 124 us; the launch traced here: 123 us
  starting transfers between devices  49.6 us (40%)
  Pallas kernels  26.4 us (21%)
  local copies, waits for them, and re-layouts  22.4 us (18%)
  waiting for transfers between devices  21.8 us (18%)
  other arithmetic  1.71 us (1%)
    ppermute x12, starting transfers between devices, exchange(): lax.ppermute(array, axes, [(a[0] * 4 + a[1], b[0] * 4 + b[1]) for a, b in...  22.5 us
    all_to_all x2, starting transfers between devices, exchange(): ends_of = lax.all_to_all(ends_of, axes, 0, 0, tiled=True)  21.4 us
    unnamed x70, local copies, waits for them, and re-layouts  20.9 us
    ppermute x4, waiting for transfers between devices, from_others(): lax.ppermute(array, 'ch', [((i + k) % ch_count, i) for i in range(ch_coun...  16.8 us
    pallas_call x1, Pallas kernels, forward(): pl.pallas_call(lambda *refs: forward_kernel(steps, pieces, plan, *refs),...  11.1 us
    pallas_call x1, Pallas kernels, backward(): pl.pallas_call(lambda *refs: backward_kernel(steps, pieces, *refs), grid=...  9.1 us
    ppermute x4, starting transfers between devices, from_others(): lax.ppermute(array, 'ch', [((i + k) % ch_count, i) for i in range(ch_coun...  5.76 us
    ppermute x12, waiting for transfers between devices, exchange(): lax.ppermute(array, axes, [(a[0] * 4 + a[1], b[0] * 4 + b[1]) for a, b in...  4.98 us
  transfers between devices with their start and end apart: 18, of which 5 were waited for; matrix products, arithmetic and copies ran while one was open for 3% of the time, Pallas kernels for 5%

profile of v3, /device:TPU:0, one launch (start us, length us, event | category | flops | bytes accessed | tf_op | source)
XLA Modules:
  0.0 122.8 jit_solution(3608302823182848644)
XLA Ops:
  0.6 3.0 %collective-permute-start = (bf16[12,64,1024]{2,1,0:T(8,128)(2,1)}, bf16[12,64,1024]{2,1,0:T(8,128)(2,1)}, u32[]{:S(2)}, u32[]{:S(2)}) collective-permute-start(bf16[12,64,1024]{2,1,0:T(8,128)(2,1)} %bitcast.20), channel_id=1, source_target_pairs={{1,0},{0,1},{3,2},{2,3},{5,4},{4,5},{7,6},{6,7},{9,8},{8,9},{11,10... | collective-permute-start | bytes 4718600 | tf_op jit(solution)/shard_map/ppermute | solution.py:393
  3.6 1.4 %copy-done = bf16[64,12,1,1,1024]{4,0,3,2,1:T(8,128)(2,1)S(1)} copy-done((bf16[64,12,1,1,1024]{4,0,3,2,1:T(8,128)(2,1)S(1)}, bf16[64,12,1,1,1024]{4,0,3,2,1:T(8,128)(2,1)}, u32[]{:S(2)}) %copy-start) | copy-done | bytes 1572888
  5.1 0.9 copy-done.4
  6.8 2.5 %rings.1 = (bf16[6,64,128]{2,1,0:T(8,128)(2,1)}, bf16[3,64,128]{2,1,0:T(8,128)(2,1)S(1)}, bf16[3,64,128]{2,1,0:T(8,128)(2,1)S(1)}, bf16[6,64,128]{2,1,0:T(8,128)(2,1)S(1)}, bf16[1,64,128]{2,1,0:T(8,128)(2,1)S(1)}) custom-call(bf16[12,64,1024]{2,1,0:T(8,128)(2,1)S(1)} %bitcast.21, bf16[1024,128]{1,0:T(8,128)(2,1)S(1)} %copy-done.4, ...), custom_call_target="tpu_custom_call" | custom-call | tf_op jit(solution)/shard_map/rings/pallas_call | solution.py:121
  12.5 1.6 %broadcast_select_fusion.1.refs_1_ = bf16[6,64,128]{2,1,0:T(8,128)(2,1)} fusion(bf16[6,64,128]{2,1,0:T(8,128)(2,1)S(1)} %collective-permute-done.1.refs_5_, bf16[6,64,128]{2,1,0:T(8,128)(2,1)} %copy-done.22, pred[6]{0:T(512)(128)(4,1)S(1)} %compare_and_fusion), kind=kLoop, calls=%fused_computation.1 | loop fusion | flops 49152 | bytes 294918 | tf_op jit(solution)/shard_map/jit(_where)/select_n | solution.py:453
  14.9 10.9 %all-to-all-start = ((bf16[16,64,128]{2,1,0:T(8,128)(2,1)}), bf16[16,64,128]{2,1,0:T(8,128)(2,1)}, u32[]{:S(2)}, u32[]{:S(2)}) async-start(bf16[16,64,128]{2,1,0:T(8,128)(2,1)} %broadcast_in_dim.27), calls=%async_computation | async-start | bytes 524288 | tf_op jit(solution)/shard_map/all_to_all | solution.py:463
  25.8 1.9 %collective-permute-start.5 = (bf16[3,64,128]{2,1,0:T(8,128)(2,1)}, bf16[3,64,128]{2,1,0:T(8,128)(2,1)S(1)}, u32[]{:S(2)}, u32[]{:S(2)}) collective-permute-start(bf16[3,64,128]{2,1,0:T(8,128)(2,1)} %copy-done.30), channel_id=1, source_target_pairs={{0,8},{2,10},{4,12},{6,14},{8,0},{10,2},{12,4},{14,6},{16,24},{18,... | collective-permute-start | bytes 147464 | tf_op jit(solution)/shard_map/ppermute | solution.py:440
  27.7 4.6 %collective-permute-start.4 = (bf16[6,64,128]{2,1,0:T(8,128)(2,1)}, bf16[6,64,128]{2,1,0:T(8,128)(2,1)S(1)}, u32[]{:S(2)}, u32[]{:S(2)}) collective-permute-start(bf16[6,64,128]{2,1,0:T(8,128)(2,1)} %broadcast_select_fusion.1.refs_1_), channel_id=1, source_target_pairs={{8,26},{16,28},{14,2},{22,4},{2,14},{4,22},{26,8},{28,16},{0,30},{... | collective-permute-start | bytes 294920 | tf_op jit(solution)/shard_map/ppermute | solution.py:440
  32.3 3.4 %collective-permute-start.3 = (bf16[6,64,128]{2,1,0:T(8,128)(2,1)}, bf16[6,64,128]{2,1,0:T(8,128)(2,1)S(1)}, u32[]{:S(2)}, u32[]{:S(2)}) collective-permute-start(bf16[6,64,128]{2,1,0:T(8,128)(2,1)} %broadcast_select_fusion.1.refs_1_), channel_id=1, source_target_pairs={{8,2},{16,4},{14,26},{22,28},{2,8},{4,16},{26,14},{28,22},{0,24},{... | collective-permute-start | bytes 294920 | tf_op jit(solution)/shard_map/ppermute | solution.py:440
  36.9 1.0 copy-done.7
  49.7 1.6 %halo.2.refs_2_.refs_4_ = bf16[13,64,128]{2,1,0:T(8,128)(2,1)S(1)} custom-call(s32[20,12]{1,0:T(8,128)S(1)} %get-tuple-element.21.refs_0_, bf16[6,64,128]{2,1,0:T(8,128)(2,1)S(1)} %copy-done.6, bf16[6,64,128]{2,1,0:T(8,128)(2,1)S(1)} %copy-done.21, bf16[6,64,128]{2,1,0:T(8,128)(2,1)S(1)} %copy-done.19, bf16[6,64,128]{2,1,0:T(8,128)(2,1)S(1)} %copy-done.17, ...), custom_call_target="tpu_custom_call" | custom-call | tf_op jit(solution)/shard_map/halo/pallas_call | solution.py:180
  52.0 7.1 %collective-permute-done.7.refs_3_.refs_5_ = bf16[13,64,128]{2,1,0:T(8,128)(2,1)S(1)} collective-permute-done((bf16[13,64,128]{2,1,0:T(8,128)(2,1)S(1)}, bf16[13,64,128]{2,1,0:T(8,128)(2,1)S(1)}, u32[]{:S(2)}, u32[]{:S(2)}) %collective-permute-start.7) | collective-permute-done | bytes 213024 | tf_op jit(solution)/shard_map/ppermute | solution.py:393
  59.1 0.9 copy-done.5
  61.7 11.1 %forward.1 = (bf16[12,64,1024]{2,1,0:T(8,128)(2,1)}, bf16[12,64,1024]{2,1,0:T(8,128)(2,1)}, bf16[6,64,128]{2,1,0:T(8,128)(2,1)S(1)}, bf16[3,64,128]{2,1,0:T(8,12...) custom-call(bf16[12,64,1024]{2,1,0:T(8,128)(2,1)S(1)} %bitcast.22, ...), custom_call_target="tpu_custom_call" | custom-call | tf_op jit(solution)/shard_map/forward/pallas_call | solution.py:268
  75.0 10.5 %all-to-all-start.1 = ((bf16[16,64,128]{2,1,0:T(8,128)(2,1)}), bf16[16,64,128]{2,1,0:T(8,128)(2,1)S(1)}, u32[]{:S(2)}, u32[]{:S(2)}) async-start(bf16[16,64,128]{2,1,0:T(8,128)(2,1)} %broadcast_in_dim.29), calls=%async_computation.1 | async-start | bytes 524288 | tf_op jit(solution)/shard_map/all_to_all | solution.py:463
  85.5 2.0 %collective-permute-start.13 = (bf16[3,64,128]{2,1,0:T(8,128)(2,1)}, bf16[3,64,128]{2,1,0:T(8,128)(2,1)S(1)}, u32[]{:S(2)}, u32[]{:S(2)}) collective-permute-start(bf16[3,64,128]{2,1,0:T(8,128)(2,1)} %copy-done.32), channel_id=1, source_target_pairs={{0,8},{2,10},{4,12},{6,14},{8,0},{10,2},{12,4},{14,6},{16,24},{18,... | collective-permute-start | bytes 147464 | tf_op jit(solution)/shard_map/ppermute | solution.py:440
  87.5 4.6 %collective-permute-start.12 = (bf16[6,64,128]{2,1,0:T(8,128)(2,1)S(1)}, bf16[6,64,128]{2,1,0:T(8,128)(2,1)S(1)}, u32[]{:S(2)}, u32[]{:S(2)}) collective-permute-start(bf16[6,64,128]{2,1,0:T(8,128)(2,1)S(1)} %broadcast_select_fusion.refs_1_), channel_id=1, source_target_pairs={{8,26},{16,28},{14,2},{22,4},{2,14},{4,22},{26,8},{28,16},{0,30},{... | collective-permute-start | bytes 294920 | tf_op jit(solution)/shard_map/ppermute | solution.py:440
  92.1 3.4 %collective-permute-start.11 = (bf16[6,64,128]{2,1,0:T(8,128)(2,1)S(1)}, bf16[6,64,128]{2,1,0:T(8,128)(2,1)S(1)}, u32[]{:S(2)}, u32[]{:S(2)}) collective-permute-start(bf16[6,64,128]{2,1,0:T(8,128)(2,1)S(1)} %broadcast_select_fusion.refs_1_), channel_id=1, source_target_pairs={{8,2},{16,4},{14,26},{22,28},{2,8},{4,16},{26,14},{28,22},{0,24},{... | collective-permute-start | bytes 294920 | tf_op jit(solution)/shard_map/ppermute | solution.py:440
  96.1 1.4 %collective-permute-done.14.refs_7_ = bf16[3,64,128]{2,1,0:T(8,128)(2,1)S(1)} collective-permute-done((bf16[3,64,128]{2,1,0:T(8,128)(2,1)}, bf16[3,64,128]{2,1,0:T(8,128)(2,1)S(1)}, u32[]{:S(2)}, u32[]{:S(2)}) %collective-permute-start.14) | collective-permute-done | bytes 49184 | tf_op jit(solution)/shard_map/ppermute | solution.py:440
  98.2 2.8 %collective-permute-done.11.refs_3_ = bf16[6,64,128]{2,1,0:T(8,128)(2,1)S(1)} collective-permute-done((bf16[6,64,128]{2,1,0:T(8,128)(2,1)S(1)}, bf16[6,64,128]{2,1,0:T(8,128)(2,1)S(1)}, u32[]{:S(2)}, u32[]{:S(2)}) %collective-permute-start.11) | collective-permute-done | bytes 98336 | tf_op jit(solution)/shard_map/ppermute | solution.py:440
  101.0 1.4 %halo.3.refs_2_.refs_4_ = bf16[13,64,128]{2,1,0:T(8,128)(2,1)S(1)} custom-call(s32[20,12]{1,0:T(8,128)S(1)} %get-tuple-element.21.refs_0_, bf16[6,64,128]{2,1,0:T(8,128)(2,1)S(1)} %broadcast_select_fusion.refs_1_, bf16[6,64,128]{2,1,0:T(8,128)(2,1)S(1)} %collective-permute-done.10.refs_2_, bf16[6,64,128]{2,1,0:T(8,128)(2,1)S(1)} %collective-permute-done.11.refs_3_, ...), custom_call_target="tpu_custom_call" | custom-call | tf_op jit(solution)/shard_map/halo/pallas_call | solution.py:180
  102.5 1.5 %collective-permute-start.15 = (bf16[13,64,128]{2,1,0:T(8,128)(2,1)S(1)}, bf16[13,64,128]{2,1,0:T(8,128)(2,1)S(1)}, u32[]{:S(2)}, u32[]{:S(2)}) collective-permute-start(bf16[13,64,128]{2,1,0:T(8,128)(2,1)S(1)} %halo.3.refs_2_.refs_4_), channel_id=1, source_target_pairs={{1,0},{0,1},{3,2},{2,3},{5,4},{4,5},{7,6},{6,7},{9,8},{8,9},{11,10... | collective-permute-start | bytes 638984 | tf_op jit(solution)/shard_map/ppermute | solution.py:393
  104.0 9.7 %collective-permute-done.15.refs_3_.refs_5_ = bf16[13,64,128]{2,1,0:T(8,128)(2,1)S(1)} collective-permute-done((bf16[13,64,128]{2,1,0:T(8,128)(2,1)S(1)}, bf16[13,64,128]{2,1,0:T(8,128)(2,1)S(1)}, u32[]{:S(2)}, u32[]{:S(2)}) %collective-permute-start.15) | collective-permute-done | bytes 213024 | tf_op jit(solution)/shard_map/ppermute | solution.py:393
  113.7 9.1 %backward.1 = bf16[12,64,1024]{2,1,0:T(8,128)(2,1)} custom-call(bf16[12,64,1024]{2,1,0:T(8,128)(2,1)} %get-tuple-element.31.refs_0_, bf16[12,64,1024]{2,1,0:T(8,128)(2,1)S(1)} %collective-permute-done.8.refs_1_, bf16[13,64,128]{2,1,0:T(8,128)(2,1)S(1)} %halo.3.refs_2_.refs_4_, bf16[13,64,128]{2,1,0:T(8,128)(2,1)S(1)} %collective-permute-done.15.refs_3_.refs_5_, ...), custom_call_target="tpu_custom_call" | custom-call | tf_op jit(solution)/shard_map/backward/pallas_call | solution.py:286
  (93 shorter events, 23.4 us)
Async XLA Ops:
  0.6 58.5 %collective-permute-start = (bf16[12,64,1024]{2,1,0:T(8,128)(2,1)}, bf16[12,64,1024]{2,1,0:T(8,128)(2,1)}, u32[]{:S(2)}, u32[]{:S(2)}) collective-permute-start(bf16[12,64,1024]{2,1,0:T(8,128)(2,1)} %bitcast.20), channel_id=1, source_target_pairs={{1,0},{0,1},{3,2},{2,3},{5,4},{4,5},{7,6},{6,7},{9,8},{8,9},{11,10... | collective-permute-start | bytes 4718600 | tf_op jit(solution)/shard_map/ppermute | solution.py:393
  6.8 52.3 %copy-start.2 = (bf16[64,12,1,1,1024]{4,0,3,2,1:T(8,128)(2,1)S(1)}, bf16[64,12,1,1,1024]{4,0,3,2,1:T(8,128)(2,1)}, u32[]{:S(2)}) copy-start(bf16[64,12,1,1,1024]{4,0,3,2,1:T(8,128)(2,1)} %param.10) | copy-start | bytes 4718596
  11.2 47.9 %copy-start.1 = (bf16[64,12,1,1,1024]{4,0,3,2,1:T(8,128)(2,1)S(1)}, bf16[64,12,1,1,1024]{4,0,3,2,1:T(8,128)(2,1)}, u32[]{:S(2)}) copy-start(bf16[64,12,1,1,1024]{4,0,3,2,1:T(8,128)(2,1)} %param.9) | copy-start | bytes 4718596
  11.2 47.9 %copy-start.3 = (bf16[128,1152]{1,0:T(8,128)(2,1)S(1)}, bf16[128,1152]{1,0:T(8,128)(2,1)}, u32[]{:S(2)}) copy-start(bf16[128,1152]{1,0:T(8,128)(2,1)} %constant.35.clone.refs_8_.refs_7_) | copy-start | bytes 884740
  11.2 0.8 collective-permute-start.1
  14.9 28.9 %all-to-all-start = ((bf16[16,64,128]{2,1,0:T(8,128)(2,1)}), bf16[16,64,128]{2,1,0:T(8,128)(2,1)}, u32[]{:S(2)}, u32[]{:S(2)}) async-start(bf16[16,64,128]{2,1,0:T(8,128)(2,1)} %broadcast_in_dim.27), calls=%async_computation | async-start | bytes 524288 | tf_op jit(solution)/shard_map/all_to_all | solution.py:463
  25.8 10.5 %collective-permute-start.5 = (bf16[3,64,128]{2,1,0:T(8,128)(2,1)}, bf16[3,64,128]{2,1,0:T(8,128)(2,1)S(1)}, u32[]{:S(2)}, u32[]{:S(2)}) collective-permute-start(bf16[3,64,128]{2,1,0:T(8,128)(2,1)} %copy-done.30), channel_id=1, source_target_pairs={{0,8},{2,10},{4,12},{6,14},{8,0},{10,2},{12,4},{14,6},{16,24},{18,... | collective-permute-start | bytes 147464 | tf_op jit(solution)/shard_map/ppermute | solution.py:440
  27.7 14.2 %collective-permute-start.4 = (bf16[6,64,128]{2,1,0:T(8,128)(2,1)}, bf16[6,64,128]{2,1,0:T(8,128)(2,1)S(1)}, u32[]{:S(2)}, u32[]{:S(2)}) collective-permute-start(bf16[6,64,128]{2,1,0:T(8,128)(2,1)} %broadcast_select_fusion.1.refs_1_), channel_id=1, source_target_pairs={{8,26},{16,28},{14,2},{22,4},{2,14},{4,22},{26,8},{28,16},{0,30},{... | collective-permute-start | bytes 294920 | tf_op jit(solution)/shard_map/ppermute | solution.py:440
  32.3 10.2 %collective-permute-start.3 = (bf16[6,64,128]{2,1,0:T(8,128)(2,1)}, bf16[6,64,128]{2,1,0:T(8,128)(2,1)S(1)}, u32[]{:S(2)}, u32[]{:S(2)}) collective-permute-start(bf16[6,64,128]{2,1,0:T(8,128)(2,1)} %broadcast_select_fusion.1.refs_1_), channel_id=1, source_target_pairs={{8,2},{16,4},{14,26},{22,28},{2,8},{4,16},{26,14},{28,22},{0,24},{... | collective-permute-start | bytes 294920 | tf_op jit(solution)/shard_map/ppermute | solution.py:440
  35.7 7.4 %collective-permute-start.2 = (bf16[6,64,128]{2,1,0:T(8,128)(2,1)}, bf16[6,64,128]{2,1,0:T(8,128)(2,1)S(1)}, u32[]{:S(2)}, u32[]{:S(2)}) collective-permute-start(bf16[6,64,128]{2,1,0:T(8,128)(2,1)} %broadcast_select_fusion.1.refs_1_), channel_id=1, source_target_pairs={{8,14},{16,22},{14,8},{22,16},{2,26},{4,28},{26,2},{28,4},{0,6},{6... | collective-permute-start | bytes 294920 | tf_op jit(solution)/shard_map/ppermute | solution.py:440
  36.9 4.3 %collective-permute-start.6 = (bf16[3,64,128]{2,1,0:T(8,128)(2,1)}, bf16[3,64,128]{2,1,0:T(8,128)(2,1)S(1)}, u32[]{:S(2)}, u32[]{:S(2)}) collective-permute-start(bf16[3,64,128]{2,1,0:T(8,128)(2,1)} %copy-done.29), channel_id=1, source_target_pairs={{0,2},{2,0},{4,6},{6,4},{8,10},{10,8},{12,14},{14,12},{16,18},{18,... | collective-permute-start | bytes 147464 | tf_op jit(solution)/shard_map/ppermute | solution.py:440
  51.4 7.7 %collective-permute-start.7 = (bf16[13,64,128]{2,1,0:T(8,128)(2,1)S(1)}, bf16[13,64,128]{2,1,0:T(8,128)(2,1)S(1)}, u32[]{:S(2)}, u32[]{:S(2)}) collective-permute-start(bf16[13,64,128]{2,1,0:T(8,128)(2,1)S(1)} %halo.2.refs_2_.refs_4_), channel_id=1, source_target_pairs={{1,0},{0,1},{3,2},{2,3},{5,4},{4,5},{7,6},{6,7},{9,8},{8,9},{11,10... | collective-permute-start | bytes 638984 | tf_op jit(solution)/shard_map/ppermute | solution.py:393
  61.7 39.3 %copy-start.15 = (bf16[128,128]{1,0:T(8,128)(2,1)S(1)}, bf16[128,128]{1,0:T(8,128)(2,1)}, u32[]{:S(2)}) copy-start(bf16[128,128]{1,0:T(8,128)(2,1)} %constant.36.clone.refs_9_) | copy-start | bytes 98308
  72.8 12.6 %copy-start.32 = (bf16[3,64,128]{2,1,0:T(8,128)(2,1)}, bf16[3,64,128]{2,1,0:T(8,128)(2,1)S(1)}, u32[]{:S(2)}) copy-start(bf16[3,64,128]{2,1,0:T(8,128)(2,1)S(1)} %get-tuple-element.36) | copy-start | bytes 147460
  72.8 40.9 %copy-start.9 = (bf16[192,384]{1,0:T(8,128)(2,1)S(1)}, bf16[192,384]{1,0:T(8,128)(2,1)}, u32[]{:S(2)}) copy-start(bf16[192,384]{1,0:T(8,128)(2,1)} %copy-done.8) | copy-start | bytes 442372
  72.8 40.9 %collective-permute-start.8 = (bf16[12,64,1024]{2,1,0:T(8,128)(2,1)}, bf16[12,64,1024]{2,1,0:T(8,128)(2,1)S(1)}, u32[]{:S(2)}, u32[]{:S(2)}) collective-permute-start(bf16[12,64,1024]{2,1,0:T(8,128)(2,1)} %get-tuple-element.31.refs_0_), channel_id=1, source_target_pairs={{1,0},{0,1},{3,2},{2,3},{5,4},{4,5},{7,6},{6,7},{9,8},{8,9},{11,10... | collective-permute-start | bytes 4718600 | tf_op jit(solution)/shard_map/ppermute | solution.py:393
  73.5 0.7 collective-permute-start.9
  75.0 26.0 %all-to-all-start.1 = ((bf16[16,64,128]{2,1,0:T(8,128)(2,1)}), bf16[16,64,128]{2,1,0:T(8,128)(2,1)S(1)}, u32[]{:S(2)}, u32[]{:S(2)}) async-start(bf16[16,64,128]{2,1,0:T(8,128)(2,1)} %broadcast_in_dim.29), calls=%async_computation.1 | async-start | bytes 524288 | tf_op jit(solution)/shard_map/all_to_all | solution.py:463
  85.5 10.6 %collective-permute-start.13 = (bf16[3,64,128]{2,1,0:T(8,128)(2,1)}, bf16[3,64,128]{2,1,0:T(8,128)(2,1)S(1)}, u32[]{:S(2)}, u32[]{:S(2)}) collective-permute-start(bf16[3,64,128]{2,1,0:T(8,128)(2,1)} %copy-done.32), channel_id=1, source_target_pairs={{0,8},{2,10},{4,12},{6,14},{8,0},{10,2},{12,4},{14,6},{16,24},{18,... | collective-permute-start | bytes 147464 | tf_op jit(solution)/shard_map/ppermute | solution.py:440
  87.5 10.7 %collective-permute-start.12 = (bf16[6,64,128]{2,1,0:T(8,128)(2,1)S(1)}, bf16[6,64,128]{2,1,0:T(8,128)(2,1)S(1)}, u32[]{:S(2)}, u32[]{:S(2)}) collective-permute-start(bf16[6,64,128]{2,1,0:T(8,128)(2,1)S(1)} %broadcast_select_fusion.refs_1_), channel_id=1, source_target_pairs={{8,26},{16,28},{14,2},{22,4},{2,14},{4,22},{26,8},{28,16},{0,30},{... | collective-permute-start | bytes 294920 | tf_op jit(solution)/shard_map/ppermute | solution.py:440
  92.1 8.9 %collective-permute-start.11 = (bf16[6,64,128]{2,1,0:T(8,128)(2,1)S(1)}, bf16[6,64,128]{2,1,0:T(8,128)(2,1)S(1)}, u32[]{:S(2)}, u32[]{:S(2)}) collective-permute-start(bf16[6,64,128]{2,1,0:T(8,128)(2,1)S(1)} %broadcast_select_fusion.refs_1_), channel_id=1, source_target_pairs={{8,2},{16,4},{14,26},{22,28},{2,8},{4,16},{26,14},{28,22},{0,24},{... | collective-permute-start | bytes 294920 | tf_op jit(solution)/shard_map/ppermute | solution.py:440
  95.5 5.6 %collective-permute-start.10 = (bf16[6,64,128]{2,1,0:T(8,128)(2,1)S(1)}, bf16[6,64,128]{2,1,0:T(8,128)(2,1)S(1)}, u32[]{:S(2)}, u32[]{:S(2)}) collective-permute-start(bf16[6,64,128]{2,1,0:T(8,128)(2,1)S(1)} %broadcast_select_fusion.refs_1_), channel_id=1, source_target_pairs={{8,14},{16,22},{14,8},{22,16},{2,26},{4,28},{26,2},{28,4},{0,6},{6... | collective-permute-start | bytes 294920 | tf_op jit(solution)/shard_map/ppermute | solution.py:440
  96.1 1.4 %collective-permute-start.14 = (bf16[3,64,128]{2,1,0:T(8,128)(2,1)}, bf16[3,64,128]{2,1,0:T(8,128)(2,1)S(1)}, u32[]{:S(2)}, u32[]{:S(2)}) collective-permute-start(bf16[3,64,128]{2,1,0:T(8,128)(2,1)} %copy-done.31), channel_id=1, source_target_pairs={{0,2},{2,0},{4,6},{6,4},{8,10},{10,8},{12,14},{14,12},{16,18},{18,... | collective-permute-start | bytes 147464 | tf_op jit(solution)/shard_map/ppermute | solution.py:440
  102.5 11.3 %collective-permute-start.15 = (bf16[13,64,128]{2,1,0:T(8,128)(2,1)S(1)}, bf16[13,64,128]{2,1,0:T(8,128)(2,1)S(1)}, u32[]{:S(2)}, u32[]{:S(2)}) collective-permute-start(bf16[13,64,128]{2,1,0:T(8,128)(2,1)S(1)} %halo.3.refs_2_.refs_4_), channel_id=1, source_target_pairs={{1,0},{0,1},{3,2},{2,3},{5,4},{4,5},{7,6},{6,7},{9,8},{8,9},{11,10... | collective-permute-start | bytes 638984 | tf_op jit(solution)/shard_map/ppermute | solution.py:393
  (29 other events, 34.6 us)

commit v4 on v3

--- a/solution.py
+++ b/solution.py
@@ -9,7 +9,7 @@
 RB = 32
 GROUP = 4
 LANES = 128
-VMEM_LIMIT = 24 * 1024 * 1024
+VMEM_LIMIT = 60 * 1024 * 1024
 STRIP_LANE = (96, 0, 32, 64)
 
 
@@ -56,57 +56,63 @@
     return lax.broadcasted_iota(jnp.int32, shape, len(shape) - 1)
 
 
-def emit_rings(step, steps, fields, plan, ring_ref, cornsel_ref, outs, packs_acc, corner_acc):
+def side_tiles(fields, first_face, ring_ref, cornsel_ref):
     chan = fields[0].shape[0]
     lane = lane_iota((chan, LANES))
     rings = [
         jnp.dot(field, ring_ref[...], preferred_element_type=jnp.float32) for field in fields
     ]
+    tiles = []
     for side in range(4):
         tile = jnp.zeros((chan, LANES), jnp.float32)
         for g, ring in enumerate(rings):
             moved = pltpu.roll(ring, ((g - side) * 32) % LANES, 1) if g != side else ring
             tile = jnp.where(lane // 32 == g, moved, tile)
-        packs_acc[side * steps + step] = tile.astype(jnp.bfloat16)
-
-    @pl.when(step == 0)
-    def _():
-        corner_acc[...] = jnp.zeros_like(corner_acc)
-
+        tiles.append(tile.astype(jnp.bfloat16))
+    corners = jnp.zeros((chan, LANES), jnp.float32)
     for g, ring in enumerate(rings):
         picked = jnp.dot(
             ring.astype(jnp.bfloat16), cornsel_ref[...], preferred_element_type=jnp.float32
         )
-        corner_acc[...] += pltpu.roll(picked, (step * GROUP + g) * 4, 1)
+        corners += pltpu.roll(picked, (first_face + g) * 4, 1)
+    return (tiles, corners)
+
+
+def hand_out(plan, steps, packs, corners, outs):
+    chosen = iter(plan.chosen_sides())
+    for out in outs[:-1]:
+        for at in range(0, out.shape[0], steps):
+            base = next(chosen) * steps
+            for q in range(steps):
+                out[at + q] = packs[base + q]
+    packed = plan.pack_corners(corners).astype(jnp.bfloat16)
+    for copy in range(outs[-1].shape[0]):
+        outs[-1][copy] = packed
+
+
+def ring_outs(faces, chan, plan):
+    steps = faces // GROUP
+    shapes = [(count * steps, chan, LANES) for count in plan.counts] + [plan.corner_shape(chan)]
+    return [jax.ShapeDtypeStruct(shape, jnp.bfloat16) for shape in shapes]
+
+
+def rings_kernel(steps, plan, field_ref, ring_ref, cornsel_ref, *refs):
+    outs, (packs, corner_acc) = (refs[:-2], refs[-2:])
+    step = pl.program_id(0)
+    fields = [field_ref[g] for g in range(GROUP)]
+    tiles, corners = side_tiles(fields, step * GROUP, ring_ref, cornsel_ref)
+    for side, tile in enumerate(tiles):
+        packs[side * steps + step] = tile
+
+    @pl.when(step == 0)
+    def _():
+        corner_acc[...] = jnp.zeros_like(corner_acc)
+
+    corner_acc[...] += corners
 
     @pl.when(step == steps - 1)
     def _():
-        chosen = iter(plan.chosen_sides())
-        for out in outs[:-1]:
-            for at in range(0, out.shape[0], steps):
-                base = next(chosen) * steps
-                for q in range(steps):
-                    out[at + q] = packs_acc[base + q]
-        outs[-1][0] = corner_acc[...].astype(jnp.bfloat16)
-
-
-def ring_outs(faces, chan, counts):
-    steps = faces // GROUP
-    tiles = [count * steps for count in counts] + [1]
-    return [jax.ShapeDtypeStruct((n, chan, LANES), jnp.bfloat16) for n in tiles]
-
-
-def ring_scratch(faces, chan):
-    steps = faces // GROUP
-    return [
-        pltpu.VMEM((4 * steps, chan, LANES), jnp.bfloat16),
-        pltpu.VMEM((chan, LANES), jnp.float32),
-    ]
-
-
-def rings_kernel(steps, plan, field_ref, ring_ref, cornsel_ref, *refs):
-    fields = [field_ref[g] for g in range(GROUP)]
-    emit_rings(pl.program_id(0), steps, fields, plan, ring_ref, cornsel_ref, refs[:-2], *refs[-2:])
+        hand_out(plan, steps, packs, corner_acc[...], outs)
 
 
 def whole_spec(array):
@@ -117,7 +123,7 @@
 def rings_of(field, plan, ring, cornsel):
     faces, chan, tile = field.shape
     steps = faces // GROUP
-    outs = ring_outs(faces, chan, plan.counts)
+    outs = ring_outs(faces, chan, plan)
     return pl.pallas_call(
         lambda *refs: rings_kernel(steps, plan, *refs),
         grid=(steps,),
@@ -128,20 +134,25 @@
         ],
         out_specs=[whole_spec(out) for out in outs],
         out_shape=outs,
-        scratch_shapes=ring_scratch(faces, chan),
+        scratch_shapes=[
+            pltpu.VMEM((4 * steps, chan, LANES), jnp.bfloat16),
+            pltpu.VMEM((chan, LANES), jnp.float32),
+        ],
         compiler_params=pltpu.CompilerParams(vmem_limit_bytes=VMEM_LIMIT),
         name="rings",
     )(field, ring, cornsel)
 
 
-def halo_kernel(faces, units, unit, *refs):
+def halo_kernel(faces, units, unit, plan, *refs):
     table, tile_refs, (rev_ref, halo_ref, pool, turn_acc) = (refs[0], refs[1:-4], refs[-4:])
     chan = halo_ref.shape[1]
     lane = lane_iota((chan, LANES))
     at = 0
-    for ref in tile_refs:
+    for ref in tile_refs[:-1]:
         pool[at : at + ref.shape[0]] = ref[...]
         at += ref.shape[0]
+    for k in range(tile_refs[-1].shape[0]):
+        pool[at + k] = plan.unpack_corners(tile_refs[-1][k])
     corner_tile = jnp.zeros((chan, LANES), jnp.float32)
     most = max(units)
     rows = 4 * most
@@ -172,13 +183,13 @@
     halo_ref[faces] = corner_tile.astype(jnp.bfloat16)
 
 
-def assemble_halo(table, tiles, rev, faces, units, unit):
+def assemble_halo(plan, table, tiles, rev, faces, units, unit):
     chan = tiles[0].shape[1]
     halo = jax.ShapeDtypeStruct((faces + 1, chan, LANES), jnp.bfloat16)
     vmem = pl.BlockSpec(memory_space=pltpu.VMEM)
     smem = pl.BlockSpec(memory_space=pltpu.SMEM)
     return pl.pallas_call(
-        lambda *refs: halo_kernel(faces, units, unit, *refs),
+        lambda *refs: halo_kernel(faces, units, unit, plan, *refs),
         in_specs=[smem] + [vmem] * (len(tiles) + 1),
         out_specs=vmem,
         out_shape=halo,
@@ -217,82 +228,120 @@
     return (above + sums[chan : 2 * chan] + below)[:, :tile]
 
 
-def forward_kernel(steps, pieces, plan, *refs):
-    field_refs, refs = (refs[:pieces], refs[pieces:])
-    halo_refs, refs = (refs[:pieces], refs[pieces:])
-    corner_refs, refs = (refs[:pieces], refs[pieces:])
-    (cot_ref, taps_ref, spread_ref, ring_ref, cornsel_ref, act_ref, gated_ref) = refs[:7]
-    outs, (stack_ref, packs_acc, corner_acc) = (refs[7:-3], refs[-3:])
-    step = pl.program_id(0)
-    fields = []
+def split_refs(refs, *counts):
+    out = []
+    for count in counts:
+        out.append(refs[:count])
+        refs = refs[count:]
+    return (*out, refs)
+
+
+def forward_kernel(step, steps, pieces, plan, *refs):
+    before = step
+    fields, halos, corners, consts, old, refs = split_refs(
+        refs, pieces, pieces, pieces, 5, 2 * before + (step > 0)
+    )
+    cot_ref, taps_ref, spread_ref, ring_ref, cornsel_ref = consts
+    act_ref, gated_ref = refs[:2]
+    made = []
     for g in range(GROUP):
-        pre = conv_face(g, step, field_refs, halo_refs, corner_refs, taps_ref, spread_ref, stack_ref)
+        pre = conv_face(g, step, fields, halos, corners, taps_ref, spread_ref, refs[-1])
         sig = 1.0 / (1.0 + jnp.exp(-pre))
         act_ref[g] = (pre * sig).astype(jnp.bfloat16)
         gated = cot_ref[g].astype(jnp.float32) * sig * (1.0 + pre * (1.0 - sig))
         gated_ref[g] = gated.astype(jnp.bfloat16)
-        fields.append(gated.astype(jnp.bfloat16))
-    emit_rings(step, steps, fields, plan, ring_ref, cornsel_ref, outs, packs_acc, corner_acc)
-
-
-def backward_kernel(steps, pieces, *refs):
-    field_refs, refs = (refs[:pieces], refs[pieces:])
-    halo_refs, refs = (refs[:pieces], refs[pieces:])
-    corner_refs, refs = (refs[:pieces], refs[pieces:])
-    (taps_ref, spread_ref, grad_ref, stack_ref) = refs
-    step = pl.program_id(0)
-    for g in range(GROUP):
-        total = conv_face(
-            g, step, field_refs, halo_refs, corner_refs, taps_ref, spread_ref, stack_ref
-        )
-        grad_ref[g] = total.astype(jnp.bfloat16)
-
-
-def conv_specs(fields, halos):
-    faces, chan, tile = fields[0].shape
-    group = lambda i: (i, 0, 0)
+        made.append(gated.astype(jnp.bfloat16))
+    tiles, corner = side_tiles(made, step * GROUP, ring_ref, cornsel_ref)
+    if step < steps - 1:
+        for side, tile in enumerate(tiles):
+            refs[2][side] = tile
+        refs[3][0] = corner.astype(jnp.bfloat16)
+        return
+    packs = refs[-2]
+    for side in range(4):
+        for q in range(before):
+            packs[side * steps + q] = old[2 * q][side]
+        packs[side * steps + step] = tiles[side]
+    for q in range(before):
+        corner += old[2 * q + 1][0].astype(jnp.float32)
+    hand_out(plan, steps, packs, corner, refs[2:-2])
+
+
+def conv_specs(fields, halos, step, own_blocks):
+    _, chan, tile = fields[0].shape
+    last = halos[0].shape[0] - 1
+    field = 0 if own_blocks else step
     return (
-        [pl.BlockSpec((GROUP, chan, tile), group) for _ in fields]
-        + [pl.BlockSpec((GROUP, chan, LANES), group) for _ in halos]
-        + [pl.BlockSpec((1, chan, LANES), lambda i: (faces, 0, 0)) for _ in halos]
+        [pl.BlockSpec((GROUP, chan, tile), lambda i: (field, 0, 0)) for _ in fields]
+        + [pl.BlockSpec((GROUP, chan, LANES), lambda i: (step, 0, 0)) for _ in halos]
+        + [pl.BlockSpec((1, chan, LANES), lambda i: (last, 0, 0)) for _ in halos]
     )
 
 
-def forward(plan, fields, halos, cot, taps, spread, ring, cornsel):
+def stack_scratch(chan, pieces, tile):
+    return pltpu.VMEM((3 * chan * pieces, tile + LANES), jnp.bfloat16)
+
+
+def forward(step, plan, fields, halos, cot, taps, spread, ring, cornsel, act, old):
     faces, chan, tile = fields[0].shape
     steps = faces // GROUP
     pieces = len(fields)
-    outs = ring_outs(faces, chan, plan.counts)
-    out = jax.ShapeDtypeStruct((faces, chan, tile), jnp.bfloat16)
-    block = pl.BlockSpec((GROUP, chan, tile), lambda i: (i, 0, 0))
+    if step < steps - 1:
+        outs = [
+            jax.ShapeDtypeStruct((4, chan, LANES), jnp.bfloat16),
+            jax.ShapeDtypeStruct((1, chan, LANES), jnp.bfloat16),
+        ]
+        scratch = []
+    else:
+        outs = ring_outs(faces, chan, plan)
+        scratch = [pltpu.VMEM((4 * steps, chan, LANES), jnp.bfloat16)]
+    whole = jax.ShapeDtypeStruct((faces, chan, tile), jnp.bfloat16)
+    chunk = jax.ShapeDtypeStruct((GROUP, chan, tile), jnp.bfloat16)
+    block = pl.BlockSpec((GROUP, chan, tile), lambda i: (step, 0, 0))
+    aside = [] if act is None else [act]
+    args = [*fields, *halos, *halos, cot, taps, spread, ring, cornsel, *old, *aside]
     return pl.pallas_call(
-        lambda *refs: forward_kernel(steps, pieces, plan, *refs),
-        grid=(steps,),
-        in_specs=conv_specs(fields, halos)
-        + [block, whole_spec(taps), whole_spec(spread), whole_spec(ring), whole_spec(cornsel)],
-        out_specs=[block, block] + [whole_spec(o) for o in outs],
-        out_shape=[out, out] + outs,
-        scratch_shapes=[pltpu.VMEM((3 * chan * pieces, tile + LANES), jnp.bfloat16)]
-        + ring_scratch(faces, chan),
+        lambda *refs: forward_kernel(step, steps, pieces, plan, *refs),
+        grid=(1,),
+        in_specs=conv_specs(fields, halos, step, False)
+        + [block, whole_spec(taps), whole_spec(spread), whole_spec(ring), whole_spec(cornsel)]
+        + [whole_spec(array) for array in old]
+        + [pl.BlockSpec(memory_space=pl.ANY) for _ in aside],
+        out_specs=[block, whole_spec(chunk)] + [whole_spec(o) for o in outs],
+        out_shape=[whole, chunk] + outs,
+        input_output_aliases={len(args) - 1: 0} if aside else {},
+        scratch_shapes=scratch + [stack_scratch(chan, pieces, tile)],
         compiler_params=pltpu.CompilerParams(vmem_limit_bytes=VMEM_LIMIT),
         name="forward",
-    )(*fields, *halos, *halos, cot, taps, spread, ring, cornsel)
-
-
-def backward(fields, halos, taps, spread):
-    faces, chan, tile = fields[0].shape
-    steps = faces // GROUP
+    )(*args)
+
+
+def backward_kernel(step, pieces, *refs):
+    fields, halos, corners, consts, refs = split_refs(refs, pieces, pieces, pieces, 2)
+    grad_ref, stack_ref = refs[-2:]
+    for g in range(GROUP):
+        total = conv_face(g, step, fields, halos, corners, *consts, stack_ref)
+        grad_ref[g] = total.astype(jnp.bfloat16)
+
+
+def backward(step, faces, fields, halos, taps, spread, grad):
+    _, chan, tile = fields[0].shape
     pieces = len(fields)
+    aside = [] if grad is None else [grad]
+    args = [*fields, *halos, *halos, taps, spread, *aside]
     return pl.pallas_call(
-        lambda *refs: backward_kernel(steps, pieces, *refs),
-        grid=(steps,),
-        in_specs=conv_specs(fields, halos) + [whole_spec(taps), whole_spec(spread)],
-        out_specs=pl.BlockSpec((GROUP, chan, tile), lambda i: (i, 0, 0)),
+        lambda *refs: backward_kernel(step, pieces, *refs),
+        grid=(1,),
+        in_specs=conv_specs(fields, halos, step, True)
+        + [whole_spec(taps), whole_spec(spread)]
+        + [pl.BlockSpec(memory_space=pl.ANY) for _ in aside],
+        out_specs=pl.BlockSpec((GROUP, chan, tile), lambda i: (step, 0, 0)),
         out_shape=jax.ShapeDtypeStruct((faces, chan, tile), jnp.bfloat16),
-        scratch_shapes=[pltpu.VMEM((3 * chan * pieces, tile + LANES), jnp.bfloat16)],
+        input_output_aliases={len(args) - 1: 0} if aside else {},
+        scratch_shapes=[stack_scratch(chan, pieces, tile)],
         compiler_params=pltpu.CompilerParams(vmem_limit_bytes=VMEM_LIMIT),
         name="backward",
-    )(*fields, *halos, *halos, taps, spread)
+    )(*args)
 
 
 def rows_of(*parts):
@@ -407,6 +456,18 @@
     def __init__(self, quads):
         self.quads = quads
 
+    def corner_shape(self, chan):
+        return (16, chan // 2, LANES)
+
+    def pack_corners(self, corners):
+        half = corners.shape[0] // 2
+        return corners[:half] + pltpu.roll(corners[half:], LANES // 2, 1)
+
+    def unpack_corners(self, packed):
+        upper = packed.astype(jnp.float32)
+        both = jnp.concatenate([upper, pltpu.roll(upper, LANES // 2, 1)], axis=0)
+        return both.astype(jnp.bfloat16)
+
     def roles(self):
         row_pos, col_pos = self.place()
         px_end = (row_pos == 0) | (row_pos == 3)
@@ -459,8 +520,7 @@
                 pairs += [((x, y), (x, 3 - y)) for x in (1, 2) for y in (1, 2)]
             across.append(swap(lines, pairs))
         corner, lines = lax.optimization_barrier((corner, lines))
-        ends_of = jnp.broadcast_to(corner, (16,) + corner.shape[1:])
-        ends_of = lax.all_to_all(ends_of, axes, 0, 0, tiled=True)
+        ends_of = lax.all_to_all(corner, axes, 0, 0, tiled=True)
         return [lines, *across, paired, near_col, near_row, ends_of]
 
     def strip_cell(self, g, s, at):
@@ -497,6 +557,15 @@
 
 class GatheredHalo(Place):
     counts = (1, 1, 1, 1, 2)
+
+    def corner_shape(self, chan):
+        return (1, chan, LANES)
+
+    def pack_corners(self, corners):
+        return corners
+
+    def unpack_corners(self, packed):
+        return packed
 
     def __init__(self, quads, px_count, py_count, col_len):
         self.quads = quads
@@ -552,7 +621,7 @@
     cornsel = jnp.asarray(corner_matrix(), jnp.bfloat16)
     spread = jnp.asarray(spread_matrix(col_len), jnp.bfloat16)
     rev = jnp.asarray(reverse_matrix(unit), jnp.bfloat16)
-    if px_count == py_count == 4 and col_len == RB:
+    if px_count == py_count == 4 and col_len == RB and chan % 32 == 0:
         plan = SquareHalo(faces // GROUP)
     else:
         plan = GatheredHalo(faces // GROUP, px_count, py_count, col_len)
@@ -565,15 +634,22 @@
         plan, edge_table, corner_table, weight, chan, (px_count, py_count), col_len, unit
     )
     tiles = plan.exchange(*parts)
-    halo = assemble_halo(table, tiles, rev, faces, units, unit)
+    halo = assemble_halo(plan, table, tiles, rev, faces, units, unit)
     halos = from_others(halo, ch_count)
-    act, gated, *parts = forward(plan, fields, halos, cot, taps, spread, ring, cornsel)
-
-    fields = from_others(gated, ch_count)
+    act, old, chunks = (None, [], [])
+    for step in range(faces // GROUP):
+        act, gated, *parts = forward(
+            step, plan, fields, halos, cot, taps, spread, ring, cornsel, act, old
+        )
+        old = old + parts
+        chunks.append(from_others(gated, ch_count))
+
     tiles = plan.exchange(*parts)
-    halo = assemble_halo(table, tiles, rev, faces, units, unit)
+    halo = assemble_halo(plan, table, tiles, rev, faces, units, unit)
     halos = from_others(halo, ch_count)
-    grad = backward(fields, halos, back_taps, spread)
+    grad = None
+    for step, fields in enumerate(chunks):
+        grad = backward(step, faces, fields, halos, back_taps, spread, grad)
 
     shape = (chan, faces, 1, 1, tile)
     return (

time: 124 us -> 123 us (level)
  local copies, waits for them, and re-layouts: 22.4 us -> 5.43 us
  Pallas kernels: 26.4 us -> 40.9 us
  waiting for transfers between devices: 21.8 us -> 24.9 us
  starting transfers between devices: 49.6 us -> 48.1 us
    unnamed x70 -> x48, local copies, waits for them, and re-layouts: 20.9 us -> 5.43 us
    pallas_call x4 -> x8, Pallas kernels: 23.3 us -> 34.7 us  [the longest x3 15.9 us: forward(): pl.pallas_call(lambda *refs: forward_kernel(step, steps, pieces, plan, *r...]
    ppermute x12, waiting for transfers between devices: 4.98 us -> 13.8 us  [exchange(): lax.ppermute(array, axes, [(a[0] * 4 + a[1], b[0] * 4 + b[1]) for a, b in...]
    ppermute x4 -> x6, waiting for transfers between devices: 16.8 us -> 11.1 us  [from_others(): lax.ppermute(array, 'ch', [((i + k) % ch_count, i) for i in range(ch_coun...]
    all_to_all x2, starting transfers between devices: 21.4 us -> 18.7 us  [exchange(): ends_of = lax.all_to_all(corner, axes, 0, 0, tiled=True)]
    pallas_call x1, Pallas kernels: 0.63 us -> 2.23 us  [setup(): pl.pallas_call(lambda *refs: setup_kernel(plan, chan, (*counts, col_len,...]
    broadcast_in_dim x2 -> x0, local copies, waits for them, and re-layouts: 1.51 us -> none  [exchange(): ends_of = jnp.broadcast_to(corner, (16,) + corner.shape[1:])]
    pallas_call x1, Pallas kernels: 2.53 us -> 3.98 us  [rings_of(): pl.pallas_call(lambda *refs: rings_kernel(steps, plan, *refs), grid=(step...]
  transfers between devices with their start and end apart: 18 -> 20, of which waited for: 5 -> 7; matrix products, arithmetic and copies ran while one was open for 3% -> 2% of each run, Pallas kernels for 5% -> 17%
where the time goes in v4:
time: 123 us; the launch traced here: 122 us
  starting transfers between devices  48.1 us (39%)
  Pallas kernels  40.9 us (33%)
  waiting for transfers between devices  24.9 us (20%)
  local copies, waits for them, and re-layouts  5.43 us (4%)
  other arithmetic  2.03 us (2%)
    ppermute x12, starting transfers between devices, exchange(): lax.ppermute(array, axes, [(a[0] * 4 + a[1], b[0] * 4 + b[1]) for a, b in...  22.7 us
    all_to_all x2, starting transfers between devices, exchange(): ends_of = lax.all_to_all(corner, axes, 0, 0, tiled=True)  18.7 us
    pallas_call x3, Pallas kernels, forward(): pl.pallas_call(lambda *refs: forward_kernel(step, steps, pieces, plan, *r...  15.9 us
    ppermute x12, waiting for transfers between devices, exchange(): lax.ppermute(array, axes, [(a[0] * 4 + a[1], b[0] * 4 + b[1]) for a, b in...  13.8 us
    pallas_call x3, Pallas kernels, backward(): pl.pallas_call(lambda *refs: backward_kernel(step, pieces, *refs), grid=(...  13.6 us
    ppermute x6, waiting for transfers between devices, from_others(): lax.ppermute(array, 'ch', [((i + k) % ch_count, i) for i in range(ch_coun...  11.1 us
    ppermute x6, starting transfers between devices, from_others(): lax.ppermute(array, 'ch', [((i + k) % ch_count, i) for i in range(ch_coun...  6.69 us
    unnamed x48, local copies, waits for them, and re-layouts  5.43 us
  transfers between devices with their start and end apart: 20, of which 7 were waited for; matrix products, arithmetic and copies ran while one was open for 2% of the time, Pallas kernels for 17%

profile of v4, /device:TPU:0, one launch (start us, length us, event | category | flops | bytes accessed | tf_op | source)
XLA Modules:
  0.0 122.4 jit_solution(14875419637082443167)
XLA Ops:
  0.6 3.0 %collective-permute-start = (bf16[12,64,1024]{2,1,0:T(8,128)(2,1)}, bf16[12,64,1024]{2,1,0:T(8,128)(2,1)S(1)}, u32[]{:S(2)}, u32[]{:S(2)}) collective-permute-start(bf16[12,64,1024]{2,1,0:T(8,128)(2,1)} %bitcast.18), channel_id=1, source_target_pairs={{1,0},{0,1},{3,2},{2,3},{5,4},{4,5},{7,6},{6,7},{9,8},{8,9},{11,10... | collective-permute-start | bytes 4718600 | tf_op jit(solution)/shard_map/ppermute | solution.py:442
  3.6 4.0 %rings.1 = (bf16[6,64,128]{2,1,0:T(8,128)(2,1)}, bf16[3,64,128]{2,1,0:T(8,128)(2,1)}, bf16[3,64,128]{2,1,0:T(8,128)(2,1)}, bf16[6,64,128]{2,1,0:T(8,128)(2,1)}, bf16[16,32,128]{2,1,0:T(8,128)(2,1)}) custom-call(bf16[12,64,1024]{2,1,0:T(8,128)(2,1)} %bitcast.19, bf16[1024,128]{1,0:T(8,128)(2,1)} %constant.33.clone.refs_1_.refs_9_, ...), custom_call_target="tpu_custom_call" | custom-call | tf_op jit(solution)/shard_map/rings/pallas_call | solution.py:127
  9.4 11.4 %all-to-all-start = ((bf16[16,32,128]{2,1,0:T(8,128)(2,1)}), bf16[16,32,128]{2,1,0:T(8,128)(2,1)S(1)}, u32[]{:S(2)}, u32[]{:S(2)}) async-start(bf16[16,32,128]{2,1,0:T(8,128)(2,1)} %get-tuple-element.36), calls=%async_computation | async-start | bytes 262144 | tf_op jit(solution)/shard_map/all_to_all | solution.py:523
  20.7 1.9 %collective-permute-start.5 = (bf16[3,64,128]{2,1,0:T(8,128)(2,1)}, bf16[3,64,128]{2,1,0:T(8,128)(2,1)S(1)}, u32[]{:S(2)}, u32[]{:S(2)}) collective-permute-start(bf16[3,64,128]{2,1,0:T(8,128)(2,1)} %get-tuple-element.34), channel_id=1, source_target_pairs={{0,8},{2,10},{4,12},{6,14},{8,0},{10,2},{12,4},{14,6},{16,24},{18,... | collective-permute-start | bytes 147464 | tf_op jit(solution)/shard_map/ppermute | solution.py:501
  23.6 4.3 %collective-permute-start.3 = (bf16[6,64,128]{2,1,0:T(8,128)(2,1)S(1)}, bf16[6,64,128]{2,1,0:T(8,128)(2,1)S(1)}, u32[]{:S(2)}, u32[]{:S(2)}) collective-permute-start(bf16[6,64,128]{2,1,0:T(8,128)(2,1)S(1)} %broadcast_select_fusion.1.refs_1_), channel_id=1, source_target_pairs={{8,2},{16,4},{14,26},{22,28},{2,8},{4,16},{26,14},{28,22},{0,24},{... | collective-permute-start | bytes 294920 | tf_op jit(solution)/shard_map/ppermute | solution.py:501
  27.9 3.3 %collective-permute-start.4 = (bf16[6,64,128]{2,1,0:T(8,128)(2,1)S(1)}, bf16[6,64,128]{2,1,0:T(8,128)(2,1)S(1)}, u32[]{:S(2)}, u32[]{:S(2)}) collective-permute-start(bf16[6,64,128]{2,1,0:T(8,128)(2,1)S(1)} %broadcast_select_fusion.1.refs_1_), channel_id=1, source_target_pairs={{8,26},{16,28},{14,2},{22,4},{2,14},{4,22},{26,8},{28,16},{0,30},{... | collective-permute-start | bytes 294920 | tf_op jit(solution)/shard_map/ppermute | solution.py:501
  31.3 2.2 %setup.1 = (s32[20,12]{1,0:T(8,128)}, bf16[192,384]{1,0:T(8,128)(2,1)}, bf16[192,384]{1,0:T(8,128)(2,1)}) custom-call(s32[3,4,12]{2,1,0:T(4,128)} %bitcast.28, s32[4,2,12]{2,1,0:T(2,128)} %bitcast.29, bf16[3,3,128,128]{3,2,1,0:T(8,128)(2,1)} %refs_2_.2), custom_call_target="tpu_custom_call" | custom-call | tf_op jit(solution)/shard_map/setup/pallas_call | solution.py:429
  33.6 3.0 %collective-permute-done.4.refs_4_ = bf16[6,64,128]{2,1,0:T(8,128)(2,1)S(1)} collective-permute-done((bf16[6,64,128]{2,1,0:T(8,128)(2,1)S(1)}, bf16[6,64,128]{2,1,0:T(8,128)(2,1)S(1)}, u32[]{:S(2)}, u32[]{:S(2)}) %collective-permute-start.4) | collective-permute-done | bytes 98336 | tf_op jit(solution)/shard_map/ppermute | solution.py:501
  37.3 2.6 %halo.2.refs_2_.refs_4_ = bf16[13,64,128]{2,1,0:T(8,128)(2,1)} custom-call(s32[20,12]{1,0:T(8,128)} %get-tuple-element.29.refs_0_, bf16[6,64,128]{2,1,0:T(8,128)(2,1)} %copy-done.12, bf16[6,64,128]{2,1,0:T(8,128)(2,1)} %copy-done.14, bf16[6,64,128]{2,1,0:T(8,128)(2,1)} %copy-done.15, bf16[6,64,128]{2,1,0:T(8,128)(2,1)} %copy-done.17, ...), custom_call_target="tpu_custom_call" | custom-call | tf_op jit(solution)/shard_map/halo/pallas_call | solution.py:191
  40.4 5.5 %collective-permute-done.7.refs_3_.refs_5_ = bf16[13,64,128]{2,1,0:T(8,128)(2,1)S(1)} collective-permute-done((bf16[13,64,128]{2,1,0:T(8,128)(2,1)}, bf16[13,64,128]{2,1,0:T(8,128)(2,1)S(1)}, u32[]{:S(2)}, u32[]{:S(2)}) %collective-permute-start.7) | collective-permute-done | bytes 213024 | tf_op jit(solution)/shard_map/ppermute | solution.py:442
  47.2 5.1 %forward.3 = (bf16[12,64,1024]{2,1,0:T(8,128)(2,1)}, bf16[4,64,1024]{2,1,0:T(8,128)(2,1)}, bf16[4,64,128]{2,1,0:T(8,128)(2,1)}, bf16[1,64,128]{2,1,0:T(8,128)(2,1)}) custom-call(bf16[12,64,1024]{2,1,0:T(8,128)(2,1)} %bitcast.20, bf16[12,64,1024]{2,1,0:T(8,128)(2,1)} %copy-done, bf16[13,64,128]{2,1,0:T(8,128)(2,1)} %halo.2.refs_2_.refs_4_, ...), custom_call_target="tpu_custom_call" | custom-call | tf_op jit(solution)/shard_map/forward/pallas_call | solution.py:303
  52.2 5.2 %forward.4 = (bf16[12,64,1024]{2,1,0:T(8,128)(2,1)}, bf16[4,64,1024]{2,1,0:T(8,128)(2,1)}, bf16[4,64,128]{2,1,0:T(8,128)(2,1)}, bf16[1,64,128]{2,1,0:T(8,128)(2,1)}) custom-call(bf16[12,64,1024]{2,1,0:T(8,128)(2,1)} %bitcast.21, bf16[12,64,1024]{2,1,0:T(8,128)(2,1)} %copy-done, ...), custom_call_target="tpu_custom_call", output_to_operand_aliasing={{0}: (13, {})} | custom-call | tf_op jit(solution)/shard_map/forward/pallas_call | solution.py:303
  57.4 5.7 %forward.5 = (bf16[12,64,1024]{2,1,0:T(8,128)(2,1)}, bf16[4,64,1024]{2,1,0:T(8,128)(2,1)}, bf16[6,64,128]{2,1,0:T(8,128)(2,1)}, bf16[3,64,128]{2,1,0:T(8,128)(2,...) custom-call(bf16[12,64,1024]{2,1,0:T(8,128)(2,1)} %bitcast.22, ...), custom_call_target="tpu_custom_call", output_to_operand_aliasing={{0}: (15, {})} | custom-call | tf_op jit(solution)/shard_map/forward/pallas_call | solution.py:303
  67.4 7.4 %all-to-all-start.1 = ((bf16[16,32,128]{2,1,0:T(8,128)(2,1)}), bf16[16,32,128]{2,1,0:T(8,128)(2,1)S(1)}, u32[]{:S(2)}, u32[]{:S(2)}) async-start(bf16[16,32,128]{2,1,0:T(8,128)(2,1)} %get-tuple-element.52), calls=%async_computation.1 | async-start | bytes 262144 | tf_op jit(solution)/shard_map/all_to_all | solution.py:523
  74.8 1.9 %collective-permute-start.13 = (bf16[3,64,128]{2,1,0:T(8,128)(2,1)}, bf16[3,64,128]{2,1,0:T(8,128)(2,1)S(1)}, u32[]{:S(2)}, u32[]{:S(2)}) collective-permute-start(bf16[3,64,128]{2,1,0:T(8,128)(2,1)} %get-tuple-element.50), channel_id=1, source_target_pairs={{0,8},{2,10},{4,12},{6,14},{8,0},{10,2},{12,4},{14,6},{16,24},{18,... | collective-permute-start | bytes 147464 | tf_op jit(solution)/shard_map/ppermute | solution.py:501
  77.7 3.1 %collective-permute-done.13.refs_6_ = bf16[3,64,128]{2,1,0:T(8,128)(2,1)S(1)} collective-permute-done((bf16[3,64,128]{2,1,0:T(8,128)(2,1)}, bf16[3,64,128]{2,1,0:T(8,128)(2,1)S(1)}, u32[]{:S(2)}, u32[]{:S(2)}) %collective-permute-start.13) | collective-permute-done | bytes 49184 | tf_op jit(solution)/shard_map/ppermute | solution.py:501
  82.2 5.7 %collective-permute-start.11 = (bf16[6,64,128]{2,1,0:T(8,128)(2,1)S(1)}, bf16[6,64,128]{2,1,0:T(8,128)(2,1)S(1)}, u32[]{:S(2)}, u32[]{:S(2)}) collective-permute-start(bf16[6,64,128]{2,1,0:T(8,128)(2,1)S(1)} %broadcast_select_fusion.refs_1_), channel_id=1, source_target_pairs={{8,2},{16,4},{14,26},{22,28},{2,8},{4,16},{26,14},{28,22},{0,24},{... | collective-permute-start | bytes 294920 | tf_op jit(solution)/shard_map/ppermute | solution.py:501
  87.9 2.4 %collective-permute-start.12 = (bf16[6,64,128]{2,1,0:T(8,128)(2,1)S(1)}, bf16[6,64,128]{2,1,0:T(8,128)(2,1)S(1)}, u32[]{:S(2)}, u32[]{:S(2)}) collective-permute-start(bf16[6,64,128]{2,1,0:T(8,128)(2,1)S(1)} %broadcast_select_fusion.refs_1_), channel_id=1, source_target_pairs={{8,26},{16,28},{14,2},{22,4},{2,14},{4,22},{26,8},{28,16},{0,30},{... | collective-permute-start | bytes 294920 | tf_op jit(solution)/shard_map/ppermute | solution.py:501
  91.2 5.4 %collective-permute-done.12.refs_4_ = bf16[6,64,128]{2,1,0:T(8,128)(2,1)S(1)} collective-permute-done((bf16[6,64,128]{2,1,0:T(8,128)(2,1)S(1)}, bf16[6,64,128]{2,1,0:T(8,128)(2,1)S(1)}, u32[]{:S(2)}, u32[]{:S(2)}) %collective-permute-start.12) | collective-permute-done | bytes 98336 | tf_op jit(solution)/shard_map/ppermute | solution.py:501
  97.8 2.6 %halo.3.refs_2_.refs_4_ = bf16[13,64,128]{2,1,0:T(8,128)(2,1)} custom-call(s32[20,12]{1,0:T(8,128)} %get-tuple-element.29.refs_0_, bf16[6,64,128]{2,1,0:T(8,128)(2,1)} %copy-done.13, bf16[6,64,128]{2,1,0:T(8,128)(2,1)} %copy-done.16, bf16[6,64,128]{2,1,0:T(8,128)(2,1)} %copy-done.18, bf16[6,64,128]{2,1,0:T(8,128)(2,1)} %copy-done.19, ...), custom_call_target="tpu_custom_call" | custom-call | tf_op jit(solution)/shard_map/halo/pallas_call | solution.py:191
  101.0 5.5 %collective-permute-done.15.refs_3_.refs_5_ = bf16[13,64,128]{2,1,0:T(8,128)(2,1)S(1)} collective-permute-done((bf16[13,64,128]{2,1,0:T(8,128)(2,1)}, bf16[13,64,128]{2,1,0:T(8,128)(2,1)S(1)}, u32[]{:S(2)}, u32[]{:S(2)}) %collective-permute-start.15) | collective-permute-done | bytes 213024 | tf_op jit(solution)/shard_map/ppermute | solution.py:442
  107.2 4.5 %backward.3.refs_8_ = bf16[12,64,1024]{2,1,0:T(8,128)(2,1)} custom-call(bf16[4,64,1024]{2,1,0:T(8,128)(2,1)} %get-tuple-element.55.refs_0_, bf16[4,64,1024]{2,1,0:T(8,128)(2,1)} %copy-done.9, bf16[13,64,128]{2,1,0:T(8,128)(2,1)} %halo.3.refs_2_.refs_4_, bf16[13,64,128]{2,1,0:T(8,128)(2,1)} %copy-done.2, bf16[13,64,128]{2,1,0:T(8,128)(2,1)} %halo.3.refs_2_.refs_4_, ...), custom_call_target="tpu_custom_call" | custom-call | tf_op jit(solution)/shard_map/backward/pallas_call | solution.py:332
  112.5 4.5 %backward.4.refs_8_ = bf16[12,64,1024]{2,1,0:T(8,128)(2,1)} custom-call(bf16[4,64,1024]{2,1,0:T(8,128)(2,1)} %get-tuple-element.54.refs_0_, bf16[4,64,1024]{2,1,0:T(8,128)(2,1)} %copy-done.8, bf16[13,64,128]{2,1,0:T(8,128)(2,1)} %halo.3.refs_2_.refs_4_, bf16[13,64,128]{2,1,0:T(8,128)(2,1)} %copy-done.2, ...), custom_call_target="tpu_custom_call", output_to_operand_aliasing={{}: (8, {})} | custom-call | tf_op jit(solution)/shard_map/backward/pallas_call | solution.py:332
  117.8 4.5 %backward.5 = bf16[12,64,1024]{2,1,0:T(8,128)(2,1)} custom-call(bf16[4,64,1024]{2,1,0:T(8,128)(2,1)} %get-tuple-element.45.refs_0_, bf16[4,64,1024]{2,1,0:T(8,128)(2,1)} %copy-done.7, bf16[13,64,128]{2,1,0:T(8,128)(2,1)} %halo.3.refs_2_.refs_4_, bf16[13,64,128]{2,1,0:T(8,128)(2,1)} %copy-done.2, ...), custom_call_target="tpu_custom_call", output_to_operand_aliasing={{}: (8, {})} | custom-call | tf_op jit(solution)/shard_map/backward/pallas_call | solution.py:332
  (77 shorter events, 16.8 us)
Async XLA Ops:
  0.6 45.3 %collective-permute-start = (bf16[12,64,1024]{2,1,0:T(8,128)(2,1)}, bf16[12,64,1024]{2,1,0:T(8,128)(2,1)S(1)}, u32[]{:S(2)}, u32[]{:S(2)}) collective-permute-start(bf16[12,64,1024]{2,1,0:T(8,128)(2,1)} %bitcast.18), channel_id=1, source_target_pairs={{1,0},{0,1},{3,2},{2,3},{5,4},{4,5},{7,6},{6,7},{9,8},{8,9},{11,10... | collective-permute-start | bytes 4718600 | tf_op jit(solution)/shard_map/ppermute | solution.py:442
  7.6 0.7 collective-permute-start.1
  8.3 28.3 %copy-start.10 = (bf16[6,64,128]{2,1,0:T(8,128)(2,1)}, bf16[6,64,128]{2,1,0:T(8,128)(2,1)S(1)}, u32[]{:S(2)}) copy-start(bf16[6,64,128]{2,1,0:T(8,128)(2,1)S(1)} %collective-permute-done.1.refs_5_) | copy-start | bytes 294916
  9.4 27.3 %copy-start.12 = (bf16[6,64,128]{2,1,0:T(8,128)(2,1)}, bf16[6,64,128]{2,1,0:T(8,128)(2,1)S(1)}, u32[]{:S(2)}) copy-start(bf16[6,64,128]{2,1,0:T(8,128)(2,1)S(1)} %broadcast_select_fusion.1.refs_1_) | copy-start | bytes 294916
  9.4 27.2 %all-to-all-start = ((bf16[16,32,128]{2,1,0:T(8,128)(2,1)}), bf16[16,32,128]{2,1,0:T(8,128)(2,1)S(1)}, u32[]{:S(2)}, u32[]{:S(2)}) async-start(bf16[16,32,128]{2,1,0:T(8,128)(2,1)} %get-tuple-element.36), calls=%async_computation | async-start | bytes 262144 | tf_op jit(solution)/shard_map/all_to_all | solution.py:523
  20.7 10.5 %collective-permute-start.5 = (bf16[3,64,128]{2,1,0:T(8,128)(2,1)}, bf16[3,64,128]{2,1,0:T(8,128)(2,1)S(1)}, u32[]{:S(2)}, u32[]{:S(2)}) collective-permute-start(bf16[3,64,128]{2,1,0:T(8,128)(2,1)} %get-tuple-element.34), channel_id=1, source_target_pairs={{0,8},{2,10},{4,12},{6,14},{8,0},{10,2},{12,4},{14,6},{16,24},{18,... | collective-permute-start | bytes 147464 | tf_op jit(solution)/shard_map/ppermute | solution.py:501
  22.7 10.9 %collective-permute-start.2 = (bf16[6,64,128]{2,1,0:T(8,128)(2,1)S(1)}, bf16[6,64,128]{2,1,0:T(8,128)(2,1)S(1)}, u32[]{:S(2)}, u32[]{:S(2)}) collective-permute-start(bf16[6,64,128]{2,1,0:T(8,128)(2,1)S(1)} %broadcast_select_fusion.1.refs_1_), channel_id=1, source_target_pairs={{8,14},{16,22},{14,8},{22,16},{2,26},{4,28},{26,2},{28,4},{0,6},{6... | collective-permute-start | bytes 294920 | tf_op jit(solution)/shard_map/ppermute | solution.py:501
  23.6 10.0 %collective-permute-start.3 = (bf16[6,64,128]{2,1,0:T(8,128)(2,1)S(1)}, bf16[6,64,128]{2,1,0:T(8,128)(2,1)S(1)}, u32[]{:S(2)}, u32[]{:S(2)}) collective-permute-start(bf16[6,64,128]{2,1,0:T(8,128)(2,1)S(1)} %broadcast_select_fusion.1.refs_1_), channel_id=1, source_target_pairs={{8,2},{16,4},{14,26},{22,28},{2,8},{4,16},{26,14},{28,22},{0,24},{... | collective-permute-start | bytes 294920 | tf_op jit(solution)/shard_map/ppermute | solution.py:501
  27.9 8.7 %collective-permute-start.4 = (bf16[6,64,128]{2,1,0:T(8,128)(2,1)S(1)}, bf16[6,64,128]{2,1,0:T(8,128)(2,1)S(1)}, u32[]{:S(2)}, u32[]{:S(2)}) collective-permute-start(bf16[6,64,128]{2,1,0:T(8,128)(2,1)S(1)} %broadcast_select_fusion.1.refs_1_), channel_id=1, source_target_pairs={{8,26},{16,28},{14,2},{22,4},{2,14},{4,22},{26,8},{28,16},{0,30},{... | collective-permute-start | bytes 294920 | tf_op jit(solution)/shard_map/ppermute | solution.py:501
  31.2 2.3 %collective-permute-start.6 = (bf16[3,64,128]{2,1,0:T(8,128)(2,1)}, bf16[3,64,128]{2,1,0:T(8,128)(2,1)S(1)}, u32[]{:S(2)}, u32[]{:S(2)}) collective-permute-start(bf16[3,64,128]{2,1,0:T(8,128)(2,1)} %get-tuple-element.35), channel_id=1, source_target_pairs={{0,2},{2,0},{4,6},{6,4},{8,10},{10,8},{12,14},{14,12},{16,18},{18,... | collective-permute-start | bytes 147464 | tf_op jit(solution)/shard_map/ppermute | solution.py:501
  39.9 6.1 %collective-permute-start.7 = (bf16[13,64,128]{2,1,0:T(8,128)(2,1)}, bf16[13,64,128]{2,1,0:T(8,128)(2,1)S(1)}, u32[]{:S(2)}, u32[]{:S(2)}) collective-permute-start(bf16[13,64,128]{2,1,0:T(8,128)(2,1)} %halo.2.refs_2_.refs_4_), channel_id=1, source_target_pairs={{1,0},{0,1},{3,2},{2,3},{5,4},{4,5},{7,6},{6,7},{9,8},{8,9},{11,10... | collective-permute-start | bytes 638984 | tf_op jit(solution)/shard_map/ppermute | solution.py:442
  63.1 3.3 %collective-permute-start.9 = (bf16[6,64,128]{2,1,0:T(8,128)(2,1)}, bf16[6,64,128]{2,1,0:T(8,128)(2,1)S(1)}, u32[]{:S(2)}, u32[]{:S(2)}) collective-permute-start(bf16[6,64,128]{2,1,0:T(8,128)(2,1)} %get-tuple-element.47), channel_id=1, source_target_pairs={{8,16},{16,8},{14,22},{22,14},{2,4},{4,2},{26,28},{28,26},{10,18},... | collective-permute-start | bytes 294920 | tf_op jit(solution)/shard_map/ppermute | solution.py:501
  63.8 37.2 %collective-permute-start.17 = (bf16[4,64,1024]{2,1,0:T(8,128)(2,1)S(1)}, bf16[4,64,1024]{2,1,0:T(8,128)(2,1)S(1)}, u32[]{:S(2)}, u32[]{:S(2)}) collective-permute-start(bf16[4,64,1024]{2,1,0:T(8,128)(2,1)S(1)} %copy-done.6), channel_id=1, source_target_pairs={{1,0},{0,1},{3,2},{2,3},{5,4},{4,5},{7,6},{6,7},{9,8},{8,9},{11,10... | collective-permute-start | bytes 1572872 | tf_op jit(solution)/shard_map/ppermute | solution.py:442
  64.4 47.3 %collective-permute-start.16 = (bf16[4,64,1024]{2,1,0:T(8,128)(2,1)S(1)}, bf16[4,64,1024]{2,1,0:T(8,128)(2,1)S(1)}, u32[]{:S(2)}, u32[]{:S(2)}) collective-permute-start(bf16[4,64,1024]{2,1,0:T(8,128)(2,1)S(1)} %copy-done.5), channel_id=1, source_target_pairs={{1,0},{0,1},{3,2},{2,3},{5,4},{4,5},{7,6},{6,7},{9,8},{8,9},{11,10... | collective-permute-start | bytes 1572872 | tf_op jit(solution)/shard_map/ppermute | solution.py:442
  65.9 51.2 %collective-permute-start.8 = (bf16[4,64,1024]{2,1,0:T(8,128)(2,1)}, bf16[4,64,1024]{2,1,0:T(8,128)(2,1)S(1)}, u32[]{:S(2)}, u32[]{:S(2)}) collective-permute-start(bf16[4,64,1024]{2,1,0:T(8,128)(2,1)} %get-tuple-element.45.refs_0_), channel_id=1, source_target_pairs={{1,0},{0,1},{3,2},{2,3},{5,4},{4,5},{7,6},{6,7},{9,8},{8,9},{11,10... | collective-permute-start | bytes 1572872 | tf_op jit(solution)/shard_map/ppermute | solution.py:442
  66.4 30.1 %copy-start.11 = (bf16[6,64,128]{2,1,0:T(8,128)(2,1)}, bf16[6,64,128]{2,1,0:T(8,128)(2,1)S(1)}, u32[]{:S(2)}) copy-start(bf16[6,64,128]{2,1,0:T(8,128)(2,1)S(1)} %collective-permute-done.9.refs_5_) | copy-start | bytes 294916
  67.4 29.1 %copy-start.13 = (bf16[6,64,128]{2,1,0:T(8,128)(2,1)}, bf16[6,64,128]{2,1,0:T(8,128)(2,1)S(1)}, u32[]{:S(2)}) copy-start(bf16[6,64,128]{2,1,0:T(8,128)(2,1)S(1)} %broadcast_select_fusion.refs_1_) | copy-start | bytes 294916
  67.4 29.1 %all-to-all-start.1 = ((bf16[16,32,128]{2,1,0:T(8,128)(2,1)}), bf16[16,32,128]{2,1,0:T(8,128)(2,1)S(1)}, u32[]{:S(2)}, u32[]{:S(2)}) async-start(bf16[16,32,128]{2,1,0:T(8,128)(2,1)} %get-tuple-element.52), calls=%async_computation.1 | async-start | bytes 262144 | tf_op jit(solution)/shard_map/all_to_all | solution.py:523
  74.8 6.0 %collective-permute-start.13 = (bf16[3,64,128]{2,1,0:T(8,128)(2,1)}, bf16[3,64,128]{2,1,0:T(8,128)(2,1)S(1)}, u32[]{:S(2)}, u32[]{:S(2)}) collective-permute-start(bf16[3,64,128]{2,1,0:T(8,128)(2,1)} %get-tuple-element.50), channel_id=1, source_target_pairs={{0,8},{2,10},{4,12},{6,14},{8,0},{10,2},{12,4},{14,6},{16,24},{18,... | collective-permute-start | bytes 147464 | tf_op jit(solution)/shard_map/ppermute | solution.py:501
  76.7 11.2 %collective-permute-start.10 = (bf16[6,64,128]{2,1,0:T(8,128)(2,1)S(1)}, bf16[6,64,128]{2,1,0:T(8,128)(2,1)S(1)}, u32[]{:S(2)}, u32[]{:S(2)}) collective-permute-start(bf16[6,64,128]{2,1,0:T(8,128)(2,1)S(1)} %broadcast_select_fusion.refs_1_), channel_id=1, source_target_pairs={{8,14},{16,22},{14,8},{22,16},{2,26},{4,28},{26,2},{28,4},{0,6},{6... | collective-permute-start | bytes 294920 | tf_op jit(solution)/shard_map/ppermute | solution.py:501
  80.8 1.4 %collective-permute-start.14 = (bf16[3,64,128]{2,1,0:T(8,128)(2,1)}, bf16[3,64,128]{2,1,0:T(8,128)(2,1)S(1)}, u32[]{:S(2)}, u32[]{:S(2)}) collective-permute-start(bf16[3,64,128]{2,1,0:T(8,128)(2,1)} %get-tuple-element.51), channel_id=1, source_target_pairs={{0,2},{2,0},{4,6},{6,4},{8,10},{10,8},{12,14},{14,12},{16,18},{18,... | collective-permute-start | bytes 147464 | tf_op jit(solution)/shard_map/ppermute | solution.py:501
  82.2 9.0 %collective-permute-start.11 = (bf16[6,64,128]{2,1,0:T(8,128)(2,1)S(1)}, bf16[6,64,128]{2,1,0:T(8,128)(2,1)S(1)}, u32[]{:S(2)}, u32[]{:S(2)}) collective-permute-start(bf16[6,64,128]{2,1,0:T(8,128)(2,1)S(1)} %broadcast_select_fusion.refs_1_), channel_id=1, source_target_pairs={{8,2},{16,4},{14,26},{22,28},{2,8},{4,16},{26,14},{28,22},{0,24},{... | collective-permute-start | bytes 294920 | tf_op jit(solution)/shard_map/ppermute | solution.py:501
  87.9 8.6 %collective-permute-start.12 = (bf16[6,64,128]{2,1,0:T(8,128)(2,1)S(1)}, bf16[6,64,128]{2,1,0:T(8,128)(2,1)S(1)}, u32[]{:S(2)}, u32[]{:S(2)}) collective-permute-start(bf16[6,64,128]{2,1,0:T(8,128)(2,1)S(1)} %broadcast_select_fusion.refs_1_), channel_id=1, source_target_pairs={{8,26},{16,28},{14,2},{22,4},{2,14},{4,22},{26,8},{28,16},{0,30},{... | collective-permute-start | bytes 294920 | tf_op jit(solution)/shard_map/ppermute | solution.py:501
  100.4 6.1 %collective-permute-start.15 = (bf16[13,64,128]{2,1,0:T(8,128)(2,1)}, bf16[13,64,128]{2,1,0:T(8,128)(2,1)S(1)}, u32[]{:S(2)}, u32[]{:S(2)}) collective-permute-start(bf16[13,64,128]{2,1,0:T(8,128)(2,1)} %halo.3.refs_2_.refs_4_), channel_id=1, source_target_pairs={{1,0},{0,1},{3,2},{2,3},{5,4},{4,5},{7,6},{6,7},{9,8},{8,9},{11,10... | collective-permute-start | bytes 638984 | tf_op jit(solution)/shard_map/ppermute | solution.py:442
  (20 other events, 84.6 us)

commit v5 on v4

--- a/solution.py
+++ b/solution.py
@@ -9,6 +9,7 @@
 RB = 32
 GROUP = 4
 LANES = 128
+CALLS = (3,)
 VMEM_LIMIT = 60 * 1024 * 1024
 STRIP_LANE = (96, 0, 32, 64)
 
@@ -57,11 +58,13 @@
 
 
 def side_tiles(fields, first_face, ring_ref, cornsel_ref):
-    chan = fields[0].shape[0]
+    chan = fields.shape[0] // GROUP
     lane = lane_iota((chan, LANES))
-    rings = [
-        jnp.dot(field, ring_ref[...], preferred_element_type=jnp.float32) for field in fields
-    ]
+    flat = jnp.dot(fields, ring_ref[...], preferred_element_type=jnp.float32)
+    picked = jnp.dot(
+        flat.astype(jnp.bfloat16), cornsel_ref[...], preferred_element_type=jnp.float32
+    )
+    rings = [flat[g * chan : (g + 1) * chan] for g in range(GROUP)]
     tiles = []
     for side in range(4):
         tile = jnp.zeros((chan, LANES), jnp.float32)
@@ -70,11 +73,8 @@
             tile = jnp.where(lane // 32 == g, moved, tile)
         tiles.append(tile.astype(jnp.bfloat16))
     corners = jnp.zeros((chan, LANES), jnp.float32)
-    for g, ring in enumerate(rings):
-        picked = jnp.dot(
-            ring.astype(jnp.bfloat16), cornsel_ref[...], preferred_element_type=jnp.float32
-        )
-        corners += pltpu.roll(picked, (first_face + g) * 4, 1)
+    for g in range(GROUP):
+        corners += pltpu.roll(picked[g * chan : (g + 1) * chan], (first_face + g) * 4, 1)
     return (tiles, corners)
 
 
@@ -99,7 +99,7 @@
 def rings_kernel(steps, plan, field_ref, ring_ref, cornsel_ref, *refs):
     outs, (packs, corner_acc) = (refs[:-2], refs[-2:])
     step = pl.program_id(0)
-    fields = [field_ref[g] for g in range(GROUP)]
+    fields = field_ref[...].reshape(-1, field_ref.shape[2])
     tiles, corners = side_tiles(fields, step * GROUP, ring_ref, cornsel_ref)
     for side, tile in enumerate(tiles):
         packs[side * steps + step] = tile
@@ -202,26 +202,32 @@
     )(table, *tiles, rev)
 
 
-def conv_face(g, step, field_refs, halo_refs, corner_refs, taps_ref, spread_ref, stack_ref):
+def sides_of(step, halo_refs, corner_refs, spread_ref, beside_ref):
+    corners = jnp.concatenate([ref[0].astype(jnp.float32) for ref in corner_refs], axis=0)
+    lane = lane_iota(corners.shape)
+    sides = []
+    for g in range(GROUP):
+        halo = jnp.concatenate([ref[g].astype(jnp.float32) for ref in halo_refs], axis=0)
+        moved = pltpu.roll(corners, (LANES - (step * GROUP + g) * 4) % LANES, 1)
+        sides.append(jnp.where(lane < 4, moved, halo).astype(jnp.bfloat16))
+    beside = jnp.dot(
+        jnp.concatenate(sides, axis=0), spread_ref[...], preferred_element_type=jnp.float32
+    )
+    beside_ref[...] = beside.astype(jnp.bfloat16).reshape(beside_ref.shape)
+
+
+def conv_face(g, field_refs, halo_refs, taps_ref, beside_ref, stack_ref):
     chan, tile = field_refs[0].shape[1:]
-    pieces = len(field_refs)
-    total = chan * pieces
+    total = chan * len(field_refs)
     width = tile + LANES
-    for k in range(pieces):
-        stack_ref[total + k * chan : total + (k + 1) * chan, :tile] = field_refs[k][g]
-        stack_ref[total + k * chan : total + (k + 1) * chan, tile:] = halo_refs[k][g]
-    halo = stack_ref[total : 2 * total, tile:].astype(jnp.float32)
-    corners = jnp.concatenate([ref[0].astype(jnp.float32) for ref in corner_refs], axis=0)
-    corners = pltpu.roll(corners, (LANES - (step * GROUP + g) * 4) % LANES, 1)
-    lane = lane_iota((total, LANES))
-    sides = jnp.where(lane < 4, corners, halo).astype(jnp.bfloat16)
-    beside = jnp.dot(sides, spread_ref[...], preferred_element_type=jnp.float32)
-    middle = stack_ref[total : 2 * total].astype(jnp.float32)
+    for k, (field, halo) in enumerate(zip(field_refs, halo_refs)):
+        stack_ref[total + k * chan : total + (k + 1) * chan, :tile] = field[g]
+        stack_ref[total + k * chan : total + (k + 1) * chan, tile:] = halo[g]
+    middle = stack_ref[total : 2 * total]
+    beside = beside_ref[g]
     col = lane_iota((total, width)) % RB
-    stack_ref[:total] = jnp.where(col == 0, beside, pltpu.roll(middle, 1, 1)).astype(jnp.bfloat16)
-    stack_ref[2 * total :] = jnp.where(
-        col == RB - 1, beside, pltpu.roll(middle, width - 1, 1)
-    ).astype(jnp.bfloat16)
+    stack_ref[:total] = jnp.where(col == 0, beside, pltpu.roll(middle, 1, 1))
+    stack_ref[2 * total :] = jnp.where(col == RB - 1, beside, pltpu.roll(middle, width - 1, 1))
     sums = jnp.dot(taps_ref[...], stack_ref[...], preferred_element_type=jnp.float32)
     above = pltpu.roll(sums[:chan], RB, 1)
     below = pltpu.roll(sums[2 * chan :], width - RB, 1)
@@ -236,109 +242,126 @@
     return (*out, refs)
 
 
-def forward_kernel(step, steps, pieces, plan, *refs):
-    before = step
-    fields, halos, corners, consts, old, refs = split_refs(
-        refs, pieces, pieces, pieces, 5, 2 * before + (step > 0)
-    )
+def forward_kernel(first, count, steps, pieces, plan, *refs):
+    olds = 3 if first else 0
+    fields, halos, corners, consts, old, refs = split_refs(refs, pieces, pieces, pieces, 5, olds)
     cot_ref, taps_ref, spread_ref, ring_ref, cornsel_ref = consts
-    act_ref, gated_ref = refs[:2]
-    made = []
+    outs, (packs, corner_acc, made, beside_ref, stacks) = (refs[:-5], refs[-5:])
+    act_ref, gated_ref = outs[:2]
+    here = pl.program_id(0)
+    step = first + here
+
+    @pl.when(here == 0)
+    def _():
+        if first:
+            packs[...] = old[0][...]
+            corner_acc[...] = old[1][0].astype(jnp.float32)
+        else:
+            corner_acc[...] = jnp.zeros_like(corner_acc)
+
+    sides_of(step, halos, corners, spread_ref, beside_ref)
+    chan = act_ref.shape[1]
     for g in range(GROUP):
-        pre = conv_face(g, step, fields, halos, corners, taps_ref, spread_ref, refs[-1])
+        pre = conv_face(g, fields, halos, taps_ref, beside_ref, stacks.at[g % 2])
         sig = 1.0 / (1.0 + jnp.exp(-pre))
         act_ref[g] = (pre * sig).astype(jnp.bfloat16)
         gated = cot_ref[g].astype(jnp.float32) * sig * (1.0 + pre * (1.0 - sig))
         gated_ref[g] = gated.astype(jnp.bfloat16)
-        made.append(gated.astype(jnp.bfloat16))
-    tiles, corner = side_tiles(made, step * GROUP, ring_ref, cornsel_ref)
-    if step < steps - 1:
-        for side, tile in enumerate(tiles):
-            refs[2][side] = tile
-        refs[3][0] = corner.astype(jnp.bfloat16)
-        return
-    packs = refs[-2]
-    for side in range(4):
-        for q in range(before):
-            packs[side * steps + q] = old[2 * q][side]
-        packs[side * steps + step] = tiles[side]
-    for q in range(before):
-        corner += old[2 * q + 1][0].astype(jnp.float32)
-    hand_out(plan, steps, packs, corner, refs[2:-2])
-
-
-def conv_specs(fields, halos, step, own_blocks):
+        made[g * chan : (g + 1) * chan] = gated.astype(jnp.bfloat16)
+    tiles, corner = side_tiles(made[...], step * GROUP, ring_ref, cornsel_ref)
+    for side, tile in enumerate(tiles):
+        packs[side * steps + step] = tile
+    corner_acc[...] += corner
+
+    @pl.when(here == count - 1)
+    def _():
+        if first + count == steps:
+            hand_out(plan, steps, packs, corner_acc[...], outs[2:])
+        else:
+            outs[2][...] = packs[...]
+            outs[3][0] = corner_acc[...].astype(jnp.bfloat16)
+
+
+def conv_specs(fields, halos, first, field_first):
     _, chan, tile = fields[0].shape
     last = halos[0].shape[0] - 1
-    field = 0 if own_blocks else step
     return (
-        [pl.BlockSpec((GROUP, chan, tile), lambda i: (field, 0, 0)) for _ in fields]
-        + [pl.BlockSpec((GROUP, chan, LANES), lambda i: (step, 0, 0)) for _ in halos]
+        [pl.BlockSpec((GROUP, chan, tile), lambda i: (field_first + i, 0, 0)) for _ in fields]
+        + [pl.BlockSpec((GROUP, chan, LANES), lambda i: (first + i, 0, 0)) for _ in halos]
         + [pl.BlockSpec((1, chan, LANES), lambda i: (last, 0, 0)) for _ in halos]
     )
 
 
-def stack_scratch(chan, pieces, tile):
-    return pltpu.VMEM((3 * chan * pieces, tile + LANES), jnp.bfloat16)
-
-
-def forward(step, plan, fields, halos, cot, taps, spread, ring, cornsel, act, old):
+def conv_scratch(chan, pieces, tile):
+    total = chan * pieces
+    return [
+        pltpu.VMEM((GROUP, total, tile + LANES), jnp.bfloat16),
+        pltpu.VMEM((2, 3 * total, tile + LANES), jnp.bfloat16),
+    ]
+
+
+def forward(first, count, plan, fields, halos, cot, taps, spread, ring, cornsel, old):
     faces, chan, tile = fields[0].shape
     steps = faces // GROUP
     pieces = len(fields)
-    if step < steps - 1:
+    if first + count < steps:
         outs = [
-            jax.ShapeDtypeStruct((4, chan, LANES), jnp.bfloat16),
+            jax.ShapeDtypeStruct((4 * steps, chan, LANES), jnp.bfloat16),
             jax.ShapeDtypeStruct((1, chan, LANES), jnp.bfloat16),
         ]
-        scratch = []
     else:
         outs = ring_outs(faces, chan, plan)
-        scratch = [pltpu.VMEM((4 * steps, chan, LANES), jnp.bfloat16)]
     whole = jax.ShapeDtypeStruct((faces, chan, tile), jnp.bfloat16)
-    chunk = jax.ShapeDtypeStruct((GROUP, chan, tile), jnp.bfloat16)
-    block = pl.BlockSpec((GROUP, chan, tile), lambda i: (step, 0, 0))
-    aside = [] if act is None else [act]
-    args = [*fields, *halos, *halos, cot, taps, spread, ring, cornsel, *old, *aside]
+    chunk = jax.ShapeDtypeStruct((count * GROUP, chan, tile), jnp.bfloat16)
+    block = pl.BlockSpec((GROUP, chan, tile), lambda i: (first + i, 0, 0))
+    args = [*fields, *halos, *halos, cot, taps, spread, ring, cornsel, *old]
     return pl.pallas_call(
-        lambda *refs: forward_kernel(step, steps, pieces, plan, *refs),
-        grid=(1,),
-        in_specs=conv_specs(fields, halos, step, False)
+        lambda *refs: forward_kernel(first, count, steps, pieces, plan, *refs),
+        grid=(count,),
+        in_specs=conv_specs(fields, halos, first, first)
         + [block, whole_spec(taps), whole_spec(spread), whole_spec(ring), whole_spec(cornsel)]
-        + [whole_spec(array) for array in old]
-        + [pl.BlockSpec(memory_space=pl.ANY) for _ in aside],
-        out_specs=[block, whole_spec(chunk)] + [whole_spec(o) for o in outs],
+        + [whole_spec(array) for array in old[:2]]
+        + [pl.BlockSpec(memory_space=pl.ANY) for _ in old[2:]],
+        out_specs=[block, pl.BlockSpec((GROUP, chan, tile), lambda i: (i, 0, 0))]
+        + [whole_spec(o) for o in outs],
         out_shape=[whole, chunk] + outs,
-        input_output_aliases={len(args) - 1: 0} if aside else {},
-        scratch_shapes=scratch + [stack_scratch(chan, pieces, tile)],
+        input_output_aliases={len(args) - 1: 0} if old else {},
+        scratch_shapes=[
+            pltpu.VMEM((4 * steps, chan, LANES), jnp.bfloat16),
+            pltpu.VMEM((chan, LANES), jnp.float32),
+            pltpu.VMEM((GROUP * chan, tile), jnp.bfloat16),
+        ]
+        + conv_scratch(chan, pieces, tile),
         compiler_params=pltpu.CompilerParams(vmem_limit_bytes=VMEM_LIMIT),
         name="forward",
     )(*args)
 
 
-def backward_kernel(step, pieces, *refs):
+def backward_kernel(first, pieces, *refs):
     fields, halos, corners, consts, refs = split_refs(refs, pieces, pieces, pieces, 2)
-    grad_ref, stack_ref = refs[-2:]
+    taps_ref, spread_ref = consts
+    grad_ref, beside_ref, stacks = refs[-3:]
+    sides_of(first + pl.program_id(0), halos, corners, spread_ref, beside_ref)
     for g in range(GROUP):
-        total = conv_face(g, step, fields, halos, corners, *consts, stack_ref)
+        total = conv_face(g, fields, halos, taps_ref, beside_ref, stacks.at[g % 2])
         grad_ref[g] = total.astype(jnp.bfloat16)
 
 
-def backward(step, faces, fields, halos, taps, spread, grad):
-    _, chan, tile = fields[0].shape
+def backward(first, faces, fields, halos, taps, spread, grad):
+    held, chan, tile = fields[0].shape
     pieces = len(fields)
     aside = [] if grad is None else [grad]
     args = [*fields, *halos, *halos, taps, spread, *aside]
     return pl.pallas_call(
-        lambda *refs: backward_kernel(step, pieces, *refs),
-        grid=(1,),
-        in_specs=conv_specs(fields, halos, step, True)
+        lambda *refs: backward_kernel(first, pieces, *refs),
+        grid=(held // GROUP,),
+        in_specs=conv_specs(fields, halos, first, 0)
         + [whole_spec(taps), whole_spec(spread)]
         + [pl.BlockSpec(memory_space=pl.ANY) for _ in aside],
-        out_specs=pl.BlockSpec((GROUP, chan, tile), lambda i: (step, 0, 0)),
+        out_specs=pl.BlockSpec((GROUP, chan, tile), lambda i: (first + i, 0, 0)),
         out_shape=jax.ShapeDtypeStruct((faces, chan, tile), jnp.bfloat16),
         input_output_aliases={len(args) - 1: 0} if aside else {},
-        scratch_shapes=[stack_scratch(chan, pieces, tile)],
+        scratch_shapes=conv_scratch(chan, pieces, tile),
         compiler_params=pltpu.CompilerParams(vmem_limit_bytes=VMEM_LIMIT),
         name="backward",
     )(*args)
@@ -519,7 +542,7 @@
             if j == 1:
                 pairs += [((x, y), (x, 3 - y)) for x in (1, 2) for y in (1, 2)]
             across.append(swap(lines, pairs))
-        corner, lines = lax.optimization_barrier((corner, lines))
+        corner, across[0] = lax.optimization_barrier((corner, across[0]))
         ends_of = lax.all_to_all(corner, axes, 0, 0, tiled=True)
         return [lines, *across, paired, near_col, near_row, ends_of]
 
@@ -636,20 +659,21 @@
     tiles = plan.exchange(*parts)
     halo = assemble_halo(plan, table, tiles, rev, faces, units, unit)
     halos = from_others(halo, ch_count)
-    act, old, chunks = (None, [], [])
-    for step in range(faces // GROUP):
+    old, chunks, first = ([], [], 0)
+    for count in CALLS:
         act, gated, *parts = forward(
-            step, plan, fields, halos, cot, taps, spread, ring, cornsel, act, old
+            first, count, plan, fields, halos, cot, taps, spread, ring, cornsel, old
         )
-        old = old + parts
-        chunks.append(from_others(gated, ch_count))
+        old = [*parts, act]
+        chunks.append((first, from_others(gated, ch_count)))
+        first += count
 
     tiles = plan.exchange(*parts)
     halo = assemble_halo(plan, table, tiles, rev, faces, units, unit)
     halos = from_others(halo, ch_count)
     grad = None
-    for step, fields in enumerate(chunks):
-        grad = backward(step, faces, fields, halos, back_taps, spread, grad)
+    for first, fields in chunks:
+        grad = backward(first, faces, fields, halos, back_taps, spread, grad)
 
     shape = (chan, faces, 1, 1, tile)
     return (

time: 123 us -> 115 us (0.935)
  Pallas kernels: 40.9 us -> 28.2 us
  waiting for transfers between devices: 24.9 us -> 28.4 us
  starting transfers between devices: 48.1 us -> 50.9 us
    pallas_call x6 -> x2, Pallas kernels: 29.5 us -> 16.7 us  [the longest x1 9.43 us: forward(): pl.pallas_call(lambda *refs: forward_kernel(first, count, steps, pieces,...]
    all_to_all x2, starting transfers between devices: 18.7 us -> 25.4 us  [exchange(): ends_of = lax.all_to_all(corner, axes, 0, 0, tiled=True)]
    ppermute x12, waiting for transfers between devices: 13.8 us -> 18.3 us  [exchange(): lax.ppermute(array, axes, [(a[0] * 4 + a[1], b[0] * 4 + b[1]) for a, b in...]
    ppermute x12, starting transfers between devices: 22.7 us -> 19.9 us  [exchange(): lax.ppermute(array, axes, [(a[0] * 4 + a[1], b[0] * 4 + b[1]) for a, b in...]
    unnamed x48 -> x40, local copies, waits for them, and re-layouts: 5.43 us -> 4.35 us
    ppermute x6 -> x4, starting transfers between devices: 6.69 us -> 5.64 us  [from_others(): lax.ppermute(array, 'ch', [((i + k) % ch_count, i) for i in range(ch_coun...]
    ppermute x6 -> x4, waiting for transfers between devices: 11.1 us -> 10.1 us  [from_others(): lax.ppermute(array, 'ch', [((i + k) % ch_count, i) for i in range(ch_coun...]
  transfers between devices with their start and end apart: 20 -> 18, of which waited for: 7 -> 8; matrix products, arithmetic and copies ran while one was open for 2% -> 2% of each run, Pallas kernels for 17% -> 10%
where the time goes in v5:
time: 115 us
  starting transfers between devices  50.9 us (44%)
  waiting for transfers between devices  28.4 us (25%)
  Pallas kernels  28.2 us (25%)
  local copies, waits for them, and re-layouts  4.35 us (4%)
  other arithmetic  2.03 us (2%)
    all_to_all x2, starting transfers between devices, exchange(): ends_of = lax.all_to_all(corner, axes, 0, 0, tiled=True)  25.4 us
    ppermute x12, starting transfers between devices, exchange(): lax.ppermute(array, axes, [(a[0] * 4 + a[1], b[0] * 4 + b[1]) for a, b in...  19.9 us
    ppermute x12, waiting for transfers between devices, exchange(): lax.ppermute(array, axes, [(a[0] * 4 + a[1], b[0] * 4 + b[1]) for a, b in...  18.3 us
    ppermute x4, waiting for transfers between devices, from_others(): lax.ppermute(array, 'ch', [((i + k) % ch_count, i) for i in range(ch_coun...  10.1 us
    pallas_call x1, Pallas kernels, forward(): pl.pallas_call(lambda *refs: forward_kernel(first, count, steps, pieces,...  9.43 us
    pallas_call x1, Pallas kernels, backward(): pl.pallas_call(lambda *refs: backward_kernel(first, pieces, *refs), grid=...  7.3 us
    ppermute x4, starting transfers between devices, from_others(): lax.ppermute(array, 'ch', [((i + k) % ch_count, i) for i in range(ch_coun...  5.64 us
    pallas_call x2, Pallas kernels, assemble_halo(): pl.pallas_call(lambda *refs: halo_kernel(faces, units, unit, plan, *refs)...  5.2 us
  transfers between devices with their start and end apart: 18, of which 8 were waited for; matrix products, arithmetic and copies ran while one was open for 2% of the time, Pallas kernels for 10%

profile of v5, /device:TPU:0, one launch (start us, length us, event | category | flops | bytes accessed | tf_op | source)
XLA Modules:
  0.0 114.8 jit_solution(15077329210974090664)
XLA Ops:
  0.6 3.0 %collective-permute-start = (bf16[12,64,1024]{2,1,0:T(8,128)(2,1)}, bf16[12,64,1024]{2,1,0:T(8,128)(2,1)S(1)}, u32[]{:S(2)}, u32[]{:S(2)}) collective-permute-start(bf16[12,64,1024]{2,1,0:T(8,128)(2,1)} %bitcast.18), channel_id=1, source_target_pairs={{1,0},{0,1},{3,2},{2,3},{5,4},{4,5},{7,6},{6,7},{9,8},{8,9},{11,10... | collective-permute-start | bytes 4718600 | tf_op jit(solution)/shard_map/ppermute | solution.py:465
  3.6 4.0 %rings.1 = (bf16[6,64,128]{2,1,0:T(8,128)(2,1)}, bf16[3,64,128]{2,1,0:T(8,128)(2,1)}, bf16[3,64,128]{2,1,0:T(8,128)(2,1)}, bf16[6,64,128]{2,1,0:T(8,128)(2,1)}, bf16[16,32,128]{2,1,0:T(8,128)(2,1)}) custom-call(bf16[12,64,1024]{2,1,0:T(8,128)(2,1)} %bitcast.19, bf16[1024,128]{1,0:T(8,128)(2,1)} %constant.33.clone.refs_1_.refs_9_, ...), custom_call_target="tpu_custom_call" | custom-call | tf_op jit(solution)/shard_map/rings/pallas_call | solution.py:127
  8.4 1.0 broadcast_select_fusion.1.refs_1_
  10.1 4.2 %collective-permute-done.2.refs_2_ = bf16[6,64,128]{2,1,0:T(8,128)(2,1)S(1)} collective-permute-done((bf16[6,64,128]{2,1,0:T(8,128)(2,1)S(1)}, bf16[6,64,128]{2,1,0:T(8,128)(2,1)S(1)}, u32[]{:S(2)}, u32[]{:S(2)}) %collective-permute-start.2) | collective-permute-done | bytes 98336 | tf_op jit(solution)/shard_map/ppermute | solution.py:524
  14.3 13.4 %all-to-all-start = ((bf16[16,32,128]{2,1,0:T(8,128)(2,1)}), bf16[16,32,128]{2,1,0:T(8,128)(2,1)S(1)}, u32[]{:S(2)}, u32[]{:S(2)}) async-start(bf16[16,32,128]{2,1,0:T(8,128)(2,1)} %get-tuple-element.28), calls=%async_computation | async-start | bytes 262144 | tf_op jit(solution)/shard_map/all_to_all | solution.py:546
  27.7 6.3 %collective-permute-start.4 = (bf16[6,64,128]{2,1,0:T(8,128)(2,1)S(1)}, bf16[6,64,128]{2,1,0:T(8,128)(2,1)S(1)}, u32[]{:S(2)}, u32[]{:S(2)}) collective-permute-start(bf16[6,64,128]{2,1,0:T(8,128)(2,1)S(1)} %broadcast_select_fusion.1.refs_1_), channel_id=1, source_target_pairs={{8,26},{16,28},{14,2},{22,4},{2,14},{4,22},{26,8},{28,16},{0,30},{... | collective-permute-start | bytes 294920 | tf_op jit(solution)/shard_map/ppermute | solution.py:524
  34.0 2.5 %collective-permute-start.3 = (bf16[6,64,128]{2,1,0:T(8,128)(2,1)S(1)}, bf16[6,64,128]{2,1,0:T(8,128)(2,1)S(1)}, u32[]{:S(2)}, u32[]{:S(2)}) collective-permute-start(bf16[6,64,128]{2,1,0:T(8,128)(2,1)S(1)} %broadcast_select_fusion.1.refs_1_), channel_id=1, source_target_pairs={{8,2},{16,4},{14,26},{22,28},{2,8},{4,16},{26,14},{28,22},{0,24},{... | collective-permute-start | bytes 294920 | tf_op jit(solution)/shard_map/ppermute | solution.py:524
  36.6 2.2 %setup.1 = (s32[20,12]{1,0:T(8,128)}, bf16[192,384]{1,0:T(8,128)(2,1)}, bf16[192,384]{1,0:T(8,128)(2,1)}) custom-call(s32[3,4,12]{2,1,0:T(4,128)} %bitcast.23, s32[4,2,12]{2,1,0:T(2,128)} %bitcast.24, bf16[3,3,128,128]{3,2,1,0:T(8,128)(2,1)} %refs_2_.2), custom_call_target="tpu_custom_call" | custom-call | tf_op jit(solution)/shard_map/setup/pallas_call | solution.py:452
  38.9 2.2 %collective-permute-done.5.refs_6_ = bf16[3,64,128]{2,1,0:T(8,128)(2,1)S(1)} collective-permute-done((bf16[3,64,128]{2,1,0:T(8,128)(2,1)}, bf16[3,64,128]{2,1,0:T(8,128)(2,1)S(1)}, u32[]{:S(2)}, u32[]{:S(2)}) %collective-permute-start.5) | collective-permute-done | bytes 49184 | tf_op jit(solution)/shard_map/ppermute | solution.py:524
  41.1 1.2 %collective-permute-done.3.refs_3_ = bf16[6,64,128]{2,1,0:T(8,128)(2,1)S(1)} collective-permute-done((bf16[6,64,128]{2,1,0:T(8,128)(2,1)S(1)}, bf16[6,64,128]{2,1,0:T(8,128)(2,1)S(1)}, u32[]{:S(2)}, u32[]{:S(2)}) %collective-permute-start.3) | collective-permute-done | bytes 98336 | tf_op jit(solution)/shard_map/ppermute | solution.py:524
  43.0 2.6 %halo.2.refs_2_.refs_4_ = bf16[13,64,128]{2,1,0:T(8,128)(2,1)} custom-call(s32[20,12]{1,0:T(8,128)} %get-tuple-element.21.refs_0_, bf16[6,64,128]{2,1,0:T(8,128)(2,1)} %copy-done.8, bf16[6,64,128]{2,1,0:T(8,128)(2,1)} %copy-done.10, bf16[6,64,128]{2,1,0:T(8,128)(2,1)} %copy-done.13, bf16[6,64,128]{2,1,0:T(8,128)(2,1)} %copy-done.12, ...), custom_call_target="tpu_custom_call" | custom-call | tf_op jit(solution)/shard_map/halo/pallas_call | solution.py:191
  46.2 5.5 %collective-permute-done.7.refs_3_.refs_5_ = bf16[13,64,128]{2,1,0:T(8,128)(2,1)S(1)} collective-permute-done((bf16[13,64,128]{2,1,0:T(8,128)(2,1)}, bf16[13,64,128]{2,1,0:T(8,128)(2,1)S(1)}, u32[]{:S(2)}, u32[]{:S(2)}) %collective-permute-start.7) | collective-permute-done | bytes 213024 | tf_op jit(solution)/shard_map/ppermute | solution.py:465
  52.9 9.4 %forward.1 = (bf16[12,64,1024]{2,1,0:T(8,128)(2,1)}, bf16[12,64,1024]{2,1,0:T(8,128)(2,1)}, bf16[6,64,128]{2,1,0:T(8,128)(2,1)}, bf16[3,64,128]{2,1,0:T(8,128)(2...) custom-call(bf16[12,64,1024]{2,1,0:T(8,128)(2,1)} %bitcast.20, ...), custom_call_target="tpu_custom_call" | custom-call | tf_op jit(solution)/shard_map/forward/pallas_call | solution.py:318
  63.6 1.0 broadcast_select_fusion.refs_1_
  64.7 5.1 %collective-permute-done.10.refs_2_ = bf16[6,64,128]{2,1,0:T(8,128)(2,1)S(1)} collective-permute-done((bf16[6,64,128]{2,1,0:T(8,128)(2,1)S(1)}, bf16[6,64,128]{2,1,0:T(8,128)(2,1)S(1)}, u32[]{:S(2)}, u32[]{:S(2)}) %collective-permute-start.10) | collective-permute-done | bytes 98336 | tf_op jit(solution)/shard_map/ppermute | solution.py:524
  69.8 11.9 %all-to-all-start.1 = ((bf16[16,32,128]{2,1,0:T(8,128)(2,1)}), bf16[16,32,128]{2,1,0:T(8,128)(2,1)S(1)}, u32[]{:S(2)}, u32[]{:S(2)}) async-start(bf16[16,32,128]{2,1,0:T(8,128)(2,1)} %get-tuple-element.38), calls=%async_computation.1 | async-start | bytes 262144 | tf_op jit(solution)/shard_map/all_to_all | solution.py:546
  81.7 6.3 %collective-permute-start.12 = (bf16[6,64,128]{2,1,0:T(8,128)(2,1)S(1)}, bf16[6,64,128]{2,1,0:T(8,128)(2,1)S(1)}, u32[]{:S(2)}, u32[]{:S(2)}) collective-permute-start(bf16[6,64,128]{2,1,0:T(8,128)(2,1)S(1)} %broadcast_select_fusion.refs_1_), channel_id=1, source_target_pairs={{8,26},{16,28},{14,2},{22,4},{2,14},{4,22},{26,8},{28,16},{0,30},{... | collective-permute-start | bytes 294920 | tf_op jit(solution)/shard_map/ppermute | solution.py:524
  88.0 2.5 %collective-permute-start.11 = (bf16[6,64,128]{2,1,0:T(8,128)(2,1)S(1)}, bf16[6,64,128]{2,1,0:T(8,128)(2,1)S(1)}, u32[]{:S(2)}, u32[]{:S(2)}) collective-permute-start(bf16[6,64,128]{2,1,0:T(8,128)(2,1)S(1)} %broadcast_select_fusion.refs_1_), channel_id=1, source_target_pairs={{8,2},{16,4},{14,26},{22,28},{2,8},{4,16},{26,14},{28,22},{0,24},{... | collective-permute-start | bytes 294920 | tf_op jit(solution)/shard_map/ppermute | solution.py:524
  90.6 4.4 %collective-permute-done.13.refs_6_ = bf16[3,64,128]{2,1,0:T(8,128)(2,1)S(1)} collective-permute-done((bf16[3,64,128]{2,1,0:T(8,128)(2,1)}, bf16[3,64,128]{2,1,0:T(8,128)(2,1)S(1)}, u32[]{:S(2)}, u32[]{:S(2)}) %collective-permute-start.13) | collective-permute-done | bytes 49184 | tf_op jit(solution)/shard_map/ppermute | solution.py:524
  95.1 1.2 %collective-permute-done.11.refs_3_ = bf16[6,64,128]{2,1,0:T(8,128)(2,1)S(1)} collective-permute-done((bf16[6,64,128]{2,1,0:T(8,128)(2,1)S(1)}, bf16[6,64,128]{2,1,0:T(8,128)(2,1)S(1)}, u32[]{:S(2)}, u32[]{:S(2)}) %collective-permute-start.11) | collective-permute-done | bytes 98336 | tf_op jit(solution)/shard_map/ppermute | solution.py:524
  97.6 2.6 %halo.3.refs_2_.refs_4_ = bf16[13,64,128]{2,1,0:T(8,128)(2,1)} custom-call(s32[20,12]{1,0:T(8,128)} %get-tuple-element.21.refs_0_, bf16[6,64,128]{2,1,0:T(8,128)(2,1)} %copy-done.9, bf16[6,64,128]{2,1,0:T(8,128)(2,1)} %copy-done.11, bf16[6,64,128]{2,1,0:T(8,128)(2,1)} %copy-done.15, bf16[6,64,128]{2,1,0:T(8,128)(2,1)} %copy-done.14, ...), custom_call_target="tpu_custom_call" | custom-call | tf_op jit(solution)/shard_map/halo/pallas_call | solution.py:191
  100.2 1.5 %collective-permute-start.15 = (bf16[13,64,128]{2,1,0:T(8,128)(2,1)}, bf16[13,64,128]{2,1,0:T(8,128)(2,1)S(1)}, u32[]{:S(2)}, u32[]{:S(2)}) collective-permute-start(bf16[13,64,128]{2,1,0:T(8,128)(2,1)} %halo.3.refs_2_.refs_4_), channel_id=1, source_target_pairs={{1,0},{0,1},{3,2},{2,3},{5,4},{4,5},{7,6},{6,7},{9,8},{8,9},{11,10... | collective-permute-start | bytes 638984 | tf_op jit(solution)/shard_map/ppermute | solution.py:465
  101.7 4.6 %collective-permute-done.15.refs_3_.refs_5_ = bf16[13,64,128]{2,1,0:T(8,128)(2,1)S(1)} collective-permute-done((bf16[13,64,128]{2,1,0:T(8,128)(2,1)}, bf16[13,64,128]{2,1,0:T(8,128)(2,1)S(1)}, u32[]{:S(2)}, u32[]{:S(2)}) %collective-permute-start.15) | collective-permute-done | bytes 213024 | tf_op jit(solution)/shard_map/ppermute | solution.py:465
  107.5 7.3 %backward.1 = bf16[12,64,1024]{2,1,0:T(8,128)(2,1)} custom-call(bf16[12,64,1024]{2,1,0:T(8,128)(2,1)} %get-tuple-element.31.refs_0_, bf16[12,64,1024]{2,1,0:T(8,128)(2,1)} %copy-done.1, bf16[13,64,128]{2,1,0:T(8,128)(2,1)} %halo.3.refs_2_.refs_4_, bf16[13,64,128]{2,1,0:T(8,128)(2,1)} %copy-done.3, bf16[13,64,128]{2,1,0:T(8,128)(2,1)} %halo.3.refs_2_.refs_4_, ...), custom_call_target="tpu_custom_call" | custom-call | tf_op jit(solution)/shard_map/backward/pallas_call | solution.py:355
  (61 shorter events, 7.9 us)
Async XLA Ops:
  0.6 51.0 %collective-permute-start = (bf16[12,64,1024]{2,1,0:T(8,128)(2,1)}, bf16[12,64,1024]{2,1,0:T(8,128)(2,1)S(1)}, u32[]{:S(2)}, u32[]{:S(2)}) collective-permute-start(bf16[12,64,1024]{2,1,0:T(8,128)(2,1)} %bitcast.18), channel_id=1, source_target_pairs={{1,0},{0,1},{3,2},{2,3},{5,4},{4,5},{7,6},{6,7},{9,8},{8,9},{11,10... | collective-permute-start | bytes 4718600 | tf_op jit(solution)/shard_map/ppermute | solution.py:465
  7.6 0.7 collective-permute-start.1
  8.3 34.0 %copy-start.6 = (bf16[6,64,128]{2,1,0:T(8,128)(2,1)}, bf16[6,64,128]{2,1,0:T(8,128)(2,1)S(1)}, u32[]{:S(2)}) copy-start(bf16[6,64,128]{2,1,0:T(8,128)(2,1)S(1)} %collective-permute-done.1.refs_5_) | copy-start | bytes 294916
  9.4 33.0 %copy-start.8 = (bf16[6,64,128]{2,1,0:T(8,128)(2,1)}, bf16[6,64,128]{2,1,0:T(8,128)(2,1)S(1)}, u32[]{:S(2)}) copy-start(bf16[6,64,128]{2,1,0:T(8,128)(2,1)S(1)} %broadcast_select_fusion.1.refs_1_) | copy-start | bytes 294916
  9.4 4.9 %collective-permute-start.2 = (bf16[6,64,128]{2,1,0:T(8,128)(2,1)S(1)}, bf16[6,64,128]{2,1,0:T(8,128)(2,1)S(1)}, u32[]{:S(2)}, u32[]{:S(2)}) collective-permute-start(bf16[6,64,128]{2,1,0:T(8,128)(2,1)S(1)} %broadcast_select_fusion.1.refs_1_), channel_id=1, source_target_pairs={{8,14},{16,22},{14,8},{22,16},{2,26},{4,28},{26,2},{28,4},{0,6},{6... | collective-permute-start | bytes 294920 | tf_op jit(solution)/shard_map/ppermute | solution.py:524
  14.3 28.1 %copy-start.10 = (bf16[6,64,128]{2,1,0:T(8,128)(2,1)}, bf16[6,64,128]{2,1,0:T(8,128)(2,1)S(1)}, u32[]{:S(2)}) copy-start(bf16[6,64,128]{2,1,0:T(8,128)(2,1)S(1)} %collective-permute-done.2.refs_2_) | copy-start | bytes 294916
  14.3 28.1 %all-to-all-start = ((bf16[16,32,128]{2,1,0:T(8,128)(2,1)}), bf16[16,32,128]{2,1,0:T(8,128)(2,1)S(1)}, u32[]{:S(2)}, u32[]{:S(2)}) async-start(bf16[16,32,128]{2,1,0:T(8,128)(2,1)} %get-tuple-element.28), calls=%async_computation | async-start | bytes 262144 | tf_op jit(solution)/shard_map/all_to_all | solution.py:546
  27.7 13.3 %collective-permute-start.4 = (bf16[6,64,128]{2,1,0:T(8,128)(2,1)S(1)}, bf16[6,64,128]{2,1,0:T(8,128)(2,1)S(1)}, u32[]{:S(2)}, u32[]{:S(2)}) collective-permute-start(bf16[6,64,128]{2,1,0:T(8,128)(2,1)S(1)} %broadcast_select_fusion.1.refs_1_), channel_id=1, source_target_pairs={{8,26},{16,28},{14,2},{22,4},{2,14},{4,22},{26,8},{28,16},{0,30},{... | collective-permute-start | bytes 294920 | tf_op jit(solution)/shard_map/ppermute | solution.py:524
  34.0 8.3 %collective-permute-start.3 = (bf16[6,64,128]{2,1,0:T(8,128)(2,1)S(1)}, bf16[6,64,128]{2,1,0:T(8,128)(2,1)S(1)}, u32[]{:S(2)}, u32[]{:S(2)}) collective-permute-start(bf16[6,64,128]{2,1,0:T(8,128)(2,1)S(1)} %broadcast_select_fusion.1.refs_1_), channel_id=1, source_target_pairs={{8,2},{16,4},{14,26},{22,28},{2,8},{4,16},{26,14},{28,22},{0,24},{... | collective-permute-start | bytes 294920 | tf_op jit(solution)/shard_map/ppermute | solution.py:524
  36.5 4.6 %collective-permute-start.5 = (bf16[3,64,128]{2,1,0:T(8,128)(2,1)}, bf16[3,64,128]{2,1,0:T(8,128)(2,1)S(1)}, u32[]{:S(2)}, u32[]{:S(2)}) collective-permute-start(bf16[3,64,128]{2,1,0:T(8,128)(2,1)} %get-tuple-element.26), channel_id=1, source_target_pairs={{0,8},{2,10},{4,12},{6,14},{8,0},{10,2},{12,4},{14,6},{16,24},{18,... | collective-permute-start | bytes 147464 | tf_op jit(solution)/shard_map/ppermute | solution.py:524
  36.6 4.5 %collective-permute-start.6 = (bf16[3,64,128]{2,1,0:T(8,128)(2,1)}, bf16[3,64,128]{2,1,0:T(8,128)(2,1)S(1)}, u32[]{:S(2)}, u32[]{:S(2)}) collective-permute-start(bf16[3,64,128]{2,1,0:T(8,128)(2,1)} %get-tuple-element.27), channel_id=1, source_target_pairs={{0,2},{2,0},{4,6},{6,4},{8,10},{10,8},{12,14},{14,12},{16,18},{18,... | collective-permute-start | bytes 147464 | tf_op jit(solution)/shard_map/ppermute | solution.py:524
  45.6 6.1 %collective-permute-start.7 = (bf16[13,64,128]{2,1,0:T(8,128)(2,1)}, bf16[13,64,128]{2,1,0:T(8,128)(2,1)S(1)}, u32[]{:S(2)}, u32[]{:S(2)}) collective-permute-start(bf16[13,64,128]{2,1,0:T(8,128)(2,1)} %halo.2.refs_2_.refs_4_), channel_id=1, source_target_pairs={{1,0},{0,1},{3,2},{2,3},{5,4},{4,5},{7,6},{6,7},{9,8},{8,9},{11,10... | collective-permute-start | bytes 638984 | tf_op jit(solution)/shard_map/ppermute | solution.py:465
  62.3 43.9 %collective-permute-start.8 = (bf16[12,64,1024]{2,1,0:T(8,128)(2,1)}, bf16[12,64,1024]{2,1,0:T(8,128)(2,1)S(1)}, u32[]{:S(2)}, u32[]{:S(2)}) collective-permute-start(bf16[12,64,1024]{2,1,0:T(8,128)(2,1)} %get-tuple-element.31.refs_0_), channel_id=1, source_target_pairs={{1,0},{0,1},{3,2},{2,3},{5,4},{4,5},{7,6},{6,7},{9,8},{8,9},{11,10... | collective-permute-start | bytes 4718600 | tf_op jit(solution)/shard_map/ppermute | solution.py:465
  62.9 0.7 collective-permute-start.9
  63.6 32.7 %copy-start.7 = (bf16[6,64,128]{2,1,0:T(8,128)(2,1)}, bf16[6,64,128]{2,1,0:T(8,128)(2,1)S(1)}, u32[]{:S(2)}) copy-start(bf16[6,64,128]{2,1,0:T(8,128)(2,1)S(1)} %collective-permute-done.9.refs_5_) | copy-start | bytes 294916
  64.6 31.7 %copy-start.9 = (bf16[6,64,128]{2,1,0:T(8,128)(2,1)}, bf16[6,64,128]{2,1,0:T(8,128)(2,1)S(1)}, u32[]{:S(2)}) copy-start(bf16[6,64,128]{2,1,0:T(8,128)(2,1)S(1)} %broadcast_select_fusion.refs_1_) | copy-start | bytes 294916
  64.6 5.1 %collective-permute-start.10 = (bf16[6,64,128]{2,1,0:T(8,128)(2,1)S(1)}, bf16[6,64,128]{2,1,0:T(8,128)(2,1)S(1)}, u32[]{:S(2)}, u32[]{:S(2)}) collective-permute-start(bf16[6,64,128]{2,1,0:T(8,128)(2,1)S(1)} %broadcast_select_fusion.refs_1_), channel_id=1, source_target_pairs={{8,14},{16,22},{14,8},{22,16},{2,26},{4,28},{26,2},{28,4},{0,6},{6... | collective-permute-start | bytes 294920 | tf_op jit(solution)/shard_map/ppermute | solution.py:524
  69.8 26.6 %copy-start.11 = (bf16[6,64,128]{2,1,0:T(8,128)(2,1)}, bf16[6,64,128]{2,1,0:T(8,128)(2,1)S(1)}, u32[]{:S(2)}) copy-start(bf16[6,64,128]{2,1,0:T(8,128)(2,1)S(1)} %collective-permute-done.10.refs_2_) | copy-start | bytes 294916
  69.8 26.5 %all-to-all-start.1 = ((bf16[16,32,128]{2,1,0:T(8,128)(2,1)}), bf16[16,32,128]{2,1,0:T(8,128)(2,1)S(1)}, u32[]{:S(2)}, u32[]{:S(2)}) async-start(bf16[16,32,128]{2,1,0:T(8,128)(2,1)} %get-tuple-element.38), calls=%async_computation.1 | async-start | bytes 262144 | tf_op jit(solution)/shard_map/all_to_all | solution.py:546
  81.7 13.3 %collective-permute-start.12 = (bf16[6,64,128]{2,1,0:T(8,128)(2,1)S(1)}, bf16[6,64,128]{2,1,0:T(8,128)(2,1)S(1)}, u32[]{:S(2)}, u32[]{:S(2)}) collective-permute-start(bf16[6,64,128]{2,1,0:T(8,128)(2,1)S(1)} %broadcast_select_fusion.refs_1_), channel_id=1, source_target_pairs={{8,26},{16,28},{14,2},{22,4},{2,14},{4,22},{26,8},{28,16},{0,30},{... | collective-permute-start | bytes 294920 | tf_op jit(solution)/shard_map/ppermute | solution.py:524
  88.0 8.3 %collective-permute-start.11 = (bf16[6,64,128]{2,1,0:T(8,128)(2,1)S(1)}, bf16[6,64,128]{2,1,0:T(8,128)(2,1)S(1)}, u32[]{:S(2)}, u32[]{:S(2)}) collective-permute-start(bf16[6,64,128]{2,1,0:T(8,128)(2,1)S(1)} %broadcast_select_fusion.refs_1_), channel_id=1, source_target_pairs={{8,2},{16,4},{14,26},{22,28},{2,8},{4,16},{26,14},{28,22},{0,24},{... | collective-permute-start | bytes 294920 | tf_op jit(solution)/shard_map/ppermute | solution.py:524
  90.5 4.6 %collective-permute-start.13 = (bf16[3,64,128]{2,1,0:T(8,128)(2,1)}, bf16[3,64,128]{2,1,0:T(8,128)(2,1)S(1)}, u32[]{:S(2)}, u32[]{:S(2)}) collective-permute-start(bf16[3,64,128]{2,1,0:T(8,128)(2,1)} %get-tuple-element.36), channel_id=1, source_target_pairs={{0,8},{2,10},{4,12},{6,14},{8,0},{10,2},{12,4},{14,6},{16,24},{18,... | collective-permute-start | bytes 147464 | tf_op jit(solution)/shard_map/ppermute | solution.py:524
  90.5 4.5 %collective-permute-start.14 = (bf16[3,64,128]{2,1,0:T(8,128)(2,1)}, bf16[3,64,128]{2,1,0:T(8,128)(2,1)S(1)}, u32[]{:S(2)}, u32[]{:S(2)}) collective-permute-start(bf16[3,64,128]{2,1,0:T(8,128)(2,1)} %get-tuple-element.37), channel_id=1, source_target_pairs={{0,2},{2,0},{4,6},{6,4},{8,10},{10,8},{12,14},{14,12},{16,18},{18,... | collective-permute-start | bytes 147464 | tf_op jit(solution)/shard_map/ppermute | solution.py:524
  100.2 6.1 %collective-permute-start.15 = (bf16[13,64,128]{2,1,0:T(8,128)(2,1)}, bf16[13,64,128]{2,1,0:T(8,128)(2,1)S(1)}, u32[]{:S(2)}, u32[]{:S(2)}) collective-permute-start(bf16[13,64,128]{2,1,0:T(8,128)(2,1)} %halo.3.refs_2_.refs_4_), channel_id=1, source_target_pairs={{1,0},{0,1},{3,2},{2,3},{5,4},{4,5},{7,6},{6,7},{9,8},{8,9},{11,10... | collective-permute-start | bytes 638984 | tf_op jit(solution)/shard_map/ppermute | solution.py:465
  (14 other events, 14.3 us)

commit v6 on v5

--- a/solution.py
+++ b/solution.py
@@ -542,9 +542,10 @@
             if j == 1:
                 pairs += [((x, y), (x, 3 - y)) for x in (1, 2) for y in (1, 2)]
             across.append(swap(lines, pairs))
-        corner, across[0] = lax.optimization_barrier((corner, across[0]))
+        arrived = [*across, paired, near_col, near_row]
+        corner, *arrived = lax.optimization_barrier((corner, *arrived))
         ends_of = lax.all_to_all(corner, axes, 0, 0, tiled=True)
-        return [lines, *across, paired, near_col, near_row, ends_of]
+        return [lines, *arrived, ends_of]
 
     def strip_cell(self, g, s, at):
         row_pos, col_pos = self.place()

time: 115 us -> 113 us (0.983)
  blocking collectives: 0 us -> 15 us
  waiting for transfers between devices: 28.4 us -> 19.4 us
  starting transfers between devices: 50.9 us -> 43.5 us
  local copies, waits for them, and re-layouts: 4.35 us -> 3.08 us
    all_to_all x2 -> x1, starting transfers between devices: 25.4 us -> 7.87 us  [exchange(): ends_of = lax.all_to_all(corner, axes, 0, 0, tiled=True)]
    ppermute x12, waiting for transfers between devices: 18.3 us -> 2.34 us  [exchange(): lax.ppermute(array, axes, [(a[0] * 4 + a[1], b[0] * 4 + b[1]) for a, b in...]
    all_to_all x0 -> x1, blocking collectives: none -> 15 us  [exchange(): ends_of = lax.all_to_all(corner, axes, 0, 0, tiled=True)]
    ppermute x12, starting transfers between devices: 19.9 us -> 30 us  [exchange(): lax.ppermute(array, axes, [(a[0] * 4 + a[1], b[0] * 4 + b[1]) for a, b in...]
    all_to_all x2 -> x1, waiting for transfers between devices: 0.01 us -> 5.71 us  [exchange(): ends_of = lax.all_to_all(corner, axes, 0, 0, tiled=True)]
    ppermute x4, waiting for transfers between devices: 10.1 us -> 11.4 us  [from_others(): lax.ppermute(array, 'ch', [((i + k) % ch_count, i) for i in range(ch_coun...]
    unnamed x40 -> x38, local copies, waits for them, and re-layouts: 4.35 us -> 3.08 us
  transfers between devices with their start and end apart: 18 -> 17, of which waited for: 8 -> 6; matrix products, arithmetic and copies ran while one was open for 2% -> 2% of each run, Pallas kernels for 10% -> 10%
where the time goes in v6:
time: 113 us; the launch traced here: 112 us
  starting transfers between devices  43.5 us (38%)
  Pallas kernels  28.2 us (25%)
  waiting for transfers between devices  19.4 us (17%)
  blocking collectives  15 us (13%)
  local copies, waits for them, and re-layouts  3.08 us (3%)
  other arithmetic  2.03 us (2%)
    ppermute x12, starting transfers between devices, exchange(): lax.ppermute(array, axes, [(a[0] * 4 + a[1], b[0] * 4 + b[1]) for a, b in...  30 us
    all_to_all x1, blocking collectives, exchange(): ends_of = lax.all_to_all(corner, axes, 0, 0, tiled=True)  15 us
    ppermute x4, waiting for transfers between devices, from_others(): lax.ppermute(array, 'ch', [((i + k) % ch_count, i) for i in range(ch_coun...  11.4 us
    pallas_call x1, Pallas kernels, forward(): pl.pallas_call(lambda *refs: forward_kernel(first, count, steps, pieces,...  9.46 us
    all_to_all x1, starting transfers between devices, exchange(): ends_of = lax.all_to_all(corner, axes, 0, 0, tiled=True)  7.87 us
    pallas_call x1, Pallas kernels, backward(): pl.pallas_call(lambda *refs: backward_kernel(first, pieces, *refs), grid=...  7.29 us
    all_to_all x1, waiting for transfers between devices, exchange(): ends_of = lax.all_to_all(corner, axes, 0, 0, tiled=True)  5.71 us
    ppermute x4, starting transfers between devices, from_others(): lax.ppermute(array, 'ch', [((i + k) % ch_count, i) for i in range(ch_coun...  5.64 us
  transfers between devices with their start and end apart: 17, of which 6 were waited for; matrix products, arithmetic and copies ran while one was open for 2% of the time, Pallas kernels for 10%

profile of v6, /device:TPU:0, one launch (start us, length us, event | category | flops | bytes accessed | tf_op | source)
XLA Modules:
  0.0 112.1 jit_solution(17308271798272349094)
XLA Ops:
  0.6 3.0 %collective-permute-start = (bf16[12,64,1024]{2,1,0:T(8,128)(2,1)}, bf16[12,64,1024]{2,1,0:T(8,128)(2,1)S(1)}, u32[]{:S(2)}, u32[]{:S(2)}) collective-permute-start(bf16[12,64,1024]{2,1,0:T(8,128)(2,1)} %bitcast.18), channel_id=1, source_target_pairs={{1,0},{0,1},{3,2},{2,3},{5,4},{4,5},{7,6},{6,7},{9,8},{8,9},{11,10... | collective-permute-start | bytes 4718600 | tf_op jit(solution)/shard_map/ppermute | solution.py:465
  3.6 4.0 %rings.1 = (bf16[6,64,128]{2,1,0:T(8,128)(2,1)}, bf16[3,64,128]{2,1,0:T(8,128)(2,1)}, bf16[3,64,128]{2,1,0:T(8,128)(2,1)}, bf16[6,64,128]{2,1,0:T(8,128)(2,1)}, bf16[16,32,128]{2,1,0:T(8,128)(2,1)}) custom-call(bf16[12,64,1024]{2,1,0:T(8,128)(2,1)} %bitcast.19, bf16[1024,128]{1,0:T(8,128)(2,1)} %constant.33.clone.refs_1_.refs_9_, ...), custom_call_target="tpu_custom_call" | custom-call | tf_op jit(solution)/shard_map/rings/pallas_call | solution.py:127
  7.6 1.6 %collective-permute-start.5 = (bf16[3,64,128]{2,1,0:T(8,128)(2,1)}, bf16[3,64,128]{2,1,0:T(8,128)(2,1)S(1)}, u32[]{:S(2)}, u32[]{:S(2)}) collective-permute-start(bf16[3,64,128]{2,1,0:T(8,128)(2,1)} %get-tuple-element.35), channel_id=1, source_target_pairs={{0,8},{2,10},{4,12},{6,14},{8,0},{10,2},{12,4},{14,6},{16,24},{18,... | collective-permute-start | bytes 147464 | tf_op jit(solution)/shard_map/ppermute | solution.py:524
  11.0 4.2 %collective-permute-start.4 = (bf16[6,64,128]{2,1,0:T(8,128)(2,1)S(1)}, bf16[6,64,128]{2,1,0:T(8,128)(2,1)S(1)}, u32[]{:S(2)}, u32[]{:S(2)}) collective-permute-start(bf16[6,64,128]{2,1,0:T(8,128)(2,1)S(1)} %broadcast_select_fusion.1.refs_1_), channel_id=1, source_target_pairs={{8,26},{16,28},{14,2},{22,4},{2,14},{4,22},{26,8},{28,16},{0,30},{... | collective-permute-start | bytes 294920 | tf_op jit(solution)/shard_map/ppermute | solution.py:524
  15.2 3.3 %collective-permute-start.3 = (bf16[6,64,128]{2,1,0:T(8,128)(2,1)S(1)}, bf16[6,64,128]{2,1,0:T(8,128)(2,1)S(1)}, u32[]{:S(2)}, u32[]{:S(2)}) collective-permute-start(bf16[6,64,128]{2,1,0:T(8,128)(2,1)S(1)} %broadcast_select_fusion.1.refs_1_), channel_id=1, source_target_pairs={{8,2},{16,4},{14,26},{22,28},{2,8},{4,16},{26,14},{28,22},{0,24},{... | collective-permute-start | bytes 294920 | tf_op jit(solution)/shard_map/ppermute | solution.py:524
  18.4 1.1 %collective-permute-start.2 = (bf16[6,64,128]{2,1,0:T(8,128)(2,1)S(1)}, bf16[6,64,128]{2,1,0:T(8,128)(2,1)S(1)}, u32[]{:S(2)}, u32[]{:S(2)}) collective-permute-start(bf16[6,64,128]{2,1,0:T(8,128)(2,1)S(1)} %broadcast_select_fusion.1.refs_1_), channel_id=1, source_target_pairs={{8,14},{16,22},{14,8},{22,16},{2,26},{4,28},{26,2},{28,4},{0,6},{6... | collective-permute-start | bytes 294920 | tf_op jit(solution)/shard_map/ppermute | solution.py:524
  19.6 5.3 %collective-permute-start.6 = (bf16[3,64,128]{2,1,0:T(8,128)(2,1)}, bf16[3,64,128]{2,1,0:T(8,128)(2,1)S(1)}, u32[]{:S(2)}, u32[]{:S(2)}) collective-permute-start(bf16[3,64,128]{2,1,0:T(8,128)(2,1)} %get-tuple-element.36), channel_id=1, source_target_pairs={{0,2},{2,0},{4,6},{6,4},{8,10},{10,8},{12,14},{14,12},{16,18},{18,... | collective-permute-start | bytes 147464 | tf_op jit(solution)/shard_map/ppermute | solution.py:524
  24.9 1.1 collective-permute-done.6.refs_7_
  26.0 7.9 %all-to-all-start = ((bf16[16,32,128]{2,1,0:T(8,128)(2,1)}), bf16[16,32,128]{2,1,0:T(8,128)(2,1)S(1)}, u32[]{:S(2)}, u32[]{:S(2)}) async-start(bf16[16,32,128]{2,1,0:T(8,128)(2,1)} %get-tuple-element.43), calls=%async_computation | async-start | bytes 262144 | tf_op jit(solution)/shard_map/all_to_all | solution.py:547
  33.9 2.2 %setup.1 = (s32[20,12]{1,0:T(8,128)}, bf16[192,384]{1,0:T(8,128)(2,1)}, bf16[192,384]{1,0:T(8,128)(2,1)}) custom-call(s32[3,4,12]{2,1,0:T(4,128)} %bitcast.23, s32[4,2,12]{2,1,0:T(2,128)} %bitcast.24, bf16[3,3,128,128]{3,2,1,0:T(8,128)(2,1)} %refs_2_.2), custom_call_target="tpu_custom_call" | custom-call | tf_op jit(solution)/shard_map/setup/pallas_call | solution.py:452
  36.2 5.7 %all-to-all-done.refs_8_ = bf16[16,32,128]{2,1,0:T(8,128)(2,1)S(1)} async-done(((bf16[16,32,128]{2,1,0:T(8,128)(2,1)}), bf16[16,32,128]{2,1,0:T(8,128)(2,1)S(1)}, u32[]{:S(2)}, u32[]{:S(2)}) %all-to-all-start) | async-done | bytes 131104 | tf_op jit(solution)/shard_map/all_to_all | solution.py:547
  42.5 2.6 %halo.2.refs_2_.refs_4_ = bf16[13,64,128]{2,1,0:T(8,128)(2,1)} custom-call(s32[20,12]{1,0:T(8,128)} %get-tuple-element.31.refs_0_, bf16[6,64,128]{2,1,0:T(8,128)(2,1)} %copy-done.6, bf16[6,64,128]{2,1,0:T(8,128)(2,1)} %copy-done.11, bf16[6,64,128]{2,1,0:T(8,128)(2,1)} %copy-done.10, bf16[6,64,128]{2,1,0:T(8,128)(2,1)} %copy-done.9, ...), custom_call_target="tpu_custom_call" | custom-call | tf_op jit(solution)/shard_map/halo/pallas_call | solution.py:191
  45.7 6.2 %collective-permute-done.7.refs_3_.refs_5_ = bf16[13,64,128]{2,1,0:T(8,128)(2,1)S(1)} collective-permute-done((bf16[13,64,128]{2,1,0:T(8,128)(2,1)}, bf16[13,64,128]{2,1,0:T(8,128)(2,1)S(1)}, u32[]{:S(2)}, u32[]{:S(2)}) %collective-permute-start.7) | collective-permute-done | bytes 213024 | tf_op jit(solution)/shard_map/ppermute | solution.py:465
  53.1 9.5 %forward.1 = (bf16[12,64,1024]{2,1,0:T(8,128)(2,1)}, bf16[12,64,1024]{2,1,0:T(8,128)(2,1)}, bf16[6,64,128]{2,1,0:T(8,128)(2,1)}, bf16[3,64,128]{2,1,0:T(8,128)(2...) custom-call(bf16[12,64,1024]{2,1,0:T(8,128)(2,1)} %bitcast.20, ...), custom_call_target="tpu_custom_call" | custom-call | tf_op jit(solution)/shard_map/forward/pallas_call | solution.py:318
  63.8 3.0 %collective-permute-start.13 = (bf16[3,64,128]{2,1,0:T(8,128)(2,1)}, bf16[3,64,128]{2,1,0:T(8,128)(2,1)S(1)}, u32[]{:S(2)}, u32[]{:S(2)}) collective-permute-start(bf16[3,64,128]{2,1,0:T(8,128)(2,1)} %get-tuple-element.50), channel_id=1, source_target_pairs={{0,8},{2,10},{4,12},{6,14},{8,0},{10,2},{12,4},{14,6},{16,24},{18,... | collective-permute-start | bytes 147464 | tf_op jit(solution)/shard_map/ppermute | solution.py:524
  67.8 2.5 %collective-permute-start.12 = (bf16[6,64,128]{2,1,0:T(8,128)(2,1)S(1)}, bf16[6,64,128]{2,1,0:T(8,128)(2,1)S(1)}, u32[]{:S(2)}, u32[]{:S(2)}) collective-permute-start(bf16[6,64,128]{2,1,0:T(8,128)(2,1)S(1)} %broadcast_select_fusion.refs_1_), channel_id=1, source_target_pairs={{8,26},{16,28},{14,2},{22,4},{2,14},{4,22},{26,8},{28,16},{0,30},{... | collective-permute-start | bytes 294920 | tf_op jit(solution)/shard_map/ppermute | solution.py:524
  70.3 3.8 %collective-permute-start.11 = (bf16[6,64,128]{2,1,0:T(8,128)(2,1)S(1)}, bf16[6,64,128]{2,1,0:T(8,128)(2,1)S(1)}, u32[]{:S(2)}, u32[]{:S(2)}) collective-permute-start(bf16[6,64,128]{2,1,0:T(8,128)(2,1)S(1)} %broadcast_select_fusion.refs_1_), channel_id=1, source_target_pairs={{8,2},{16,4},{14,26},{22,28},{2,8},{4,16},{26,14},{28,22},{0,24},{... | collective-permute-start | bytes 294920 | tf_op jit(solution)/shard_map/ppermute | solution.py:524
  74.1 2.4 %collective-permute-start.10 = (bf16[6,64,128]{2,1,0:T(8,128)(2,1)S(1)}, bf16[6,64,128]{2,1,0:T(8,128)(2,1)S(1)}, u32[]{:S(2)}, u32[]{:S(2)}) collective-permute-start(bf16[6,64,128]{2,1,0:T(8,128)(2,1)S(1)} %broadcast_select_fusion.refs_1_), channel_id=1, source_target_pairs={{8,14},{16,22},{14,8},{22,16},{2,26},{4,28},{26,2},{28,4},{0,6},{6... | collective-permute-start | bytes 294920 | tf_op jit(solution)/shard_map/ppermute | solution.py:524
  76.4 1.6 %collective-permute-start.14 = (bf16[3,64,128]{2,1,0:T(8,128)(2,1)}, bf16[3,64,128]{2,1,0:T(8,128)(2,1)S(1)}, u32[]{:S(2)}, u32[]{:S(2)}) collective-permute-start(bf16[3,64,128]{2,1,0:T(8,128)(2,1)} %get-tuple-element.51), channel_id=1, source_target_pairs={{0,2},{2,0},{4,6},{6,4},{8,10},{10,8},{12,14},{14,12},{16,18},{18,... | collective-permute-start | bytes 147464 | tf_op jit(solution)/shard_map/ppermute | solution.py:524
  79.2 15.0 %all_to_all.10.refs_8_ = bf16[16,32,128]{2,1,0:T(8,128)(2,1)} all-to-all(bf16[16,32,128]{2,1,0:T(8,128)(2,1)} %get-tuple-element.58), channel_id=1, replica_groups=mesh['px'=4,'py'=4,'ch'=2] {'px','py'}, dimensions={0} | all-to-all | bytes 262144 | tf_op jit(solution)/shard_map/all_to_all | solution.py:547
  94.3 2.6 %halo.3.refs_2_.refs_4_ = bf16[13,64,128]{2,1,0:T(8,128)(2,1)} custom-call(s32[20,12]{1,0:T(8,128)} %get-tuple-element.31.refs_0_, bf16[6,64,128]{2,1,0:T(8,128)(2,1)} %copy-done.8, bf16[6,64,128]{2,1,0:T(8,128)(2,1)} %copy-done.14, bf16[6,64,128]{2,1,0:T(8,128)(2,1)} %copy-done.13, bf16[6,64,128]{2,1,0:T(8,128)(2,1)} %copy-done.12, ...), custom_call_target="tpu_custom_call" | custom-call | tf_op jit(solution)/shard_map/halo/pallas_call | solution.py:191
  96.9 1.5 %collective-permute-start.15 = (bf16[13,64,128]{2,1,0:T(8,128)(2,1)}, bf16[13,64,128]{2,1,0:T(8,128)(2,1)S(1)}, u32[]{:S(2)}, u32[]{:S(2)}) collective-permute-start(bf16[13,64,128]{2,1,0:T(8,128)(2,1)} %halo.3.refs_2_.refs_4_), channel_id=1, source_target_pairs={{1,0},{0,1},{3,2},{2,3},{5,4},{4,5},{7,6},{6,7},{9,8},{8,9},{11,10... | collective-permute-start | bytes 638984 | tf_op jit(solution)/shard_map/ppermute | solution.py:465
  98.4 5.2 %collective-permute-done.15.refs_3_.refs_5_ = bf16[13,64,128]{2,1,0:T(8,128)(2,1)S(1)} collective-permute-done((bf16[13,64,128]{2,1,0:T(8,128)(2,1)}, bf16[13,64,128]{2,1,0:T(8,128)(2,1)S(1)}, u32[]{:S(2)}, u32[]{:S(2)}) %collective-permute-start.15) | collective-permute-done | bytes 213024 | tf_op jit(solution)/shard_map/ppermute | solution.py:465
  104.8 7.3 %backward.1 = bf16[12,64,1024]{2,1,0:T(8,128)(2,1)} custom-call(bf16[12,64,1024]{2,1,0:T(8,128)(2,1)} %get-tuple-element.46.refs_0_, bf16[12,64,1024]{2,1,0:T(8,128)(2,1)} %copy-done.1, bf16[13,64,128]{2,1,0:T(8,128)(2,1)} %halo.3.refs_2_.refs_4_, bf16[13,64,128]{2,1,0:T(8,128)(2,1)} %copy-done.3, bf16[13,64,128]{2,1,0:T(8,128)(2,1)} %halo.3.refs_2_.refs_4_, ...), custom_call_target="tpu_custom_call" | custom-call | tf_op jit(solution)/shard_map/backward/pallas_call | solution.py:355
  (58 shorter events, 8.8 us)
Async XLA Ops:
  0.6 51.2 %collective-permute-start = (bf16[12,64,1024]{2,1,0:T(8,128)(2,1)}, bf16[12,64,1024]{2,1,0:T(8,128)(2,1)S(1)}, u32[]{:S(2)}, u32[]{:S(2)}) collective-permute-start(bf16[12,64,1024]{2,1,0:T(8,128)(2,1)} %bitcast.18), channel_id=1, source_target_pairs={{1,0},{0,1},{3,2},{2,3},{5,4},{4,5},{7,6},{6,7},{9,8},{8,9},{11,10... | collective-permute-start | bytes 4718600 | tf_op jit(solution)/shard_map/ppermute | solution.py:465
  7.6 12.0 %collective-permute-start.5 = (bf16[3,64,128]{2,1,0:T(8,128)(2,1)}, bf16[3,64,128]{2,1,0:T(8,128)(2,1)S(1)}, u32[]{:S(2)}, u32[]{:S(2)}) collective-permute-start(bf16[3,64,128]{2,1,0:T(8,128)(2,1)} %get-tuple-element.35), channel_id=1, source_target_pairs={{0,8},{2,10},{4,12},{6,14},{8,0},{10,2},{12,4},{14,6},{16,24},{18,... | collective-permute-start | bytes 147464 | tf_op jit(solution)/shard_map/ppermute | solution.py:524
  9.2 0.7 collective-permute-start.1
  9.9 31.9 %copy-start.5 = (bf16[6,64,128]{2,1,0:T(8,128)(2,1)}, bf16[6,64,128]{2,1,0:T(8,128)(2,1)S(1)}, u32[]{:S(2)}) copy-start(bf16[6,64,128]{2,1,0:T(8,128)(2,1)S(1)} %collective-permute-done.1.refs_5_) | copy-start | bytes 294916
  10.9 30.9 %copy-start.6 = (bf16[6,64,128]{2,1,0:T(8,128)(2,1)}, bf16[6,64,128]{2,1,0:T(8,128)(2,1)S(1)}, u32[]{:S(2)}) copy-start(bf16[6,64,128]{2,1,0:T(8,128)(2,1)S(1)} %broadcast_select_fusion.1.refs_1_) | copy-start | bytes 294916
  11.0 15.1 %collective-permute-start.4 = (bf16[6,64,128]{2,1,0:T(8,128)(2,1)S(1)}, bf16[6,64,128]{2,1,0:T(8,128)(2,1)S(1)}, u32[]{:S(2)}, u32[]{:S(2)}) collective-permute-start(bf16[6,64,128]{2,1,0:T(8,128)(2,1)S(1)} %broadcast_select_fusion.1.refs_1_), channel_id=1, source_target_pairs={{8,26},{16,28},{14,2},{22,4},{2,14},{4,22},{26,8},{28,16},{0,30},{... | collective-permute-start | bytes 294920 | tf_op jit(solution)/shard_map/ppermute | solution.py:524
  15.2 10.8 %collective-permute-start.3 = (bf16[6,64,128]{2,1,0:T(8,128)(2,1)S(1)}, bf16[6,64,128]{2,1,0:T(8,128)(2,1)S(1)}, u32[]{:S(2)}, u32[]{:S(2)}) collective-permute-start(bf16[6,64,128]{2,1,0:T(8,128)(2,1)S(1)} %broadcast_select_fusion.1.refs_1_), channel_id=1, source_target_pairs={{8,2},{16,4},{14,26},{22,28},{2,8},{4,16},{26,14},{28,22},{0,24},{... | collective-permute-start | bytes 294920 | tf_op jit(solution)/shard_map/ppermute | solution.py:524
  18.4 7.6 %collective-permute-start.2 = (bf16[6,64,128]{2,1,0:T(8,128)(2,1)S(1)}, bf16[6,64,128]{2,1,0:T(8,128)(2,1)S(1)}, u32[]{:S(2)}, u32[]{:S(2)}) collective-permute-start(bf16[6,64,128]{2,1,0:T(8,128)(2,1)S(1)} %broadcast_select_fusion.1.refs_1_), channel_id=1, source_target_pairs={{8,14},{16,22},{14,8},{22,16},{2,26},{4,28},{26,2},{28,4},{0,6},{6... | collective-permute-start | bytes 294920 | tf_op jit(solution)/shard_map/ppermute | solution.py:524
  19.6 22.3 %copy-start.15 = (bf16[3,64,128]{2,1,0:T(8,128)(2,1)}, bf16[3,64,128]{2,1,0:T(8,128)(2,1)S(1)}, u32[]{:S(2)}) copy-start(bf16[3,64,128]{2,1,0:T(8,128)(2,1)S(1)} %collective-permute-done.5.refs_6_) | copy-start | bytes 147460
  19.6 6.4 %collective-permute-start.6 = (bf16[3,64,128]{2,1,0:T(8,128)(2,1)}, bf16[3,64,128]{2,1,0:T(8,128)(2,1)S(1)}, u32[]{:S(2)}, u32[]{:S(2)}) collective-permute-start(bf16[3,64,128]{2,1,0:T(8,128)(2,1)} %get-tuple-element.36), channel_id=1, source_target_pairs={{0,2},{2,0},{4,6},{6,4},{8,10},{10,8},{12,14},{14,12},{16,18},{18,... | collective-permute-start | bytes 147464 | tf_op jit(solution)/shard_map/ppermute | solution.py:524
  26.0 15.9 %copy-start.10 = (bf16[6,64,128]{2,1,0:T(8,128)(2,1)}, bf16[6,64,128]{2,1,0:T(8,128)(2,1)S(1)}, u32[]{:S(2)}) copy-start(bf16[6,64,128]{2,1,0:T(8,128)(2,1)S(1)} %collective-permute-done.3.refs_3_) | copy-start | bytes 294916
  26.0 15.8 %all-to-all-start = ((bf16[16,32,128]{2,1,0:T(8,128)(2,1)}), bf16[16,32,128]{2,1,0:T(8,128)(2,1)S(1)}, u32[]{:S(2)}, u32[]{:S(2)}) async-start(bf16[16,32,128]{2,1,0:T(8,128)(2,1)} %get-tuple-element.43), calls=%async_computation | async-start | bytes 262144 | tf_op jit(solution)/shard_map/all_to_all | solution.py:547
  45.1 6.7 %collective-permute-start.7 = (bf16[13,64,128]{2,1,0:T(8,128)(2,1)}, bf16[13,64,128]{2,1,0:T(8,128)(2,1)S(1)}, u32[]{:S(2)}, u32[]{:S(2)}) collective-permute-start(bf16[13,64,128]{2,1,0:T(8,128)(2,1)} %halo.2.refs_2_.refs_4_), channel_id=1, source_target_pairs={{1,0},{0,1},{3,2},{2,3},{5,4},{4,5},{7,6},{6,7},{9,8},{8,9},{11,10... | collective-permute-start | bytes 638984 | tf_op jit(solution)/shard_map/ppermute | solution.py:465
  62.5 41.1 %collective-permute-start.8 = (bf16[12,64,1024]{2,1,0:T(8,128)(2,1)}, bf16[12,64,1024]{2,1,0:T(8,128)(2,1)S(1)}, u32[]{:S(2)}, u32[]{:S(2)}) collective-permute-start(bf16[12,64,1024]{2,1,0:T(8,128)(2,1)} %get-tuple-element.46.refs_0_), channel_id=1, source_target_pairs={{1,0},{0,1},{3,2},{2,3},{5,4},{4,5},{7,6},{6,7},{9,8},{8,9},{11,10... | collective-permute-start | bytes 4718600 | tf_op jit(solution)/shard_map/ppermute | solution.py:465
  63.1 3.7 %collective-permute-start.9 = (bf16[6,64,128]{2,1,0:T(8,128)(2,1)}, bf16[6,64,128]{2,1,0:T(8,128)(2,1)S(1)}, u32[]{:S(2)}, u32[]{:S(2)}) collective-permute-start(bf16[6,64,128]{2,1,0:T(8,128)(2,1)} %get-tuple-element.47), channel_id=1, source_target_pairs={{8,16},{16,8},{14,22},{22,14},{2,4},{4,2},{26,28},{28,26},{10,18},... | collective-permute-start | bytes 294920 | tf_op jit(solution)/shard_map/ppermute | solution.py:524
  63.8 12.6 %collective-permute-start.13 = (bf16[3,64,128]{2,1,0:T(8,128)(2,1)}, bf16[3,64,128]{2,1,0:T(8,128)(2,1)S(1)}, u32[]{:S(2)}, u32[]{:S(2)}) collective-permute-start(bf16[3,64,128]{2,1,0:T(8,128)(2,1)} %get-tuple-element.50), channel_id=1, source_target_pairs={{0,8},{2,10},{4,12},{6,14},{8,0},{10,2},{12,4},{14,6},{16,24},{18,... | collective-permute-start | bytes 147464 | tf_op jit(solution)/shard_map/ppermute | solution.py:524
  66.8 27.5 %copy-start.7 = (bf16[6,64,128]{2,1,0:T(8,128)(2,1)}, bf16[6,64,128]{2,1,0:T(8,128)(2,1)S(1)}, u32[]{:S(2)}) copy-start(bf16[6,64,128]{2,1,0:T(8,128)(2,1)S(1)} %collective-permute-done.9.refs_5_) | copy-start | bytes 294916
  67.8 26.5 %copy-start.8 = (bf16[6,64,128]{2,1,0:T(8,128)(2,1)}, bf16[6,64,128]{2,1,0:T(8,128)(2,1)S(1)}, u32[]{:S(2)}) copy-start(bf16[6,64,128]{2,1,0:T(8,128)(2,1)S(1)} %broadcast_select_fusion.refs_1_) | copy-start | bytes 294916
  67.8 11.3 %collective-permute-start.12 = (bf16[6,64,128]{2,1,0:T(8,128)(2,1)S(1)}, bf16[6,64,128]{2,1,0:T(8,128)(2,1)S(1)}, u32[]{:S(2)}, u32[]{:S(2)}) collective-permute-start(bf16[6,64,128]{2,1,0:T(8,128)(2,1)S(1)} %broadcast_select_fusion.refs_1_), channel_id=1, source_target_pairs={{8,26},{16,28},{14,2},{22,4},{2,14},{4,22},{26,8},{28,16},{0,30},{... | collective-permute-start | bytes 294920 | tf_op jit(solution)/shard_map/ppermute | solution.py:524
  70.3 8.8 %collective-permute-start.11 = (bf16[6,64,128]{2,1,0:T(8,128)(2,1)S(1)}, bf16[6,64,128]{2,1,0:T(8,128)(2,1)S(1)}, u32[]{:S(2)}, u32[]{:S(2)}) collective-permute-start(bf16[6,64,128]{2,1,0:T(8,128)(2,1)S(1)} %broadcast_select_fusion.refs_1_), channel_id=1, source_target_pairs={{8,2},{16,4},{14,26},{22,28},{2,8},{4,16},{26,14},{28,22},{0,24},{... | collective-permute-start | bytes 294920 | tf_op jit(solution)/shard_map/ppermute | solution.py:524
  74.1 5.2 %collective-permute-start.10 = (bf16[6,64,128]{2,1,0:T(8,128)(2,1)S(1)}, bf16[6,64,128]{2,1,0:T(8,128)(2,1)S(1)}, u32[]{:S(2)}, u32[]{:S(2)}) collective-permute-start(bf16[6,64,128]{2,1,0:T(8,128)(2,1)S(1)} %broadcast_select_fusion.refs_1_), channel_id=1, source_target_pairs={{8,14},{16,22},{14,8},{22,16},{2,26},{4,28},{26,2},{28,4},{0,6},{6... | collective-permute-start | bytes 294920 | tf_op jit(solution)/shard_map/ppermute | solution.py:524
  76.4 17.8 %copy-start.16 = (bf16[3,64,128]{2,1,0:T(8,128)(2,1)}, bf16[3,64,128]{2,1,0:T(8,128)(2,1)S(1)}, u32[]{:S(2)}) copy-start(bf16[3,64,128]{2,1,0:T(8,128)(2,1)S(1)} %collective-permute-done.13.refs_6_) | copy-start | bytes 147460
  76.4 2.7 %collective-permute-start.14 = (bf16[3,64,128]{2,1,0:T(8,128)(2,1)}, bf16[3,64,128]{2,1,0:T(8,128)(2,1)S(1)}, u32[]{:S(2)}, u32[]{:S(2)}) collective-permute-start(bf16[3,64,128]{2,1,0:T(8,128)(2,1)} %get-tuple-element.51), channel_id=1, source_target_pairs={{0,2},{2,0},{4,6},{6,4},{8,10},{10,8},{12,14},{14,12},{16,18},{18,... | collective-permute-start | bytes 147464 | tf_op jit(solution)/shard_map/ppermute | solution.py:524
  96.9 6.7 %collective-permute-start.15 = (bf16[13,64,128]{2,1,0:T(8,128)(2,1)}, bf16[13,64,128]{2,1,0:T(8,128)(2,1)S(1)}, u32[]{:S(2)}, u32[]{:S(2)}) collective-permute-start(bf16[13,64,128]{2,1,0:T(8,128)(2,1)} %halo.3.refs_2_.refs_4_), channel_id=1, source_target_pairs={{1,0},{0,1},{3,2},{2,3},{5,4},{4,5},{7,6},{6,7},{9,8},{8,9},{11,10... | collective-permute-start | bytes 638984 | tf_op jit(solution)/shard_map/ppermute | solution.py:465
  (12 other events, 112.7 us)

commit v7 on v5

--- a/solution.py
+++ b/solution.py
@@ -12,6 +12,7 @@
 CALLS = (3,)
 VMEM_LIMIT = 60 * 1024 * 1024
 STRIP_LANE = (96, 0, 32, 64)
+HALF = 48
 
 
 def ring_matrix(col_len):
@@ -80,20 +81,21 @@
 
 def hand_out(plan, steps, packs, corners, outs):
     chosen = iter(plan.chosen_sides())
-    for out in outs[:-1]:
-        for at in range(0, out.shape[0], steps):
+    for out, count, extra in zip(outs, plan.counts, plan.extras):
+        for at in range(count):
             base = next(chosen) * steps
             for q in range(steps):
-                out[at + q] = packs[base + q]
-    packed = plan.pack_corners(corners).astype(jnp.bfloat16)
-    for copy in range(outs[-1].shape[0]):
-        outs[-1][copy] = packed
+                out[at * steps + q] = packs[base + q]
+        if extra is not None:
+            moved = pltpu.roll(corners, extra, 1) if extra else corners
+            out[count * steps] = moved.astype(jnp.bfloat16)
+    outs[-1][0] = corners.astype(jnp.bfloat16)
 
 
 def ring_outs(faces, chan, plan):
     steps = faces // GROUP
-    shapes = [(count * steps, chan, LANES) for count in plan.counts] + [plan.corner_shape(chan)]
-    return [jax.ShapeDtypeStruct(shape, jnp.bfloat16) for shape in shapes]
+    tiles = [n * steps + (extra is not None) for n, extra in zip(plan.counts, plan.extras)]
+    return [jax.ShapeDtypeStruct((n, chan, LANES), jnp.bfloat16) for n in (*tiles, 1)]
 
 
 def rings_kernel(steps, plan, field_ref, ring_ref, cornsel_ref, *refs):
@@ -143,16 +145,14 @@
     )(field, ring, cornsel)
 
 
-def halo_kernel(faces, units, unit, plan, *refs):
+def halo_kernel(faces, units, unit, *refs):
     table, tile_refs, (rev_ref, halo_ref, pool, turn_acc) = (refs[0], refs[1:-4], refs[-4:])
     chan = halo_ref.shape[1]
     lane = lane_iota((chan, LANES))
     at = 0
-    for ref in tile_refs[:-1]:
+    for ref in tile_refs:
         pool[at : at + ref.shape[0]] = ref[...]
         at += ref.shape[0]
-    for k in range(tile_refs[-1].shape[0]):
-        pool[at + k] = plan.unpack_corners(tile_refs[-1][k])
     corner_tile = jnp.zeros((chan, LANES), jnp.float32)
     most = max(units)
     rows = 4 * most
@@ -183,13 +183,13 @@
     halo_ref[faces] = corner_tile.astype(jnp.bfloat16)
 
 
-def assemble_halo(plan, table, tiles, rev, faces, units, unit):
+def assemble_halo(table, tiles, rev, faces, units, unit):
     chan = tiles[0].shape[1]
     halo = jax.ShapeDtypeStruct((faces + 1, chan, LANES), jnp.bfloat16)
     vmem = pl.BlockSpec(memory_space=pltpu.VMEM)
     smem = pl.BlockSpec(memory_space=pltpu.SMEM)
     return pl.pallas_call(
-        lambda *refs: halo_kernel(faces, units, unit, plan, *refs),
+        lambda *refs: halo_kernel(faces, units, unit, *refs),
         in_specs=[smem] + [vmem] * (len(tiles) + 1),
         out_specs=vmem,
         out_shape=halo,
@@ -475,21 +475,11 @@
 
 class SquareHalo(Place):
     counts = (2, 1, 1, 2)
+    extras = (None, 0, HALF, None)
 
     def __init__(self, quads):
         self.quads = quads
-
-    def corner_shape(self, chan):
-        return (16, chan // 2, LANES)
-
-    def pack_corners(self, corners):
-        half = corners.shape[0] // 2
-        return corners[:half] + pltpu.roll(corners[half:], LANES // 2, 1)
-
-    def unpack_corners(self, packed):
-        upper = packed.astype(jnp.float32)
-        both = jnp.concatenate([upper, pltpu.roll(upper, LANES // 2, 1)], axis=0)
-        return both.astype(jnp.bfloat16)
+        self.span = 2 * quads + 1
 
     def roles(self):
         row_pos, col_pos = self.place()
@@ -532,63 +522,101 @@
         paired = swap(pair, beside)
         near_col = swap(col_side, [((x, y), (x ^ 1, y)) for x, y in every])
         near_row = swap(row_side, [((x, y), (x, y ^ 1)) for x, y in every])
-        _, _, middle, _, seg = self.roles()
-        slot = lax.broadcasted_iota(jnp.int32, (2 * self.quads, 1, 1), 0) // self.quads
-        lines = jnp.where(middle & (slot != seg - 1), paired, lines)
+        small = lambda pairs: swap(corner, pairs)
+        diagonal = [
+            small([((x, y), (x ^ 1, y ^ 1)) for x, y in every]),
+            small([((x, y), (3 - x, y ^ 1)) for x, y in every if x in (1, 2)]),
+            small([((x, y), (x ^ 1, 3 - y)) for x, y in every if y in (1, 2)]),
+            small([((x, y), (3 - x, 3 - y)) for x, y in every if x in (1, 2) and y in (1, 2)]),
+        ]
+        lines = self.line_message(lines, paired, near_col, near_row)
         across = []
         for j in (1, 2, 3):
-            pairs = [(spot(side, k), spot(side ^ j, k)) for side in range(4) for k in (1, 2)]
+            pairs = [
+                (spot(side, k), spot(side ^ j, k if j == 3 else 3 - k))
+                for side in range(4)
+                for k in (1, 2)
+            ]
             pairs += [(corners[c], corners[c ^ j]) for c in range(4)]
             if j == 1:
                 pairs += [((x, y), (x, 3 - y)) for x in (1, 2) for y in (1, 2)]
             across.append(swap(lines, pairs))
-        corner, across[0] = lax.optimization_barrier((corner, across[0]))
-        ends_of = lax.all_to_all(corner, axes, 0, 0, tiled=True)
-        return [lines, *across, paired, near_col, near_row, ends_of]
+        return [lines, *across, paired, near_col, near_row, *diagonal]
+
+    def line_message(self, *parts):
+        vmem = pl.BlockSpec(memory_space=pltpu.VMEM)
+
+        def kernel(lines_ref, paired_ref, col_ref, row_ref, out_ref):
+            _, _, middle, _, seg = self.roles()
+            for at in range(2 * self.quads):
+                theirs = middle & (seg - 1 != at // self.quads)
+                out_ref[at] = jnp.where(theirs, paired_ref[at], lines_ref[at])
+            out_ref[2 * self.quads] = col_ref[self.quads] + row_ref[self.quads]
+
+        return pl.pallas_call(
+            kernel,
+            in_specs=[vmem] * 4,
+            out_specs=vmem,
+            out_shape=jax.ShapeDtypeStruct((self.span, *parts[0].shape[1:]), jnp.bfloat16),
+            compiler_params=pltpu.CompilerParams(vmem_limit_bytes=VMEM_LIMIT),
+            name="lines",
+        )(*parts)
+
+    def owner(self, s, k):
+        far = jnp.where(k >= 2, 1, 0)
+        return jnp.where(s < 2, 2 * far + s, 2 * (s - 2) + far)
+
+    def me(self):
+        row_pos, col_pos = self.place()
+        return jnp.where(row_pos > 0, 2, 0) + jnp.where(col_pos > 0, 1, 0)
 
     def strip_cell(self, g, s, at):
-        row_pos, col_pos = self.place()
         _, corner, _, side, _ = self.roles()
-        slot = 2 * self.quads
         k = at // RB
-        me = jnp.where(row_pos > 0, 2, 0) + jnp.where(col_pos > 0, 1, 0)
-        far = jnp.where(k > 0, 1, 0)
-        owner = jnp.where(s < 2, 2 * far + s, 2 * (s - 2) + far)
-        at_corner = (me ^ owner) * slot + (s // 2) * self.quads
-        at_middle = (side ^ s) * slot + (k - 1) * self.quads
+        at_corner = (self.me() ^ self.owner(s, k)) * self.span + (s // 2) * self.quads
+        at_middle = (side ^ s) * self.span + (k - 1) * self.quads
         return (jnp.where(corner, at_corner, at_middle) + g // GROUP, (g % GROUP) * 32)
 
     def near_cell(self, edge, face):
         row_pos, col_pos = self.place()
         px_end, _, _, _, seg = self.roles()
-        slot = 2 * self.quads
-        paired = 4 * slot + (seg - 1) * self.quads
-        near_col, near_row = (5 * slot, 5 * slot + self.quads)
+        paired = 4 * self.span + (seg - 1) * self.quads
+        near_col = 4 * self.span + 2 * self.quads
+        near_row = near_col + self.quads + 1
         by_col = jnp.where(row_pos % 2 == 3 - edge, near_col, paired)
-        by_row = jnp.where(col_pos % 2 == 1 - edge, near_row, jnp.where(px_end, paired, slot))
+        rest = jnp.where(px_end, paired, self.span)
+        by_row = jnp.where(col_pos % 2 == 1 - edge, near_row, rest)
         return jnp.where(edge < 2, by_row, by_col) + face // GROUP
 
     def corner_cell(self, g, s, at):
-        seg, hi = (at // RB, jnp.where(at % RB == 0, 0, 1))
-        owner = jnp.where(s < 2, seg * 4 + 3 * s, 12 * (s - 2) + seg)
+        _, corner, _, side, seg = self.roles()
+        k, hi = (at // RB, jnp.where(at % RB == 0, 0, 1))
+        end = (k == 0) | (k == 3)
+        line_tile, line_lane = self.strip_cell(g, s, at)
+        owner = self.owner(s, k)
+        source = self.me() ^ owner
+        half = jnp.where(s < 2, 0, HALF)
+        for j in range(4):
+            their_side = side ^ j
+            their_seg = seg if j in (0, 3) else 3 - seg
+            hit = jnp.logical_not(corner) & (self.owner(their_side, their_seg) == owner)
+            source = jnp.where(hit, j, source)
+            half = jnp.where(hit, jnp.where(their_side < 2, 0, HALF), half)
         q = jnp.where(s < 2, 2 * s + hi, s - 2 + 2 * hi)
-        return (12 * self.quads + owner, g * 4 + q)
+        in_line = (corner & end) | jnp.logical_not(corner | end)
+        tile = jnp.where(in_line, line_tile, source * self.span + 2 * self.quads)
+        return (tile, jnp.where(in_line, line_lane + at % RB, half + g * 4 + q))
 
     def diagonal_cell(self, face, q, px, py):
-        return (12 * self.quads + px * 4 + py, face * 4 + q)
+        row_pos, col_pos = self.place()
+        far = jnp.where(px == (row_pos ^ 1), 0, 1) + jnp.where(py == (col_pos ^ 1), 0, 2)
+        return (4 * self.span + 4 * self.quads + 2 + far, face * 4 + q)
 
 
 class GatheredHalo(Place):
     counts = (1, 1, 1, 1, 2)
 
-    def corner_shape(self, chan):
-        return (1, chan, LANES)
-
-    def pack_corners(self, corners):
-        return corners
-
-    def unpack_corners(self, packed):
-        return packed
+    extras = (None,) * 5
 
     def __init__(self, quads, px_count, py_count, col_len):
         self.quads = quads
@@ -644,7 +672,7 @@
     cornsel = jnp.asarray(corner_matrix(), jnp.bfloat16)
     spread = jnp.asarray(spread_matrix(col_len), jnp.bfloat16)
     rev = jnp.asarray(reverse_matrix(unit), jnp.bfloat16)
-    if px_count == py_count == 4 and col_len == RB and chan % 32 == 0:
+    if px_count == py_count == 4 and col_len == RB and 4 * faces <= HALF:
         plan = SquareHalo(faces // GROUP)
     else:
         plan = GatheredHalo(faces // GROUP, px_count, py_count, col_len)
@@ -657,7 +685,7 @@
         plan, edge_table, corner_table, weight, chan, (px_count, py_count), col_len, unit
     )
     tiles = plan.exchange(*parts)
-    halo = assemble_halo(plan, table, tiles, rev, faces, units, unit)
+    halo = assemble_halo(table, tiles, rev, faces, units, unit)
     halos = from_others(halo, ch_count)
     old, chunks, first = ([], [], 0)
     for count in CALLS:
@@ -669,7 +697,7 @@
         first += count
 
     tiles = plan.exchange(*parts)
-    halo = assemble_halo(plan, table, tiles, rev, faces, units, unit)
+    halo = assemble_halo(table, tiles, rev, faces, units, unit)
     halos = from_others(halo, ch_count)
     grad = None
     for first, fields in chunks:

time: 115 us -> 116 us (level)
  waiting for transfers between devices: 28.4 us -> 17.2 us
  starting transfers between devices: 50.9 us -> 60.4 us
  Pallas kernels: 28.2 us -> 31.3 us
  other arithmetic: 2.03 us -> 0 us
  local copies, waits for them, and re-layouts: 4.35 us -> 5.71 us
    ppermute x12 -> x20, starting transfers between devices: 19.9 us -> 54.4 us  [exchange(): lax.ppermute(array, axes, [(a[0] * 4 + a[1], b[0] * 4 + b[1]) for a, b in...]
    all_to_all x2 -> x0, starting transfers between devices: 25.4 us -> none  [exchange(): ends_of = lax.all_to_all(corner, axes, 0, 0, tiled=True)]
    ppermute x12 -> x20, waiting for transfers between devices: 18.3 us -> 7.09 us  [exchange(): lax.ppermute(array, axes, [(a[0] * 4 + a[1], b[0] * 4 + b[1]) for a, b in...]
    pallas_call x2 -> x4, Pallas kernels: 5.2 us -> 8.46 us  [the longest x2 5.17 us: assemble_halo(): pl.pallas_call(lambda *refs: halo_kernel(faces, units, unit, *refs), in_s...]
    select_n x2 -> x0, other arithmetic: 2.02 us -> none  [exchange(): lines = jnp.where(middle & (slot != seg - 1), paired, lines)]
    unnamed x40 -> x48, local copies, waits for them, and re-layouts: 4.35 us -> 5.71 us
  transfers between devices with their start and end apart: 18 -> 24, of which waited for: 8 -> 5; matrix products, arithmetic and copies ran while one was open for 2% -> 0% of each run, Pallas kernels for 10% -> 13%
where the time goes in v7:
time: 116 us
  starting transfers between devices  60.4 us (52%)
  Pallas kernels  31.3 us (27%)
  waiting for transfers between devices  17.2 us (15%)
  local copies, waits for them, and re-layouts  5.71 us (5%)
    ppermute x20, starting transfers between devices, exchange(): lax.ppermute(array, axes, [(a[0] * 4 + a[1], b[0] * 4 + b[1]) for a, b in...  54.4 us
    ppermute x4, waiting for transfers between devices, from_others(): lax.ppermute(array, 'ch', [((i + k) % ch_count, i) for i in range(ch_coun...  10.2 us
    pallas_call x1, Pallas kernels, forward(): pl.pallas_call(lambda *refs: forward_kernel(first, count, steps, pieces,...  9.4 us
    pallas_call x1, Pallas kernels, backward(): pl.pallas_call(lambda *refs: backward_kernel(first, pieces, *refs), grid=...  7.29 us
    ppermute x20, waiting for transfers between devices, exchange(): lax.ppermute(array, axes, [(a[0] * 4 + a[1], b[0] * 4 + b[1]) for a, b in...  7.09 us
    ppermute x4, starting transfers between devices, from_others(): lax.ppermute(array, 'ch', [((i + k) % ch_count, i) for i in range(ch_coun...  5.94 us
    unnamed x48, local copies, waits for them, and re-layouts  5.71 us
    pallas_call x2, Pallas kernels, assemble_halo(): pl.pallas_call(lambda *refs: halo_kernel(faces, units, unit, *refs), in_s...  5.17 us
  transfers between devices with their start and end apart: 24, of which 5 were waited for; matrix products, arithmetic and copies ran while one was open for 0% of the time, Pallas kernels for 13%

profile of v7, /device:TPU:0, one launch (start us, length us, event | category | flops | bytes accessed | tf_op | source)
XLA Modules:
  0.0 115.7 jit_solution(14722777539504993173)
XLA Ops:
  0.6 3.0 %collective-permute-start = (bf16[12,64,1024]{2,1,0:T(8,128)(2,1)}, bf16[12,64,1024]{2,1,0:T(8,128)(2,1)S(1)}, u32[]{:S(2)}, u32[]{:S(2)}) collective-permute-start(bf16[12,64,1024]{2,1,0:T(8,128)(2,1)} %bitcast.18), channel_id=1, source_target_pairs={{1,0},{0,1},{3,2},{2,3},{5,4},{4,5},{7,6},{6,7},{9,8},{8,9},{11,10... | collective-permute-start | bytes 4718600 | tf_op jit(solution)/shard_map/ppermute | solution.py:465
  3.6 4.0 %rings.1 = (bf16[6,64,128]{2,1,0:T(8,128)(2,1)}, bf16[4,64,128]{2,1,0:T(8,128)(2,1)}, bf16[4,64,128]{2,1,0:T(8,128)(2,1)}, bf16[6,64,128]{2,1,0:T(8,128)(2,1)}, bf16[1,64,128]{2,1,0:T(8,128)(2,1)}) custom-call(bf16[12,64,1024]{2,1,0:T(8,128)(2,1)} %bitcast.19, bf16[1024,128]{1,0:T(8,128)(2,1)} %constant.8.clone.refs_1_.refs_9_, ...), custom_call_target="tpu_custom_call" | custom-call | tf_op jit(solution)/shard_map/rings/pallas_call | solution.py:129
  8.3 4.5 %collective-permute-start.2 = (bf16[4,64,128]{2,1,0:T(8,128)(2,1)}, bf16[4,64,128]{2,1,0:T(8,128)(2,1)S(1)}, u32[]{:S(2)}, u32[]{:S(2)}) collective-permute-start(bf16[4,64,128]{2,1,0:T(8,128)(2,1)} %get-tuple-element.20), channel_id=1, source_target_pairs={{0,8},{2,10},{4,12},{6,14},{8,0},{10,2},{12,4},{14,6},{16,24},{18,... | collective-permute-start | bytes 196616 | tf_op jit(solution)/shard_map/ppermute | solution.py:514
  12.7 2.7 %collective-permute-done.2.col_ref.refs_6_ = bf16[4,64,128]{2,1,0:T(8,128)(2,1)S(1)} collective-permute-done((bf16[4,64,128]{2,1,0:T(8,128)(2,1)}, bf16[4,64,128]{2,1,0:T(8,128)(2,1)S(1)}, u32[]{:S(2)}, u32[]{:S(2)}) %collective-permute-start.2) | collective-permute-done | bytes 65568 | tf_op jit(solution)/shard_map/ppermute | solution.py:514
  16.1 1.6 %lines.2.refs_1_ = bf16[7,64,128]{2,1,0:T(8,128)(2,1)} custom-call(bf16[6,64,128]{2,1,0:T(8,128)(2,1)} %get-tuple-element.18.lines_ref, bf16[6,64,128]{2,1,0:T(8,128)(2,1)} %copy-done.4, bf16[4,64,128]{2,1,0:T(8,128)(2,1)} %copy-done.6, bf16[4,64,128]{2,1,0:T(8,128)(2,1)} %copy-done.7), custom_call_target="tpu_custom_call" | custom-call | tf_op jit(solution)/shard_map/lines/pallas_call | solution.py:556
  17.7 2.7 %collective-permute-start.6 = (bf16[7,64,128]{2,1,0:T(8,128)(2,1)}, bf16[7,64,128]{2,1,0:T(8,128)(2,1)S(1)}, u32[]{:S(2)}, u32[]{:S(2)}) collective-permute-start(bf16[7,64,128]{2,1,0:T(8,128)(2,1)} %lines.2.refs_1_), channel_id=1, source_target_pairs={{8,26},{16,28},{14,2},{22,4},{2,14},{4,22},{26,8},{28,16},{0,30},{... | collective-permute-start | bytes 344072 | tf_op jit(solution)/shard_map/ppermute | solution.py:514
  20.5 4.4 %collective-permute-start.5 = (bf16[7,64,128]{2,1,0:T(8,128)(2,1)}, bf16[7,64,128]{2,1,0:T(8,128)(2,1)S(1)}, u32[]{:S(2)}, u32[]{:S(2)}) collective-permute-start(bf16[7,64,128]{2,1,0:T(8,128)(2,1)} %lines.2.refs_1_), channel_id=1, source_target_pairs={{8,4},{16,2},{14,28},{22,26},{2,16},{4,8},{26,22},{28,14},{0,24},{... | collective-permute-start | bytes 344072 | tf_op jit(solution)/shard_map/ppermute | solution.py:514
  28.4 14.1 %collective-permute-start.7 = (bf16[1,64,128]{2,1,0:T(8,128)(2,1)}, bf16[1,64,128]{2,1,0:T(8,128)(2,1)S(1)}, u32[]{:S(2)}, u32[]{:S(2)}) collective-permute-start(bf16[1,64,128]{2,1,0:T(8,128)(2,1)} %get-tuple-element.22), channel_id=1, source_target_pairs={{0,10},{2,8},{4,14},{6,12},{8,2},{10,0},{12,6},{14,4},{16,26},{18,... | collective-permute-start | bytes 49160 | tf_op jit(solution)/shard_map/ppermute | solution.py:514
  42.5 2.2 %setup.1 = (s32[20,12]{1,0:T(8,128)}, bf16[192,384]{1,0:T(8,128)(2,1)}, bf16[192,384]{1,0:T(8,128)(2,1)}) custom-call(s32[3,4,12]{2,1,0:T(4,128)} %bitcast.23, s32[4,2,12]{2,1,0:T(2,128)} %bitcast.24, bf16[3,3,128,128]{3,2,1,0:T(8,128)(2,1)} %refs_2_.2), custom_call_target="tpu_custom_call" | custom-call | tf_op jit(solution)/shard_map/setup/pallas_call | solution.py:452
  45.4 2.6 %halo.2.refs_2_.refs_4_ = bf16[13,64,128]{2,1,0:T(8,128)(2,1)} custom-call(s32[20,12]{1,0:T(8,128)} %get-tuple-element.17.refs_0_, bf16[7,64,128]{2,1,0:T(8,128)(2,1)} %lines.2.refs_1_, bf16[7,64,128]{2,1,0:T(8,128)(2,1)} %copy-done.13, bf16[7,64,128]{2,1,0:T(8,128)(2,1)} %copy-done.11, bf16[7,64,128]{2,1,0:T(8,128)(2,1)} %copy-done.10, ...), custom_call_target="tpu_custom_call" | custom-call | tf_op jit(solution)/shard_map/halo/pallas_call | solution.py:191
  48.6 5.5 %collective-permute-done.11.refs_3_.refs_5_ = bf16[13,64,128]{2,1,0:T(8,128)(2,1)S(1)} collective-permute-done((bf16[13,64,128]{2,1,0:T(8,128)(2,1)}, bf16[13,64,128]{2,1,0:T(8,128)(2,1)S(1)}, u32[]{:S(2)}, u32[]{:S(2)}) %collective-permute-start.11) | collective-permute-done | bytes 213024 | tf_op jit(solution)/shard_map/ppermute | solution.py:465
  55.3 9.4 %forward.1 = (bf16[12,64,1024]{2,1,0:T(8,128)(2,1)}, bf16[12,64,1024]{2,1,0:T(8,128)(2,1)}, bf16[6,64,128]{2,1,0:T(8,128)(2,1)}, bf16[4,64,128]{2,1,0:T(8,128)(2...) custom-call(bf16[12,64,1024]{2,1,0:T(8,128)(2,1)} %bitcast.20, ...), custom_call_target="tpu_custom_call" | custom-call | tf_op jit(solution)/shard_map/forward/pallas_call | solution.py:318
  66.0 2.7 %collective-permute-start.14 = (bf16[4,64,128]{2,1,0:T(8,128)(2,1)}, bf16[4,64,128]{2,1,0:T(8,128)(2,1)S(1)}, u32[]{:S(2)}, u32[]{:S(2)}) collective-permute-start(bf16[4,64,128]{2,1,0:T(8,128)(2,1)} %get-tuple-element.28), channel_id=1, source_target_pairs={{0,8},{2,10},{4,12},{6,14},{8,0},{10,2},{12,4},{14,6},{16,24},{18,... | collective-permute-start | bytes 196616 | tf_op jit(solution)/shard_map/ppermute | solution.py:514
  68.7 2.7 %collective-permute-done.14.col_ref.refs_6_ = bf16[4,64,128]{2,1,0:T(8,128)(2,1)S(1)} collective-permute-done((bf16[4,64,128]{2,1,0:T(8,128)(2,1)}, bf16[4,64,128]{2,1,0:T(8,128)(2,1)S(1)}, u32[]{:S(2)}, u32[]{:S(2)}) %collective-permute-start.14) | collective-permute-done | bytes 65568 | tf_op jit(solution)/shard_map/ppermute | solution.py:514
  72.1 1.6 %lines.3.refs_1_ = bf16[7,64,128]{2,1,0:T(8,128)(2,1)} custom-call(bf16[6,64,128]{2,1,0:T(8,128)(2,1)} %get-tuple-element.26.lines_ref, bf16[6,64,128]{2,1,0:T(8,128)(2,1)} %copy-done.5, bf16[4,64,128]{2,1,0:T(8,128)(2,1)} %copy-done.8, bf16[4,64,128]{2,1,0:T(8,128)(2,1)} %copy-done.9), custom_call_target="tpu_custom_call" | custom-call | tf_op jit(solution)/shard_map/lines/pallas_call | solution.py:556
  73.7 1.9 %collective-permute-start.18 = (bf16[7,64,128]{2,1,0:T(8,128)(2,1)}, bf16[7,64,128]{2,1,0:T(8,128)(2,1)S(1)}, u32[]{:S(2)}, u32[]{:S(2)}) collective-permute-start(bf16[7,64,128]{2,1,0:T(8,128)(2,1)} %lines.3.refs_1_), channel_id=1, source_target_pairs={{8,26},{16,28},{14,2},{22,4},{2,14},{4,22},{26,8},{28,16},{0,30},{... | collective-permute-start | bytes 344072 | tf_op jit(solution)/shard_map/ppermute | solution.py:514
  75.6 4.2 %collective-permute-start.17 = (bf16[7,64,128]{2,1,0:T(8,128)(2,1)}, bf16[7,64,128]{2,1,0:T(8,128)(2,1)S(1)}, u32[]{:S(2)}, u32[]{:S(2)}) collective-permute-start(bf16[7,64,128]{2,1,0:T(8,128)(2,1)} %lines.3.refs_1_), channel_id=1, source_target_pairs={{8,4},{16,2},{14,28},{22,26},{2,16},{4,8},{26,22},{28,14},{0,24},{... | collective-permute-start | bytes 344072 | tf_op jit(solution)/shard_map/ppermute | solution.py:514
  79.8 2.5 %collective-permute-start.16 = (bf16[7,64,128]{2,1,0:T(8,128)(2,1)}, bf16[7,64,128]{2,1,0:T(8,128)(2,1)S(1)}, u32[]{:S(2)}, u32[]{:S(2)}) collective-permute-start(bf16[7,64,128]{2,1,0:T(8,128)(2,1)} %lines.3.refs_1_), channel_id=1, source_target_pairs={{8,22},{16,14},{14,16},{22,8},{2,28},{4,26},{26,4},{28,2},{0,6},{6... | collective-permute-start | bytes 344072 | tf_op jit(solution)/shard_map/ppermute | solution.py:514
  84.4 10.7 %collective-permute-start.19 = (bf16[1,64,128]{2,1,0:T(8,128)(2,1)}, bf16[1,64,128]{2,1,0:T(8,128)(2,1)S(1)}, u32[]{:S(2)}, u32[]{:S(2)}) collective-permute-start(bf16[1,64,128]{2,1,0:T(8,128)(2,1)} %get-tuple-element.30), channel_id=1, source_target_pairs={{0,10},{2,8},{4,14},{6,12},{8,2},{10,0},{12,6},{14,4},{16,26},{18,... | collective-permute-start | bytes 49160 | tf_op jit(solution)/shard_map/ppermute | solution.py:514
  95.1 1.7 %collective-permute-done.19.refs_8_ = bf16[1,64,128]{2,1,0:T(8,128)(2,1)S(1)} collective-permute-done((bf16[1,64,128]{2,1,0:T(8,128)(2,1)}, bf16[1,64,128]{2,1,0:T(8,128)(2,1)S(1)}, u32[]{:S(2)}, u32[]{:S(2)}) %collective-permute-start.19) | collective-permute-done | bytes 16416 | tf_op jit(solution)/shard_map/ppermute | solution.py:514
  98.1 2.6 %halo.3.refs_2_.refs_4_ = bf16[13,64,128]{2,1,0:T(8,128)(2,1)} custom-call(s32[20,12]{1,0:T(8,128)} %get-tuple-element.17.refs_0_, bf16[7,64,128]{2,1,0:T(8,128)(2,1)} %lines.3.refs_1_, bf16[7,64,128]{2,1,0:T(8,128)(2,1)} %copy-done.15, bf16[7,64,128]{2,1,0:T(8,128)(2,1)} %copy-done.14, bf16[7,64,128]{2,1,0:T(8,128)(2,1)} %copy-done.12, ...), custom_call_target="tpu_custom_call" | custom-call | tf_op jit(solution)/shard_map/halo/pallas_call | solution.py:191
  100.7 1.8 %collective-permute-start.23 = (bf16[13,64,128]{2,1,0:T(8,128)(2,1)}, bf16[13,64,128]{2,1,0:T(8,128)(2,1)S(1)}, u32[]{:S(2)}, u32[]{:S(2)}) collective-permute-start(bf16[13,64,128]{2,1,0:T(8,128)(2,1)} %halo.3.refs_2_.refs_4_), channel_id=1, source_target_pairs={{1,0},{0,1},{3,2},{2,3},{5,4},{4,5},{7,6},{6,7},{9,8},{8,9},{11,10... | collective-permute-start | bytes 638984 | tf_op jit(solution)/shard_map/ppermute | solution.py:465
  102.5 4.6 %collective-permute-done.23.refs_3_.refs_5_ = bf16[13,64,128]{2,1,0:T(8,128)(2,1)S(1)} collective-permute-done((bf16[13,64,128]{2,1,0:T(8,128)(2,1)}, bf16[13,64,128]{2,1,0:T(8,128)(2,1)S(1)}, u32[]{:S(2)}, u32[]{:S(2)}) %collective-permute-start.23) | collective-permute-done | bytes 213024 | tf_op jit(solution)/shard_map/ppermute | solution.py:465
  108.4 7.3 %backward.1 = bf16[12,64,1024]{2,1,0:T(8,128)(2,1)} custom-call(bf16[12,64,1024]{2,1,0:T(8,128)(2,1)} %get-tuple-element.25.refs_0_, bf16[12,64,1024]{2,1,0:T(8,128)(2,1)} %copy-done.1, bf16[13,64,128]{2,1,0:T(8,128)(2,1)} %halo.3.refs_2_.refs_4_, bf16[13,64,128]{2,1,0:T(8,128)(2,1)} %copy-done.3, bf16[13,64,128]{2,1,0:T(8,128)(2,1)} %halo.3.refs_2_.refs_4_, ...), custom_call_target="tpu_custom_call" | custom-call | tf_op jit(solution)/shard_map/backward/pallas_call | solution.py:355
  (80 shorter events, 13.7 us)
Async XLA Ops:
  0.6 53.5 %collective-permute-start = (bf16[12,64,1024]{2,1,0:T(8,128)(2,1)}, bf16[12,64,1024]{2,1,0:T(8,128)(2,1)S(1)}, u32[]{:S(2)}, u32[]{:S(2)}) collective-permute-start(bf16[12,64,1024]{2,1,0:T(8,128)(2,1)} %bitcast.18), channel_id=1, source_target_pairs={{1,0},{0,1},{3,2},{2,3},{5,4},{4,5},{7,6},{6,7},{9,8},{8,9},{11,10... | collective-permute-start | bytes 4718600 | tf_op jit(solution)/shard_map/ppermute | solution.py:465
  7.6 7.8 %collective-permute-start.1 = (bf16[6,64,128]{2,1,0:T(8,128)(2,1)}, bf16[6,64,128]{2,1,0:T(8,128)(2,1)S(1)}, u32[]{:S(2)}, u32[]{:S(2)}) collective-permute-start(bf16[6,64,128]{2,1,0:T(8,128)(2,1)} %get-tuple-element.19), channel_id=1, source_target_pairs={{8,16},{16,8},{14,22},{22,14},{2,4},{4,2},{26,28},{28,26},{10,18},... | collective-permute-start | bytes 294920 | tf_op jit(solution)/shard_map/ppermute | solution.py:514
  8.3 7.1 %collective-permute-start.2 = (bf16[4,64,128]{2,1,0:T(8,128)(2,1)}, bf16[4,64,128]{2,1,0:T(8,128)(2,1)S(1)}, u32[]{:S(2)}, u32[]{:S(2)}) collective-permute-start(bf16[4,64,128]{2,1,0:T(8,128)(2,1)} %get-tuple-element.20), channel_id=1, source_target_pairs={{0,8},{2,10},{4,12},{6,14},{8,0},{10,2},{12,4},{14,6},{16,24},{18,... | collective-permute-start | bytes 196616 | tf_op jit(solution)/shard_map/ppermute | solution.py:514
  12.7 2.7 %collective-permute-start.3 = (bf16[4,64,128]{2,1,0:T(8,128)(2,1)}, bf16[4,64,128]{2,1,0:T(8,128)(2,1)S(1)}, u32[]{:S(2)}, u32[]{:S(2)}) collective-permute-start(bf16[4,64,128]{2,1,0:T(8,128)(2,1)} %get-tuple-element.21), channel_id=1, source_target_pairs={{0,2},{2,0},{4,6},{6,4},{8,10},{10,8},{12,14},{14,12},{16,18},{18,... | collective-permute-start | bytes 196616 | tf_op jit(solution)/shard_map/ppermute | solution.py:514
  17.7 27.0 %collective-permute-start.6 = (bf16[7,64,128]{2,1,0:T(8,128)(2,1)}, bf16[7,64,128]{2,1,0:T(8,128)(2,1)S(1)}, u32[]{:S(2)}, u32[]{:S(2)}) collective-permute-start(bf16[7,64,128]{2,1,0:T(8,128)(2,1)} %lines.2.refs_1_), channel_id=1, source_target_pairs={{8,26},{16,28},{14,2},{22,4},{2,14},{4,22},{26,8},{28,16},{0,30},{... | collective-permute-start | bytes 344072 | tf_op jit(solution)/shard_map/ppermute | solution.py:514
  20.5 24.3 %collective-permute-start.5 = (bf16[7,64,128]{2,1,0:T(8,128)(2,1)}, bf16[7,64,128]{2,1,0:T(8,128)(2,1)S(1)}, u32[]{:S(2)}, u32[]{:S(2)}) collective-permute-start(bf16[7,64,128]{2,1,0:T(8,128)(2,1)} %lines.2.refs_1_), channel_id=1, source_target_pairs={{8,4},{16,2},{14,28},{22,26},{2,16},{4,8},{26,22},{28,14},{0,24},{... | collective-permute-start | bytes 344072 | tf_op jit(solution)/shard_map/ppermute | solution.py:514
  24.9 19.9 %collective-permute-start.4 = (bf16[7,64,128]{2,1,0:T(8,128)(2,1)}, bf16[7,64,128]{2,1,0:T(8,128)(2,1)S(1)}, u32[]{:S(2)}, u32[]{:S(2)}) collective-permute-start(bf16[7,64,128]{2,1,0:T(8,128)(2,1)} %lines.2.refs_1_), channel_id=1, source_target_pairs={{8,22},{16,14},{14,16},{22,8},{2,28},{4,26},{26,4},{28,2},{0,6},{6... | collective-permute-start | bytes 344072 | tf_op jit(solution)/shard_map/ppermute | solution.py:514
  26.4 0.7 collective-permute-start.10
  27.0 0.7 collective-permute-start.9
  27.7 0.7 collective-permute-start.8
  28.4 16.3 %collective-permute-start.7 = (bf16[1,64,128]{2,1,0:T(8,128)(2,1)}, bf16[1,64,128]{2,1,0:T(8,128)(2,1)S(1)}, u32[]{:S(2)}, u32[]{:S(2)}) collective-permute-start(bf16[1,64,128]{2,1,0:T(8,128)(2,1)} %get-tuple-element.22), channel_id=1, source_target_pairs={{0,10},{2,8},{4,14},{6,12},{8,2},{10,0},{12,6},{14,4},{16,26},{18,... | collective-permute-start | bytes 49160 | tf_op jit(solution)/shard_map/ppermute | solution.py:514
  48.0 6.1 %collective-permute-start.11 = (bf16[13,64,128]{2,1,0:T(8,128)(2,1)}, bf16[13,64,128]{2,1,0:T(8,128)(2,1)S(1)}, u32[]{:S(2)}, u32[]{:S(2)}) collective-permute-start(bf16[13,64,128]{2,1,0:T(8,128)(2,1)} %halo.2.refs_2_.refs_4_), channel_id=1, source_target_pairs={{1,0},{0,1},{3,2},{2,3},{5,4},{4,5},{7,6},{6,7},{9,8},{8,9},{11,10... | collective-permute-start | bytes 638984 | tf_op jit(solution)/shard_map/ppermute | solution.py:465
  64.7 42.5 %collective-permute-start.12 = (bf16[12,64,1024]{2,1,0:T(8,128)(2,1)}, bf16[12,64,1024]{2,1,0:T(8,128)(2,1)S(1)}, u32[]{:S(2)}, u32[]{:S(2)}) collective-permute-start(bf16[12,64,1024]{2,1,0:T(8,128)(2,1)} %get-tuple-element.25.refs_0_), channel_id=1, source_target_pairs={{1,0},{0,1},{3,2},{2,3},{5,4},{4,5},{7,6},{6,7},{9,8},{8,9},{11,10... | collective-permute-start | bytes 4718600 | tf_op jit(solution)/shard_map/ppermute | solution.py:465
  65.3 6.1 %collective-permute-start.13 = (bf16[6,64,128]{2,1,0:T(8,128)(2,1)}, bf16[6,64,128]{2,1,0:T(8,128)(2,1)S(1)}, u32[]{:S(2)}, u32[]{:S(2)}) collective-permute-start(bf16[6,64,128]{2,1,0:T(8,128)(2,1)} %get-tuple-element.27), channel_id=1, source_target_pairs={{8,16},{16,8},{14,22},{22,14},{2,4},{4,2},{26,28},{28,26},{10,18},... | collective-permute-start | bytes 294920 | tf_op jit(solution)/shard_map/ppermute | solution.py:514
  66.0 5.4 %collective-permute-start.14 = (bf16[4,64,128]{2,1,0:T(8,128)(2,1)}, bf16[4,64,128]{2,1,0:T(8,128)(2,1)S(1)}, u32[]{:S(2)}, u32[]{:S(2)}) collective-permute-start(bf16[4,64,128]{2,1,0:T(8,128)(2,1)} %get-tuple-element.28), channel_id=1, source_target_pairs={{0,8},{2,10},{4,12},{6,14},{8,0},{10,2},{12,4},{14,6},{16,24},{18,... | collective-permute-start | bytes 196616 | tf_op jit(solution)/shard_map/ppermute | solution.py:514
  68.7 2.7 %collective-permute-start.15 = (bf16[4,64,128]{2,1,0:T(8,128)(2,1)}, bf16[4,64,128]{2,1,0:T(8,128)(2,1)S(1)}, u32[]{:S(2)}, u32[]{:S(2)}) collective-permute-start(bf16[4,64,128]{2,1,0:T(8,128)(2,1)} %get-tuple-element.29), channel_id=1, source_target_pairs={{0,2},{2,0},{4,6},{6,4},{8,10},{10,8},{12,14},{14,12},{16,18},{18,... | collective-permute-start | bytes 196616 | tf_op jit(solution)/shard_map/ppermute | solution.py:514
  73.7 23.1 %collective-permute-start.18 = (bf16[7,64,128]{2,1,0:T(8,128)(2,1)}, bf16[7,64,128]{2,1,0:T(8,128)(2,1)S(1)}, u32[]{:S(2)}, u32[]{:S(2)}) collective-permute-start(bf16[7,64,128]{2,1,0:T(8,128)(2,1)} %lines.3.refs_1_), channel_id=1, source_target_pairs={{8,26},{16,28},{14,2},{22,4},{2,14},{4,22},{26,8},{28,16},{0,30},{... | collective-permute-start | bytes 344072 | tf_op jit(solution)/shard_map/ppermute | solution.py:514
  75.6 21.1 %collective-permute-start.17 = (bf16[7,64,128]{2,1,0:T(8,128)(2,1)}, bf16[7,64,128]{2,1,0:T(8,128)(2,1)S(1)}, u32[]{:S(2)}, u32[]{:S(2)}) collective-permute-start(bf16[7,64,128]{2,1,0:T(8,128)(2,1)} %lines.3.refs_1_), channel_id=1, source_target_pairs={{8,4},{16,2},{14,28},{22,26},{2,16},{4,8},{26,22},{28,14},{0,24},{... | collective-permute-start | bytes 344072 | tf_op jit(solution)/shard_map/ppermute | solution.py:514
  79.8 17.0 %collective-permute-start.16 = (bf16[7,64,128]{2,1,0:T(8,128)(2,1)}, bf16[7,64,128]{2,1,0:T(8,128)(2,1)S(1)}, u32[]{:S(2)}, u32[]{:S(2)}) collective-permute-start(bf16[7,64,128]{2,1,0:T(8,128)(2,1)} %lines.3.refs_1_), channel_id=1, source_target_pairs={{8,22},{16,14},{14,16},{22,8},{2,28},{4,26},{26,4},{28,2},{0,6},{6... | collective-permute-start | bytes 344072 | tf_op jit(solution)/shard_map/ppermute | solution.py:514
  82.3 0.7 collective-permute-start.22
  83.0 0.7 collective-permute-start.21
  83.7 0.7 collective-permute-start.20
  84.4 12.4 %collective-permute-start.19 = (bf16[1,64,128]{2,1,0:T(8,128)(2,1)}, bf16[1,64,128]{2,1,0:T(8,128)(2,1)S(1)}, u32[]{:S(2)}, u32[]{:S(2)}) collective-permute-start(bf16[1,64,128]{2,1,0:T(8,128)(2,1)} %get-tuple-element.30), channel_id=1, source_target_pairs={{0,10},{2,8},{4,14},{6,12},{8,2},{10,0},{12,6},{14,4},{16,26},{18,... | collective-permute-start | bytes 49160 | tf_op jit(solution)/shard_map/ppermute | solution.py:514
  100.7 6.4 %collective-permute-start.23 = (bf16[13,64,128]{2,1,0:T(8,128)(2,1)}, bf16[13,64,128]{2,1,0:T(8,128)(2,1)S(1)}, u32[]{:S(2)}, u32[]{:S(2)}) collective-permute-start(bf16[13,64,128]{2,1,0:T(8,128)(2,1)} %halo.3.refs_2_.refs_4_), channel_id=1, source_target_pairs={{1,0},{0,1},{3,2},{2,3},{5,4},{4,5},{7,6},{6,7},{9,8},{8,9},{11,10... | collective-permute-start | bytes 638984 | tf_op jit(solution)/shard_map/ppermute | solution.py:465
  (24 other events, 103.4 us)

commit v8 on v7

--- a/solution.py
+++ b/solution.py
@@ -508,7 +508,7 @@
             jnp.where(corner, col_line, side),
         ]
 
-    def exchange(self, pair, col_side, row_side, lines, corner):
+    def exchange(self, table, pair, col_side, row_side, lines, corner):
         every = [(x, y) for x in range(4) for y in range(4)]
         axes = ("px", "py")
         swap = lambda array, pairs: lax.ppermute(
@@ -519,9 +519,6 @@
         spot = lambda side, seg: ((seg, 0), (seg, 3), (0, seg), (3, seg))[side]
         beside = [(spot(side, k), spot(side, 3 - k)) for side in range(4) for k in (1, 2)]
         beside += [((x, y), (3 - x, y)) for x in (1, 2) for y in (1, 2)]
-        paired = swap(pair, beside)
-        near_col = swap(col_side, [((x, y), (x ^ 1, y)) for x, y in every])
-        near_row = swap(row_side, [((x, y), (x, y ^ 1)) for x, y in every])
         small = lambda pairs: swap(corner, pairs)
         diagonal = [
             small([((x, y), (x ^ 1, y ^ 1)) for x, y in every]),
@@ -529,6 +526,12 @@
             small([((x, y), (x ^ 1, 3 - y)) for x, y in every if y in (1, 2)]),
             small([((x, y), (3 - x, 3 - y)) for x, y in every if x in (1, 2) and y in (1, 2)]),
         ]
+        pair, col_side, row_side, _, *diagonal = lax.optimization_barrier(
+            (pair, col_side, row_side, table, *diagonal)
+        )
+        paired = swap(pair, beside)
+        near_col = swap(col_side, [((x, y), (x ^ 1, y)) for x, y in every])
+        near_row = swap(row_side, [((x, y), (x, y ^ 1)) for x, y in every])
         lines = self.line_message(lines, paired, near_col, near_row)
         across = []
         for j in (1, 2, 3):
@@ -627,7 +630,7 @@
         row_pos, col_pos = self.place()
         return [0, 1, 2, 3, jnp.where(col_pos == 0, 0, 1), jnp.where(row_pos == 0, 2, 3)]
 
-    def exchange(self, top, bottom, left, right, lines, corner):
+    def exchange(self, table, top, bottom, left, right, lines, corner):
         px_count, py_count = self.size
         up = lambda n: [(i, i + 1) for i in range(n - 1)]
         down = lambda n: [(i + 1, i) for i in range(n - 1)]
@@ -684,7 +687,7 @@
     table, taps, back_taps = setup(
         plan, edge_table, corner_table, weight, chan, (px_count, py_count), col_len, unit
     )
-    tiles = plan.exchange(*parts)
+    tiles = plan.exchange(table, *parts)
     halo = assemble_halo(table, tiles, rev, faces, units, unit)
     halos = from_others(halo, ch_count)
     old, chunks, first = ([], [], 0)
@@ -696,7 +699,7 @@
         chunks.append((first, from_others(gated, ch_count)))
         first += count
 
-    tiles = plan.exchange(*parts)
+    tiles = plan.exchange(table, *parts)
     halo = assemble_halo(table, tiles, rev, faces, units, unit)
     halos = from_others(halo, ch_count)
     grad = None

time: 116 us -> 118 us (1.017)
  waiting for transfers between devices: 17.2 us -> 28.6 us
  starting transfers between devices: 60.4 us -> 51.3 us
    ppermute x20, starting transfers between devices: 54.4 us -> 45.6 us  [exchange(): lax.ppermute(array, axes, [(a[0] * 4 + a[1], b[0] * 4 + b[1]) for a, b in...]
    ppermute x20, waiting for transfers between devices: 7.09 us -> 15.3 us  [exchange(): lax.ppermute(array, axes, [(a[0] * 4 + a[1], b[0] * 4 + b[1]) for a, b in...]
    ppermute x4, waiting for transfers between devices: 10.2 us -> 13.3 us  [from_others(): lax.ppermute(array, 'ch', [((i + k) % ch_count, i) for i in range(ch_coun...]
  transfers between devices with their start and end apart: 24 -> 24, of which waited for: 5 -> 11; matrix products, arithmetic and copies ran while one was open for 0% -> 0% of each run, Pallas kernels for 13% -> 12%
where the time goes in v8:
time: 118 us; the launch traced here: 117 us
  starting transfers between devices  51.3 us (43%)
  Pallas kernels  31.3 us (27%)
  waiting for transfers between devices  28.6 us (24%)
  local copies, waits for them, and re-layouts  5.07 us (4%)
    ppermute x20, starting transfers between devices, exchange(): lax.ppermute(array, axes, [(a[0] * 4 + a[1], b[0] * 4 + b[1]) for a, b in...  45.6 us
    ppermute x20, waiting for transfers between devices, exchange(): lax.ppermute(array, axes, [(a[0] * 4 + a[1], b[0] * 4 + b[1]) for a, b in...  15.3 us
    ppermute x4, waiting for transfers between devices, from_others(): lax.ppermute(array, 'ch', [((i + k) % ch_count, i) for i in range(ch_coun...  13.3 us
    pallas_call x1, Pallas kernels, forward(): pl.pallas_call(lambda *refs: forward_kernel(first, count, steps, pieces,...  9.39 us
    pallas_call x1, Pallas kernels, backward(): pl.pallas_call(lambda *refs: backward_kernel(first, pieces, *refs), grid=...  7.3 us
    ppermute x4, starting transfers between devices, from_others(): lax.ppermute(array, 'ch', [((i + k) % ch_count, i) for i in range(ch_coun...  5.71 us
    pallas_call x2, Pallas kernels, assemble_halo(): pl.pallas_call(lambda *refs: halo_kernel(faces, units, unit, *refs), in_s...  5.17 us
    unnamed x48, local copies, waits for them, and re-layouts  5.07 us
  transfers between devices with their start and end apart: 24, of which 11 were waited for; matrix products, arithmetic and copies ran while one was open for 0% of the time, Pallas kernels for 12%

profile of v8, /device:TPU:0, one launch (start us, length us, event | category | flops | bytes accessed | tf_op | source)
XLA Modules:
  0.0 117.2 jit_solution(6791966081380229600)
XLA Ops:
  0.6 3.0 %collective-permute-start = (bf16[12,64,1024]{2,1,0:T(8,128)(2,1)}, bf16[12,64,1024]{2,1,0:T(8,128)(2,1)S(1)}, u32[]{:S(2)}, u32[]{:S(2)}) collective-permute-start(bf16[12,64,1024]{2,1,0:T(8,128)(2,1)} %bitcast.18), channel_id=1, source_target_pairs={{1,0},{0,1},{3,2},{2,3},{5,4},{4,5},{7,6},{6,7},{9,8},{8,9},{11,10... | collective-permute-start | bytes 4718600 | tf_op jit(solution)/shard_map/ppermute | solution.py:465
  3.6 3.9 %rings.1 = (bf16[6,64,128]{2,1,0:T(8,128)(2,1)}, bf16[4,64,128]{2,1,0:T(8,128)(2,1)}, bf16[4,64,128]{2,1,0:T(8,128)(2,1)}, bf16[6,64,128]{2,1,0:T(8,128)(2,1)}, bf16[1,64,128]{2,1,0:T(8,128)(2,1)}) custom-call(bf16[12,64,1024]{2,1,0:T(8,128)(2,1)} %bitcast.19, bf16[1024,128]{1,0:T(8,128)(2,1)} %constant.8.clone.refs_1_.refs_9_, ...), custom_call_target="tpu_custom_call" | custom-call | tf_op jit(solution)/shard_map/rings/pallas_call | solution.py:129
  9.6 7.7 %collective-permute-start.1 = (bf16[1,64,128]{2,1,0:T(8,128)(2,1)}, bf16[1,64,128]{2,1,0:T(8,128)(2,1)S(1)}, u32[]{:S(2)}, u32[]{:S(2)}) collective-permute-start(bf16[1,64,128]{2,1,0:T(8,128)(2,1)} %get-tuple-element.36), channel_id=1, source_target_pairs={{0,10},{2,8},{4,14},{6,12},{8,2},{10,0},{12,6},{14,4},{16,26},{18,... | collective-permute-start | bytes 49160 | tf_op jit(solution)/shard_map/ppermute | solution.py:514
  17.2 2.2 %setup.1 = (s32[20,12]{1,0:T(8,128)}, bf16[192,384]{1,0:T(8,128)(2,1)}, bf16[192,384]{1,0:T(8,128)(2,1)}) custom-call(s32[3,4,12]{2,1,0:T(4,128)} %bitcast.23, s32[4,2,12]{2,1,0:T(2,128)} %bitcast.24, bf16[3,3,128,128]{3,2,1,0:T(8,128)(2,1)} %refs_2_.2), custom_call_target="tpu_custom_call" | custom-call | tf_op jit(solution)/shard_map/setup/pallas_call | solution.py:452
  20.2 4.4 %collective-permute-start.6 = (bf16[4,64,128]{2,1,0:T(8,128)(2,1)}, bf16[4,64,128]{2,1,0:T(8,128)(2,1)S(1)}, u32[]{:S(2)}, u32[]{:S(2)}) collective-permute-start(bf16[4,64,128]{2,1,0:T(8,128)(2,1)} %get-tuple-element.38), channel_id=1, source_target_pairs={{0,8},{2,10},{4,12},{6,14},{8,0},{10,2},{12,4},{14,6},{16,24},{18,... | collective-permute-start | bytes 196616 | tf_op jit(solution)/shard_map/ppermute | solution.py:514
  24.6 2.5 %collective-permute-done.6.col_ref.refs_6_ = bf16[4,64,128]{2,1,0:T(8,128)(2,1)S(1)} collective-permute-done((bf16[4,64,128]{2,1,0:T(8,128)(2,1)}, bf16[4,64,128]{2,1,0:T(8,128)(2,1)S(1)}, u32[]{:S(2)}, u32[]{:S(2)}) %collective-permute-start.6) | collective-permute-done | bytes 65568 | tf_op jit(solution)/shard_map/ppermute | solution.py:514
  27.8 1.6 %lines.2.refs_1_ = bf16[7,64,128]{2,1,0:T(8,128)(2,1)} custom-call(bf16[6,64,128]{2,1,0:T(8,128)(2,1)} %get-tuple-element.32.lines_ref, bf16[6,64,128]{2,1,0:T(8,128)(2,1)} %copy-done.5, bf16[4,64,128]{2,1,0:T(8,128)(2,1)} %copy-done.7, bf16[4,64,128]{2,1,0:T(8,128)(2,1)} %copy-done.9), custom_call_target="tpu_custom_call" | custom-call | tf_op jit(solution)/shard_map/lines/pallas_call | solution.py:559
  29.4 2.2 %collective-permute-start.10 = (bf16[7,64,128]{2,1,0:T(8,128)(2,1)}, bf16[7,64,128]{2,1,0:T(8,128)(2,1)S(1)}, u32[]{:S(2)}, u32[]{:S(2)}) collective-permute-start(bf16[7,64,128]{2,1,0:T(8,128)(2,1)} %lines.2.refs_1_), channel_id=1, source_target_pairs={{8,26},{16,28},{14,2},{22,4},{2,14},{4,22},{26,8},{28,16},{0,30},{... | collective-permute-start | bytes 344072 | tf_op jit(solution)/shard_map/ppermute | solution.py:514
  31.6 4.0 %collective-permute-start.9 = (bf16[7,64,128]{2,1,0:T(8,128)(2,1)}, bf16[7,64,128]{2,1,0:T(8,128)(2,1)S(1)}, u32[]{:S(2)}, u32[]{:S(2)}) collective-permute-start(bf16[7,64,128]{2,1,0:T(8,128)(2,1)} %lines.2.refs_1_), channel_id=1, source_target_pairs={{8,4},{16,2},{14,28},{22,26},{2,16},{4,8},{26,22},{28,14},{0,24},{... | collective-permute-start | bytes 344072 | tf_op jit(solution)/shard_map/ppermute | solution.py:514
  35.6 2.4 %collective-permute-start.8 = (bf16[7,64,128]{2,1,0:T(8,128)(2,1)}, bf16[7,64,128]{2,1,0:T(8,128)(2,1)S(1)}, u32[]{:S(2)}, u32[]{:S(2)}) collective-permute-start(bf16[7,64,128]{2,1,0:T(8,128)(2,1)} %lines.2.refs_1_), channel_id=1, source_target_pairs={{8,22},{16,14},{14,16},{22,8},{2,28},{4,26},{26,4},{28,2},{0,6},{6... | collective-permute-start | bytes 344072 | tf_op jit(solution)/shard_map/ppermute | solution.py:514
  39.6 2.0 %collective-permute-done.9.refs_3_ = bf16[7,64,128]{2,1,0:T(8,128)(2,1)S(1)} collective-permute-done((bf16[7,64,128]{2,1,0:T(8,128)(2,1)}, bf16[7,64,128]{2,1,0:T(8,128)(2,1)S(1)}, u32[]{:S(2)}, u32[]{:S(2)}) %collective-permute-start.9) | collective-permute-done | bytes 114720 | tf_op jit(solution)/shard_map/ppermute | solution.py:514
  42.9 2.6 %halo.2.refs_2_.refs_4_ = bf16[13,64,128]{2,1,0:T(8,128)(2,1)} custom-call(s32[20,12]{1,0:T(8,128)} %get-tuple-element.31.refs_0_, bf16[7,64,128]{2,1,0:T(8,128)(2,1)} %lines.2.refs_1_, bf16[7,64,128]{2,1,0:T(8,128)(2,1)} %copy-done.15, bf16[7,64,128]{2,1,0:T(8,128)(2,1)} %copy-done.13, bf16[7,64,128]{2,1,0:T(8,128)(2,1)} %copy-done.11, ...), custom_call_target="tpu_custom_call" | custom-call | tf_op jit(solution)/shard_map/halo/pallas_call | solution.py:191
  46.0 6.7 %collective-permute-done.11.refs_3_.refs_5_ = bf16[13,64,128]{2,1,0:T(8,128)(2,1)S(1)} collective-permute-done((bf16[13,64,128]{2,1,0:T(8,128)(2,1)}, bf16[13,64,128]{2,1,0:T(8,128)(2,1)S(1)}, u32[]{:S(2)}, u32[]{:S(2)}) %collective-permute-start.11) | collective-permute-done | bytes 213024 | tf_op jit(solution)/shard_map/ppermute | solution.py:465
  53.9 9.4 %forward.1 = (bf16[12,64,1024]{2,1,0:T(8,128)(2,1)}, bf16[12,64,1024]{2,1,0:T(8,128)(2,1)}, bf16[6,64,128]{2,1,0:T(8,128)(2,1)}, bf16[4,64,128]{2,1,0:T(8,128)(2...) custom-call(bf16[12,64,1024]{2,1,0:T(8,128)(2,1)} %bitcast.20, ...), custom_call_target="tpu_custom_call" | custom-call | tf_op jit(solution)/shard_map/forward/pallas_call | solution.py:318
  66.0 6.0 %collective-permute-start.13 = (bf16[1,64,128]{2,1,0:T(8,128)(2,1)}, bf16[1,64,128]{2,1,0:T(8,128)(2,1)S(1)}, u32[]{:S(2)}, u32[]{:S(2)}) collective-permute-start(bf16[1,64,128]{2,1,0:T(8,128)(2,1)} %get-tuple-element.51), channel_id=1, source_target_pairs={{0,10},{2,8},{4,14},{6,12},{8,2},{10,0},{12,6},{14,4},{16,26},{18,... | collective-permute-start | bytes 49160 | tf_op jit(solution)/shard_map/ppermute | solution.py:514
  74.3 5.0 %collective-permute-start.18 = (bf16[4,64,128]{2,1,0:T(8,128)(2,1)}, bf16[4,64,128]{2,1,0:T(8,128)(2,1)S(1)}, u32[]{:S(2)}, u32[]{:S(2)}) collective-permute-start(bf16[4,64,128]{2,1,0:T(8,128)(2,1)} %get-tuple-element.53), channel_id=1, source_target_pairs={{0,8},{2,10},{4,12},{6,14},{8,0},{10,2},{12,4},{14,6},{16,24},{18,... | collective-permute-start | bytes 196616 | tf_op jit(solution)/shard_map/ppermute | solution.py:514
  79.3 2.5 %collective-permute-done.18.col_ref.refs_6_ = bf16[4,64,128]{2,1,0:T(8,128)(2,1)S(1)} collective-permute-done((bf16[4,64,128]{2,1,0:T(8,128)(2,1)}, bf16[4,64,128]{2,1,0:T(8,128)(2,1)S(1)}, u32[]{:S(2)}, u32[]{:S(2)}) %collective-permute-start.18) | collective-permute-done | bytes 65568 | tf_op jit(solution)/shard_map/ppermute | solution.py:514
  82.5 1.6 %lines.3.refs_1_ = bf16[7,64,128]{2,1,0:T(8,128)(2,1)} custom-call(bf16[6,64,128]{2,1,0:T(8,128)(2,1)} %get-tuple-element.47.lines_ref, bf16[6,64,128]{2,1,0:T(8,128)(2,1)} %copy-done.4, bf16[4,64,128]{2,1,0:T(8,128)(2,1)} %copy-done.6, bf16[4,64,128]{2,1,0:T(8,128)(2,1)} %copy-done.8), custom_call_target="tpu_custom_call" | custom-call | tf_op jit(solution)/shard_map/lines/pallas_call | solution.py:559
  84.1 2.2 %collective-permute-start.22 = (bf16[7,64,128]{2,1,0:T(8,128)(2,1)}, bf16[7,64,128]{2,1,0:T(8,128)(2,1)S(1)}, u32[]{:S(2)}, u32[]{:S(2)}) collective-permute-start(bf16[7,64,128]{2,1,0:T(8,128)(2,1)} %lines.3.refs_1_), channel_id=1, source_target_pairs={{8,26},{16,28},{14,2},{22,4},{2,14},{4,22},{26,8},{28,16},{0,30},{... | collective-permute-start | bytes 344072 | tf_op jit(solution)/shard_map/ppermute | solution.py:514
  86.4 4.5 %collective-permute-start.21 = (bf16[7,64,128]{2,1,0:T(8,128)(2,1)}, bf16[7,64,128]{2,1,0:T(8,128)(2,1)S(1)}, u32[]{:S(2)}, u32[]{:S(2)}) collective-permute-start(bf16[7,64,128]{2,1,0:T(8,128)(2,1)} %lines.3.refs_1_), channel_id=1, source_target_pairs={{8,4},{16,2},{14,28},{22,26},{2,16},{4,8},{26,22},{28,14},{0,24},{... | collective-permute-start | bytes 344072 | tf_op jit(solution)/shard_map/ppermute | solution.py:514
  90.8 1.9 %collective-permute-start.20 = (bf16[7,64,128]{2,1,0:T(8,128)(2,1)}, bf16[7,64,128]{2,1,0:T(8,128)(2,1)S(1)}, u32[]{:S(2)}, u32[]{:S(2)}) collective-permute-start(bf16[7,64,128]{2,1,0:T(8,128)(2,1)} %lines.3.refs_1_), channel_id=1, source_target_pairs={{8,22},{16,14},{14,16},{22,8},{2,28},{4,26},{26,4},{28,2},{0,6},{6... | collective-permute-start | bytes 344072 | tf_op jit(solution)/shard_map/ppermute | solution.py:514
  98.0 2.6 %halo.3.refs_2_.refs_4_ = bf16[13,64,128]{2,1,0:T(8,128)(2,1)} custom-call(s32[20,12]{1,0:T(8,128)} %get-tuple-element.31.refs_0_, bf16[7,64,128]{2,1,0:T(8,128)(2,1)} %lines.3.refs_1_, bf16[7,64,128]{2,1,0:T(8,128)(2,1)} %copy-done.14, bf16[7,64,128]{2,1,0:T(8,128)(2,1)} %copy-done.12, bf16[7,64,128]{2,1,0:T(8,128)(2,1)} %copy-done.10, ...), custom_call_target="tpu_custom_call" | custom-call | tf_op jit(solution)/shard_map/halo/pallas_call | solution.py:191
  102.1 6.5 %collective-permute-done.23.refs_3_.refs_5_ = bf16[13,64,128]{2,1,0:T(8,128)(2,1)S(1)} collective-permute-done((bf16[13,64,128]{2,1,0:T(8,128)(2,1)}, bf16[13,64,128]{2,1,0:T(8,128)(2,1)S(1)}, u32[]{:S(2)}, u32[]{:S(2)}) %collective-permute-start.23) | collective-permute-done | bytes 213024 | tf_op jit(solution)/shard_map/ppermute | solution.py:465
  109.9 7.3 %backward.1 = bf16[12,64,1024]{2,1,0:T(8,128)(2,1)} custom-call(bf16[12,64,1024]{2,1,0:T(8,128)(2,1)} %get-tuple-element.46.refs_0_, bf16[12,64,1024]{2,1,0:T(8,128)(2,1)} %copy-done.1, bf16[13,64,128]{2,1,0:T(8,128)(2,1)} %halo.3.refs_2_.refs_4_, bf16[13,64,128]{2,1,0:T(8,128)(2,1)} %copy-done.3, bf16[13,64,128]{2,1,0:T(8,128)(2,1)} %halo.3.refs_2_.refs_4_, ...), custom_call_target="tpu_custom_call" | custom-call | tf_op jit(solution)/shard_map/backward/pallas_call | solution.py:355
  (80 shorter events, 21.4 us)
Async XLA Ops:
  0.6 52.1 %collective-permute-start = (bf16[12,64,1024]{2,1,0:T(8,128)(2,1)}, bf16[12,64,1024]{2,1,0:T(8,128)(2,1)S(1)}, u32[]{:S(2)}, u32[]{:S(2)}) collective-permute-start(bf16[12,64,1024]{2,1,0:T(8,128)(2,1)} %bitcast.18), channel_id=1, source_target_pairs={{1,0},{0,1},{3,2},{2,3},{5,4},{4,5},{7,6},{6,7},{9,8},{8,9},{11,10... | collective-permute-start | bytes 4718600 | tf_op jit(solution)/shard_map/ppermute | solution.py:465
  7.6 11.9 %collective-permute-start.4 = (bf16[1,64,128]{2,1,0:T(8,128)(2,1)}, bf16[1,64,128]{2,1,0:T(8,128)(2,1)S(1)}, u32[]{:S(2)}, u32[]{:S(2)}) collective-permute-start(bf16[1,64,128]{2,1,0:T(8,128)(2,1)} %get-tuple-element.36), channel_id=1, source_target_pairs={{10,20},{12,18},{18,12},{20,10},{11,21},{13,19},{19,13},{21,11}} | collective-permute-start | bytes 49160 | tf_op jit(solution)/shard_map/ppermute | solution.py:514
  8.2 11.2 %collective-permute-start.3 = (bf16[1,64,128]{2,1,0:T(8,128)(2,1)}, bf16[1,64,128]{2,1,0:T(8,128)(2,1)S(1)}, u32[]{:S(2)}, u32[]{:S(2)}) collective-permute-start(bf16[1,64,128]{2,1,0:T(8,128)(2,1)} %get-tuple-element.36), channel_id=1, source_target_pairs={{2,12},{4,10},{10,4},{12,2},{18,28},{20,26},{26,20},{28,18},{3,13}... | collective-permute-start | bytes 49160 | tf_op jit(solution)/shard_map/ppermute | solution.py:514
  8.9 10.6 %collective-permute-start.2 = (bf16[1,64,128]{2,1,0:T(8,128)(2,1)}, bf16[1,64,128]{2,1,0:T(8,128)(2,1)S(1)}, u32[]{:S(2)}, u32[]{:S(2)}) collective-permute-start(bf16[1,64,128]{2,1,0:T(8,128)(2,1)} %get-tuple-element.36), channel_id=1, source_target_pairs={{8,18},{10,16},{12,22},{14,20},{16,10},{18,8},{20,14},{22,12},{9,1... | collective-permute-start | bytes 49160 | tf_op jit(solution)/shard_map/ppermute | solution.py:514
  9.6 9.9 %collective-permute-start.1 = (bf16[1,64,128]{2,1,0:T(8,128)(2,1)}, bf16[1,64,128]{2,1,0:T(8,128)(2,1)S(1)}, u32[]{:S(2)}, u32[]{:S(2)}) collective-permute-start(bf16[1,64,128]{2,1,0:T(8,128)(2,1)} %get-tuple-element.36), channel_id=1, source_target_pairs={{0,10},{2,8},{4,14},{6,12},{8,2},{10,0},{12,6},{14,4},{16,26},{18,... | collective-permute-start | bytes 49160 | tf_op jit(solution)/shard_map/ppermute | solution.py:514
  19.5 7.6 %collective-permute-start.5 = (bf16[6,64,128]{2,1,0:T(8,128)(2,1)}, bf16[6,64,128]{2,1,0:T(8,128)(2,1)S(1)}, u32[]{:S(2)}, u32[]{:S(2)}) collective-permute-start(bf16[6,64,128]{2,1,0:T(8,128)(2,1)} %get-tuple-element.37), channel_id=1, source_target_pairs={{8,16},{16,8},{14,22},{22,14},{2,4},{4,2},{26,28},{28,26},{10,18},... | collective-permute-start | bytes 294920 | tf_op jit(solution)/shard_map/ppermute | solution.py:514
  20.2 6.9 %collective-permute-start.6 = (bf16[4,64,128]{2,1,0:T(8,128)(2,1)}, bf16[4,64,128]{2,1,0:T(8,128)(2,1)S(1)}, u32[]{:S(2)}, u32[]{:S(2)}) collective-permute-start(bf16[4,64,128]{2,1,0:T(8,128)(2,1)} %get-tuple-element.38), channel_id=1, source_target_pairs={{0,8},{2,10},{4,12},{6,14},{8,0},{10,2},{12,4},{14,6},{16,24},{18,... | collective-permute-start | bytes 196616 | tf_op jit(solution)/shard_map/ppermute | solution.py:514
  24.6 2.5 %collective-permute-start.7 = (bf16[4,64,128]{2,1,0:T(8,128)(2,1)}, bf16[4,64,128]{2,1,0:T(8,128)(2,1)S(1)}, u32[]{:S(2)}, u32[]{:S(2)}) collective-permute-start(bf16[4,64,128]{2,1,0:T(8,128)(2,1)} %get-tuple-element.39), channel_id=1, source_target_pairs={{0,2},{2,0},{4,6},{6,4},{8,10},{10,8},{12,14},{14,12},{16,18},{18,... | collective-permute-start | bytes 196616 | tf_op jit(solution)/shard_map/ppermute | solution.py:514
  29.4 10.1 %collective-permute-start.10 = (bf16[7,64,128]{2,1,0:T(8,128)(2,1)}, bf16[7,64,128]{2,1,0:T(8,128)(2,1)S(1)}, u32[]{:S(2)}, u32[]{:S(2)}) collective-permute-start(bf16[7,64,128]{2,1,0:T(8,128)(2,1)} %lines.2.refs_1_), channel_id=1, source_target_pairs={{8,26},{16,28},{14,2},{22,4},{2,14},{4,22},{26,8},{28,16},{0,30},{... | collective-permute-start | bytes 344072 | tf_op jit(solution)/shard_map/ppermute | solution.py:514
  31.6 9.9 %collective-permute-start.9 = (bf16[7,64,128]{2,1,0:T(8,128)(2,1)}, bf16[7,64,128]{2,1,0:T(8,128)(2,1)S(1)}, u32[]{:S(2)}, u32[]{:S(2)}) collective-permute-start(bf16[7,64,128]{2,1,0:T(8,128)(2,1)} %lines.2.refs_1_), channel_id=1, source_target_pairs={{8,4},{16,2},{14,28},{22,26},{2,16},{4,8},{26,22},{28,14},{0,24},{... | collective-permute-start | bytes 344072 | tf_op jit(solution)/shard_map/ppermute | solution.py:514
  35.6 6.6 %collective-permute-start.8 = (bf16[7,64,128]{2,1,0:T(8,128)(2,1)}, bf16[7,64,128]{2,1,0:T(8,128)(2,1)S(1)}, u32[]{:S(2)}, u32[]{:S(2)}) collective-permute-start(bf16[7,64,128]{2,1,0:T(8,128)(2,1)} %lines.2.refs_1_), channel_id=1, source_target_pairs={{8,22},{16,14},{14,16},{22,8},{2,28},{4,26},{26,4},{28,2},{0,6},{6... | collective-permute-start | bytes 344072 | tf_op jit(solution)/shard_map/ppermute | solution.py:514
  45.5 7.3 %collective-permute-start.11 = (bf16[13,64,128]{2,1,0:T(8,128)(2,1)}, bf16[13,64,128]{2,1,0:T(8,128)(2,1)S(1)}, u32[]{:S(2)}, u32[]{:S(2)}) collective-permute-start(bf16[13,64,128]{2,1,0:T(8,128)(2,1)} %halo.2.refs_2_.refs_4_), channel_id=1, source_target_pairs={{1,0},{0,1},{3,2},{2,3},{5,4},{4,5},{7,6},{6,7},{9,8},{8,9},{11,10... | collective-permute-start | bytes 638984 | tf_op jit(solution)/shard_map/ppermute | solution.py:465
  63.3 45.3 %collective-permute-start.12 = (bf16[12,64,1024]{2,1,0:T(8,128)(2,1)}, bf16[12,64,1024]{2,1,0:T(8,128)(2,1)S(1)}, u32[]{:S(2)}, u32[]{:S(2)}) collective-permute-start(bf16[12,64,1024]{2,1,0:T(8,128)(2,1)} %get-tuple-element.46.refs_0_), channel_id=1, source_target_pairs={{1,0},{0,1},{3,2},{2,3},{5,4},{4,5},{7,6},{6,7},{9,8},{8,9},{11,10... | collective-permute-start | bytes 4718600 | tf_op jit(solution)/shard_map/ppermute | solution.py:465
  64.0 8.0 %collective-permute-start.16 = (bf16[1,64,128]{2,1,0:T(8,128)(2,1)}, bf16[1,64,128]{2,1,0:T(8,128)(2,1)S(1)}, u32[]{:S(2)}, u32[]{:S(2)}) collective-permute-start(bf16[1,64,128]{2,1,0:T(8,128)(2,1)} %get-tuple-element.51), channel_id=1, source_target_pairs={{10,20},{12,18},{18,12},{20,10},{11,21},{13,19},{19,13},{21,11}} | collective-permute-start | bytes 49160 | tf_op jit(solution)/shard_map/ppermute | solution.py:514
  64.6 7.4 %collective-permute-start.15 = (bf16[1,64,128]{2,1,0:T(8,128)(2,1)}, bf16[1,64,128]{2,1,0:T(8,128)(2,1)S(1)}, u32[]{:S(2)}, u32[]{:S(2)}) collective-permute-start(bf16[1,64,128]{2,1,0:T(8,128)(2,1)} %get-tuple-element.51), channel_id=1, source_target_pairs={{2,12},{4,10},{10,4},{12,2},{18,28},{20,26},{26,20},{28,18},{3,13}... | collective-permute-start | bytes 49160 | tf_op jit(solution)/shard_map/ppermute | solution.py:514
  65.3 6.7 %collective-permute-start.14 = (bf16[1,64,128]{2,1,0:T(8,128)(2,1)}, bf16[1,64,128]{2,1,0:T(8,128)(2,1)S(1)}, u32[]{:S(2)}, u32[]{:S(2)}) collective-permute-start(bf16[1,64,128]{2,1,0:T(8,128)(2,1)} %get-tuple-element.51), channel_id=1, source_target_pairs={{8,18},{10,16},{12,22},{14,20},{16,10},{18,8},{20,14},{22,12},{9,1... | collective-permute-start | bytes 49160 | tf_op jit(solution)/shard_map/ppermute | solution.py:514
  66.0 7.7 %collective-permute-start.13 = (bf16[1,64,128]{2,1,0:T(8,128)(2,1)}, bf16[1,64,128]{2,1,0:T(8,128)(2,1)S(1)}, u32[]{:S(2)}, u32[]{:S(2)}) collective-permute-start(bf16[1,64,128]{2,1,0:T(8,128)(2,1)} %get-tuple-element.51), channel_id=1, source_target_pairs={{0,10},{2,8},{4,14},{6,12},{8,2},{10,0},{12,6},{14,4},{16,26},{18,... | collective-permute-start | bytes 49160 | tf_op jit(solution)/shard_map/ppermute | solution.py:514
  73.6 8.2 %collective-permute-start.17 = (bf16[6,64,128]{2,1,0:T(8,128)(2,1)}, bf16[6,64,128]{2,1,0:T(8,128)(2,1)S(1)}, u32[]{:S(2)}, u32[]{:S(2)}) collective-permute-start(bf16[6,64,128]{2,1,0:T(8,128)(2,1)} %get-tuple-element.52), channel_id=1, source_target_pairs={{8,16},{16,8},{14,22},{22,14},{2,4},{4,2},{26,28},{28,26},{10,18},... | collective-permute-start | bytes 294920 | tf_op jit(solution)/shard_map/ppermute | solution.py:514
  74.3 7.5 %collective-permute-start.18 = (bf16[4,64,128]{2,1,0:T(8,128)(2,1)}, bf16[4,64,128]{2,1,0:T(8,128)(2,1)S(1)}, u32[]{:S(2)}, u32[]{:S(2)}) collective-permute-start(bf16[4,64,128]{2,1,0:T(8,128)(2,1)} %get-tuple-element.53), channel_id=1, source_target_pairs={{0,8},{2,10},{4,12},{6,14},{8,0},{10,2},{12,4},{14,6},{16,24},{18,... | collective-permute-start | bytes 196616 | tf_op jit(solution)/shard_map/ppermute | solution.py:514
  79.3 2.5 %collective-permute-start.19 = (bf16[4,64,128]{2,1,0:T(8,128)(2,1)}, bf16[4,64,128]{2,1,0:T(8,128)(2,1)S(1)}, u32[]{:S(2)}, u32[]{:S(2)}) collective-permute-start(bf16[4,64,128]{2,1,0:T(8,128)(2,1)} %get-tuple-element.54), channel_id=1, source_target_pairs={{0,2},{2,0},{4,6},{6,4},{8,10},{10,8},{12,14},{14,12},{16,18},{18,... | collective-permute-start | bytes 196616 | tf_op jit(solution)/shard_map/ppermute | solution.py:514
  84.1 10.2 %collective-permute-start.22 = (bf16[7,64,128]{2,1,0:T(8,128)(2,1)}, bf16[7,64,128]{2,1,0:T(8,128)(2,1)S(1)}, u32[]{:S(2)}, u32[]{:S(2)}) collective-permute-start(bf16[7,64,128]{2,1,0:T(8,128)(2,1)} %lines.3.refs_1_), channel_id=1, source_target_pairs={{8,26},{16,28},{14,2},{22,4},{2,14},{4,22},{26,8},{28,16},{0,30},{... | collective-permute-start | bytes 344072 | tf_op jit(solution)/shard_map/ppermute | solution.py:514
  86.4 9.6 %collective-permute-start.21 = (bf16[7,64,128]{2,1,0:T(8,128)(2,1)}, bf16[7,64,128]{2,1,0:T(8,128)(2,1)S(1)}, u32[]{:S(2)}, u32[]{:S(2)}) collective-permute-start(bf16[7,64,128]{2,1,0:T(8,128)(2,1)} %lines.3.refs_1_), channel_id=1, source_target_pairs={{8,4},{16,2},{14,28},{22,26},{2,16},{4,8},{26,22},{28,14},{0,24},{... | collective-permute-start | bytes 344072 | tf_op jit(solution)/shard_map/ppermute | solution.py:514
  90.8 6.5 %collective-permute-start.20 = (bf16[7,64,128]{2,1,0:T(8,128)(2,1)}, bf16[7,64,128]{2,1,0:T(8,128)(2,1)S(1)}, u32[]{:S(2)}, u32[]{:S(2)}) collective-permute-start(bf16[7,64,128]{2,1,0:T(8,128)(2,1)} %lines.3.refs_1_), channel_id=1, source_target_pairs={{8,22},{16,14},{14,16},{22,8},{2,28},{4,26},{26,4},{28,2},{0,6},{6... | collective-permute-start | bytes 344072 | tf_op jit(solution)/shard_map/ppermute | solution.py:514
  100.6 8.1 %collective-permute-start.23 = (bf16[13,64,128]{2,1,0:T(8,128)(2,1)}, bf16[13,64,128]{2,1,0:T(8,128)(2,1)S(1)}, u32[]{:S(2)}, u32[]{:S(2)}) collective-permute-start(bf16[13,64,128]{2,1,0:T(8,128)(2,1)} %halo.3.refs_2_.refs_4_), channel_id=1, source_target_pairs={{1,0},{0,1},{3,2},{2,3},{5,4},{4,5},{7,6},{6,7},{9,8},{8,9},{11,10... | collective-permute-start | bytes 638984 | tf_op jit(solution)/shard_map/ppermute | solution.py:465
  (24 other events, 207.2 us)

commit v9 on v5

--- a/solution.py
+++ b/solution.py
@@ -542,7 +542,6 @@
             if j == 1:
                 pairs += [((x, y), (x, 3 - y)) for x in (1, 2) for y in (1, 2)]
             across.append(swap(lines, pairs))
-        corner, across[0] = lax.optimization_barrier((corner, across[0]))
         ends_of = lax.all_to_all(corner, axes, 0, 0, tiled=True)
         return [lines, *across, paired, near_col, near_row, ends_of]
 

time: 115 us -> 106 us (0.922)
  starting transfers between devices: 50.9 us -> 45.7 us
  waiting for transfers between devices: 28.4 us -> 24.5 us
    ppermute x12, waiting for transfers between devices: 18.3 us -> 4.39 us  [exchange(): lax.ppermute(array, axes, [(a[0] * 4 + a[1], b[0] * 4 + b[1]) for a, b in...]
    all_to_all x2, starting transfers between devices: 25.4 us -> 12.1 us  [exchange(): ends_of = lax.all_to_all(corner, axes, 0, 0, tiled=True)]
    ppermute x4, waiting for transfers between devices: 10.1 us -> 20.1 us  [from_others(): lax.ppermute(array, 'ch', [((i + k) % ch_count, i) for i in range(ch_coun...]
    ppermute x12, starting transfers between devices: 19.9 us -> 27.9 us  [exchange(): lax.ppermute(array, axes, [(a[0] * 4 + a[1], b[0] * 4 + b[1]) for a, b in...]
  transfers between devices with their start and end apart: 18 -> 18, of which waited for: 8 -> 4; matrix products, arithmetic and copies ran while one was open for 2% -> 2% of each run, Pallas kernels for 10% -> 11%
where the time goes in v9:
time: 106 us
  starting transfers between devices  45.7 us (43%)
  Pallas kernels  28.1 us (27%)
  waiting for transfers between devices  24.5 us (23%)
  local copies, waits for them, and re-layouts  4.42 us (4%)
  other arithmetic  2.03 us (2%)
    ppermute x12, starting transfers between devices, exchange(): lax.ppermute(array, axes, [(a[0] * 4 + a[1], b[0] * 4 + b[1]) for a, b in...  27.9 us
    ppermute x4, waiting for transfers between devices, from_others(): lax.ppermute(array, 'ch', [((i + k) % ch_count, i) for i in range(ch_coun...  20.1 us
    all_to_all x2, starting transfers between devices, exchange(): ends_of = lax.all_to_all(corner, axes, 0, 0, tiled=True)  12.1 us
    pallas_call x1, Pallas kernels, forward(): pl.pallas_call(lambda *refs: forward_kernel(first, count, steps, pieces,...  9.42 us
    pallas_call x1, Pallas kernels, backward(): pl.pallas_call(lambda *refs: backward_kernel(first, pieces, *refs), grid=...  7.3 us
    ppermute x4, starting transfers between devices, from_others(): lax.ppermute(array, 'ch', [((i + k) % ch_count, i) for i in range(ch_coun...  5.65 us
    pallas_call x2, Pallas kernels, assemble_halo(): pl.pallas_call(lambda *refs: halo_kernel(faces, units, unit, plan, *refs)...  5.2 us
    unnamed x40, local copies, waits for them, and re-layouts  4.42 us
  transfers between devices with their start and end apart: 18, of which 4 were waited for; matrix products, arithmetic and copies ran while one was open for 2% of the time, Pallas kernels for 11%

profile of v9, /device:TPU:0, one launch (start us, length us, event | category | flops | bytes accessed | tf_op | source)
XLA Modules:
  0.0 105.7 jit_solution(7556050020380450019)
XLA Ops:
  0.6 3.0 %collective-permute-start = (bf16[12,64,1024]{2,1,0:T(8,128)(2,1)}, bf16[12,64,1024]{2,1,0:T(8,128)(2,1)S(1)}, u32[]{:S(2)}, u32[]{:S(2)}) collective-permute-start(bf16[12,64,1024]{2,1,0:T(8,128)(2,1)} %bitcast.18), channel_id=1, source_target_pairs={{1,0},{0,1},{3,2},{2,3},{5,4},{4,5},{7,6},{6,7},{9,8},{8,9},{11,10... | collective-permute-start | bytes 4718600 | tf_op jit(solution)/shard_map/ppermute | solution.py:465
  3.6 4.0 %rings.1 = (bf16[6,64,128]{2,1,0:T(8,128)(2,1)}, bf16[3,64,128]{2,1,0:T(8,128)(2,1)}, bf16[3,64,128]{2,1,0:T(8,128)(2,1)}, bf16[6,64,128]{2,1,0:T(8,128)(2,1)}, bf16[16,32,128]{2,1,0:T(8,128)(2,1)}) custom-call(bf16[12,64,1024]{2,1,0:T(8,128)(2,1)} %bitcast.19, bf16[1024,128]{1,0:T(8,128)(2,1)} %constant.33.clone.refs_1_.refs_9_, ...), custom_call_target="tpu_custom_call" | custom-call | tf_op jit(solution)/shard_map/rings/pallas_call | solution.py:127
  7.6 5.9 %all-to-all-start = ((bf16[16,32,128]{2,1,0:T(8,128)(2,1)}), bf16[16,32,128]{2,1,0:T(8,128)(2,1)S(1)}, u32[]{:S(2)}, u32[]{:S(2)}) async-start(bf16[16,32,128]{2,1,0:T(8,128)(2,1)} %get-tuple-element.22), calls=%async_computation | async-start | bytes 262144 | tf_op jit(solution)/shard_map/all_to_all | solution.py:545
  13.6 1.9 %collective-permute-start.5 = (bf16[3,64,128]{2,1,0:T(8,128)(2,1)}, bf16[3,64,128]{2,1,0:T(8,128)(2,1)S(1)}, u32[]{:S(2)}, u32[]{:S(2)}) collective-permute-start(bf16[3,64,128]{2,1,0:T(8,128)(2,1)} %get-tuple-element.20), channel_id=1, source_target_pairs={{0,8},{2,10},{4,12},{6,14},{8,0},{10,2},{12,4},{14,6},{16,24},{18,... | collective-permute-start | bytes 147464 | tf_op jit(solution)/shard_map/ppermute | solution.py:524
  16.2 1.0 broadcast_select_fusion.1.refs_1_
  17.3 4.6 %collective-permute-start.4 = (bf16[6,64,128]{2,1,0:T(8,128)(2,1)S(1)}, bf16[6,64,128]{2,1,0:T(8,128)(2,1)S(1)}, u32[]{:S(2)}, u32[]{:S(2)}) collective-permute-start(bf16[6,64,128]{2,1,0:T(8,128)(2,1)S(1)} %broadcast_select_fusion.1.refs_1_), channel_id=1, source_target_pairs={{8,26},{16,28},{14,2},{22,4},{2,14},{4,22},{26,8},{28,16},{0,30},{... | collective-permute-start | bytes 294920 | tf_op jit(solution)/shard_map/ppermute | solution.py:524
  21.9 3.4 %collective-permute-start.3 = (bf16[6,64,128]{2,1,0:T(8,128)(2,1)S(1)}, bf16[6,64,128]{2,1,0:T(8,128)(2,1)S(1)}, u32[]{:S(2)}, u32[]{:S(2)}) collective-permute-start(bf16[6,64,128]{2,1,0:T(8,128)(2,1)S(1)} %broadcast_select_fusion.1.refs_1_), channel_id=1, source_target_pairs={{8,2},{16,4},{14,26},{22,28},{2,8},{4,16},{26,14},{28,22},{0,24},{... | collective-permute-start | bytes 294920 | tf_op jit(solution)/shard_map/ppermute | solution.py:524
  25.9 5.5 %collective-permute-start.6 = (bf16[3,64,128]{2,1,0:T(8,128)(2,1)}, bf16[3,64,128]{2,1,0:T(8,128)(2,1)S(1)}, u32[]{:S(2)}, u32[]{:S(2)}) collective-permute-start(bf16[3,64,128]{2,1,0:T(8,128)(2,1)} %get-tuple-element.21), channel_id=1, source_target_pairs={{0,2},{2,0},{4,6},{6,4},{8,10},{10,8},{12,14},{14,12},{16,18},{18,... | collective-permute-start | bytes 147464 | tf_op jit(solution)/shard_map/ppermute | solution.py:524
  31.4 2.2 %setup.1 = (s32[20,12]{1,0:T(8,128)}, bf16[192,384]{1,0:T(8,128)(2,1)}, bf16[192,384]{1,0:T(8,128)(2,1)}) custom-call(s32[3,4,12]{2,1,0:T(4,128)} %bitcast.23, s32[4,2,12]{2,1,0:T(2,128)} %bitcast.24, bf16[3,3,128,128]{3,2,1,0:T(8,128)(2,1)} %refs_2_.2), custom_call_target="tpu_custom_call" | custom-call | tf_op jit(solution)/shard_map/setup/pallas_call | solution.py:452
  34.4 2.6 %halo.2.refs_2_.refs_4_ = bf16[13,64,128]{2,1,0:T(8,128)(2,1)} custom-call(s32[20,12]{1,0:T(8,128)} %get-tuple-element.17.refs_0_, bf16[6,64,128]{2,1,0:T(8,128)(2,1)} %copy-done.8, bf16[6,64,128]{2,1,0:T(8,128)(2,1)} %copy-done.13, bf16[6,64,128]{2,1,0:T(8,128)(2,1)} %copy-done.11, bf16[6,64,128]{2,1,0:T(8,128)(2,1)} %copy-done.10, ...), custom_call_target="tpu_custom_call" | custom-call | tf_op jit(solution)/shard_map/halo/pallas_call | solution.py:191
  37.5 7.8 %collective-permute-done.7.refs_3_.refs_5_ = bf16[13,64,128]{2,1,0:T(8,128)(2,1)S(1)} collective-permute-done((bf16[13,64,128]{2,1,0:T(8,128)(2,1)}, bf16[13,64,128]{2,1,0:T(8,128)(2,1)S(1)}, u32[]{:S(2)}, u32[]{:S(2)}) %collective-permute-start.7) | collective-permute-done | bytes 213024 | tf_op jit(solution)/shard_map/ppermute | solution.py:465
  45.3 0.7 copy-done.2
  46.5 9.4 %forward.1 = (bf16[12,64,1024]{2,1,0:T(8,128)(2,1)}, bf16[12,64,1024]{2,1,0:T(8,128)(2,1)}, bf16[6,64,128]{2,1,0:T(8,128)(2,1)}, bf16[3,64,128]{2,1,0:T(8,128)(2...) custom-call(bf16[12,64,1024]{2,1,0:T(8,128)(2,1)} %bitcast.20, ...), custom_call_target="tpu_custom_call" | custom-call | tf_op jit(solution)/shard_map/forward/pallas_call | solution.py:318
  57.2 6.2 %all-to-all-start.1 = ((bf16[16,32,128]{2,1,0:T(8,128)(2,1)}), bf16[16,32,128]{2,1,0:T(8,128)(2,1)S(1)}, u32[]{:S(2)}, u32[]{:S(2)}) async-start(bf16[16,32,128]{2,1,0:T(8,128)(2,1)} %get-tuple-element.30), calls=%async_computation.1 | async-start | bytes 262144 | tf_op jit(solution)/shard_map/all_to_all | solution.py:545
  63.4 1.9 %collective-permute-start.13 = (bf16[3,64,128]{2,1,0:T(8,128)(2,1)}, bf16[3,64,128]{2,1,0:T(8,128)(2,1)S(1)}, u32[]{:S(2)}, u32[]{:S(2)}) collective-permute-start(bf16[3,64,128]{2,1,0:T(8,128)(2,1)} %get-tuple-element.28), channel_id=1, source_target_pairs={{0,8},{2,10},{4,12},{6,14},{8,0},{10,2},{12,4},{14,6},{16,24},{18,... | collective-permute-start | bytes 147464 | tf_op jit(solution)/shard_map/ppermute | solution.py:524
  65.4 1.0 broadcast_select_fusion.refs_1_
  66.4 4.6 %collective-permute-start.12 = (bf16[6,64,128]{2,1,0:T(8,128)(2,1)S(1)}, bf16[6,64,128]{2,1,0:T(8,128)(2,1)S(1)}, u32[]{:S(2)}, u32[]{:S(2)}) collective-permute-start(bf16[6,64,128]{2,1,0:T(8,128)(2,1)S(1)} %broadcast_select_fusion.refs_1_), channel_id=1, source_target_pairs={{8,26},{16,28},{14,2},{22,4},{2,14},{4,22},{26,8},{28,16},{0,30},{... | collective-permute-start | bytes 294920 | tf_op jit(solution)/shard_map/ppermute | solution.py:524
  71.0 3.4 %collective-permute-start.11 = (bf16[6,64,128]{2,1,0:T(8,128)(2,1)S(1)}, bf16[6,64,128]{2,1,0:T(8,128)(2,1)S(1)}, u32[]{:S(2)}, u32[]{:S(2)}) collective-permute-start(bf16[6,64,128]{2,1,0:T(8,128)(2,1)S(1)} %broadcast_select_fusion.refs_1_), channel_id=1, source_target_pairs={{8,2},{16,4},{14,26},{22,28},{2,8},{4,16},{26,14},{28,22},{0,24},{... | collective-permute-start | bytes 294920 | tf_op jit(solution)/shard_map/ppermute | solution.py:524
  75.0 1.4 %collective-permute-done.14.refs_7_ = bf16[3,64,128]{2,1,0:T(8,128)(2,1)S(1)} collective-permute-done((bf16[3,64,128]{2,1,0:T(8,128)(2,1)}, bf16[3,64,128]{2,1,0:T(8,128)(2,1)S(1)}, u32[]{:S(2)}, u32[]{:S(2)}) %collective-permute-start.14) | collective-permute-done | bytes 49184 | tf_op jit(solution)/shard_map/ppermute | solution.py:524
  76.5 2.9 %collective-permute-done.11.refs_3_ = bf16[6,64,128]{2,1,0:T(8,128)(2,1)S(1)} collective-permute-done((bf16[6,64,128]{2,1,0:T(8,128)(2,1)S(1)}, bf16[6,64,128]{2,1,0:T(8,128)(2,1)S(1)}, u32[]{:S(2)}, u32[]{:S(2)}) %collective-permute-start.11) | collective-permute-done | bytes 98336 | tf_op jit(solution)/shard_map/ppermute | solution.py:524
  80.7 2.6 %halo.3.refs_2_.refs_4_ = bf16[13,64,128]{2,1,0:T(8,128)(2,1)} custom-call(s32[20,12]{1,0:T(8,128)} %get-tuple-element.17.refs_0_, bf16[6,64,128]{2,1,0:T(8,128)(2,1)} %copy-done.9, bf16[6,64,128]{2,1,0:T(8,128)(2,1)} %copy-done.15, bf16[6,64,128]{2,1,0:T(8,128)(2,1)} %copy-done.14, bf16[6,64,128]{2,1,0:T(8,128)(2,1)} %copy-done.12, ...), custom_call_target="tpu_custom_call" | custom-call | tf_op jit(solution)/shard_map/halo/pallas_call | solution.py:191
  83.3 1.5 %collective-permute-start.15 = (bf16[13,64,128]{2,1,0:T(8,128)(2,1)}, bf16[13,64,128]{2,1,0:T(8,128)(2,1)S(1)}, u32[]{:S(2)}, u32[]{:S(2)}) collective-permute-start(bf16[13,64,128]{2,1,0:T(8,128)(2,1)} %halo.3.refs_2_.refs_4_), channel_id=1, source_target_pairs={{1,0},{0,1},{3,2},{2,3},{5,4},{4,5},{7,6},{6,7},{9,8},{8,9},{11,10... | collective-permute-start | bytes 638984 | tf_op jit(solution)/shard_map/ppermute | solution.py:465
  84.8 12.4 %collective-permute-done.15.refs_3_.refs_5_ = bf16[13,64,128]{2,1,0:T(8,128)(2,1)S(1)} collective-permute-done((bf16[13,64,128]{2,1,0:T(8,128)(2,1)}, bf16[13,64,128]{2,1,0:T(8,128)(2,1)S(1)}, u32[]{:S(2)}, u32[]{:S(2)}) %collective-permute-start.15) | collective-permute-done | bytes 213024 | tf_op jit(solution)/shard_map/ppermute | solution.py:465
  98.4 7.3 %backward.1 = bf16[12,64,1024]{2,1,0:T(8,128)(2,1)} custom-call(bf16[12,64,1024]{2,1,0:T(8,128)(2,1)} %get-tuple-element.25.refs_0_, bf16[12,64,1024]{2,1,0:T(8,128)(2,1)} %copy-done.1, bf16[13,64,128]{2,1,0:T(8,128)(2,1)} %halo.3.refs_2_.refs_4_, bf16[13,64,128]{2,1,0:T(8,128)(2,1)} %copy-done.3, bf16[13,64,128]{2,1,0:T(8,128)(2,1)} %halo.3.refs_2_.refs_4_, ...), custom_call_target="tpu_custom_call" | custom-call | tf_op jit(solution)/shard_map/backward/pallas_call | solution.py:355
  (61 shorter events, 7.5 us)
Async XLA Ops:
  0.6 44.7 %collective-permute-start = (bf16[12,64,1024]{2,1,0:T(8,128)(2,1)}, bf16[12,64,1024]{2,1,0:T(8,128)(2,1)S(1)}, u32[]{:S(2)}, u32[]{:S(2)}) collective-permute-start(bf16[12,64,1024]{2,1,0:T(8,128)(2,1)} %bitcast.18), channel_id=1, source_target_pairs={{1,0},{0,1},{3,2},{2,3},{5,4},{4,5},{7,6},{6,7},{9,8},{8,9},{11,10... | collective-permute-start | bytes 4718600 | tf_op jit(solution)/shard_map/ppermute | solution.py:465
  7.6 26.1 %all-to-all-start = ((bf16[16,32,128]{2,1,0:T(8,128)(2,1)}), bf16[16,32,128]{2,1,0:T(8,128)(2,1)S(1)}, u32[]{:S(2)}, u32[]{:S(2)}) async-start(bf16[16,32,128]{2,1,0:T(8,128)(2,1)} %get-tuple-element.22), calls=%async_computation | async-start | bytes 262144 | tf_op jit(solution)/shard_map/all_to_all | solution.py:545
  13.6 12.3 %collective-permute-start.5 = (bf16[3,64,128]{2,1,0:T(8,128)(2,1)}, bf16[3,64,128]{2,1,0:T(8,128)(2,1)S(1)}, u32[]{:S(2)}, u32[]{:S(2)}) collective-permute-start(bf16[3,64,128]{2,1,0:T(8,128)(2,1)} %get-tuple-element.20), channel_id=1, source_target_pairs={{0,8},{2,10},{4,12},{6,14},{8,0},{10,2},{12,4},{14,6},{16,24},{18,... | collective-permute-start | bytes 147464 | tf_op jit(solution)/shard_map/ppermute | solution.py:524
  15.5 0.7 collective-permute-start.1
  16.2 17.5 %copy-start.6 = (bf16[6,64,128]{2,1,0:T(8,128)(2,1)}, bf16[6,64,128]{2,1,0:T(8,128)(2,1)S(1)}, u32[]{:S(2)}) copy-start(bf16[6,64,128]{2,1,0:T(8,128)(2,1)S(1)} %collective-permute-done.1.refs_5_) | copy-start | bytes 294916
  17.2 16.5 %copy-start.8 = (bf16[6,64,128]{2,1,0:T(8,128)(2,1)}, bf16[6,64,128]{2,1,0:T(8,128)(2,1)S(1)}, u32[]{:S(2)}) copy-start(bf16[6,64,128]{2,1,0:T(8,128)(2,1)S(1)} %broadcast_select_fusion.1.refs_1_) | copy-start | bytes 294916
  17.3 16.4 %collective-permute-start.4 = (bf16[6,64,128]{2,1,0:T(8,128)(2,1)S(1)}, bf16[6,64,128]{2,1,0:T(8,128)(2,1)S(1)}, u32[]{:S(2)}, u32[]{:S(2)}) collective-permute-start(bf16[6,64,128]{2,1,0:T(8,128)(2,1)S(1)} %broadcast_select_fusion.1.refs_1_), channel_id=1, source_target_pairs={{8,26},{16,28},{14,2},{22,4},{2,14},{4,22},{26,8},{28,16},{0,30},{... | collective-permute-start | bytes 294920 | tf_op jit(solution)/shard_map/ppermute | solution.py:524
  21.9 11.7 %collective-permute-start.3 = (bf16[6,64,128]{2,1,0:T(8,128)(2,1)S(1)}, bf16[6,64,128]{2,1,0:T(8,128)(2,1)S(1)}, u32[]{:S(2)}, u32[]{:S(2)}) collective-permute-start(bf16[6,64,128]{2,1,0:T(8,128)(2,1)S(1)} %broadcast_select_fusion.1.refs_1_), channel_id=1, source_target_pairs={{8,2},{16,4},{14,26},{22,28},{2,8},{4,16},{26,14},{28,22},{0,24},{... | collective-permute-start | bytes 294920 | tf_op jit(solution)/shard_map/ppermute | solution.py:524
  25.3 8.4 %collective-permute-start.2 = (bf16[6,64,128]{2,1,0:T(8,128)(2,1)S(1)}, bf16[6,64,128]{2,1,0:T(8,128)(2,1)S(1)}, u32[]{:S(2)}, u32[]{:S(2)}) collective-permute-start(bf16[6,64,128]{2,1,0:T(8,128)(2,1)S(1)} %broadcast_select_fusion.1.refs_1_), channel_id=1, source_target_pairs={{8,14},{16,22},{14,8},{22,16},{2,26},{4,28},{26,2},{28,4},{0,6},{6... | collective-permute-start | bytes 294920 | tf_op jit(solution)/shard_map/ppermute | solution.py:524
  25.9 7.8 %copy-start.16 = (bf16[3,64,128]{2,1,0:T(8,128)(2,1)}, bf16[3,64,128]{2,1,0:T(8,128)(2,1)S(1)}, u32[]{:S(2)}) copy-start(bf16[3,64,128]{2,1,0:T(8,128)(2,1)S(1)} %collective-permute-done.5.refs_6_) | copy-start | bytes 147460
  25.9 7.7 %collective-permute-start.6 = (bf16[3,64,128]{2,1,0:T(8,128)(2,1)}, bf16[3,64,128]{2,1,0:T(8,128)(2,1)S(1)}, u32[]{:S(2)}, u32[]{:S(2)}) collective-permute-start(bf16[3,64,128]{2,1,0:T(8,128)(2,1)} %get-tuple-element.21), channel_id=1, source_target_pairs={{0,2},{2,0},{4,6},{6,4},{8,10},{10,8},{12,14},{14,12},{16,18},{18,... | collective-permute-start | bytes 147464 | tf_op jit(solution)/shard_map/ppermute | solution.py:524
  37.0 8.3 %collective-permute-start.7 = (bf16[13,64,128]{2,1,0:T(8,128)(2,1)}, bf16[13,64,128]{2,1,0:T(8,128)(2,1)S(1)}, u32[]{:S(2)}, u32[]{:S(2)}) collective-permute-start(bf16[13,64,128]{2,1,0:T(8,128)(2,1)} %halo.2.refs_2_.refs_4_), channel_id=1, source_target_pairs={{1,0},{0,1},{3,2},{2,3},{5,4},{4,5},{7,6},{6,7},{9,8},{8,9},{11,10... | collective-permute-start | bytes 638984 | tf_op jit(solution)/shard_map/ppermute | solution.py:465
  55.9 41.2 %collective-permute-start.8 = (bf16[12,64,1024]{2,1,0:T(8,128)(2,1)}, bf16[12,64,1024]{2,1,0:T(8,128)(2,1)S(1)}, u32[]{:S(2)}, u32[]{:S(2)}) collective-permute-start(bf16[12,64,1024]{2,1,0:T(8,128)(2,1)} %get-tuple-element.25.refs_0_), channel_id=1, source_target_pairs={{1,0},{0,1},{3,2},{2,3},{5,4},{4,5},{7,6},{6,7},{9,8},{8,9},{11,10... | collective-permute-start | bytes 4718600 | tf_op jit(solution)/shard_map/ppermute | solution.py:465
  56.6 8.8 %collective-permute-start.9 = (bf16[6,64,128]{2,1,0:T(8,128)(2,1)}, bf16[6,64,128]{2,1,0:T(8,128)(2,1)S(1)}, u32[]{:S(2)}, u32[]{:S(2)}) collective-permute-start(bf16[6,64,128]{2,1,0:T(8,128)(2,1)} %get-tuple-element.26), channel_id=1, source_target_pairs={{8,16},{16,8},{14,22},{22,14},{2,4},{4,2},{26,28},{28,26},{10,18},... | collective-permute-start | bytes 294920 | tf_op jit(solution)/shard_map/ppermute | solution.py:524
  57.2 22.2 %all-to-all-start.1 = ((bf16[16,32,128]{2,1,0:T(8,128)(2,1)}), bf16[16,32,128]{2,1,0:T(8,128)(2,1)S(1)}, u32[]{:S(2)}, u32[]{:S(2)}) async-start(bf16[16,32,128]{2,1,0:T(8,128)(2,1)} %get-tuple-element.30), calls=%async_computation.1 | async-start | bytes 262144 | tf_op jit(solution)/shard_map/all_to_all | solution.py:545
  63.4 11.6 %collective-permute-start.13 = (bf16[3,64,128]{2,1,0:T(8,128)(2,1)}, bf16[3,64,128]{2,1,0:T(8,128)(2,1)S(1)}, u32[]{:S(2)}, u32[]{:S(2)}) collective-permute-start(bf16[3,64,128]{2,1,0:T(8,128)(2,1)} %get-tuple-element.28), channel_id=1, source_target_pairs={{0,8},{2,10},{4,12},{6,14},{8,0},{10,2},{12,4},{14,6},{16,24},{18,... | collective-permute-start | bytes 147464 | tf_op jit(solution)/shard_map/ppermute | solution.py:524
  65.4 14.1 %copy-start.7 = (bf16[6,64,128]{2,1,0:T(8,128)(2,1)}, bf16[6,64,128]{2,1,0:T(8,128)(2,1)S(1)}, u32[]{:S(2)}) copy-start(bf16[6,64,128]{2,1,0:T(8,128)(2,1)S(1)} %collective-permute-done.9.refs_5_) | copy-start | bytes 294916
  66.4 13.0 %copy-start.9 = (bf16[6,64,128]{2,1,0:T(8,128)(2,1)}, bf16[6,64,128]{2,1,0:T(8,128)(2,1)S(1)}, u32[]{:S(2)}) copy-start(bf16[6,64,128]{2,1,0:T(8,128)(2,1)S(1)} %broadcast_select_fusion.refs_1_) | copy-start | bytes 294916
  66.4 10.1 %collective-permute-start.12 = (bf16[6,64,128]{2,1,0:T(8,128)(2,1)S(1)}, bf16[6,64,128]{2,1,0:T(8,128)(2,1)S(1)}, u32[]{:S(2)}, u32[]{:S(2)}) collective-permute-start(bf16[6,64,128]{2,1,0:T(8,128)(2,1)S(1)} %broadcast_select_fusion.refs_1_), channel_id=1, source_target_pairs={{8,26},{16,28},{14,2},{22,4},{2,14},{4,22},{26,8},{28,16},{0,30},{... | collective-permute-start | bytes 294920 | tf_op jit(solution)/shard_map/ppermute | solution.py:524
  71.0 8.4 %collective-permute-start.11 = (bf16[6,64,128]{2,1,0:T(8,128)(2,1)S(1)}, bf16[6,64,128]{2,1,0:T(8,128)(2,1)S(1)}, u32[]{:S(2)}, u32[]{:S(2)}) collective-permute-start(bf16[6,64,128]{2,1,0:T(8,128)(2,1)S(1)} %broadcast_select_fusion.refs_1_), channel_id=1, source_target_pairs={{8,2},{16,4},{14,26},{22,28},{2,8},{4,16},{26,14},{28,22},{0,24},{... | collective-permute-start | bytes 294920 | tf_op jit(solution)/shard_map/ppermute | solution.py:524
  74.4 5.0 %collective-permute-start.10 = (bf16[6,64,128]{2,1,0:T(8,128)(2,1)S(1)}, bf16[6,64,128]{2,1,0:T(8,128)(2,1)S(1)}, u32[]{:S(2)}, u32[]{:S(2)}) collective-permute-start(bf16[6,64,128]{2,1,0:T(8,128)(2,1)S(1)} %broadcast_select_fusion.refs_1_), channel_id=1, source_target_pairs={{8,14},{16,22},{14,8},{22,16},{2,26},{4,28},{26,2},{28,4},{0,6},{6... | collective-permute-start | bytes 294920 | tf_op jit(solution)/shard_map/ppermute | solution.py:524
  75.0 4.4 %copy-start.17 = (bf16[3,64,128]{2,1,0:T(8,128)(2,1)}, bf16[3,64,128]{2,1,0:T(8,128)(2,1)S(1)}, u32[]{:S(2)}) copy-start(bf16[3,64,128]{2,1,0:T(8,128)(2,1)S(1)} %collective-permute-done.13.refs_6_) | copy-start | bytes 147460
  75.0 1.4 %collective-permute-start.14 = (bf16[3,64,128]{2,1,0:T(8,128)(2,1)}, bf16[3,64,128]{2,1,0:T(8,128)(2,1)S(1)}, u32[]{:S(2)}, u32[]{:S(2)}) collective-permute-start(bf16[3,64,128]{2,1,0:T(8,128)(2,1)} %get-tuple-element.29), channel_id=1, source_target_pairs={{0,2},{2,0},{4,6},{6,4},{8,10},{10,8},{12,14},{14,12},{16,18},{18,... | collective-permute-start | bytes 147464 | tf_op jit(solution)/shard_map/ppermute | solution.py:524
  83.3 13.8 %collective-permute-start.15 = (bf16[13,64,128]{2,1,0:T(8,128)(2,1)}, bf16[13,64,128]{2,1,0:T(8,128)(2,1)S(1)}, u32[]{:S(2)}, u32[]{:S(2)}) collective-permute-start(bf16[13,64,128]{2,1,0:T(8,128)(2,1)} %halo.3.refs_2_.refs_4_), channel_id=1, source_target_pairs={{1,0},{0,1},{3,2},{2,3},{5,4},{4,5},{7,6},{6,7},{9,8},{8,9},{11,10... | collective-permute-start | bytes 638984 | tf_op jit(solution)/shard_map/ppermute | solution.py:465
  (14 other events, 15.1 us)

commit v10 on v9

--- a/solution.py
+++ b/solution.py
@@ -9,7 +9,7 @@
 RB = 32
 GROUP = 4
 LANES = 128
-CALLS = (3,)
+CALLS = (2, 1)
 VMEM_LIMIT = 60 * 1024 * 1024
 STRIP_LANE = (96, 0, 32, 64)
 

time: 106 us -> 107 us (level)
  waiting for transfers between devices: 24.5 us -> 18.9 us
  Pallas kernels: 28.1 us -> 32.8 us
    ppermute x4 -> x5, waiting for transfers between devices: 20.1 us -> 14.1 us  [from_others(): lax.ppermute(array, 'ch', [((i + k) % ch_count, i) for i in range(ch_coun...]
    pallas_call x1 -> x2, Pallas kernels: 9.42 us -> 11.9 us  [forward(): pl.pallas_call(lambda *refs: forward_kernel(first, count, steps, pieces,...]
    pallas_call x1 -> x2, Pallas kernels: 7.3 us -> 9.43 us  [backward(): pl.pallas_call(lambda *refs: backward_kernel(first, pieces, *refs), grid=...]
    unnamed x40 -> x42, local copies, waits for them, and re-layouts: 4.42 us -> 5 us
    ppermute x4 -> x5, starting transfers between devices: 5.65 us -> 6.18 us  [from_others(): lax.ppermute(array, 'ch', [((i + k) % ch_count, i) for i in range(ch_coun...]
  transfers between devices with their start and end apart: 18 -> 19, of which waited for: 4 -> 4; matrix products, arithmetic and copies ran while one was open for 2% -> 2% of each run, Pallas kernels for 11% -> 21%
where the time goes in v10:
time: 107 us; the launch traced here: 106 us
  starting transfers between devices  46.4 us (43%)
  Pallas kernels  32.8 us (31%)
  waiting for transfers between devices  18.9 us (18%)
  local copies, waits for them, and re-layouts  5 us (5%)
  other arithmetic  2.03 us (2%)
    ppermute x12, starting transfers between devices, exchange(): lax.ppermute(array, axes, [(a[0] * 4 + a[1], b[0] * 4 + b[1]) for a, b in...  28.1 us
    ppermute x5, waiting for transfers between devices, from_others(): lax.ppermute(array, 'ch', [((i + k) % ch_count, i) for i in range(ch_coun...  14.1 us
    all_to_all x2, starting transfers between devices, exchange(): ends_of = lax.all_to_all(corner, axes, 0, 0, tiled=True)  12.1 us
    pallas_call x2, Pallas kernels, forward(): pl.pallas_call(lambda *refs: forward_kernel(first, count, steps, pieces,...  11.9 us
    pallas_call x2, Pallas kernels, backward(): pl.pallas_call(lambda *refs: backward_kernel(first, pieces, *refs), grid=...  9.43 us
    ppermute x5, starting transfers between devices, from_others(): lax.ppermute(array, 'ch', [((i + k) % ch_count, i) for i in range(ch_coun...  6.18 us
    pallas_call x2, Pallas kernels, assemble_halo(): pl.pallas_call(lambda *refs: halo_kernel(faces, units, unit, plan, *refs)...  5.21 us
    unnamed x42, local copies, waits for them, and re-layouts  5 us
  transfers between devices with their start and end apart: 19, of which 4 were waited for; matrix products, arithmetic and copies ran while one was open for 2% of the time, Pallas kernels for 21%

profile of v10, /device:TPU:0, one launch (start us, length us, event | category | flops | bytes accessed | tf_op | source)
XLA Modules:
  0.0 106.1 jit_solution(7470616236395695879)
XLA Ops:
  0.6 3.0 %collective-permute-start = (bf16[12,64,1024]{2,1,0:T(8,128)(2,1)}, bf16[12,64,1024]{2,1,0:T(8,128)(2,1)S(1)}, u32[]{:S(2)}, u32[]{:S(2)}) collective-permute-start(bf16[12,64,1024]{2,1,0:T(8,128)(2,1)} %bitcast.18), channel_id=1, source_target_pairs={{1,0},{0,1},{3,2},{2,3},{5,4},{4,5},{7,6},{6,7},{9,8},{8,9},{11,10... | collective-permute-start | bytes 4718600 | tf_op jit(solution)/shard_map/ppermute | solution.py:465
  3.6 4.0 %rings.1 = (bf16[6,64,128]{2,1,0:T(8,128)(2,1)}, bf16[3,64,128]{2,1,0:T(8,128)(2,1)}, bf16[3,64,128]{2,1,0:T(8,128)(2,1)}, bf16[6,64,128]{2,1,0:T(8,128)(2,1)}, bf16[16,32,128]{2,1,0:T(8,128)(2,1)}) custom-call(bf16[12,64,1024]{2,1,0:T(8,128)(2,1)} %bitcast.19, bf16[1024,128]{1,0:T(8,128)(2,1)} %constant.33.clone.refs_1_.refs_9_, ...), custom_call_target="tpu_custom_call" | custom-call | tf_op jit(solution)/shard_map/rings/pallas_call | solution.py:127
  7.6 5.9 %all-to-all-start = ((bf16[16,32,128]{2,1,0:T(8,128)(2,1)}), bf16[16,32,128]{2,1,0:T(8,128)(2,1)S(1)}, u32[]{:S(2)}, u32[]{:S(2)}) async-start(bf16[16,32,128]{2,1,0:T(8,128)(2,1)} %get-tuple-element.26), calls=%async_computation | async-start | bytes 262144 | tf_op jit(solution)/shard_map/all_to_all | solution.py:545
  13.6 1.9 %collective-permute-start.5 = (bf16[3,64,128]{2,1,0:T(8,128)(2,1)}, bf16[3,64,128]{2,1,0:T(8,128)(2,1)S(1)}, u32[]{:S(2)}, u32[]{:S(2)}) collective-permute-start(bf16[3,64,128]{2,1,0:T(8,128)(2,1)} %get-tuple-element.24), channel_id=1, source_target_pairs={{0,8},{2,10},{4,12},{6,14},{8,0},{10,2},{12,4},{14,6},{16,24},{18,... | collective-permute-start | bytes 147464 | tf_op jit(solution)/shard_map/ppermute | solution.py:524
  16.2 1.0 broadcast_select_fusion.1.refs_1_
  17.3 4.6 %collective-permute-start.4 = (bf16[6,64,128]{2,1,0:T(8,128)(2,1)S(1)}, bf16[6,64,128]{2,1,0:T(8,128)(2,1)S(1)}, u32[]{:S(2)}, u32[]{:S(2)}) collective-permute-start(bf16[6,64,128]{2,1,0:T(8,128)(2,1)S(1)} %broadcast_select_fusion.1.refs_1_), channel_id=1, source_target_pairs={{8,26},{16,28},{14,2},{22,4},{2,14},{4,22},{26,8},{28,16},{0,30},{... | collective-permute-start | bytes 294920 | tf_op jit(solution)/shard_map/ppermute | solution.py:524
  21.9 3.4 %collective-permute-start.3 = (bf16[6,64,128]{2,1,0:T(8,128)(2,1)S(1)}, bf16[6,64,128]{2,1,0:T(8,128)(2,1)S(1)}, u32[]{:S(2)}, u32[]{:S(2)}) collective-permute-start(bf16[6,64,128]{2,1,0:T(8,128)(2,1)S(1)} %broadcast_select_fusion.1.refs_1_), channel_id=1, source_target_pairs={{8,2},{16,4},{14,26},{22,28},{2,8},{4,16},{26,14},{28,22},{0,24},{... | collective-permute-start | bytes 294920 | tf_op jit(solution)/shard_map/ppermute | solution.py:524
  25.9 5.5 %collective-permute-start.6 = (bf16[3,64,128]{2,1,0:T(8,128)(2,1)}, bf16[3,64,128]{2,1,0:T(8,128)(2,1)S(1)}, u32[]{:S(2)}, u32[]{:S(2)}) collective-permute-start(bf16[3,64,128]{2,1,0:T(8,128)(2,1)} %get-tuple-element.25), channel_id=1, source_target_pairs={{0,2},{2,0},{4,6},{6,4},{8,10},{10,8},{12,14},{14,12},{16,18},{18,... | collective-permute-start | bytes 147464 | tf_op jit(solution)/shard_map/ppermute | solution.py:524
  31.4 2.2 %setup.1 = (s32[20,12]{1,0:T(8,128)}, bf16[192,384]{1,0:T(8,128)(2,1)}, bf16[192,384]{1,0:T(8,128)(2,1)}) custom-call(s32[3,4,12]{2,1,0:T(4,128)} %bitcast.26, s32[4,2,12]{2,1,0:T(2,128)} %bitcast.27, bf16[3,3,128,128]{3,2,1,0:T(8,128)(2,1)} %refs_2_.2), custom_call_target="tpu_custom_call" | custom-call | tf_op jit(solution)/shard_map/setup/pallas_call | solution.py:452
  34.4 2.6 %halo.2.refs_2_.refs_4_ = bf16[13,64,128]{2,1,0:T(8,128)(2,1)} custom-call(s32[20,12]{1,0:T(8,128)} %get-tuple-element.21.refs_0_, bf16[6,64,128]{2,1,0:T(8,128)(2,1)} %copy-done.9, bf16[6,64,128]{2,1,0:T(8,128)(2,1)} %copy-done.13, bf16[6,64,128]{2,1,0:T(8,128)(2,1)} %copy-done.12, bf16[6,64,128]{2,1,0:T(8,128)(2,1)} %copy-done.11, ...), custom_call_target="tpu_custom_call" | custom-call | tf_op jit(solution)/shard_map/halo/pallas_call | solution.py:191
  37.5 7.8 %collective-permute-done.7.refs_3_.refs_5_ = bf16[13,64,128]{2,1,0:T(8,128)(2,1)S(1)} collective-permute-done((bf16[13,64,128]{2,1,0:T(8,128)(2,1)}, bf16[13,64,128]{2,1,0:T(8,128)(2,1)S(1)}, u32[]{:S(2)}, u32[]{:S(2)}) %collective-permute-start.7) | collective-permute-done | bytes 213024 | tf_op jit(solution)/shard_map/ppermute | solution.py:465
  46.5 7.1 %forward.2 = (bf16[12,64,1024]{2,1,0:T(8,128)(2,1)}, bf16[8,64,1024]{2,1,0:T(8,128)(2,1)}, bf16[12,64,128]{2,1,0:T(8,128)(2,1)}, bf16[1,64,128]{2,1,0:T(8,128)(2,1)}) custom-call(bf16[12,64,1024]{2,1,0:T(8,128)(2,1)} %bitcast.20, bf16[12,64,1024]{2,1,0:T(8,128)(2,1)} %copy-done, bf16[13,64,128]{2,1,0:T(8,128)(2,1)} %halo.2.refs_2_.refs_4_, ...), custom_call_target="tpu_custom_call" | custom-call | tf_op jit(solution)/shard_map/forward/pallas_call | solution.py:318
  54.2 4.9 %forward.3 = (bf16[12,64,1024]{2,1,0:T(8,128)(2,1)}, bf16[4,64,1024]{2,1,0:T(8,128)(2,1)}, bf16[6,64,128]{2,1,0:T(8,128)(2,1)}, bf16[3,64,128]{2,1,0:T(8,128)(2,...) custom-call(bf16[12,64,1024]{2,1,0:T(8,128)(2,1)} %bitcast.21, ...), custom_call_target="tpu_custom_call", output_to_operand_aliasing={{0}: (13, {})} | custom-call | tf_op jit(solution)/shard_map/forward/pallas_call | solution.py:318
  59.7 6.2 %all-to-all-start.1 = ((bf16[16,32,128]{2,1,0:T(8,128)(2,1)}), bf16[16,32,128]{2,1,0:T(8,128)(2,1)S(1)}, u32[]{:S(2)}, u32[]{:S(2)}) async-start(bf16[16,32,128]{2,1,0:T(8,128)(2,1)} %get-tuple-element.37), calls=%async_computation.1 | async-start | bytes 262144 | tf_op jit(solution)/shard_map/all_to_all | solution.py:545
  65.9 1.9 %collective-permute-start.13 = (bf16[3,64,128]{2,1,0:T(8,128)(2,1)}, bf16[3,64,128]{2,1,0:T(8,128)(2,1)S(1)}, u32[]{:S(2)}, u32[]{:S(2)}) collective-permute-start(bf16[3,64,128]{2,1,0:T(8,128)(2,1)} %get-tuple-element.35), channel_id=1, source_target_pairs={{0,8},{2,10},{4,12},{6,14},{8,0},{10,2},{12,4},{14,6},{16,24},{18,... | collective-permute-start | bytes 147464 | tf_op jit(solution)/shard_map/ppermute | solution.py:524
  67.9 1.5 %collective-permute-start.8 = (bf16[4,64,1024]{2,1,0:T(8,128)(2,1)}, bf16[4,64,1024]{2,1,0:T(8,128)(2,1)S(1)}, u32[]{:S(2)}, u32[]{:S(2)}) collective-permute-start(bf16[4,64,1024]{2,1,0:T(8,128)(2,1)} %get-tuple-element.32.refs_0_), channel_id=1, source_target_pairs={{1,0},{0,1},{3,2},{2,3},{5,4},{4,5},{7,6},{6,7},{9,8},{8,9},{11,10... | collective-permute-start | bytes 1572872 | tf_op jit(solution)/shard_map/ppermute | solution.py:465
  69.4 1.0 broadcast_select_fusion.refs_1_
  70.4 5.0 %collective-permute-start.12 = (bf16[6,64,128]{2,1,0:T(8,128)(2,1)S(1)}, bf16[6,64,128]{2,1,0:T(8,128)(2,1)S(1)}, u32[]{:S(2)}, u32[]{:S(2)}) collective-permute-start(bf16[6,64,128]{2,1,0:T(8,128)(2,1)S(1)} %broadcast_select_fusion.refs_1_), channel_id=1, source_target_pairs={{8,26},{16,28},{14,2},{22,4},{2,14},{4,22},{26,8},{28,16},{0,30},{... | collective-permute-start | bytes 294920 | tf_op jit(solution)/shard_map/ppermute | solution.py:524
  75.4 3.5 %collective-permute-start.11 = (bf16[6,64,128]{2,1,0:T(8,128)(2,1)S(1)}, bf16[6,64,128]{2,1,0:T(8,128)(2,1)S(1)}, u32[]{:S(2)}, u32[]{:S(2)}) collective-permute-start(bf16[6,64,128]{2,1,0:T(8,128)(2,1)S(1)} %broadcast_select_fusion.refs_1_), channel_id=1, source_target_pairs={{8,2},{16,4},{14,26},{22,28},{2,8},{4,16},{26,14},{28,22},{0,24},{... | collective-permute-start | bytes 294920 | tf_op jit(solution)/shard_map/ppermute | solution.py:524
  79.6 4.4 %collective-permute-done.11.refs_3_ = bf16[6,64,128]{2,1,0:T(8,128)(2,1)S(1)} collective-permute-done((bf16[6,64,128]{2,1,0:T(8,128)(2,1)S(1)}, bf16[6,64,128]{2,1,0:T(8,128)(2,1)S(1)}, u32[]{:S(2)}, u32[]{:S(2)}) %collective-permute-start.11) | collective-permute-done | bytes 98336 | tf_op jit(solution)/shard_map/ppermute | solution.py:524
  85.3 2.6 %halo.3.refs_2_.refs_4_ = bf16[13,64,128]{2,1,0:T(8,128)(2,1)} custom-call(s32[20,12]{1,0:T(8,128)} %get-tuple-element.21.refs_0_, bf16[6,64,128]{2,1,0:T(8,128)(2,1)} %copy-done.10, bf16[6,64,128]{2,1,0:T(8,128)(2,1)} %copy-done.16, bf16[6,64,128]{2,1,0:T(8,128)(2,1)} %copy-done.15, bf16[6,64,128]{2,1,0:T(8,128)(2,1)} %copy-done.14, ...), custom_call_target="tpu_custom_call" | custom-call | tf_op jit(solution)/shard_map/halo/pallas_call | solution.py:191
  88.5 6.4 %collective-permute-done.15.refs_3_.refs_5_ = bf16[13,64,128]{2,1,0:T(8,128)(2,1)S(1)} collective-permute-done((bf16[13,64,128]{2,1,0:T(8,128)(2,1)}, bf16[13,64,128]{2,1,0:T(8,128)(2,1)S(1)}, u32[]{:S(2)}, u32[]{:S(2)}) %collective-permute-start.15) | collective-permute-done | bytes 213024 | tf_op jit(solution)/shard_map/ppermute | solution.py:465
  95.9 5.6 %backward.2.refs_8_ = bf16[12,64,1024]{2,1,0:T(8,128)(2,1)} custom-call(bf16[8,64,1024]{2,1,0:T(8,128)(2,1)} %get-tuple-element.39.refs_0_, bf16[8,64,1024]{2,1,0:T(8,128)(2,1)} %copy-done.3, bf16[13,64,128]{2,1,0:T(8,128)(2,1)} %halo.3.refs_2_.refs_4_, bf16[13,64,128]{2,1,0:T(8,128)(2,1)} %copy-done.2, bf16[13,64,128]{2,1,0:T(8,128)(2,1)} %halo.3.refs_2_.refs_4_, ...), custom_call_target="tpu_custom_call" | custom-call | tf_op jit(solution)/shard_map/backward/pallas_call | solution.py:355
  102.2 3.9 %backward.3 = bf16[12,64,1024]{2,1,0:T(8,128)(2,1)} custom-call(bf16[4,64,1024]{2,1,0:T(8,128)(2,1)} %get-tuple-element.32.refs_0_, bf16[4,64,1024]{2,1,0:T(8,128)(2,1)} %copy-done.6, bf16[13,64,128]{2,1,0:T(8,128)(2,1)} %halo.3.refs_2_.refs_4_, bf16[13,64,128]{2,1,0:T(8,128)(2,1)} %copy-done.2, ...), custom_call_target="tpu_custom_call", output_to_operand_aliasing={{}: (8, {})} | custom-call | tf_op jit(solution)/shard_map/backward/pallas_call | solution.py:355
  (67 shorter events, 9.2 us)
Async XLA Ops:
  0.6 44.7 %collective-permute-start = (bf16[12,64,1024]{2,1,0:T(8,128)(2,1)}, bf16[12,64,1024]{2,1,0:T(8,128)(2,1)S(1)}, u32[]{:S(2)}, u32[]{:S(2)}) collective-permute-start(bf16[12,64,1024]{2,1,0:T(8,128)(2,1)} %bitcast.18), channel_id=1, source_target_pairs={{1,0},{0,1},{3,2},{2,3},{5,4},{4,5},{7,6},{6,7},{9,8},{8,9},{11,10... | collective-permute-start | bytes 4718600 | tf_op jit(solution)/shard_map/ppermute | solution.py:465
  7.6 26.1 %all-to-all-start = ((bf16[16,32,128]{2,1,0:T(8,128)(2,1)}), bf16[16,32,128]{2,1,0:T(8,128)(2,1)S(1)}, u32[]{:S(2)}, u32[]{:S(2)}) async-start(bf16[16,32,128]{2,1,0:T(8,128)(2,1)} %get-tuple-element.26), calls=%async_computation | async-start | bytes 262144 | tf_op jit(solution)/shard_map/all_to_all | solution.py:545
  13.6 12.3 %collective-permute-start.5 = (bf16[3,64,128]{2,1,0:T(8,128)(2,1)}, bf16[3,64,128]{2,1,0:T(8,128)(2,1)S(1)}, u32[]{:S(2)}, u32[]{:S(2)}) collective-permute-start(bf16[3,64,128]{2,1,0:T(8,128)(2,1)} %get-tuple-element.24), channel_id=1, source_target_pairs={{0,8},{2,10},{4,12},{6,14},{8,0},{10,2},{12,4},{14,6},{16,24},{18,... | collective-permute-start | bytes 147464 | tf_op jit(solution)/shard_map/ppermute | solution.py:524
  15.5 0.7 collective-permute-start.1
  16.2 17.5 %copy-start.7 = (bf16[6,64,128]{2,1,0:T(8,128)(2,1)}, bf16[6,64,128]{2,1,0:T(8,128)(2,1)S(1)}, u32[]{:S(2)}) copy-start(bf16[6,64,128]{2,1,0:T(8,128)(2,1)S(1)} %collective-permute-done.1.refs_5_) | copy-start | bytes 294916
  17.2 16.5 %copy-start.9 = (bf16[6,64,128]{2,1,0:T(8,128)(2,1)}, bf16[6,64,128]{2,1,0:T(8,128)(2,1)S(1)}, u32[]{:S(2)}) copy-start(bf16[6,64,128]{2,1,0:T(8,128)(2,1)S(1)} %broadcast_select_fusion.1.refs_1_) | copy-start | bytes 294916
  17.3 16.4 %collective-permute-start.4 = (bf16[6,64,128]{2,1,0:T(8,128)(2,1)S(1)}, bf16[6,64,128]{2,1,0:T(8,128)(2,1)S(1)}, u32[]{:S(2)}, u32[]{:S(2)}) collective-permute-start(bf16[6,64,128]{2,1,0:T(8,128)(2,1)S(1)} %broadcast_select_fusion.1.refs_1_), channel_id=1, source_target_pairs={{8,26},{16,28},{14,2},{22,4},{2,14},{4,22},{26,8},{28,16},{0,30},{... | collective-permute-start | bytes 294920 | tf_op jit(solution)/shard_map/ppermute | solution.py:524
  21.9 11.7 %collective-permute-start.3 = (bf16[6,64,128]{2,1,0:T(8,128)(2,1)S(1)}, bf16[6,64,128]{2,1,0:T(8,128)(2,1)S(1)}, u32[]{:S(2)}, u32[]{:S(2)}) collective-permute-start(bf16[6,64,128]{2,1,0:T(8,128)(2,1)S(1)} %broadcast_select_fusion.1.refs_1_), channel_id=1, source_target_pairs={{8,2},{16,4},{14,26},{22,28},{2,8},{4,16},{26,14},{28,22},{0,24},{... | collective-permute-start | bytes 294920 | tf_op jit(solution)/shard_map/ppermute | solution.py:524
  25.3 8.4 %collective-permute-start.2 = (bf16[6,64,128]{2,1,0:T(8,128)(2,1)S(1)}, bf16[6,64,128]{2,1,0:T(8,128)(2,1)S(1)}, u32[]{:S(2)}, u32[]{:S(2)}) collective-permute-start(bf16[6,64,128]{2,1,0:T(8,128)(2,1)S(1)} %broadcast_select_fusion.1.refs_1_), channel_id=1, source_target_pairs={{8,14},{16,22},{14,8},{22,16},{2,26},{4,28},{26,2},{28,4},{0,6},{6... | collective-permute-start | bytes 294920 | tf_op jit(solution)/shard_map/ppermute | solution.py:524
  25.9 7.7 %collective-permute-start.6 = (bf16[3,64,128]{2,1,0:T(8,128)(2,1)}, bf16[3,64,128]{2,1,0:T(8,128)(2,1)S(1)}, u32[]{:S(2)}, u32[]{:S(2)}) collective-permute-start(bf16[3,64,128]{2,1,0:T(8,128)(2,1)} %get-tuple-element.25), channel_id=1, source_target_pairs={{0,2},{2,0},{4,6},{6,4},{8,10},{10,8},{12,14},{14,12},{16,18},{18,... | collective-permute-start | bytes 147464 | tf_op jit(solution)/shard_map/ppermute | solution.py:524
  37.0 8.3 %collective-permute-start.7 = (bf16[13,64,128]{2,1,0:T(8,128)(2,1)}, bf16[13,64,128]{2,1,0:T(8,128)(2,1)S(1)}, u32[]{:S(2)}, u32[]{:S(2)}) collective-permute-start(bf16[13,64,128]{2,1,0:T(8,128)(2,1)} %halo.2.refs_2_.refs_4_), channel_id=1, source_target_pairs={{1,0},{0,1},{3,2},{2,3},{5,4},{4,5},{7,6},{6,7},{9,8},{8,9},{11,10... | collective-permute-start | bytes 638984 | tf_op jit(solution)/shard_map/ppermute | solution.py:465
  53.6 41.2 %collective-permute-start.16 = (bf16[8,64,1024]{2,1,0:T(8,128)(2,1)}, bf16[8,64,1024]{2,1,0:T(8,128)(2,1)S(1)}, u32[]{:S(2)}, u32[]{:S(2)}) collective-permute-start(bf16[8,64,1024]{2,1,0:T(8,128)(2,1)} %get-tuple-element.39.refs_0_), channel_id=1, source_target_pairs={{1,0},{0,1},{3,2},{2,3},{5,4},{4,5},{7,6},{6,7},{9,8},{8,9},{11,10... | collective-permute-start | bytes 3145736 | tf_op jit(solution)/shard_map/ppermute | solution.py:465
  59.1 10.3 %collective-permute-start.9 = (bf16[6,64,128]{2,1,0:T(8,128)(2,1)}, bf16[6,64,128]{2,1,0:T(8,128)(2,1)S(1)}, u32[]{:S(2)}, u32[]{:S(2)}) collective-permute-start(bf16[6,64,128]{2,1,0:T(8,128)(2,1)} %get-tuple-element.33), channel_id=1, source_target_pairs={{8,16},{16,8},{14,22},{22,14},{2,4},{4,2},{26,28},{28,26},{10,18},... | collective-permute-start | bytes 294920 | tf_op jit(solution)/shard_map/ppermute | solution.py:524
  59.7 24.3 %all-to-all-start.1 = ((bf16[16,32,128]{2,1,0:T(8,128)(2,1)}), bf16[16,32,128]{2,1,0:T(8,128)(2,1)S(1)}, u32[]{:S(2)}, u32[]{:S(2)}) async-start(bf16[16,32,128]{2,1,0:T(8,128)(2,1)} %get-tuple-element.37), calls=%async_computation.1 | async-start | bytes 262144 | tf_op jit(solution)/shard_map/all_to_all | solution.py:545
  65.9 9.5 %collective-permute-start.13 = (bf16[3,64,128]{2,1,0:T(8,128)(2,1)}, bf16[3,64,128]{2,1,0:T(8,128)(2,1)S(1)}, u32[]{:S(2)}, u32[]{:S(2)}) collective-permute-start(bf16[3,64,128]{2,1,0:T(8,128)(2,1)} %get-tuple-element.35), channel_id=1, source_target_pairs={{0,8},{2,10},{4,12},{6,14},{8,0},{10,2},{12,4},{14,6},{16,24},{18,... | collective-permute-start | bytes 147464 | tf_op jit(solution)/shard_map/ppermute | solution.py:524
  67.9 11.1 %collective-permute-start.14 = (bf16[3,64,128]{2,1,0:T(8,128)(2,1)}, bf16[3,64,128]{2,1,0:T(8,128)(2,1)S(1)}, u32[]{:S(2)}, u32[]{:S(2)}) collective-permute-start(bf16[3,64,128]{2,1,0:T(8,128)(2,1)} %get-tuple-element.36), channel_id=1, source_target_pairs={{0,2},{2,0},{4,6},{6,4},{8,10},{10,8},{12,14},{14,12},{16,18},{18,... | collective-permute-start | bytes 147464 | tf_op jit(solution)/shard_map/ppermute | solution.py:524
  67.9 33.6 %collective-permute-start.8 = (bf16[4,64,1024]{2,1,0:T(8,128)(2,1)}, bf16[4,64,1024]{2,1,0:T(8,128)(2,1)S(1)}, u32[]{:S(2)}, u32[]{:S(2)}) collective-permute-start(bf16[4,64,1024]{2,1,0:T(8,128)(2,1)} %get-tuple-element.32.refs_0_), channel_id=1, source_target_pairs={{1,0},{0,1},{3,2},{2,3},{5,4},{4,5},{7,6},{6,7},{9,8},{8,9},{11,10... | collective-permute-start | bytes 1572872 | tf_op jit(solution)/shard_map/ppermute | solution.py:465
  69.4 14.6 %copy-start.8 = (bf16[6,64,128]{2,1,0:T(8,128)(2,1)}, bf16[6,64,128]{2,1,0:T(8,128)(2,1)S(1)}, u32[]{:S(2)}) copy-start(bf16[6,64,128]{2,1,0:T(8,128)(2,1)S(1)} %collective-permute-done.9.refs_5_) | copy-start | bytes 294916
  70.4 13.6 %copy-start.10 = (bf16[6,64,128]{2,1,0:T(8,128)(2,1)}, bf16[6,64,128]{2,1,0:T(8,128)(2,1)S(1)}, u32[]{:S(2)}) copy-start(bf16[6,64,128]{2,1,0:T(8,128)(2,1)S(1)} %broadcast_select_fusion.refs_1_) | copy-start | bytes 294916
  70.4 9.2 %collective-permute-start.12 = (bf16[6,64,128]{2,1,0:T(8,128)(2,1)S(1)}, bf16[6,64,128]{2,1,0:T(8,128)(2,1)S(1)}, u32[]{:S(2)}, u32[]{:S(2)}) collective-permute-start(bf16[6,64,128]{2,1,0:T(8,128)(2,1)S(1)} %broadcast_select_fusion.refs_1_), channel_id=1, source_target_pairs={{8,26},{16,28},{14,2},{22,4},{2,14},{4,22},{26,8},{28,16},{0,30},{... | collective-permute-start | bytes 294920 | tf_op jit(solution)/shard_map/ppermute | solution.py:524
  75.4 8.6 %copy-start.18 = (bf16[3,64,128]{2,1,0:T(8,128)(2,1)}, bf16[3,64,128]{2,1,0:T(8,128)(2,1)S(1)}, u32[]{:S(2)}) copy-start(bf16[3,64,128]{2,1,0:T(8,128)(2,1)S(1)} %collective-permute-done.13.refs_6_) | copy-start | bytes 147460
  75.4 8.6 %collective-permute-start.11 = (bf16[6,64,128]{2,1,0:T(8,128)(2,1)S(1)}, bf16[6,64,128]{2,1,0:T(8,128)(2,1)S(1)}, u32[]{:S(2)}, u32[]{:S(2)}) collective-permute-start(bf16[6,64,128]{2,1,0:T(8,128)(2,1)S(1)} %broadcast_select_fusion.refs_1_), channel_id=1, source_target_pairs={{8,2},{16,4},{14,26},{22,28},{2,8},{4,16},{26,14},{28,22},{0,24},{... | collective-permute-start | bytes 294920 | tf_op jit(solution)/shard_map/ppermute | solution.py:524
  79.0 5.0 %collective-permute-start.10 = (bf16[6,64,128]{2,1,0:T(8,128)(2,1)S(1)}, bf16[6,64,128]{2,1,0:T(8,128)(2,1)S(1)}, u32[]{:S(2)}, u32[]{:S(2)}) collective-permute-start(bf16[6,64,128]{2,1,0:T(8,128)(2,1)S(1)} %broadcast_select_fusion.refs_1_), channel_id=1, source_target_pairs={{8,14},{16,22},{14,8},{22,16},{2,26},{4,28},{26,2},{28,4},{0,6},{6... | collective-permute-start | bytes 294920 | tf_op jit(solution)/shard_map/ppermute | solution.py:524
  87.9 6.9 %collective-permute-start.15 = (bf16[13,64,128]{2,1,0:T(8,128)(2,1)}, bf16[13,64,128]{2,1,0:T(8,128)(2,1)S(1)}, u32[]{:S(2)}, u32[]{:S(2)}) collective-permute-start(bf16[13,64,128]{2,1,0:T(8,128)(2,1)} %halo.3.refs_2_.refs_4_), channel_id=1, source_target_pairs={{1,0},{0,1},{3,2},{2,3},{5,4},{4,5},{7,6},{6,7},{9,8},{8,9},{11,10... | collective-permute-start | bytes 638984 | tf_op jit(solution)/shard_map/ppermute | solution.py:465
  (16 other events, 27.0 us)
